TPU v7x, 32 devices: a whole 2x2x4 slice. The times are simulated.
32 devices in a mesh: rows: 16 (over z, y, x), cols: 2 (over core).
Axes of the slice: x: 2, y: 2, z: 4, core: 2. Of those that a mesh axis runs over, the one named last changes fastest.
Arguments:
- canvas: bfloat16 [128, 256, 256], P('rows', 'cols'), may hold values from -16 to 16
- conv_weight: bfloat16 [3, 3, 256, 512], replicated, may hold values from -0.125 to 0.125
- conv_bias: bfloat16 [512], replicated, may hold values from -3 to 3
- target_gram: float32 [512, 512], P(('rows', 'cols')), may hold values from -6 to 6
Outputs:
- gram: float32 [512, 512], P(('rows', 'cols'))
- grad_canvas: bfloat16 [128, 256, 256], P('rows', 'cols')
All inputs are finite; a program needn't handle non-finite values.
Results may differ from a plain program's by a relative error of at most 0.009.
Values may be sent and summed in bfloat16 or wider, within the bound.
No kernel may reach another device: no remote copies, remote signals or barrier semaphores. Data moves between devices by JAX's collectives and lax.ppermute only.
A program may use at most 64 MiB of HBM per device.

v0:
```python
import functools
import math

import jax
import jax.numpy as jnp
from jax import lax
from jax.experimental import pallas as pl
from jax.experimental.pallas import tpu as pltpu
from jax.sharding import PartitionSpec as P

gelu_scale = math.sqrt(2.0 / math.pi)
tile = 128
edge = 16
f32, bf16 = jnp.float32, jnp.bfloat16


def tile_pairs(width):
    count = width // tile
    return [(i, j) for i in range(count) for j in range(i, count)]


def swap_rows(pairs, values):
    count = lax.axis_size("rows")

    def perm(low):
        partner = {i: i for i in range(count)}
        partner.update({i: i + 1 for i in low})
        partner.update({i + 1: i for i in low})
        return list(partner.items())

    return [lax.ppermute(value, "rows", perm(low)) for low, value in zip(pairs, values)]


def shift_cols(last, first):
    count = lax.axis_size("cols")
    forward = [(i, i + 1) for i in range(count - 1)]
    backward = [(target, source) for source, target in forward]
    return lax.ppermute(last, "cols", forward), lax.ppermute(first, "cols", backward)


def device_index():
    return lax.axis_index("rows") * lax.axis_size("cols") + lax.axis_index("cols")


def swap(value, bit):
    total = lax.axis_size("rows") * lax.axis_size("cols")
    return lax.ppermute(value, ("rows", "cols"), [(i, i ^ (1 << bit | 1)) for i in range(total)])


def local(body, out_shape, name, *operands, **kwargs):
    return pl.pallas_call(
        body,
        out_shape=out_shape,
        in_specs=[pl.BlockSpec(memory_space=pltpu.VMEM)] * len(operands),
        compiler_params=pltpu.CompilerParams(vmem_limit_bytes=8 * 1024 * 1024),
        name=name,
        **kwargs,
    )(*operands)


def side_of(bit):
    index = device_index()
    if bit > 0:
        return lax.rem(index // (1 << bit), 2)
    bits = (lax.axis_size("rows") * lax.axis_size("cols")).bit_length() - 1
    return lax.rem(sum(lax.rem(index // (1 << k), 2) for k in range(bits)), 2)


def rows_at(index, count):
    return pl.ds(pl.multiple_of(index * count, count), count)


def halve(keep, got, bit):
    half = keep.shape[0] // 2

    def body(keep_ref, got_ref, send_ref, stay_ref):
        side = side_of(bit)
        away, here = rows_at(1 - side, half), rows_at(side, half)
        send_ref[...] = (keep_ref[away, :] + got_ref[away, :].astype(f32)).astype(bf16)
        stay_ref[...] = keep_ref[here, :] + got_ref[here, :].astype(f32)

    shape = (half, keep.shape[1])
    return local(
        body,
        (jax.ShapeDtypeStruct(shape, bf16), jax.ShapeDtypeStruct(shape, f32)),
        "halve",
        keep,
        got,
    )


def add(keep, got):
    def body(keep_ref, got_ref, sum_ref):
        sum_ref[...] = (keep_ref[...].astype(f32) + got_ref[...].astype(f32)).astype(bf16)

    return local(body, jax.ShapeDtypeStruct(got.shape, bf16), "add", keep, got)


def join(mine, other, bit):
    def body(mine_ref, other_ref, both_ref):
        side = side_of(bit)
        both_ref[:, pl.ds(side, 1)] = mine_ref[...][:, None]
        both_ref[:, pl.ds(1 - side, 1)] = other_ref[...][:, None]

    shape = (mine.shape[0], 2, *mine.shape[1:])
    return local(body, jax.ShapeDtypeStruct(shape, mine.dtype), "join", mine, other)


def join_cores(mine, other):
    def body(mine_ref, other_ref, both_ref):
        side = side_of(0)
        for chip in range(mine.shape[0]):
            core = lax.rem(side + chip.bit_count(), 2)
            both_ref[chip, pl.ds(core, 1)] = mine_ref[chip][None]
            both_ref[chip, pl.ds(1 - core, 1)] = other_ref[chip][None]

    shape = (mine.shape[0], 2, *mine.shape[1:])
    return local(body, jax.ShapeDtypeStruct(shape, mine.dtype), "join_cores", mine, other)


def gather_step(rows, bit, after):
    share = rows.shape[-2:]
    send, _ = lax.optimization_barrier((rows, after))
    got = swap(send, bit)
    both = join(send, got, bit) if bit > 0 else join_cores(send, got)
    return both.reshape(-1, *share)


def sum_all(send, keep, rows):
    bits = (lax.axis_size("rows") * lax.axis_size("cols")).bit_length() - 1
    halving = list(range(1, min(3, bits)))
    order = list(reversed(range(bits)))

    def step(value, bit):
        nonlocal rows
        got = swap(value, bit)
        if order:
            rows = gather_step(rows, order.pop(0), value)
        return got

    got = swap(send, 0)
    for bit in halving:
        send, keep = halve(keep, got, bit)
        got = step(send, bit)
    mine = add(keep, got)
    for bit in range(len(halving) + 1, bits):
        mine = add(mine, step(mine, bit))
    for bit in reversed(halving):
        mine = join(mine[None], step(mine, bit)[None], bit).reshape(-1, mine.shape[1])
    other = swap(mine, 0)
    for bit in order:
        rows = gather_step(rows, bit, mine)
    return mine, other, rows


def gelu_pair(value):
    square = value * value
    tangent = jnp.tanh(value * (gelu_scale + gelu_scale * 0.044715 * square))
    half = 0.5 * value
    plus = 0.5 + 0.5 * tangent
    grad = plus + half * (1.0 - tangent * tangent) * (
        gelu_scale + gelu_scale * 3.0 * 0.044715 * square
    )
    return value * plus, grad


def column(value, c):
    return jnp.concatenate([value[r, c : c + 1] for r in range(value.shape[0])], axis=0)


def rim_kernel(canvas_ref, *out_refs):
    cols = canvas_ref.shape[1]
    begin = canvas_ref[:, 0:16, :].astype(f32)
    end = canvas_ref[:, cols - 16 :, :].astype(f32)
    for c in range(2):
        pair = column(begin, c), column(end, 14 + c)
        if len(out_refs) == 1:
            out_refs[0][c] = jnp.where(lax.axis_index("cols") == 0, pair[1], pair[0]).astype(bf16)
        else:
            out_refs[0][c], out_refs[1][c] = pair[0].astype(bf16), pair[1].astype(bf16)


def payload_kernel(canvas_ref, target_ref, *refs):
    even_ref, odd_ref, left_ref, right_ref, half_ref = refs[-5:]
    rows, cols, width = canvas_ref.shape
    half_ref[0] = target_ref[...].astype(bf16)
    if len(refs) == 6:
        here = lax.axis_index("cols")
        other = refs[0][...].astype(f32)
        left_ref[...] = jnp.where(here == 0, 0.0, other).astype(bf16)
        right_ref[...] = jnp.where(here == 0, other, 0.0).astype(bf16)
    else:
        left_ref[...], right_ref[...] = refs[0][...], refs[1][...]
    beyond = [ref[c].astype(f32) for ref in (left_ref, right_ref) for c in range(2)]

    def fill(ref, r):
        for k in range(2):
            ref[k * cols : (k + 1) * cols, :] = canvas_ref[r + k]
        rim = [part[r + k : r + k + 1] for k in range(2) for part in beyond]
        rim = jnp.concatenate([*rim, jnp.zeros((8, width), f32)], axis=0)
        ref[2 * cols :, :] = rim.astype(bf16)

    odd = lax.rem(lax.axis_index("rows"), 2)

    @pl.when(odd == 0)
    def _():
        fill(even_ref, rows - 2)
        fill(odd_ref, 0)

    @pl.when(odd == 1)
    def _():
        fill(even_ref, 0)
        fill(odd_ref, rows - 2)


def fill_row(cat_ref, r, row, before, after):
    cols, width = row.shape
    wide = row.astype(f32)
    place = lax.broadcasted_iota(jnp.int32, (cols, width), 0)
    at = slice(r * cols, (r + 1) * cols)
    moved = jnp.where(place == 0, before, pltpu.roll(wide, 1, 0))
    cat_ref[at, 0:width] = moved.astype(bf16)
    cat_ref[at, width : 2 * width] = row.astype(bf16)
    moved = jnp.where(place == cols - 1, after, pltpu.roll(wide, cols - 1, 0))
    cat_ref[at, 2 * width : 3 * width] = moved.astype(bf16)


def gram_tiles(feat, gram_ref, base_ref=None):
    width = feat.shape[1]
    half = width // 2
    product = functools.partial(
        lax.dot_general,
        dimension_numbers=(((0,), (0,)), ((), ())),
        preferred_element_type=f32,
    )
    upper = product(feat[:, :half], feat)
    lower = product(feat[:, half:], feat[:, half:])
    for n, (i, j) in enumerate(tile_pairs(width)):
        at = slice(n * tile, (n + 1) * tile)
        if i * tile < half:
            part = upper[i * tile : (i + 1) * tile, j * tile : (j + 1) * tile]
        else:
            k, m = i * tile - half, j * tile - half
            part = lower[k : k + tile, m : m + tile]
        gram_ref[at, :] = part if base_ref is None else part + base_ref[at, :]


def inner_kernel(
    shape, own_ref, left_ref, right_ref, kernel_ref, bias_ref,
    feat_ref, slope_ref, gram_ref, row_ref, cat_ref,
):
    row_ref[...] = bias_ref[...].astype(f32).reshape(row_ref.shape)
    tile_rows, tile_cols, in_width, out_width, step = shape
    lefts, rights = left_ref[1].astype(f32), right_ref[0].astype(f32)
    for r in range(tile_rows):
        fill_row(cat_ref, r, own_ref[r], lefts[r : r + 1], rights[r : r + 1])
    bias = row_ref[...]
    root = 1.0 / math.sqrt(out_width)
    span = 3 * in_width
    for h in range(0, tile_rows - 2, step):
        total = bias
        for a in range(3):
            total = total + jnp.dot(
                cat_ref[(h + a) * tile_cols : (h + a + step) * tile_cols, :],
                kernel_ref[a * span : (a + 1) * span, :],
                preferred_element_type=f32,
            )
        features, slope = gelu_pair(total)
        at = slice(h * tile_cols, (h + step) * tile_cols)
        feat_ref[at, :] = features.astype(bf16)
        slope_ref[at, :] = (slope * root).astype(bf16)
    gram_tiles(feat_ref[...], gram_ref)


def outer_kernel(
    shape, own_ref, even_ref, odd_ref, left_ref, right_ref, kernel_ref, bias_ref, base_ref,
    feat_ref, slope_ref, send_ref, keep_ref, cat_ref, edge_ref, low_ref, high_ref, gram_ref,
):
    tile_rows, tile_cols, in_width, out_width, step = shape
    odd = lax.rem(lax.axis_index("rows"), 2)
    row = lax.axis_index("rows")
    low_ref[...] = jnp.where(odd == 0, odd_ref[...], even_ref[...])
    high_ref[...] = jnp.where(odd == 0, even_ref[...], odd_ref[...])

    @pl.when(row == 0)
    def _():
        low_ref[...] = jnp.zeros_like(low_ref)

    @pl.when(row == lax.axis_size("rows") - 1)
    def _():
        high_ref[...] = jnp.zeros_like(high_ref)

    first = (lax.axis_index("rows") > 0).astype(f32)
    last = (lax.axis_index("rows") < lax.axis_size("rows") - 1).astype(f32)
    left = (lax.axis_index("cols") > 0).astype(f32)
    right = (lax.axis_index("cols") < lax.axis_size("cols") - 1).astype(f32)
    main = 2 * tile_cols
    low_rim, high_rim = low_ref[main:, :].astype(f32), high_ref[main:, :].astype(f32)
    own_begin = column(own_ref[:, 0:16, :].astype(f32), 0)
    own_end = column(own_ref[:, tile_cols - 16 :, :].astype(f32), 15)

    def sides(c, own):
        return jnp.concatenate(
            [low_rim[c : c + 1], low_rim[4 + c : 5 + c], own, high_rim[c : c + 1], high_rim[4 + c : 5 + c]],
            axis=0,
        )

    def ends(c, own):
        c16 = c // 16 * 16
        piece = lambda ref, k: ref[k + c16 : k + c16 + 16, :].astype(f32)[c - c16 : c - c16 + 1]
        rows = [piece(low_ref, 0), piece(low_ref, tile_cols), own]
        return jnp.concatenate([*rows, piece(high_ref, 0), piece(high_ref, tile_cols)], axis=0)

    lefts = [
        sides(0, left_ref[0].astype(f32)), sides(1, left_ref[1].astype(f32)), ends(0, own_begin)
    ]
    rights = [
        ends(tile_cols - 1, own_end), sides(2, right_ref[0].astype(f32)), sides(3, right_ref[1].astype(f32))
    ]
    span = 3 * in_width
    lines = [0, 1, 2, 3, tile_rows, tile_rows + 1, tile_rows + 2, tile_rows + 3]
    for r, line in enumerate(lines):
        if line < 2:
            row = low_ref[line * tile_cols : (line + 1) * tile_cols, :]
        elif line < tile_rows + 2:
            row = own_ref[line - 2]
        else:
            k = line - tile_rows - 2
            row = high_ref[k * tile_cols : (k + 1) * tile_cols, :]
        fill_row(cat_ref, r, row, lefts[1][line : line + 1], rights[1][line : line + 1])
    blank = jnp.zeros((edge - tile_rows - 2, in_width), f32)
    for a in range(3):
        for b in range(3):
            piece = jnp.concatenate(
                [lefts[b][a : a + tile_rows + 2], blank, rights[b][a : a + tile_rows + 2], blank],
                axis=0,
            )
            at = (3 * a + b) * in_width
            edge_ref[:, at : at + in_width] = piece.astype(bf16)
    bias = bias_ref[...]
    root = 1.0 / math.sqrt(out_width)
    totals = [bias, bias, bias]
    for a in range(3):
        weights = kernel_ref[a * span : (a + 1) * span, :]
        for k in range(2):
            totals[k] = totals[k] + jnp.dot(
                cat_ref[(4 * k + a) * tile_cols : (4 * k + a + 2) * tile_cols, :],
                weights,
                preferred_element_type=f32,
            )
        totals[2] = totals[2] + jnp.dot(
            edge_ref[:, a * span : (a + 1) * span], weights, preferred_element_type=f32
        )
    for k in range(2):
        features, slope = gelu_pair(totals[k])
        slope = slope * root
        at = k * main
        feat_ref[at : at + main, :] = features.astype(bf16)
        scale = (first, 1.0) if k == 0 else (1.0, last)
        slope_ref[at : at + tile_cols, :] = (slope[:tile_cols] * scale[0]).astype(bf16)
        slope_ref[at + tile_cols : at + main, :] = (slope[tile_cols:] * scale[1]).astype(bf16)
    features, slope = gelu_pair(totals[2])
    line = lax.broadcasted_iota(jnp.int32, (2 * edge, out_width), 0)
    weight = jnp.where(line < edge, left, right)
    weight = jnp.where(line % edge == 0, weight * first, weight)
    weight = jnp.where(line % edge == tile_rows + 1, weight * last, weight)
    feat_ref[2 * main :, :] = features.astype(bf16)
    slope_ref[2 * main :, :] = (slope * root * weight).astype(bf16)
    gram_tiles(feat_ref[tile_cols : 3 * tile_cols, :], gram_ref, base_ref)
    half = send_ref.shape[0]
    side = side_of(0)
    send_ref[...] = gram_ref[rows_at(1 - side, half), :].astype(bf16)
    keep_ref[...] = gram_ref[rows_at(side, half), :]


def backward_kernel(
    shape, pixel_total, mine_ref, other_ref, target_ref, in_feat_ref, in_slope_ref, out_feat_ref, out_slope_ref,
    kernel_ref, own_gram_ref, out_ref, gram_ref, full_ref, sym_ref, cat_ref,
):
    tile_rows, tile_cols, in_width, out_width, step = shape
    half = mine_ref.shape[0]
    side = side_of(0)
    gram_ref[rows_at(side, half), :] = mine_ref[...].astype(f32)
    gram_ref[rows_at(1 - side, half), :] = other_ref[...].astype(f32)
    for n, (i, j) in enumerate(tile_pairs(out_width)):
        at_i, at_j = slice(i * tile, (i + 1) * tile), slice(j * tile, (j + 1) * tile)
        at = slice(n * tile, (n + 1) * tile)
        gram = gram_ref[at, :] * (1.0 / pixel_total)
        both = 2.0 * gram - (target_ref[at_i, at_j].astype(f32) + target_ref[at_j, at_i].astype(f32).T)
        full_ref[at_i, at_j] = gram
        sym_ref[at_i, at_j] = both.astype(bf16)
        if i != j:
            full_ref[at_j, at_i] = gram.T
            sym_ref[at_j, at_i] = both.T.astype(bf16)
    share = own_gram_ref.shape[0]
    start = device_index() * share
    if share % 8 == 0:
        own_gram_ref[...] = full_ref[pl.ds(pl.multiple_of(start, 8), share), :]
    else:
        group = full_ref[pl.ds(pl.multiple_of(start // 8 * 8, 8), 8), :]
        picked = group[0:share]
        for k in range(share, 8, share):
            picked = jnp.where(start % 8 == k, group[k : k + share], picked)
        own_gram_ref[...] = picked

    def grad_of(feat_ref, slope_ref, at):
        product = jnp.dot(feat_ref[at, :], sym_ref[...], preferred_element_type=f32)
        return product * slope_ref[at, :].astype(f32)

    main = 2 * tile_cols
    edges = grad_of(out_feat_ref, out_slope_ref, slice(2 * main, None))
    lines = [
        (out_feat_ref, out_slope_ref, 0, 0),
        (out_feat_ref, out_slope_ref, main, tile_rows),
    ] + [
        (in_feat_ref, in_slope_ref, h * tile_cols, h + 2) for h in range(0, tile_rows - 2, step)
    ]
    for feat_ref, slope_ref, begin, r in lines:
        grad = grad_of(feat_ref, slope_ref, slice(begin, begin + step * tile_cols))
        for k in range(step):
            fill_row(
                cat_ref, r + k, grad[k * tile_cols : (k + 1) * tile_cols],
                edges[r + k : r + k + 1], edges[edge + r + k : edge + r + k + 1],
            )
    for h in range(0, tile_rows, step):
        total = jnp.zeros((step * tile_cols, in_width), f32)
        for a in range(3):
            for b in range(3):
                total = total + lax.dot_general(
                    cat_ref[
                        (h + 2 - a) * tile_cols : (h + 2 - a + step) * tile_cols,
                        (2 - b) * out_width : (3 - b) * out_width,
                    ],
                    kernel_ref[(3 * a + b) * in_width : (3 * a + b + 1) * in_width, :],
                    (((1,), (1,)), ((), ())),
                    preferred_element_type=f32,
                )
        out_ref[h * tile_cols : (h + step) * tile_cols, :] = total.astype(bf16)


def on_device(canvas, conv_weight, conv_bias, target_gram):
    tile_rows, tile_cols, in_width = canvas.shape
    out_width = conv_weight.shape[3]
    pixel_total = tile_rows * tile_cols * lax.axis_size("rows") * lax.axis_size("cols")
    shape = (tile_rows, tile_cols, in_width, out_width, 2)
    kernel = conv_weight.reshape(9 * in_width, out_width)
    params = pltpu.CompilerParams(vmem_limit_bytes=24 * 1024 * 1024)
    vmem = pl.BlockSpec(memory_space=pltpu.VMEM)
    packed_shape = jax.ShapeDtypeStruct((len(tile_pairs(out_width)) * tile, tile), f32)

    rim_shape = jax.ShapeDtypeStruct((2, tile_rows, in_width), bf16)
    two = lax.axis_size("cols") == 2
    rims = local(
        rim_kernel,
        (rim_shape,) * (1 if two else 2),
        "column_rims",
        canvas,
        cost_estimate=pl.CostEstimate(flops=4_000_000_000, bytes_accessed=600_000, transcendentals=0),
    )
    if two:
        beyond = [lax.ppermute(rims[0], "cols", [(0, 1), (1, 0)])]
    else:
        beyond = shift_cols(rims[1], rims[0])
    payload_shape = jax.ShapeDtypeStruct((2 * tile_cols + edge, in_width), bf16)
    half_shape = jax.ShapeDtypeStruct((1, *target_gram.shape), bf16)
    even, odd, left, right, rows = local(
        payload_kernel,
        (payload_shape, payload_shape, rim_shape, rim_shape, half_shape),
        "row_payload",
        canvas,
        target_gram,
        *beyond,
    )
    count = lax.axis_size("rows")
    even, odd = swap_rows([range(0, count - 1, 2), range(1, count - 1, 2)], [even, odd])

    inner = (tile_rows - 2) * tile_cols
    in_feat, in_slope, in_gram, bias = pl.pallas_call(
        functools.partial(inner_kernel, shape),
        out_shape=(
            jax.ShapeDtypeStruct((inner, out_width), bf16),
            jax.ShapeDtypeStruct((inner, out_width), bf16),
            packed_shape,
            jax.ShapeDtypeStruct((1, out_width), f32),
        ),
        in_specs=[vmem] * 5,
        scratch_shapes=[pltpu.VMEM((tile_rows * tile_cols, 3 * in_width), bf16)],
        compiler_params=params,
        name="inner_rows",
        cost_estimate=pl.CostEstimate(
            flops=2 * inner * (9 * in_width + out_width) * out_width,
            bytes_accessed=6_000_000,
            transcendentals=inner * out_width,
        ),
    )(canvas, left, right, kernel, conv_bias)

    outer = 4 * tile_cols + 2 * edge
    half_gram = (packed_shape.shape[0] // 2, tile)
    out_feat, out_slope, send, keep = pl.pallas_call(
        functools.partial(outer_kernel, shape),
        out_shape=(
            jax.ShapeDtypeStruct((outer, out_width), bf16),
            jax.ShapeDtypeStruct((outer, out_width), bf16),
            jax.ShapeDtypeStruct(half_gram, bf16),
            jax.ShapeDtypeStruct(half_gram, f32),
        ),
        in_specs=[vmem] * 8,
        scratch_shapes=[
            pltpu.VMEM((8 * tile_cols, 3 * in_width), bf16),
            pltpu.VMEM((2 * edge, 9 * in_width), bf16),
            pltpu.VMEM(payload_shape.shape, bf16),
            pltpu.VMEM(payload_shape.shape, bf16),
            pltpu.VMEM(packed_shape.shape, f32),
        ],
        compiler_params=params,
        name="outer_rows",
    )(canvas, even, odd, left, right, kernel, bias, in_gram)

    mine, other, rows = sum_all(send, keep, rows)

    own_gram, grad = pl.pallas_call(
        functools.partial(backward_kernel, shape, pixel_total),
        out_shape=(
            jax.ShapeDtypeStruct(target_gram.shape, f32),
            jax.ShapeDtypeStruct((tile_rows * tile_cols, in_width), bf16),
        ),
        in_specs=[vmem] * 8,
        scratch_shapes=[
            pltpu.VMEM(packed_shape.shape, f32),
            pltpu.VMEM((out_width, out_width), f32),
            pltpu.VMEM((out_width, out_width), bf16),
            pltpu.VMEM(((tile_rows + 2) * tile_cols, 3 * out_width), bf16),
        ],
        compiler_params=params,
        name="grad_conv",
    )(mine, other, rows.reshape(out_width, out_width), in_feat, in_slope, out_feat, out_slope, kernel)
    return own_gram, grad.reshape(tile_rows, tile_cols, in_width)


def solution(mesh):
    return jax.shard_map(
        on_device,
        mesh=mesh,
        in_specs=(P("rows", "cols", None), P(), P(), P(("rows", "cols"), None)),
        out_specs=(P(("rows", "cols"), None), P("rows", "cols", None)),
        check_vma=False,
    )
```

profile of v0, /device:TPU:0, one launch (start us, length us, event | category | flops | bytes accessed | tf_op | source)
XLA Modules:
  0.0 51.2 jit_solution(5278781907933434142)
XLA Ops:
  0.6 1.0 %copy-done.1 = bf16[8,128,256]{2,1,0:T(8,128)(2,1)S(1)} copy-done((bf16[8,128,256]{2,1,0:T(8,128)(2,1)S(1)}, bf16[8,128,256]{2,1,0:T(8,128)(2,1)}, u32[]{:S(2)}) %copy-start.1) | copy-done | bytes 524312
  1.7 0.5 %collective-permute-start = (bf16[2,8,256]{2,1,0:T(8,128)(2,1)S(1)}, bf16[2,8,256]{2,1,0:T(8,128)(2,1)S(1)}, u32[]{:S(2)}, u32[]{:S(2)}) collective-permute-start(bf16[2,8,256]{2,1,0:T(8,128)(2,1)S(1)} %column_rims.1), channel_id=1, source_target_pairs={{0,1},{1,0},{2,3},{3,2},{4,5},{5,4},{6,7},{7,6},{8,9},{9,8},{10,11... | collective-permute-start | bytes 24584 | tf_op jit(solution)/shard_map/ppermute | solution.py:461
  2.2 0.8 %collective-permute-done.refs_0_ = bf16[2,8,256]{2,1,0:T(8,128)(2,1)S(1)} collective-permute-done((bf16[2,8,256]{2,1,0:T(8,128)(2,1)S(1)}, bf16[2,8,256]{2,1,0:T(8,128)(2,1)S(1)}, u32[]{:S(2)}, u32[]{:S(2)}) %collective-permute-start) | collective-permute-done | bytes 8224 | tf_op jit(solution)/shard_map/ppermute | solution.py:461
  3.1 2.9 %collective-permute-start.1 = (bf16[272,256]{1,0:T(8,128)(2,1)S(1)}, bf16[272,256]{1,0:T(8,128)(2,1)S(1)}, u32[]{:S(2)}, u32[]{:S(2)}) collective-permute-start(bf16[272,256]{1,0:T(8,128)(2,1)S(1)} %get-tuple-element.26), channel_id=1, source_target_pairs={{0,2},{2,0},{4,6},{6,4},{8,10},{10,8},{12,14},{14,12},{16,18},{18,... | collective-permute-start | bytes 417800 | tf_op jit(solution)/shard_map/ppermute | solution.py:31
  6.0 0.7 %collective-permute-start.2 = (bf16[272,256]{1,0:T(8,128)(2,1)S(1)}, bf16[272,256]{1,0:T(8,128)(2,1)S(1)}, u32[]{:S(2)}, u32[]{:S(2)}) collective-permute-start(bf16[272,256]{1,0:T(8,128)(2,1)S(1)} %get-tuple-element.27), channel_id=1, source_target_pairs={{0,0},{2,4},{4,2},{6,8},{8,6},{10,12},{12,10},{14,16},{16,14},{18,... | collective-permute-start | bytes 417800 | tf_op jit(solution)/shard_map/ppermute | solution.py:31
  6.7 2.8 %inner_rows.1 = (bf16[768,512]{1,0:T(8,128)(2,1)S(1)}, bf16[768,512]{1,0:T(8,128)(2,1)S(1)}, f32[1280,128]{1,0:T(8,128)S(1)}, f32[1,512]{1,0:T(1,128)S(1)}) custom-call(bf16[8,128,256]{2,1,0:T(8,128)(2,1)S(1)} %copy-done.2, bf16[2,8,256]{2,1,0:T(8,128)(2,1)S(1)} %get-tuple-element.28.left_ref, bf16[2,8,256]{2,1,0:T(8,128)(2,1)S(1)} %get-tuple-element.29.right_ref, ...), custom_call_target="tpu_custom_call" | custom-call | flops 2214592512 | bytes 6000000 | tf_op jit(solution)/shard_map/inner_rows/pallas_call | solution.py:478
  9.5 0.5 %collective-permute-done.1.even_ref = bf16[272,256]{1,0:T(8,128)(2,1)S(1)} collective-permute-done((bf16[272,256]{1,0:T(8,128)(2,1)S(1)}, bf16[272,256]{1,0:T(8,128)(2,1)S(1)}, u32[]{:S(2)}, u32[]{:S(2)}) %collective-permute-start.1) | collective-permute-done | bytes 139296 | tf_op jit(solution)/shard_map/ppermute | solution.py:31
  10.0 2.4 %outer_rows.1 = (bf16[544,512]{1,0:T(8,128)(2,1)S(1)}, bf16[544,512]{1,0:T(8,128)(2,1)S(1)}, bf16[640,128]{1,0:T(8,128)(2,1)S(1)}, f32[640,128]{1,0:T(8,128)S(1)}) custom-call(bf16[8,128,256]{2,1,0:T(8,128)(2,1)S(1)} %copy-done.2, bf16[272,256]{1,0:T(8,128)(2,1)S(1)} %collective-permute-done.1.even_ref, bf16[272,256]{1,0:T(8,128)(2,1)S(1)} %collective-permute-done.2.odd_ref, ...), custom_call_target="tpu_custom_call" | custom-call | tf_op jit(solution)/shard_map/outer_rows/pallas_call | solution.py:499
  12.4 0.1 collective-permute-start.3
  12.5 1.4 %collective-permute-done.3.got_ref = bf16[640,128]{1,0:T(8,128)(2,1)S(1)} collective-permute-done((bf16[640,128]{1,0:T(8,128)(2,1)S(1)}, bf16[640,128]{1,0:T(8,128)(2,1)S(1)}, u32[]{:S(2)}, u32[]{:S(2)}) %collective-permute-start.3) | collective-permute-done | bytes 163872 | tf_op jit(solution)/shard_map/ppermute | solution.py:47
  13.9 5.5 %collective-permute-start.4 = (bf16[320,128]{1,0:T(8,128)(2,1)S(1)}, bf16[320,128]{1,0:T(8,128)(2,1)S(1)}, u32[]{:S(2)}, u32[]{:S(2)}) collective-permute-start(bf16[320,128]{1,0:T(8,128)(2,1)S(1)} %get-tuple-element.35), channel_id=1, source_target_pairs={{0,3},{1,2},{2,1},{3,0},{4,7},{5,6},{6,5},{7,4},{8,11},{9,10},{10,... | collective-permute-start | bytes 245768 | tf_op jit(solution)/shard_map/ppermute | solution.py:47
  19.4 2.6 %collective-permute-start.11 = (bf16[1,16,512]{2,1,0:T(8,128)(2,1)S(1)}, bf16[1,16,512]{2,1,0:T(8,128)(2,1)S(1)}, u32[]{:S(2)}, u32[]{:S(2)}) collective-permute-start(bf16[1,16,512]{2,1,0:T(8,128)(2,1)S(1)} %get-tuple-element.39.mine_ref), channel_id=1, source_target_pairs={{0,17},{1,16},{2,19},{3,18},{4,21},{5,20},{6,23},{7,22},{8,25},{9,... | collective-permute-start | bytes 49160 | tf_op jit(solution)/shard_map/ppermute | solution.py:47
  21.9 0.0 collective-permute-done.4.got_ref
  21.9 2.0 %collective-permute-start.5 = (bf16[160,128]{1,0:T(8,128)(2,1)S(1)}, bf16[160,128]{1,0:T(8,128)(2,1)S(1)}, u32[]{:S(2)}, u32[]{:S(2)}) collective-permute-start(bf16[160,128]{1,0:T(8,128)(2,1)S(1)} %get-tuple-element.37), channel_id=1, source_target_pairs={{0,5},{1,4},{2,7},{3,6},{4,1},{5,0},{6,3},{7,2},{8,13},{9,12},{10,... | collective-permute-start | bytes 122888 | tf_op jit(solution)/shard_map/ppermute | solution.py:47
  24.0 1.6 %collective-permute-start.12 = (bf16[2,16,512]{2,1,0:T(8,128)(2,1)S(1)}, bf16[2,16,512]{2,1,0:T(8,128)(2,1)S(1)}, u32[]{:S(2)}, u32[]{:S(2)}) collective-permute-start(bf16[2,16,512]{2,1,0:T(8,128)(2,1)S(1)} %bitcast.28), channel_id=1, source_target_pairs={{0,9},{1,8},{2,11},{3,10},{4,13},{5,12},{6,15},{7,14},{8,1},{9,0},... | collective-permute-start | bytes 98312 | tf_op jit(solution)/shard_map/ppermute | solution.py:47
  25.6 1.8 %collective-permute-done.12.other_ref = bf16[2,16,512]{2,1,0:T(8,128)(2,1)S(1)} collective-permute-done((bf16[2,16,512]{2,1,0:T(8,128)(2,1)S(1)}, bf16[2,16,512]{2,1,0:T(8,128)(2,1)S(1)}, u32[]{:S(2)}, u32[]{:S(2)}) %collective-permute-start.12) | collective-permute-done | bytes 32800 | tf_op jit(solution)/shard_map/ppermute | solution.py:47
  27.4 0.0 collective-permute-done.5.got_ref
  27.4 1.0 %collective-permute-start.13 = (bf16[4,16,512]{2,1,0:T(8,128)(2,1)S(1)}, bf16[4,16,512]{2,1,0:T(8,128)(2,1)S(1)}, u32[]{:S(2)}, u32[]{:S(2)}) collective-permute-start(bf16[4,16,512]{2,1,0:T(8,128)(2,1)S(1)} %bitcast.25), channel_id=1, source_target_pairs={{0,5},{1,4},{2,7},{3,6},{4,1},{5,0},{6,3},{7,2},{8,13},{9,12},{10,... | collective-permute-start | bytes 196616 | tf_op jit(solution)/shard_map/ppermute | solution.py:47
  28.5 1.7 %collective-permute-start.6 = (bf16[160,128]{1,0:T(8,128)(2,1)S(1)}, bf16[160,128]{1,0:T(8,128)(2,1)S(1)}, u32[]{:S(2)}, u32[]{:S(2)}) collective-permute-start(bf16[160,128]{1,0:T(8,128)(2,1)S(1)} %add.3.keep_ref), channel_id=1, source_target_pairs={{0,9},{1,8},{2,11},{3,10},{4,13},{5,12},{6,15},{7,14},{8,1},{9,0},... | collective-permute-start | bytes 122888 | tf_op jit(solution)/shard_map/ppermute | solution.py:47
  30.2 1.7 %collective-permute-done.6.got_ref = bf16[160,128]{1,0:T(8,128)(2,1)S(1)} collective-permute-done((bf16[160,128]{1,0:T(8,128)(2,1)S(1)}, bf16[160,128]{1,0:T(8,128)(2,1)S(1)}, u32[]{:S(2)}, u32[]{:S(2)}) %collective-permute-start.6) | collective-permute-done | bytes 40992 | tf_op jit(solution)/shard_map/ppermute | solution.py:47
  32.0 0.9 %collective-permute-start.14 = (bf16[8,16,512]{2,1,0:T(8,128)(2,1)S(1)}, bf16[8,16,512]{2,1,0:T(8,128)(2,1)S(1)}, u32[]{:S(2)}, u32[]{:S(2)}) collective-permute-start(bf16[8,16,512]{2,1,0:T(8,128)(2,1)S(1)} %bitcast.21), channel_id=1, source_target_pairs={{0,3},{1,2},{2,1},{3,0},{4,7},{5,6},{6,5},{7,4},{8,11},{9,10},{10,... | collective-permute-start | bytes 393224 | tf_op jit(solution)/shard_map/ppermute | solution.py:47
  32.8 2.5 %collective-permute-start.7 = (bf16[160,128]{1,0:T(8,128)(2,1)S(1)}, bf16[160,128]{1,0:T(8,128)(2,1)S(1)}, u32[]{:S(2)}, u32[]{:S(2)}) collective-permute-start(bf16[160,128]{1,0:T(8,128)(2,1)S(1)} %add.4.keep_ref), channel_id=1, source_target_pairs={{0,17},{1,16},{2,19},{3,18},{4,21},{5,20},{6,23},{7,22},{8,25},{9,... | collective-permute-start | bytes 122888 | tf_op jit(solution)/shard_map/ppermute | solution.py:47
  35.3 1.8 %collective-permute-done.7.got_ref = bf16[160,128]{1,0:T(8,128)(2,1)S(1)} collective-permute-done((bf16[160,128]{1,0:T(8,128)(2,1)S(1)}, bf16[160,128]{1,0:T(8,128)(2,1)S(1)}, u32[]{:S(2)}, u32[]{:S(2)}) %collective-permute-start.7) | collective-permute-done | bytes 40992 | tf_op jit(solution)/shard_map/ppermute | solution.py:47
  37.2 1.5 %collective-permute-start.8 = (bf16[160,128]{1,0:T(8,128)(2,1)S(1)}, bf16[160,128]{1,0:T(8,128)(2,1)S(1)}, u32[]{:S(2)}, u32[]{:S(2)}) collective-permute-start(bf16[160,128]{1,0:T(8,128)(2,1)S(1)} %add.5), channel_id=1, source_target_pairs={{0,5},{1,4},{2,7},{3,6},{4,1},{5,0},{6,3},{7,2},{8,13},{9,12},{10,... | collective-permute-start | bytes 122888 | tf_op jit(solution)/shard_map/ppermute | solution.py:47
  38.7 0.2 collective-permute-start.15
  39.0 1.7 %collective-permute-done.8 = bf16[160,128]{1,0:T(8,128)(2,1)S(1)} collective-permute-done((bf16[160,128]{1,0:T(8,128)(2,1)S(1)}, bf16[160,128]{1,0:T(8,128)(2,1)S(1)}, u32[]{:S(2)}, u32[]{:S(2)}) %collective-permute-start.8) | collective-permute-done | bytes 40992 | tf_op jit(solution)/shard_map/ppermute | solution.py:47
  40.7 1.4 %collective-permute-start.9 = (bf16[320,128]{1,0:T(8,128)(2,1)S(1)}, bf16[320,128]{1,0:T(8,128)(2,1)S(1)}, u32[]{:S(2)}, u32[]{:S(2)}) collective-permute-start(bf16[320,128]{1,0:T(8,128)(2,1)S(1)} %bitcast.23), channel_id=1, source_target_pairs={{0,3},{1,2},{2,1},{3,0},{4,7},{5,6},{6,5},{7,4},{8,11},{9,10},{10,... | collective-permute-start | bytes 245768 | tf_op jit(solution)/shard_map/ppermute | solution.py:47
  42.1 3.0 %collective-permute-done.9 = bf16[320,128]{1,0:T(8,128)(2,1)S(1)} collective-permute-done((bf16[320,128]{1,0:T(8,128)(2,1)S(1)}, bf16[320,128]{1,0:T(8,128)(2,1)S(1)}, u32[]{:S(2)}, u32[]{:S(2)}) %collective-permute-start.9) | collective-permute-done | bytes 81952 | tf_op jit(solution)/shard_map/ppermute | solution.py:47
  45.1 0.3 collective-permute-start.10
  45.4 0.1 join_cores.1
  45.5 1.0 %collective-permute-done.10.other_ref = bf16[640,128]{1,0:T(8,128)(2,1)S(1)} collective-permute-done((bf16[640,128]{1,0:T(8,128)(2,1)S(1)}, bf16[640,128]{1,0:T(8,128)(2,1)S(1)}, u32[]{:S(2)}, u32[]{:S(2)}) %collective-permute-start.10) | collective-permute-done | bytes 163872 | tf_op jit(solution)/shard_map/ppermute | solution.py:47
  46.5 4.6 %grad_conv.1 = (f32[16,512]{1,0:T(8,128)}, bf16[1024,256]{1,0:T(8,128)(2,1)}) custom-call(bf16[640,128]{1,0:T(8,128)(2,1)S(1)} %bitcast.20, bf16[640,128]{1,0:T(8,128)(2,1)S(1)} %collective-permute-done.10.other_ref, bf16[512,512]{1,0:T(8,128)(2,1)S(1)} %bitcast.16, bf16[768,512]{1,0:T(8,128)(2,1)S(1)} %get-tuple-element.44.in_feat_ref, ...), custom_call_target="tpu_custom_call" | custom-call | tf_op jit(solution)/shard_map/grad_conv/pallas_call | solution.py:521
  (27 shorter events, 0.3 us)
Async XLA Ops:
  0.6 1.0 %copy-start.1 = (bf16[8,128,256]{2,1,0:T(8,128)(2,1)S(1)}, bf16[8,128,256]{2,1,0:T(8,128)(2,1)}, u32[]{:S(2)}) copy-start(bf16[8,128,256]{2,1,0:T(8,128)(2,1)} %own_ref.3) | copy-start | bytes 1572868
  1.7 1.4 %copy-start.3 = (f32[16,512]{1,0:T(8,128)S(1)}, f32[16,512]{1,0:T(8,128)}, u32[]{:S(2)}) copy-start(f32[16,512]{1,0:T(8,128)} %target_ref.1) | copy-start | bytes 98308
  1.7 5.0 %copy-start = (bf16[3,3,256,512]{3,2,1,0:T(8,128)(2,1)S(1)}, bf16[3,3,256,512]{3,2,1,0:T(8,128)(2,1)}, u32[]{:S(2)}) copy-start(bf16[3,3,256,512]{3,2,1,0:T(8,128)(2,1)} %param.5) | copy-start | bytes 7077892
  1.7 5.0 %copy-start.2 = (bf16[8,128,256]{2,1,0:T(8,128)(2,1)S(1)}, bf16[8,128,256]{2,1,0:T(8,128)(2,1)}, u32[]{:S(2)}) copy-start(bf16[8,128,256]{2,1,0:T(8,128)(2,1)} %own_ref.3) | copy-start | bytes 1572868
  1.7 5.0 %copy-start.4 = (bf16[512]{0:T(512)(128)(2,1)S(1)}, bf16[512]{0:T(512)(128)(2,1)}, u32[]{:S(2)}) copy-start(bf16[512]{0:T(512)(128)(2,1)} %bias_ref.1) | copy-start | bytes 3076
  1.7 1.3 %collective-permute-start = (bf16[2,8,256]{2,1,0:T(8,128)(2,1)S(1)}, bf16[2,8,256]{2,1,0:T(8,128)(2,1)S(1)}, u32[]{:S(2)}, u32[]{:S(2)}) collective-permute-start(bf16[2,8,256]{2,1,0:T(8,128)(2,1)S(1)} %column_rims.1), channel_id=1, source_target_pairs={{0,1},{1,0},{2,3},{3,2},{4,5},{5,4},{6,7},{7,6},{8,9},{9,8},{10,11... | collective-permute-start | bytes 24584 | tf_op jit(solution)/shard_map/ppermute | solution.py:461
  3.1 6.9 %collective-permute-start.1 = (bf16[272,256]{1,0:T(8,128)(2,1)S(1)}, bf16[272,256]{1,0:T(8,128)(2,1)S(1)}, u32[]{:S(2)}, u32[]{:S(2)}) collective-permute-start(bf16[272,256]{1,0:T(8,128)(2,1)S(1)} %get-tuple-element.26), channel_id=1, source_target_pairs={{0,2},{2,0},{4,6},{6,4},{8,10},{10,8},{12,14},{14,12},{16,18},{18,... | collective-permute-start | bytes 417800 | tf_op jit(solution)/shard_map/ppermute | solution.py:31
  6.0 4.0 %collective-permute-start.2 = (bf16[272,256]{1,0:T(8,128)(2,1)S(1)}, bf16[272,256]{1,0:T(8,128)(2,1)S(1)}, u32[]{:S(2)}, u32[]{:S(2)}) collective-permute-start(bf16[272,256]{1,0:T(8,128)(2,1)S(1)} %get-tuple-element.27), channel_id=1, source_target_pairs={{0,0},{2,4},{4,2},{6,8},{8,6},{10,12},{12,10},{14,16},{16,14},{18,... | collective-permute-start | bytes 417800 | tf_op jit(solution)/shard_map/ppermute | solution.py:31
  12.4 1.5 %collective-permute-start.3 = (bf16[640,128]{1,0:T(8,128)(2,1)S(1)}, bf16[640,128]{1,0:T(8,128)(2,1)S(1)}, u32[]{:S(2)}, u32[]{:S(2)}) collective-permute-start(bf16[640,128]{1,0:T(8,128)(2,1)S(1)} %get-tuple-element.33), channel_id=1, source_target_pairs={{0,1},{1,0},{2,3},{3,2},{4,5},{5,4},{6,7},{7,6},{8,9},{9,8},{10,11... | collective-permute-start | bytes 491528 | tf_op jit(solution)/shard_map/ppermute | solution.py:47
  13.9 8.0 %collective-permute-start.4 = (bf16[320,128]{1,0:T(8,128)(2,1)S(1)}, bf16[320,128]{1,0:T(8,128)(2,1)S(1)}, u32[]{:S(2)}, u32[]{:S(2)}) collective-permute-start(bf16[320,128]{1,0:T(8,128)(2,1)S(1)} %get-tuple-element.35), channel_id=1, source_target_pairs={{0,3},{1,2},{2,1},{3,0},{4,7},{5,6},{6,5},{7,4},{8,11},{9,10},{10,... | collective-permute-start | bytes 245768 | tf_op jit(solution)/shard_map/ppermute | solution.py:47
  19.4 4.6 %collective-permute-start.11 = (bf16[1,16,512]{2,1,0:T(8,128)(2,1)S(1)}, bf16[1,16,512]{2,1,0:T(8,128)(2,1)S(1)}, u32[]{:S(2)}, u32[]{:S(2)}) collective-permute-start(bf16[1,16,512]{2,1,0:T(8,128)(2,1)S(1)} %get-tuple-element.39.mine_ref), channel_id=1, source_target_pairs={{0,17},{1,16},{2,19},{3,18},{4,21},{5,20},{6,23},{7,22},{8,25},{9,... | collective-permute-start | bytes 49160 | tf_op jit(solution)/shard_map/ppermute | solution.py:47
  21.9 5.4 %collective-permute-start.5 = (bf16[160,128]{1,0:T(8,128)(2,1)S(1)}, bf16[160,128]{1,0:T(8,128)(2,1)S(1)}, u32[]{:S(2)}, u32[]{:S(2)}) collective-permute-start(bf16[160,128]{1,0:T(8,128)(2,1)S(1)} %get-tuple-element.37), channel_id=1, source_target_pairs={{0,5},{1,4},{2,7},{3,6},{4,1},{5,0},{6,3},{7,2},{8,13},{9,12},{10,... | collective-permute-start | bytes 122888 | tf_op jit(solution)/shard_map/ppermute | solution.py:47
  24.0 3.4 %collective-permute-start.12 = (bf16[2,16,512]{2,1,0:T(8,128)(2,1)S(1)}, bf16[2,16,512]{2,1,0:T(8,128)(2,1)S(1)}, u32[]{:S(2)}, u32[]{:S(2)}) collective-permute-start(bf16[2,16,512]{2,1,0:T(8,128)(2,1)S(1)} %bitcast.28), channel_id=1, source_target_pairs={{0,9},{1,8},{2,11},{3,10},{4,13},{5,12},{6,15},{7,14},{8,1},{9,0},... | collective-permute-start | bytes 98312 | tf_op jit(solution)/shard_map/ppermute | solution.py:47
  27.4 4.5 %collective-permute-start.13 = (bf16[4,16,512]{2,1,0:T(8,128)(2,1)S(1)}, bf16[4,16,512]{2,1,0:T(8,128)(2,1)S(1)}, u32[]{:S(2)}, u32[]{:S(2)}) collective-permute-start(bf16[4,16,512]{2,1,0:T(8,128)(2,1)S(1)} %bitcast.25), channel_id=1, source_target_pairs={{0,5},{1,4},{2,7},{3,6},{4,1},{5,0},{6,3},{7,2},{8,13},{9,12},{10,... | collective-permute-start | bytes 196616 | tf_op jit(solution)/shard_map/ppermute | solution.py:47
  28.5 3.4 %collective-permute-start.6 = (bf16[160,128]{1,0:T(8,128)(2,1)S(1)}, bf16[160,128]{1,0:T(8,128)(2,1)S(1)}, u32[]{:S(2)}, u32[]{:S(2)}) collective-permute-start(bf16[160,128]{1,0:T(8,128)(2,1)S(1)} %add.3.keep_ref), channel_id=1, source_target_pairs={{0,9},{1,8},{2,11},{3,10},{4,13},{5,12},{6,15},{7,14},{8,1},{9,0},... | collective-permute-start | bytes 122888 | tf_op jit(solution)/shard_map/ppermute | solution.py:47
  32.0 6.7 %collective-permute-start.14 = (bf16[8,16,512]{2,1,0:T(8,128)(2,1)S(1)}, bf16[8,16,512]{2,1,0:T(8,128)(2,1)S(1)}, u32[]{:S(2)}, u32[]{:S(2)}) collective-permute-start(bf16[8,16,512]{2,1,0:T(8,128)(2,1)S(1)} %bitcast.21), channel_id=1, source_target_pairs={{0,3},{1,2},{2,1},{3,0},{4,7},{5,6},{6,5},{7,4},{8,11},{9,10},{10,... | collective-permute-start | bytes 393224 | tf_op jit(solution)/shard_map/ppermute | solution.py:47
  32.8 4.3 %collective-permute-start.7 = (bf16[160,128]{1,0:T(8,128)(2,1)S(1)}, bf16[160,128]{1,0:T(8,128)(2,1)S(1)}, u32[]{:S(2)}, u32[]{:S(2)}) collective-permute-start(bf16[160,128]{1,0:T(8,128)(2,1)S(1)} %add.4.keep_ref), channel_id=1, source_target_pairs={{0,17},{1,16},{2,19},{3,18},{4,21},{5,20},{6,23},{7,22},{8,25},{9,... | collective-permute-start | bytes 122888 | tf_op jit(solution)/shard_map/ppermute | solution.py:47
  37.2 3.5 %collective-permute-start.8 = (bf16[160,128]{1,0:T(8,128)(2,1)S(1)}, bf16[160,128]{1,0:T(8,128)(2,1)S(1)}, u32[]{:S(2)}, u32[]{:S(2)}) collective-permute-start(bf16[160,128]{1,0:T(8,128)(2,1)S(1)} %add.5), channel_id=1, source_target_pairs={{0,5},{1,4},{2,7},{3,6},{4,1},{5,0},{6,3},{7,2},{8,13},{9,12},{10,... | collective-permute-start | bytes 122888 | tf_op jit(solution)/shard_map/ppermute | solution.py:47
  38.7 6.7 %collective-permute-start.15 = (bf16[16,16,512]{2,1,0:T(8,128)(2,1)S(1)}, bf16[16,16,512]{2,1,0:T(8,128)(2,1)S(1)}, u32[]{:S(2)}, u32[]{:S(2)}) collective-permute-start(bf16[16,16,512]{2,1,0:T(8,128)(2,1)S(1)} %bitcast.17), channel_id=1, source_target_pairs={{0,1},{1,0},{2,3},{3,2},{4,5},{5,4},{6,7},{7,6},{8,9},{9,8},{10,11... | collective-permute-start | bytes 786440 | tf_op jit(solution)/shard_map/ppermute | solution.py:47
  40.7 4.4 %collective-permute-start.9 = (bf16[320,128]{1,0:T(8,128)(2,1)S(1)}, bf16[320,128]{1,0:T(8,128)(2,1)S(1)}, u32[]{:S(2)}, u32[]{:S(2)}) collective-permute-start(bf16[320,128]{1,0:T(8,128)(2,1)S(1)} %bitcast.23), channel_id=1, source_target_pairs={{0,3},{1,2},{2,1},{3,0},{4,7},{5,6},{6,5},{7,4},{8,11},{9,10},{10,... | collective-permute-start | bytes 245768 | tf_op jit(solution)/shard_map/ppermute | solution.py:47
  45.1 1.5 %collective-permute-start.10 = (bf16[640,128]{1,0:T(8,128)(2,1)S(1)}, bf16[640,128]{1,0:T(8,128)(2,1)S(1)}, u32[]{:S(2)}, u32[]{:S(2)}) collective-permute-start(bf16[640,128]{1,0:T(8,128)(2,1)S(1)} %bitcast.19), channel_id=1, source_target_pairs={{0,1},{1,0},{2,3},{3,2},{4,5},{5,4},{6,7},{7,6},{8,9},{9,8},{10,11... | collective-permute-start | bytes 491528 | tf_op jit(solution)/shard_map/ppermute | solution.py:47
where the time goes:
time: 51.6 us; the launch traced here: 51.2 us
  starting transfers between devices  25.4 us (49%)
  waiting for transfers between devices  13.8 us (27%)
  Pallas kernels  10.1 us (20%)
  local copies, waits for them, and re-layouts  1.05 us (2%)
  between operations  0.8 us (2%)
    ppermute x13, starting transfers between devices, swap(): lax.ppermute(value, ('rows', 'cols'), [(i, i ^ (1 << bit | 1)) for i in r...  21.4 us
    ppermute x13, waiting for transfers between devices, swap(): lax.ppermute(value, ('rows', 'cols'), [(i, i ^ (1 << bit | 1)) for i in r...  12.4 us
    pallas_call x1, Pallas kernels, on_device(): pl.pallas_call(functools.partial(backward_kernel, shape, pixel_total), ou...  4.63 us
    ppermute x2, starting transfers between devices, swap_rows(): lax.ppermute(value, 'rows', perm(low))  3.55 us
    pallas_call x1, Pallas kernels, on_device(): pl.pallas_call(functools.partial(inner_kernel, shape), out_shape=(jax.Sha...  2.78 us
    pallas_call x1, Pallas kernels, on_device(): pl.pallas_call(functools.partial(outer_kernel, shape), out_shape=(jax.Sha...  2.38 us
    unnamed x10, local copies, waits for them, and re-layouts  1.05 us
  transfers between devices with their start and end apart: 16, of which 9 were waited for; matrix products, arithmetic and copies ran while one was open for 0% of the time, Pallas kernels for 6%

commit v1 on v0

--- a/solution.py
+++ b/solution.py
@@ -118,39 +118,48 @@
     return local(body, jax.ShapeDtypeStruct(shape, mine.dtype), "join_cores", mine, other)
 
 
-def gather_step(rows, bit, after):
-    share = rows.shape[-2:]
-    send, _ = lax.optimization_barrier((rows, after))
-    got = swap(send, bit)
-    both = join(send, got, bit) if bit > 0 else join_cores(send, got)
-    return both.reshape(-1, *share)
-
-
-def sum_all(send, keep, rows):
+class Gather:
+    def __init__(self, rows):
+        self.rows, self.done = rows, []
+
+    def step(self, bit, after, until=None):
+        share = self.rows.shape[-2:]
+        send, _ = lax.optimization_barrier((self.rows, after))
+        got = swap(send, bit)
+        if until is not None:
+            got, _ = lax.optimization_barrier((got, until))
+        if bit > 0:
+            lead = 1 << sum(other > bit for other in self.done)
+            send, got = (part.reshape(lead, -1, *share) for part in (send, got))
+            self.rows = join(send, got, bit).reshape(-1, *share)
+        else:
+            self.rows = join_cores(send, got).reshape(-1, *share)
+        self.done.append(bit)
+
+    def before(self, value):
+        value, self.rows = lax.optimization_barrier((value, self.rows))
+        return value
+
+
+def sum_all(send, keep, beside):
     bits = (lax.axis_size("rows") * lax.axis_size("cols")).bit_length() - 1
     halving = list(range(1, min(3, bits)))
-    order = list(reversed(range(bits)))
-
-    def step(value, bit):
-        nonlocal rows
+
+    def step(value, bit, name):
         got = swap(value, bit)
-        if order:
-            rows = gather_step(rows, order.pop(0), value)
-        return got
-
-    got = swap(send, 0)
+        return beside(name, value, got)
+
+    got = step(send, 0, "cores")
     for bit in halving:
         send, keep = halve(keep, got, bit)
-        got = step(send, bit)
+        got = step(send, bit, f"halve {bit}")
     mine = add(keep, got)
     for bit in range(len(halving) + 1, bits):
-        mine = add(mine, step(mine, bit))
+        mine = add(mine, step(mine, bit, f"add {bit}"))
     for bit in reversed(halving):
-        mine = join(mine[None], step(mine, bit)[None], bit).reshape(-1, mine.shape[1])
-    other = swap(mine, 0)
-    for bit in order:
-        rows = gather_step(rows, bit, mine)
-    return mine, other, rows
+        got = step(mine, bit, f"join {bit}")
+        mine = join(mine[None], got[None], bit).reshape(-1, mine.shape[1])
+    return mine, step(mine, 0, "halves")
 
 
 def gelu_pair(value):
@@ -213,16 +222,27 @@
         fill(odd_ref, rows - 2)
 
 
-def fill_row(cat_ref, r, row, before, after):
+def moved_rows(row, before, after):
     cols, width = row.shape
     wide = row.astype(f32)
     place = lax.broadcasted_iota(jnp.int32, (cols, width), 0)
-    at = slice(r * cols, (r + 1) * cols)
-    moved = jnp.where(place == 0, before, pltpu.roll(wide, 1, 0))
-    cat_ref[at, 0:width] = moved.astype(bf16)
-    cat_ref[at, width : 2 * width] = row.astype(bf16)
-    moved = jnp.where(place == cols - 1, after, pltpu.roll(wide, cols - 1, 0))
-    cat_ref[at, 2 * width : 3 * width] = moved.astype(bf16)
+    right = jnp.where(place == 0, before, pltpu.roll(wide, 1, 0))
+    left = jnp.where(place == cols - 1, after, pltpu.roll(wide, cols - 1, 0))
+    return right.astype(bf16), row.astype(bf16), left.astype(bf16)
+
+
+def fill_row(cat_ref, r, row, before, after):
+    cols, width = row.shape
+    for b, part in enumerate(moved_rows(row, before, after)):
+        cat_ref[r * cols : (r + 1) * cols, b * width : (b + 1) * width] = part
+
+
+def fill_patches(cat_ref, spots, row, before, after):
+    cols, width = row.shape
+    for b, part in enumerate(moved_rows(row, before, after)):
+        for r, a in spots:
+            at = (3 * a + b) * width
+            cat_ref[r * cols : (r + 1) * cols, at : at + width] = part
 
 
 def gram_tiles(feat, gram_ref, base_ref=None):
@@ -253,28 +273,22 @@
     tile_rows, tile_cols, in_width, out_width, step = shape
     lefts, rights = left_ref[1].astype(f32), right_ref[0].astype(f32)
     for r in range(tile_rows):
-        fill_row(cat_ref, r, own_ref[r], lefts[r : r + 1], rights[r : r + 1])
-    bias = row_ref[...]
+        spots = [(r - a, a) for a in range(3) if 0 <= r - a < tile_rows - 2]
+        fill_patches(cat_ref, spots, own_ref[r], lefts[r : r + 1], rights[r : r + 1])
     root = 1.0 / math.sqrt(out_width)
-    span = 3 * in_width
-    for h in range(0, tile_rows - 2, step):
-        total = bias
-        for a in range(3):
-            total = total + jnp.dot(
-                cat_ref[(h + a) * tile_cols : (h + a + step) * tile_cols, :],
-                kernel_ref[a * span : (a + 1) * span, :],
-                preferred_element_type=f32,
-            )
+    for at in (slice(0, out_width // 2), slice(out_width // 2, out_width)):
+        total = row_ref[:, at] + jnp.dot(
+            cat_ref[...], kernel_ref[:, at], preferred_element_type=f32
+        )
         features, slope = gelu_pair(total)
-        at = slice(h * tile_cols, (h + step) * tile_cols)
-        feat_ref[at, :] = features.astype(bf16)
-        slope_ref[at, :] = (slope * root).astype(bf16)
+        feat_ref[:, at] = features.astype(bf16)
+        slope_ref[:, at] = (slope * root).astype(bf16)
     gram_tiles(feat_ref[...], gram_ref)
 
 
 def outer_kernel(
     shape, own_ref, even_ref, odd_ref, left_ref, right_ref, kernel_ref, bias_ref, base_ref,
-    feat_ref, slope_ref, send_ref, keep_ref, cat_ref, edge_ref, low_ref, high_ref, gram_ref,
+    feat_ref, slope_ref, send_ref, keep_ref, cat_ref, low_ref, high_ref, gram_ref,
 ):
     tile_rows, tile_cols, in_width, out_width, step = shape
     odd = lax.rem(lax.axis_index("rows"), 2)
@@ -317,7 +331,6 @@
     rights = [
         ends(tile_cols - 1, own_end), sides(2, right_ref[0].astype(f32)), sides(3, right_ref[1].astype(f32))
     ]
-    span = 3 * in_width
     lines = [0, 1, 2, 3, tile_rows, tile_rows + 1, tile_rows + 2, tile_rows + 3]
     for r, line in enumerate(lines):
         if line < 2:
@@ -327,7 +340,9 @@
         else:
             k = line - tile_rows - 2
             row = high_ref[k * tile_cols : (k + 1) * tile_cols, :]
-        fill_row(cat_ref, r, row, lefts[1][line : line + 1], rights[1][line : line + 1])
+        group, r = r // 4, r % 4
+        spots = [(2 * group + r - a, a) for a in range(3) if 0 <= r - a < 2]
+        fill_patches(cat_ref, spots, row, lefts[1][line : line + 1], rights[1][line : line + 1])
     blank = jnp.zeros((edge - tile_rows - 2, in_width), f32)
     for a in range(3):
         for b in range(3):
@@ -336,36 +351,23 @@
                 axis=0,
             )
             at = (3 * a + b) * in_width
-            edge_ref[:, at : at + in_width] = piece.astype(bf16)
-    bias = bias_ref[...]
+            cat_ref[2 * main :, at : at + in_width] = piece.astype(bf16)
     root = 1.0 / math.sqrt(out_width)
-    totals = [bias, bias, bias]
-    for a in range(3):
-        weights = kernel_ref[a * span : (a + 1) * span, :]
-        for k in range(2):
-            totals[k] = totals[k] + jnp.dot(
-                cat_ref[(4 * k + a) * tile_cols : (4 * k + a + 2) * tile_cols, :],
-                weights,
-                preferred_element_type=f32,
-            )
-        totals[2] = totals[2] + jnp.dot(
-            edge_ref[:, a * span : (a + 1) * span], weights, preferred_element_type=f32
-        )
-    for k in range(2):
-        features, slope = gelu_pair(totals[k])
-        slope = slope * root
-        at = k * main
-        feat_ref[at : at + main, :] = features.astype(bf16)
-        scale = (first, 1.0) if k == 0 else (1.0, last)
-        slope_ref[at : at + tile_cols, :] = (slope[:tile_cols] * scale[0]).astype(bf16)
-        slope_ref[at + tile_cols : at + main, :] = (slope[tile_cols:] * scale[1]).astype(bf16)
-    features, slope = gelu_pair(totals[2])
-    line = lax.broadcasted_iota(jnp.int32, (2 * edge, out_width), 0)
+    line = lax.broadcasted_iota(jnp.int32, (2 * edge, out_width // 2), 0)
     weight = jnp.where(line < edge, left, right)
     weight = jnp.where(line % edge == 0, weight * first, weight)
     weight = jnp.where(line % edge == tile_rows + 1, weight * last, weight)
-    feat_ref[2 * main :, :] = features.astype(bf16)
-    slope_ref[2 * main :, :] = (slope * root * weight).astype(bf16)
+    for at in (slice(0, out_width // 2), slice(out_width // 2, out_width)):
+        total = bias_ref[:, at] + jnp.dot(
+            cat_ref[...], kernel_ref[:, at], preferred_element_type=f32
+        )
+        features, slope = gelu_pair(total)
+        slope = slope * root
+        feat_ref[:, at] = features.astype(bf16)
+        slope_ref[0:tile_cols, at] = (slope[:tile_cols] * first).astype(bf16)
+        slope_ref[tile_cols : 3 * tile_cols, at] = slope[tile_cols : 3 * tile_cols].astype(bf16)
+        slope_ref[3 * tile_cols : 2 * main, at] = (slope[3 * tile_cols : 2 * main] * last).astype(bf16)
+        slope_ref[2 * main :, at] = (slope[2 * main :] * weight).astype(bf16)
     gram_tiles(feat_ref[tile_cols : 3 * tile_cols, :], gram_ref, base_ref)
     half = send_ref.shape[0]
     side = side_of(0)
@@ -373,9 +375,22 @@
     keep_ref[...] = gram_ref[rows_at(side, half), :]
 
 
+def prepare_kernel(kernel_ref, target_ref, turned_ref, both_ref):
+    taps, in_width, out_width = 9, kernel_ref.shape[0] // 9, kernel_ref.shape[1]
+    for n in range(taps):
+        to = (n // 3 * 3 + 2 - n % 3) * out_width
+        turned_ref[to : to + out_width, :] = kernel_ref[n * in_width : (n + 1) * in_width, :].T
+    for i, j in tile_pairs(out_width):
+        at_i, at_j = slice(i * tile, (i + 1) * tile), slice(j * tile, (j + 1) * tile)
+        both = target_ref[at_i, at_j].astype(f32) + target_ref[at_j, at_i].astype(f32).T
+        both_ref[at_i, at_j] = both
+        if i != j:
+            both_ref[at_j, at_i] = both.T
+
+
 def backward_kernel(
-    shape, pixel_total, mine_ref, other_ref, target_ref, in_feat_ref, in_slope_ref, out_feat_ref, out_slope_ref,
-    kernel_ref, own_gram_ref, out_ref, gram_ref, full_ref, sym_ref, cat_ref,
+    shape, pixel_total, mine_ref, other_ref, both_ref, in_feat_ref, in_slope_ref, out_feat_ref, out_slope_ref,
+    turned_ref, own_gram_ref, out_ref, gram_ref, full_ref, sym_ref, cat_ref,
 ):
     tile_rows, tile_cols, in_width, out_width, step = shape
     half = mine_ref.shape[0]
@@ -384,14 +399,13 @@
     gram_ref[rows_at(1 - side, half), :] = other_ref[...].astype(f32)
     for n, (i, j) in enumerate(tile_pairs(out_width)):
         at_i, at_j = slice(i * tile, (i + 1) * tile), slice(j * tile, (j + 1) * tile)
-        at = slice(n * tile, (n + 1) * tile)
-        gram = gram_ref[at, :] * (1.0 / pixel_total)
-        both = 2.0 * gram - (target_ref[at_i, at_j].astype(f32) + target_ref[at_j, at_i].astype(f32).T)
+        gram = gram_ref[n * tile : (n + 1) * tile, :] * (1.0 / pixel_total)
         full_ref[at_i, at_j] = gram
-        sym_ref[at_i, at_j] = both.astype(bf16)
+        sym_ref[at_i, at_j] = (2.0 * gram - both_ref[at_i, at_j]).astype(bf16)
         if i != j:
-            full_ref[at_j, at_i] = gram.T
-            sym_ref[at_j, at_i] = both.T.astype(bf16)
+            gram = gram.T
+            full_ref[at_j, at_i] = gram
+            sym_ref[at_j, at_i] = (2.0 * gram - both_ref[at_j, at_i]).astype(bf16)
     share = own_gram_ref.shape[0]
     start = device_index() * share
     if share % 8 == 0:
@@ -422,20 +436,15 @@
                 cat_ref, r + k, grad[k * tile_cols : (k + 1) * tile_cols],
                 edges[r + k : r + k + 1], edges[edge + r + k : edge + r + k + 1],
             )
-    for h in range(0, tile_rows, step):
-        total = jnp.zeros((step * tile_cols, in_width), f32)
-        for a in range(3):
-            for b in range(3):
-                total = total + lax.dot_general(
-                    cat_ref[
-                        (h + 2 - a) * tile_cols : (h + 2 - a + step) * tile_cols,
-                        (2 - b) * out_width : (3 - b) * out_width,
-                    ],
-                    kernel_ref[(3 * a + b) * in_width : (3 * a + b + 1) * in_width, :],
-                    (((1,), (1,)), ((), ())),
-                    preferred_element_type=f32,
-                )
-        out_ref[h * tile_cols : (h + step) * tile_cols, :] = total.astype(bf16)
+    total = 0.0
+    span = 3 * out_width
+    for a in range(3):
+        total = total + jnp.dot(
+            cat_ref[(2 - a) * tile_cols : (2 - a + tile_rows) * tile_cols, :],
+            turned_ref[a * span : (a + 1) * span, :],
+            preferred_element_type=f32,
+        )
+    out_ref[...] = total.astype(bf16)
 
 
 def on_device(canvas, conv_weight, conv_bias, target_gram):
@@ -474,6 +483,10 @@
     count = lax.axis_size("rows")
     even, odd = swap_rows([range(0, count - 1, 2), range(1, count - 1, 2)], [even, odd])
 
+    bits = (lax.axis_size("rows") * lax.axis_size("cols")).bit_length() - 1
+    gather = Gather(rows)
+    far = list(reversed(range(3, bits)))
+    gather.step(far[0], left)
     inner = (tile_rows - 2) * tile_cols
     in_feat, in_slope, in_gram, bias = pl.pallas_call(
         functools.partial(inner_kernel, shape),
@@ -484,7 +497,7 @@
             jax.ShapeDtypeStruct((1, out_width), f32),
         ),
         in_specs=[vmem] * 5,
-        scratch_shapes=[pltpu.VMEM((tile_rows * tile_cols, 3 * in_width), bf16)],
+        scratch_shapes=[pltpu.VMEM((inner, 9 * in_width), bf16)],
         compiler_params=params,
         name="inner_rows",
         cost_estimate=pl.CostEstimate(
@@ -494,6 +507,7 @@
         ),
     )(canvas, left, right, kernel, conv_bias)
 
+    in_gram = gather.before(in_gram)
     outer = 4 * tile_cols + 2 * edge
     half_gram = (packed_shape.shape[0] // 2, tile)
     out_feat, out_slope, send, keep = pl.pallas_call(
@@ -506,8 +520,7 @@
         ),
         in_specs=[vmem] * 8,
         scratch_shapes=[
-            pltpu.VMEM((8 * tile_cols, 3 * in_width), bf16),
-            pltpu.VMEM((2 * edge, 9 * in_width), bf16),
+            pltpu.VMEM((outer, 9 * in_width), bf16),
             pltpu.VMEM(payload_shape.shape, bf16),
             pltpu.VMEM(payload_shape.shape, bf16),
             pltpu.VMEM(packed_shape.shape, f32),
@@ -516,8 +529,34 @@
         name="outer_rows",
     )(canvas, even, odd, left, right, kernel, bias, in_gram)
 
-    mine, other, rows = sum_all(send, keep, rows)
-
+    exchanges = {"cores": far[1:2], "halve 2": [*far[2:], 1], "add 3": [2], "add 4": [0]}
+    prepared = []
+
+    def beside(name, sent, got):
+        for bit in exchanges.get(name, []):
+            gather.step(bit, sent, got)
+        if name != "join 1":
+            return got
+        rows, _ = lax.optimization_barrier((gather.rows, sent))
+        prepared.extend(
+            pl.pallas_call(
+                prepare_kernel,
+                out_shape=(
+                    jax.ShapeDtypeStruct((9 * out_width, in_width), bf16),
+                    jax.ShapeDtypeStruct((out_width, out_width), f32),
+                ),
+                in_specs=[vmem] * 2,
+                compiler_params=params,
+                name="prepare",
+                cost_estimate=pl.CostEstimate(
+                    flops=2_000_000_000, bytes_accessed=6_000_000, transcendentals=0
+                ),
+            )(kernel, rows.reshape(out_width, out_width))
+        )
+        return lax.optimization_barrier((got, *prepared))[0]
+
+    mine, other = sum_all(send, keep, beside)
+    turned, both = prepared
     own_gram, grad = pl.pallas_call(
         functools.partial(backward_kernel, shape, pixel_total),
         out_shape=(
@@ -533,7 +572,7 @@
         ],
         compiler_params=params,
         name="grad_conv",
-    )(mine, other, rows.reshape(out_width, out_width), in_feat, in_slope, out_feat, out_slope, kernel)
+    )(mine, other, both, in_feat, in_slope, out_feat, out_slope, turned)
     return own_gram, grad.reshape(tile_rows, tile_cols, in_width)
 
 

time: 51.6 us -> 54.4 us (1.054)
  waiting for transfers between devices: 13.8 us -> 19 us
  starting transfers between devices: 25.4 us -> 22.2 us
  Pallas kernels: 10.1 us -> 11.1 us
    ppermute x13, waiting for transfers between devices: 12.4 us -> 17.5 us  [swap(): lax.ppermute(value, ('rows', 'cols'), [(i, i ^ (1 << bit | 1)) for i in r...]
    ppermute x13, starting transfers between devices: 21.4 us -> 19.6 us  [swap(): lax.ppermute(value, ('rows', 'cols'), [(i, i ^ (1 << bit | 1)) for i in r...]
    ppermute x2, starting transfers between devices: 3.55 us -> 2.15 us  [swap_rows(): lax.ppermute(value, 'rows', perm(low))]
    pallas_call x0 -> x1, Pallas kernels: none -> 0.98 us  [beside(): pl.pallas_call(prepare_kernel, out_shape=(jax.ShapeDtypeStruct((9 * out_w...]
  transfers between devices with their start and end apart: 16 -> 16, of which waited for: 9 -> 11; matrix products, arithmetic and copies ran while one was open for 0% -> 0% of each run, Pallas kernels for 6% -> 8%
where the time goes in v1:
time: 54.4 us; the launch traced here: 54.2 us
  starting transfers between devices  22.2 us (41%)
  waiting for transfers between devices  19 us (35%)
  Pallas kernels  11.1 us (20%)
  local copies, waits for them, and re-layouts  1.05 us (2%)
  between operations  0.81 us (1%)
    ppermute x13, starting transfers between devices, swap(): lax.ppermute(value, ('rows', 'cols'), [(i, i ^ (1 << bit | 1)) for i in r...  19.6 us
    ppermute x13, waiting for transfers between devices, swap(): lax.ppermute(value, ('rows', 'cols'), [(i, i ^ (1 << bit | 1)) for i in r...  17.5 us
    pallas_call x1, Pallas kernels, on_device(): pl.pallas_call(functools.partial(backward_kernel, shape, pixel_total), ou...  4.47 us
    pallas_call x1, Pallas kernels, on_device(): pl.pallas_call(functools.partial(inner_kernel, shape), out_shape=(jax.Sha...  2.98 us
    pallas_call x1, Pallas kernels, on_device(): pl.pallas_call(functools.partial(outer_kernel, shape), out_shape=(jax.Sha...  2.3 us
    ppermute x2, starting transfers between devices, swap_rows(): lax.ppermute(value, 'rows', perm(low))  2.15 us
  transfers between devices with their start and end apart: 16, of which 11 were waited for; matrix products, arithmetic and copies ran while one was open for 0% of the time, Pallas kernels for 8%

profile of v1, /device:TPU:0, one launch (start us, length us, event | category | flops | bytes accessed | tf_op | source)
XLA Modules:
  0.0 54.2 jit_solution(13017429534019174816)
XLA Ops:
  0.6 1.0 %copy-done.1 = bf16[8,128,256]{2,1,0:T(8,128)(2,1)S(1)} copy-done((bf16[8,128,256]{2,1,0:T(8,128)(2,1)S(1)}, bf16[8,128,256]{2,1,0:T(8,128)(2,1)}, u32[]{:S(2)}) %copy-start.1) | copy-done | bytes 524312
  1.7 0.5 collective-permute-start
  2.2 0.8 %collective-permute-done.refs_0_ = bf16[2,8,256]{2,1,0:T(8,128)(2,1)S(1)} collective-permute-done((bf16[2,8,256]{2,1,0:T(8,128)(2,1)S(1)}, bf16[2,8,256]{2,1,0:T(8,128)(2,1)S(1)}, u32[]{:S(2)}, u32[]{:S(2)}) %collective-permute-start) | collective-permute-done | bytes 8224 | tf_op jit(solution)/shard_map/ppermute | solution.py:470
  3.1 3.8 %collective-permute-start.3 = (bf16[1,16,512]{2,1,0:T(8,128)(2,1)S(1)}, bf16[1,16,512]{2,1,0:T(8,128)(2,1)S(1)}, u32[]{:S(2)}, u32[]{:S(2)}) collective-permute-start(bf16[1,16,512]{2,1,0:T(8,128)(2,1)S(1)} %get-tuple-element.43), channel_id=1, source_target_pairs={{0,17},{1,16},{2,19},{3,18},{4,21},{5,20},{6,23},{7,22},{8,25},{9,... | collective-permute-start | bytes 49160 | tf_op jit(solution)/shard_map/ppermute | solution.py:47
  6.9 1.5 %collective-permute-start.1 = (bf16[272,256]{1,0:T(8,128)(2,1)S(1)}, bf16[272,256]{1,0:T(8,128)(2,1)S(1)}, u32[]{:S(2)}, u32[]{:S(2)}) collective-permute-start(bf16[272,256]{1,0:T(8,128)(2,1)S(1)} %get-tuple-element.36), channel_id=1, source_target_pairs={{0,2},{2,0},{4,6},{6,4},{8,10},{10,8},{12,14},{14,12},{16,18},{18,... | collective-permute-start | bytes 417800 | tf_op jit(solution)/shard_map/ppermute | solution.py:31
  8.4 0.7 %collective-permute-start.2 = (bf16[272,256]{1,0:T(8,128)(2,1)S(1)}, bf16[272,256]{1,0:T(8,128)(2,1)S(1)}, u32[]{:S(2)}, u32[]{:S(2)}) collective-permute-start(bf16[272,256]{1,0:T(8,128)(2,1)S(1)} %get-tuple-element.37), channel_id=1, source_target_pairs={{0,0},{2,4},{4,2},{6,8},{8,6},{10,12},{12,10},{14,16},{16,14},{18,... | collective-permute-start | bytes 417800 | tf_op jit(solution)/shard_map/ppermute | solution.py:31
  9.1 3.0 %inner_rows.1 = (bf16[768,512]{1,0:T(8,128)(2,1)S(1)}, bf16[768,512]{1,0:T(8,128)(2,1)S(1)}, f32[1280,128]{1,0:T(8,128)S(1)}, f32[1,512]{1,0:T(1,128)S(1)}) custom-call(bf16[8,128,256]{2,1,0:T(8,128)(2,1)S(1)} %copy-done.2, bf16[2,8,256]{2,1,0:T(8,128)(2,1)S(1)} %get-tuple-element.38.left_ref, bf16[2,8,256]{2,1,0:T(8,128)(2,1)S(1)} %get-tuple-element.39.right_ref, ...), custom_call_target="tpu_custom_call" | custom-call | flops 2214592512 | bytes 6000000 | tf_op jit(solution)/shard_map/inner_rows/pallas_call | solution.py:491
  12.1 0.7 %collective-permute-done.1.even_ref = bf16[272,256]{1,0:T(8,128)(2,1)S(1)} collective-permute-done((bf16[272,256]{1,0:T(8,128)(2,1)S(1)}, bf16[272,256]{1,0:T(8,128)(2,1)S(1)}, u32[]{:S(2)}, u32[]{:S(2)}) %collective-permute-start.1) | collective-permute-done | bytes 139296 | tf_op jit(solution)/shard_map/ppermute | solution.py:31
  12.8 2.3 %outer_rows.1 = (bf16[544,512]{1,0:T(8,128)(2,1)S(1)}, bf16[544,512]{1,0:T(8,128)(2,1)S(1)}, bf16[640,128]{1,0:T(8,128)(2,1)S(1)}, f32[640,128]{1,0:T(8,128)S(1)}) custom-call(bf16[8,128,256]{2,1,0:T(8,128)(2,1)S(1)} %copy-done.2, bf16[272,256]{1,0:T(8,128)(2,1)S(1)} %collective-permute-done.1.even_ref, bf16[272,256]{1,0:T(8,128)(2,1)S(1)} %collective-permute-done.2.odd_ref, ...), custom_call_target="tpu_custom_call" | custom-call | tf_op jit(solution)/shard_map/outer_rows/pallas_call | solution.py:513
  15.2 1.4 %collective-permute-done.4.got_ref = bf16[640,128]{1,0:T(8,128)(2,1)S(1)} collective-permute-done((bf16[640,128]{1,0:T(8,128)(2,1)S(1)}, bf16[640,128]{1,0:T(8,128)(2,1)S(1)}, u32[]{:S(2)}, u32[]{:S(2)}) %collective-permute-start.4) | collective-permute-done | bytes 163872 | tf_op jit(solution)/shard_map/ppermute | solution.py:47
  16.6 5.2 %collective-permute-start.5 = (bf16[320,128]{1,0:T(8,128)(2,1)S(1)}, bf16[320,128]{1,0:T(8,128)(2,1)S(1)}, u32[]{:S(2)}, u32[]{:S(2)}) collective-permute-start(bf16[320,128]{1,0:T(8,128)(2,1)S(1)} %get-tuple-element.48), channel_id=1, source_target_pairs={{0,3},{1,2},{2,1},{3,0},{4,7},{5,6},{6,5},{7,4},{8,11},{9,10},{10,... | collective-permute-start | bytes 245768 | tf_op jit(solution)/shard_map/ppermute | solution.py:47
  21.8 1.5 %collective-permute-start.11 = (bf16[2,16,512]{2,1,0:T(8,128)(2,1)S(1)}, bf16[2,16,512]{2,1,0:T(8,128)(2,1)S(1)}, u32[]{:S(2)}, u32[]{:S(2)}) collective-permute-start(bf16[2,16,512]{2,1,0:T(8,128)(2,1)S(1)} %bitcast.41), channel_id=1, source_target_pairs={{0,9},{1,8},{2,11},{3,10},{4,13},{5,12},{6,15},{7,14},{8,1},{9,0},... | collective-permute-start | bytes 98312 | tf_op jit(solution)/shard_map/ppermute | solution.py:47
  23.4 1.8 %collective-permute-done.11 = bf16[2,16,512]{2,1,0:T(8,128)(2,1)S(1)} collective-permute-done((bf16[2,16,512]{2,1,0:T(8,128)(2,1)S(1)}, bf16[2,16,512]{2,1,0:T(8,128)(2,1)S(1)}, u32[]{:S(2)}, u32[]{:S(2)}) %collective-permute-start.11) | collective-permute-done | bytes 32800 | tf_op jit(solution)/shard_map/ppermute | solution.py:47
  25.2 1.1 %collective-permute-start.12 = (bf16[4,16,512]{2,1,0:T(8,128)(2,1)S(1)}, bf16[4,16,512]{2,1,0:T(8,128)(2,1)S(1)}, u32[]{:S(2)}, u32[]{:S(2)}) collective-permute-start(bf16[4,16,512]{2,1,0:T(8,128)(2,1)S(1)} %bitcast.38), channel_id=1, source_target_pairs={{0,3},{1,2},{2,1},{3,0},{4,7},{5,6},{6,5},{7,4},{8,11},{9,10},{10,... | collective-permute-start | bytes 196616 | tf_op jit(solution)/shard_map/ppermute | solution.py:47
  26.4 1.5 %collective-permute-start.6 = (bf16[160,128]{1,0:T(8,128)(2,1)S(1)}, bf16[160,128]{1,0:T(8,128)(2,1)S(1)}, u32[]{:S(2)}, u32[]{:S(2)}) collective-permute-start(bf16[160,128]{1,0:T(8,128)(2,1)S(1)} %get-tuple-element.50), channel_id=1, source_target_pairs={{0,5},{1,4},{2,7},{3,6},{4,1},{5,0},{6,3},{7,2},{8,13},{9,12},{10,... | collective-permute-start | bytes 122888 | tf_op jit(solution)/shard_map/ppermute | solution.py:47
  27.8 2.0 %collective-permute-done.6.got_ref = bf16[160,128]{1,0:T(8,128)(2,1)S(1)} collective-permute-done((bf16[160,128]{1,0:T(8,128)(2,1)S(1)}, bf16[160,128]{1,0:T(8,128)(2,1)S(1)}, u32[]{:S(2)}, u32[]{:S(2)}) %collective-permute-start.6) | collective-permute-done | bytes 40992 | tf_op jit(solution)/shard_map/ppermute | solution.py:47
  29.9 1.5 %collective-permute-start.13 = (bf16[8,16,512]{2,1,0:T(8,128)(2,1)S(1)}, bf16[8,16,512]{2,1,0:T(8,128)(2,1)S(1)}, u32[]{:S(2)}, u32[]{:S(2)}) collective-permute-start(bf16[8,16,512]{2,1,0:T(8,128)(2,1)S(1)} %bitcast.34), channel_id=1, source_target_pairs={{0,5},{1,4},{2,7},{3,6},{4,1},{5,0},{6,3},{7,2},{8,13},{9,12},{10,... | collective-permute-start | bytes 393224 | tf_op jit(solution)/shard_map/ppermute | solution.py:47
  31.4 1.3 %collective-permute-start.7 = (bf16[160,128]{1,0:T(8,128)(2,1)S(1)}, bf16[160,128]{1,0:T(8,128)(2,1)S(1)}, u32[]{:S(2)}, u32[]{:S(2)}) collective-permute-start(bf16[160,128]{1,0:T(8,128)(2,1)S(1)} %add.3.keep_ref), channel_id=1, source_target_pairs={{0,9},{1,8},{2,11},{3,10},{4,13},{5,12},{6,15},{7,14},{8,1},{9,0},... | collective-permute-start | bytes 122888 | tf_op jit(solution)/shard_map/ppermute | solution.py:47
  32.7 2.2 %collective-permute-done.7.got_ref = bf16[160,128]{1,0:T(8,128)(2,1)S(1)} collective-permute-done((bf16[160,128]{1,0:T(8,128)(2,1)S(1)}, bf16[160,128]{1,0:T(8,128)(2,1)S(1)}, u32[]{:S(2)}, u32[]{:S(2)}) %collective-permute-start.7) | collective-permute-done | bytes 40992 | tf_op jit(solution)/shard_map/ppermute | solution.py:47
  34.9 0.3 collective-permute-done.13
  35.3 0.4 collective-permute-start.14
  35.6 0.9 %collective-permute-start.8 = (bf16[160,128]{1,0:T(8,128)(2,1)S(1)}, bf16[160,128]{1,0:T(8,128)(2,1)S(1)}, u32[]{:S(2)}, u32[]{:S(2)}) collective-permute-start(bf16[160,128]{1,0:T(8,128)(2,1)S(1)} %add.4.keep_ref), channel_id=1, source_target_pairs={{0,17},{1,16},{2,19},{3,18},{4,21},{5,20},{6,23},{7,22},{8,25},{9,... | collective-permute-start | bytes 122888 | tf_op jit(solution)/shard_map/ppermute | solution.py:47
  36.5 3.6 %collective-permute-done.8.got_ref = bf16[160,128]{1,0:T(8,128)(2,1)S(1)} collective-permute-done((bf16[160,128]{1,0:T(8,128)(2,1)S(1)}, bf16[160,128]{1,0:T(8,128)(2,1)S(1)}, u32[]{:S(2)}, u32[]{:S(2)}) %collective-permute-start.8) | collective-permute-done | bytes 40992 | tf_op jit(solution)/shard_map/ppermute | solution.py:47
  40.1 1.3 %collective-permute-start.9 = (bf16[160,128]{1,0:T(8,128)(2,1)S(1)}, bf16[160,128]{1,0:T(8,128)(2,1)S(1)}, u32[]{:S(2)}, u32[]{:S(2)}) collective-permute-start(bf16[160,128]{1,0:T(8,128)(2,1)S(1)} %add.5), channel_id=1, source_target_pairs={{0,5},{1,4},{2,7},{3,6},{4,1},{5,0},{6,3},{7,2},{8,13},{9,12},{10,... | collective-permute-start | bytes 122888 | tf_op jit(solution)/shard_map/ppermute | solution.py:47
  41.4 2.3 %collective-permute-done.9 = bf16[160,128]{1,0:T(8,128)(2,1)S(1)} collective-permute-done((bf16[160,128]{1,0:T(8,128)(2,1)S(1)}, bf16[160,128]{1,0:T(8,128)(2,1)S(1)}, u32[]{:S(2)}, u32[]{:S(2)}) %collective-permute-start.9) | collective-permute-done | bytes 40992 | tf_op jit(solution)/shard_map/ppermute | solution.py:47
  43.7 0.8 %collective-permute-start.10 = (bf16[320,128]{1,0:T(8,128)(2,1)S(1)}, bf16[320,128]{1,0:T(8,128)(2,1)S(1)}, u32[]{:S(2)}, u32[]{:S(2)}) collective-permute-start(bf16[320,128]{1,0:T(8,128)(2,1)S(1)} %bitcast.36), channel_id=1, source_target_pairs={{0,3},{1,2},{2,1},{3,0},{4,7},{5,6},{6,5},{7,4},{8,11},{9,10},{10,... | collective-permute-start | bytes 245768 | tf_op jit(solution)/shard_map/ppermute | solution.py:47
  44.5 0.1 join_cores.1
  44.6 1.0 %prepare.1 = (bf16[4608,256]{1,0:T(8,128)(2,1)S(1)}, f32[512,512]{1,0:T(8,128)S(1)}) custom-call(bf16[2304,512]{1,0:T(8,128)(2,1)S(1)} %bitcast.28, bf16[512,512]{1,0:T(8,128)(2,1)S(1)} %bitcast.33), custom_call_target="tpu_custom_call" | custom-call | flops 2000000000 | bytes 6000000 | tf_op jit(solution)/shard_map/prepare/pallas_call | solution.py:542
  45.6 2.6 %collective-permute-done.10 = bf16[320,128]{1,0:T(8,128)(2,1)S(1)} collective-permute-done((bf16[320,128]{1,0:T(8,128)(2,1)S(1)}, bf16[320,128]{1,0:T(8,128)(2,1)S(1)}, u32[]{:S(2)}, u32[]{:S(2)}) %collective-permute-start.10) | collective-permute-done | bytes 81952 | tf_op jit(solution)/shard_map/ppermute | solution.py:47
  48.3 0.2 collective-permute-start.15
  48.5 1.3 %collective-permute-done.15.other_ref = bf16[640,128]{1,0:T(8,128)(2,1)S(1)} collective-permute-done((bf16[640,128]{1,0:T(8,128)(2,1)S(1)}, bf16[640,128]{1,0:T(8,128)(2,1)S(1)}, u32[]{:S(2)}, u32[]{:S(2)}) %collective-permute-start.15) | collective-permute-done | bytes 163872 | tf_op jit(solution)/shard_map/ppermute | solution.py:47
  49.7 4.5 %grad_conv.1 = (f32[16,512]{1,0:T(8,128)}, bf16[1024,256]{1,0:T(8,128)(2,1)}) custom-call(bf16[640,128]{1,0:T(8,128)(2,1)S(1)} %bitcast.32, bf16[640,128]{1,0:T(8,128)(2,1)S(1)} %collective-permute-done.15.other_ref, f32[512,512]{1,0:T(8,128)S(1)} %get-tuple-element.62.both_ref, bf16[768,512]{1,0:T(8,128)(2,1)S(1)} %get-tuple-element.64.in_feat_ref, ...), custom_call_target="tpu_custom_call" | custom-call | tf_op jit(solution)/shard_map/grad_conv/pallas_call | solution.py:560
  (28 shorter events, 0.4 us)
Async XLA Ops:
  0.6 1.0 %copy-start.1 = (bf16[8,128,256]{2,1,0:T(8,128)(2,1)S(1)}, bf16[8,128,256]{2,1,0:T(8,128)(2,1)}, u32[]{:S(2)}) copy-start(bf16[8,128,256]{2,1,0:T(8,128)(2,1)} %own_ref.3) | copy-start | bytes 1572868
  1.7 1.4 %copy-start.3 = (f32[16,512]{1,0:T(8,128)S(1)}, f32[16,512]{1,0:T(8,128)}, u32[]{:S(2)}) copy-start(f32[16,512]{1,0:T(8,128)} %target_ref.1) | copy-start | bytes 98308
  1.7 7.4 %copy-start = (bf16[3,3,256,512]{3,2,1,0:T(8,128)(2,1)S(1)}, bf16[3,3,256,512]{3,2,1,0:T(8,128)(2,1)}, u32[]{:S(2)}) copy-start(bf16[3,3,256,512]{3,2,1,0:T(8,128)(2,1)} %param.5) | copy-start | bytes 7077892
  1.7 7.4 %copy-start.2 = (bf16[8,128,256]{2,1,0:T(8,128)(2,1)S(1)}, bf16[8,128,256]{2,1,0:T(8,128)(2,1)}, u32[]{:S(2)}) copy-start(bf16[8,128,256]{2,1,0:T(8,128)(2,1)} %own_ref.3) | copy-start | bytes 1572868
  1.7 7.4 %copy-start.4 = (bf16[512]{0:T(512)(128)(2,1)S(1)}, bf16[512]{0:T(512)(128)(2,1)}, u32[]{:S(2)}) copy-start(bf16[512]{0:T(512)(128)(2,1)} %bias_ref.1) | copy-start | bytes 3076
  1.7 1.3 %collective-permute-start = (bf16[2,8,256]{2,1,0:T(8,128)(2,1)S(1)}, bf16[2,8,256]{2,1,0:T(8,128)(2,1)S(1)}, u32[]{:S(2)}, u32[]{:S(2)}) collective-permute-start(bf16[2,8,256]{2,1,0:T(8,128)(2,1)S(1)} %column_rims.1), channel_id=1, source_target_pairs={{0,1},{1,0},{2,3},{3,2},{4,5},{5,4},{6,7},{7,6},{8,9},{9,8},{10,11... | collective-permute-start | bytes 24584 | tf_op jit(solution)/shard_map/ppermute | solution.py:470
  3.1 8.9 %collective-permute-start.3 = (bf16[1,16,512]{2,1,0:T(8,128)(2,1)S(1)}, bf16[1,16,512]{2,1,0:T(8,128)(2,1)S(1)}, u32[]{:S(2)}, u32[]{:S(2)}) collective-permute-start(bf16[1,16,512]{2,1,0:T(8,128)(2,1)S(1)} %get-tuple-element.43), channel_id=1, source_target_pairs={{0,17},{1,16},{2,19},{3,18},{4,21},{5,20},{6,23},{7,22},{8,25},{9,... | collective-permute-start | bytes 49160 | tf_op jit(solution)/shard_map/ppermute | solution.py:47
  6.9 5.9 %collective-permute-start.1 = (bf16[272,256]{1,0:T(8,128)(2,1)S(1)}, bf16[272,256]{1,0:T(8,128)(2,1)S(1)}, u32[]{:S(2)}, u32[]{:S(2)}) collective-permute-start(bf16[272,256]{1,0:T(8,128)(2,1)S(1)} %get-tuple-element.36), channel_id=1, source_target_pairs={{0,2},{2,0},{4,6},{6,4},{8,10},{10,8},{12,14},{14,12},{16,18},{18,... | collective-permute-start | bytes 417800 | tf_op jit(solution)/shard_map/ppermute | solution.py:31
  8.4 4.4 %collective-permute-start.2 = (bf16[272,256]{1,0:T(8,128)(2,1)S(1)}, bf16[272,256]{1,0:T(8,128)(2,1)S(1)}, u32[]{:S(2)}, u32[]{:S(2)}) collective-permute-start(bf16[272,256]{1,0:T(8,128)(2,1)S(1)} %get-tuple-element.37), channel_id=1, source_target_pairs={{0,0},{2,4},{4,2},{6,8},{8,6},{10,12},{12,10},{14,16},{16,14},{18,... | collective-permute-start | bytes 417800 | tf_op jit(solution)/shard_map/ppermute | solution.py:31
  15.1 1.5 %collective-permute-start.4 = (bf16[640,128]{1,0:T(8,128)(2,1)S(1)}, bf16[640,128]{1,0:T(8,128)(2,1)S(1)}, u32[]{:S(2)}, u32[]{:S(2)}) collective-permute-start(bf16[640,128]{1,0:T(8,128)(2,1)S(1)} %get-tuple-element.46), channel_id=1, source_target_pairs={{0,1},{1,0},{2,3},{3,2},{4,5},{5,4},{6,7},{7,6},{8,9},{9,8},{10,11... | collective-permute-start | bytes 491528 | tf_op jit(solution)/shard_map/ppermute | solution.py:47
  16.6 8.6 %collective-permute-start.5 = (bf16[320,128]{1,0:T(8,128)(2,1)S(1)}, bf16[320,128]{1,0:T(8,128)(2,1)S(1)}, u32[]{:S(2)}, u32[]{:S(2)}) collective-permute-start(bf16[320,128]{1,0:T(8,128)(2,1)S(1)} %get-tuple-element.48), channel_id=1, source_target_pairs={{0,3},{1,2},{2,1},{3,0},{4,7},{5,6},{6,5},{7,4},{8,11},{9,10},{10,... | collective-permute-start | bytes 245768 | tf_op jit(solution)/shard_map/ppermute | solution.py:47
  21.8 3.4 %collective-permute-start.11 = (bf16[2,16,512]{2,1,0:T(8,128)(2,1)S(1)}, bf16[2,16,512]{2,1,0:T(8,128)(2,1)S(1)}, u32[]{:S(2)}, u32[]{:S(2)}) collective-permute-start(bf16[2,16,512]{2,1,0:T(8,128)(2,1)S(1)} %bitcast.41), channel_id=1, source_target_pairs={{0,9},{1,8},{2,11},{3,10},{4,13},{5,12},{6,15},{7,14},{8,1},{9,0},... | collective-permute-start | bytes 98312 | tf_op jit(solution)/shard_map/ppermute | solution.py:47
  25.2 4.6 %collective-permute-start.12 = (bf16[4,16,512]{2,1,0:T(8,128)(2,1)S(1)}, bf16[4,16,512]{2,1,0:T(8,128)(2,1)S(1)}, u32[]{:S(2)}, u32[]{:S(2)}) collective-permute-start(bf16[4,16,512]{2,1,0:T(8,128)(2,1)S(1)} %bitcast.38), channel_id=1, source_target_pairs={{0,3},{1,2},{2,1},{3,0},{4,7},{5,6},{6,5},{7,4},{8,11},{9,10},{10,... | collective-permute-start | bytes 196616 | tf_op jit(solution)/shard_map/ppermute | solution.py:47
  26.4 3.4 %collective-permute-start.6 = (bf16[160,128]{1,0:T(8,128)(2,1)S(1)}, bf16[160,128]{1,0:T(8,128)(2,1)S(1)}, u32[]{:S(2)}, u32[]{:S(2)}) collective-permute-start(bf16[160,128]{1,0:T(8,128)(2,1)S(1)} %get-tuple-element.50), channel_id=1, source_target_pairs={{0,5},{1,4},{2,7},{3,6},{4,1},{5,0},{6,3},{7,2},{8,13},{9,12},{10,... | collective-permute-start | bytes 122888 | tf_op jit(solution)/shard_map/ppermute | solution.py:47
  29.9 5.4 %collective-permute-start.13 = (bf16[8,16,512]{2,1,0:T(8,128)(2,1)S(1)}, bf16[8,16,512]{2,1,0:T(8,128)(2,1)S(1)}, u32[]{:S(2)}, u32[]{:S(2)}) collective-permute-start(bf16[8,16,512]{2,1,0:T(8,128)(2,1)S(1)} %bitcast.34), channel_id=1, source_target_pairs={{0,5},{1,4},{2,7},{3,6},{4,1},{5,0},{6,3},{7,2},{8,13},{9,12},{10,... | collective-permute-start | bytes 393224 | tf_op jit(solution)/shard_map/ppermute | solution.py:47
  31.4 3.5 %collective-permute-start.7 = (bf16[160,128]{1,0:T(8,128)(2,1)S(1)}, bf16[160,128]{1,0:T(8,128)(2,1)S(1)}, u32[]{:S(2)}, u32[]{:S(2)}) collective-permute-start(bf16[160,128]{1,0:T(8,128)(2,1)S(1)} %add.3.keep_ref), channel_id=1, source_target_pairs={{0,9},{1,8},{2,11},{3,10},{4,13},{5,12},{6,15},{7,14},{8,1},{9,0},... | collective-permute-start | bytes 122888 | tf_op jit(solution)/shard_map/ppermute | solution.py:47
  35.3 9.2 %collective-permute-start.14 = (bf16[16,16,512]{2,1,0:T(8,128)(2,1)S(1)}, bf16[16,16,512]{2,1,0:T(8,128)(2,1)S(1)}, u32[]{:S(2)}, u32[]{:S(2)}) collective-permute-start(bf16[16,16,512]{2,1,0:T(8,128)(2,1)S(1)} %bitcast.29), channel_id=1, source_target_pairs={{0,1},{1,0},{2,3},{3,2},{4,5},{5,4},{6,7},{7,6},{8,9},{9,8},{10,11... | collective-permute-start | bytes 786440 | tf_op jit(solution)/shard_map/ppermute | solution.py:47
  35.6 4.4 %collective-permute-start.8 = (bf16[160,128]{1,0:T(8,128)(2,1)S(1)}, bf16[160,128]{1,0:T(8,128)(2,1)S(1)}, u32[]{:S(2)}, u32[]{:S(2)}) collective-permute-start(bf16[160,128]{1,0:T(8,128)(2,1)S(1)} %add.4.keep_ref), channel_id=1, source_target_pairs={{0,17},{1,16},{2,19},{3,18},{4,21},{5,20},{6,23},{7,22},{8,25},{9,... | collective-permute-start | bytes 122888 | tf_op jit(solution)/shard_map/ppermute | solution.py:47
  40.1 3.6 %collective-permute-start.9 = (bf16[160,128]{1,0:T(8,128)(2,1)S(1)}, bf16[160,128]{1,0:T(8,128)(2,1)S(1)}, u32[]{:S(2)}, u32[]{:S(2)}) collective-permute-start(bf16[160,128]{1,0:T(8,128)(2,1)S(1)} %add.5), channel_id=1, source_target_pairs={{0,5},{1,4},{2,7},{3,6},{4,1},{5,0},{6,3},{7,2},{8,13},{9,12},{10,... | collective-permute-start | bytes 122888 | tf_op jit(solution)/shard_map/ppermute | solution.py:47
  43.7 4.5 %collective-permute-start.10 = (bf16[320,128]{1,0:T(8,128)(2,1)S(1)}, bf16[320,128]{1,0:T(8,128)(2,1)S(1)}, u32[]{:S(2)}, u32[]{:S(2)}) collective-permute-start(bf16[320,128]{1,0:T(8,128)(2,1)S(1)} %bitcast.36), channel_id=1, source_target_pairs={{0,3},{1,2},{2,1},{3,0},{4,7},{5,6},{6,5},{7,4},{8,11},{9,10},{10,... | collective-permute-start | bytes 245768 | tf_op jit(solution)/shard_map/ppermute | solution.py:47
  48.3 1.5 %collective-permute-start.15 = (bf16[640,128]{1,0:T(8,128)(2,1)S(1)}, bf16[640,128]{1,0:T(8,128)(2,1)S(1)}, u32[]{:S(2)}, u32[]{:S(2)}) collective-permute-start(bf16[640,128]{1,0:T(8,128)(2,1)S(1)} %bitcast.31), channel_id=1, source_target_pairs={{0,1},{1,0},{2,3},{3,2},{4,5},{5,4},{6,7},{7,6},{8,9},{9,8},{10,11... | collective-permute-start | bytes 491528 | tf_op jit(solution)/shard_map/ppermute | solution.py:47

commit v2 on v1

--- a/solution.py
+++ b/solution.py
@@ -70,6 +70,10 @@
     return pl.ds(pl.multiple_of(index * count, count), count)
 
 
+waiting = pl.CostEstimate(flops=1_500_000_000, bytes_accessed=100_000, transcendentals=0)
+chained = pl.CostEstimate(flops=8_000_000_000, bytes_accessed=100_000, transcendentals=0)
+
+
 def halve(keep, got, bit):
     half = keep.shape[0] // 2
 
@@ -86,6 +90,7 @@
         "halve",
         keep,
         got,
+        cost_estimate=chained,
     )
 
 
@@ -93,20 +98,20 @@
     def body(keep_ref, got_ref, sum_ref):
         sum_ref[...] = (keep_ref[...].astype(f32) + got_ref[...].astype(f32)).astype(bf16)
 
-    return local(body, jax.ShapeDtypeStruct(got.shape, bf16), "add", keep, got)
-
-
-def join(mine, other, bit):
+    return local(body, jax.ShapeDtypeStruct(got.shape, bf16), "add", keep, got, cost_estimate=chained)
+
+
+def join(mine, other, bit, **kwargs):
     def body(mine_ref, other_ref, both_ref):
         side = side_of(bit)
         both_ref[:, pl.ds(side, 1)] = mine_ref[...][:, None]
         both_ref[:, pl.ds(1 - side, 1)] = other_ref[...][:, None]
 
     shape = (mine.shape[0], 2, *mine.shape[1:])
-    return local(body, jax.ShapeDtypeStruct(shape, mine.dtype), "join", mine, other)
-
-
-def join_cores(mine, other):
+    return local(body, jax.ShapeDtypeStruct(shape, mine.dtype), "join", mine, other, **kwargs)
+
+
+def join_cores(mine, other, **kwargs):
     def body(mine_ref, other_ref, both_ref):
         side = side_of(0)
         for chip in range(mine.shape[0]):
@@ -115,30 +120,32 @@
             both_ref[chip, pl.ds(1 - core, 1)] = other_ref[chip][None]
 
     shape = (mine.shape[0], 2, *mine.shape[1:])
-    return local(body, jax.ShapeDtypeStruct(shape, mine.dtype), "join_cores", mine, other)
+    return local(body, jax.ShapeDtypeStruct(shape, mine.dtype), "join_cores", mine, other, **kwargs)
 
 
 class Gather:
     def __init__(self, rows):
-        self.rows, self.done = rows, []
-
-    def step(self, bit, after, until=None):
+        self.rows, self.got, self.done = rows, None, []
+
+    def settle(self, after):
+        if self.got is None:
+            self.rows, _ = lax.optimization_barrier((self.rows, after))
+            return
         share = self.rows.shape[-2:]
-        send, _ = lax.optimization_barrier((self.rows, after))
-        got = swap(send, bit)
-        if until is not None:
-            got, _ = lax.optimization_barrier((got, until))
+        got, _ = lax.optimization_barrier((self.got, after))
+        bit = self.done[-1]
         if bit > 0:
             lead = 1 << sum(other > bit for other in self.done)
-            send, got = (part.reshape(lead, -1, *share) for part in (send, got))
-            self.rows = join(send, got, bit).reshape(-1, *share)
+            mine, got = (part.reshape(lead, -1, *share) for part in (self.rows, got))
+            both = join(mine, got, bit, cost_estimate=waiting)
         else:
-            self.rows = join_cores(send, got).reshape(-1, *share)
+            both = join_cores(self.rows, got, cost_estimate=waiting)
+        self.rows, self.got = both.reshape(-1, *share), None
+
+    def step(self, bit, after):
+        self.settle(after)
+        self.got = swap(self.rows, bit)
         self.done.append(bit)
-
-    def before(self, value):
-        value, self.rows = lax.optimization_barrier((value, self.rows))
-        return value
 
 
 def sum_all(send, keep, beside):
@@ -158,7 +165,7 @@
         mine = add(mine, step(mine, bit, f"add {bit}"))
     for bit in reversed(halving):
         got = step(mine, bit, f"join {bit}")
-        mine = join(mine[None], got[None], bit).reshape(-1, mine.shape[1])
+        mine = join(mine[None], got[None], bit, cost_estimate=chained).reshape(-1, mine.shape[1])
     return mine, step(mine, 0, "halves")
 
 
@@ -273,16 +280,22 @@
     tile_rows, tile_cols, in_width, out_width, step = shape
     lefts, rights = left_ref[1].astype(f32), right_ref[0].astype(f32)
     for r in range(tile_rows):
-        spots = [(r - a, a) for a in range(3) if 0 <= r - a < tile_rows - 2]
-        fill_patches(cat_ref, spots, own_ref[r], lefts[r : r + 1], rights[r : r + 1])
+        fill_row(cat_ref, r, own_ref[r], lefts[r : r + 1], rights[r : r + 1])
+    bias = row_ref[...]
     root = 1.0 / math.sqrt(out_width)
-    for at in (slice(0, out_width // 2), slice(out_width // 2, out_width)):
-        total = row_ref[:, at] + jnp.dot(
-            cat_ref[...], kernel_ref[:, at], preferred_element_type=f32
-        )
+    span = 3 * in_width
+    for h in range(0, tile_rows - 2, step):
+        total = bias
+        for a in range(3):
+            total = total + jnp.dot(
+                cat_ref[(h + a) * tile_cols : (h + a + step) * tile_cols, :],
+                kernel_ref[a * span : (a + 1) * span, :],
+                preferred_element_type=f32,
+            )
         features, slope = gelu_pair(total)
-        feat_ref[:, at] = features.astype(bf16)
-        slope_ref[:, at] = (slope * root).astype(bf16)
+        at = slice(h * tile_cols, (h + step) * tile_cols)
+        feat_ref[at, :] = features.astype(bf16)
+        slope_ref[at, :] = (slope * root).astype(bf16)
     gram_tiles(feat_ref[...], gram_ref)
 
 
@@ -423,28 +436,46 @@
 
     main = 2 * tile_cols
     edges = grad_of(out_feat_ref, out_slope_ref, slice(2 * main, None))
-    lines = [
-        (out_feat_ref, out_slope_ref, 0, 0),
-        (out_feat_ref, out_slope_ref, main, tile_rows),
-    ] + [
-        (in_feat_ref, in_slope_ref, h * tile_cols, h + 2) for h in range(0, tile_rows - 2, step)
-    ]
-    for feat_ref, slope_ref, begin, r in lines:
-        grad = grad_of(feat_ref, slope_ref, slice(begin, begin + step * tile_cols))
+    lines = [(out_feat_ref, out_slope_ref, 0)]
+    lines += [(in_feat_ref, in_slope_ref, h * tile_cols) for h in range(0, tile_rows - 2, step)]
+    lines += [(out_feat_ref, out_slope_ref, main)]
+    grads = {}
+
+    def upstream(c):
+        feat_ref, slope_ref, begin = lines[c]
+        grads[c] = grad_of(feat_ref, slope_ref, slice(begin, begin + step * tile_cols))
+
+    def fill(c):
         for k in range(step):
+            r = c * step + k
             fill_row(
-                cat_ref, r + k, grad[k * tile_cols : (k + 1) * tile_cols],
-                edges[r + k : r + k + 1], edges[edge + r + k : edge + r + k + 1],
+                cat_ref, r, grads[c][k * tile_cols : (k + 1) * tile_cols],
+                edges[r : r + 1], edges[edge + r : edge + r + 1],
             )
-    total = 0.0
+
     span = 3 * out_width
-    for a in range(3):
-        total = total + jnp.dot(
-            cat_ref[(2 - a) * tile_cols : (2 - a + tile_rows) * tile_cols, :],
-            turned_ref[a * span : (a + 1) * span, :],
-            preferred_element_type=f32,
-        )
-    out_ref[...] = total.astype(bf16)
+
+    def convolve(begin, count):
+        total = 0.0
+        for a in range(3):
+            total = total + jnp.dot(
+                cat_ref[(begin + 2 - a) * tile_cols : (begin + 2 - a + count) * tile_cols, :],
+                turned_ref[a * span : (a + 1) * span, :],
+                preferred_element_type=f32,
+            )
+        out_ref[begin * tile_cols : (begin + count) * tile_cols, :] = total.astype(bf16)
+
+    last = len(lines) - 1
+    middle = last // 2
+    half_rows = middle * step
+    upstream(0)
+    for c in range(last):
+        upstream(c + 1)
+        fill(c)
+        if c == middle:
+            convolve(0, half_rows)
+    fill(last)
+    convolve(half_rows, tile_rows - half_rows)
 
 
 def on_device(canvas, conv_weight, conv_bias, target_gram):
@@ -481,12 +512,11 @@
         *beyond,
     )
     count = lax.axis_size("rows")
-    even, odd = swap_rows([range(0, count - 1, 2), range(1, count - 1, 2)], [even, odd])
+    odd, even = swap_rows([range(1, count - 1, 2), range(0, count - 1, 2)], [odd, even])
 
     bits = (lax.axis_size("rows") * lax.axis_size("cols")).bit_length() - 1
     gather = Gather(rows)
     far = list(reversed(range(3, bits)))
-    gather.step(far[0], left)
     inner = (tile_rows - 2) * tile_cols
     in_feat, in_slope, in_gram, bias = pl.pallas_call(
         functools.partial(inner_kernel, shape),
@@ -497,7 +527,7 @@
             jax.ShapeDtypeStruct((1, out_width), f32),
         ),
         in_specs=[vmem] * 5,
-        scratch_shapes=[pltpu.VMEM((inner, 9 * in_width), bf16)],
+        scratch_shapes=[pltpu.VMEM((tile_rows * tile_cols, 3 * in_width), bf16)],
         compiler_params=params,
         name="inner_rows",
         cost_estimate=pl.CostEstimate(
@@ -507,7 +537,6 @@
         ),
     )(canvas, left, right, kernel, conv_bias)
 
-    in_gram = gather.before(in_gram)
     outer = 4 * tile_cols + 2 * edge
     half_gram = (packed_shape.shape[0] // 2, tile)
     out_feat, out_slope, send, keep = pl.pallas_call(
@@ -529,15 +558,15 @@
         name="outer_rows",
     )(canvas, even, odd, left, right, kernel, bias, in_gram)
 
-    exchanges = {"cores": far[1:2], "halve 2": [*far[2:], 1], "add 3": [2], "add 4": [0]}
+    exchanges = {"halve 1": far[:1], "halve 2": far[1:], "add 3": [2], "add 4": [1], "join 2": [0]}
     prepared = []
 
     def beside(name, sent, got):
         for bit in exchanges.get(name, []):
-            gather.step(bit, sent, got)
+            gather.step(bit, sent)
         if name != "join 1":
             return got
-        rows, _ = lax.optimization_barrier((gather.rows, sent))
+        gather.settle(sent)
         prepared.extend(
             pl.pallas_call(
                 prepare_kernel,
@@ -551,7 +580,7 @@
                 cost_estimate=pl.CostEstimate(
                     flops=2_000_000_000, bytes_accessed=6_000_000, transcendentals=0
                 ),
-            )(kernel, rows.reshape(out_width, out_width))
+            )(kernel, gather.rows.reshape(out_width, out_width))
         )
         return lax.optimization_barrier((got, *prepared))[0]
 

time: 54.4 us -> 49.5 us (0.910)
  waiting for transfers between devices: 19 us -> 12.7 us
  starting transfers between devices: 22.2 us -> 24 us
    ppermute x13, waiting for transfers between devices: 17.5 us -> 11.3 us  [swap(): lax.ppermute(value, ('rows', 'cols'), [(i, i ^ (1 << bit | 1)) for i in r...]
    ppermute x2, starting transfers between devices: 2.15 us -> 3.55 us  [swap_rows(): lax.ppermute(value, 'rows', perm(low))]
  transfers between devices with their start and end apart: 16 -> 16, of which waited for: 11 -> 10; matrix products, arithmetic and copies ran while one was open for 0% -> 0% of each run, Pallas kernels for 8% -> 8%
where the time goes in v2:
time: 49.5 us; the launch traced here: 49.3 us
  starting transfers between devices  24 us (48%)
  waiting for transfers between devices  12.7 us (26%)
  Pallas kernels  10.8 us (22%)
  local copies, waits for them, and re-layouts  1.05 us (2%)
  between operations  0.77 us (2%)
    ppermute x13, starting transfers between devices, swap(): lax.ppermute(value, ('rows', 'cols'), [(i, i ^ (1 << bit | 1)) for i in r...  19.9 us
    ppermute x13, waiting for transfers between devices, swap(): lax.ppermute(value, ('rows', 'cols'), [(i, i ^ (1 << bit | 1)) for i in r...  11.3 us
    pallas_call x1, Pallas kernels, on_device(): pl.pallas_call(functools.partial(backward_kernel, shape, pixel_total), ou...  4.44 us
    ppermute x2, starting transfers between devices, swap_rows(): lax.ppermute(value, 'rows', perm(low))  3.55 us
    pallas_call x1, Pallas kernels, on_device(): pl.pallas_call(functools.partial(inner_kernel, shape), out_shape=(jax.Sha...  2.79 us
    pallas_call x1, Pallas kernels, on_device(): pl.pallas_call(functools.partial(outer_kernel, shape), out_shape=(jax.Sha...  2.3 us
    unnamed x10, local copies, waits for them, and re-layouts  1.05 us
  transfers between devices with their start and end apart: 16, of which 10 were waited for; matrix products, arithmetic and copies ran while one was open for 0% of the time, Pallas kernels for 8%

profile of v2, /device:TPU:0, one launch (start us, length us, event | category | flops | bytes accessed | tf_op | source)
XLA Modules:
  0.0 49.3 jit_solution(4808453741685879618)
XLA Ops:
  0.6 1.0 %copy-done.1 = bf16[8,128,256]{2,1,0:T(8,128)(2,1)S(1)} copy-done((bf16[8,128,256]{2,1,0:T(8,128)(2,1)S(1)}, bf16[8,128,256]{2,1,0:T(8,128)(2,1)}, u32[]{:S(2)}) %copy-start.1) | copy-done | bytes 524312
  1.7 0.5 %collective-permute-start = (bf16[2,8,256]{2,1,0:T(8,128)(2,1)S(1)}, bf16[2,8,256]{2,1,0:T(8,128)(2,1)S(1)}, u32[]{:S(2)}, u32[]{:S(2)}) collective-permute-start(bf16[2,8,256]{2,1,0:T(8,128)(2,1)S(1)} %column_rims.1), channel_id=1, source_target_pairs={{0,1},{1,0},{2,3},{3,2},{4,5},{5,4},{6,7},{7,6},{8,9},{9,8},{10,11... | collective-permute-start | bytes 24584 | tf_op jit(solution)/shard_map/ppermute | solution.py:501
  2.2 0.8 %collective-permute-done.refs_0_ = bf16[2,8,256]{2,1,0:T(8,128)(2,1)S(1)} collective-permute-done((bf16[2,8,256]{2,1,0:T(8,128)(2,1)S(1)}, bf16[2,8,256]{2,1,0:T(8,128)(2,1)S(1)}, u32[]{:S(2)}, u32[]{:S(2)}) %collective-permute-start) | collective-permute-done | bytes 8224 | tf_op jit(solution)/shard_map/ppermute | solution.py:501
  3.1 2.9 %collective-permute-start.1 = (bf16[272,256]{1,0:T(8,128)(2,1)S(1)}, bf16[272,256]{1,0:T(8,128)(2,1)S(1)}, u32[]{:S(2)}, u32[]{:S(2)}) collective-permute-start(bf16[272,256]{1,0:T(8,128)(2,1)S(1)} %get-tuple-element.30), channel_id=1, source_target_pairs={{0,2},{2,0},{4,6},{6,4},{8,10},{10,8},{12,14},{14,12},{16,18},{18,... | collective-permute-start | bytes 417800 | tf_op jit(solution)/shard_map/ppermute | solution.py:31
  6.0 0.7 %collective-permute-start.2 = (bf16[272,256]{1,0:T(8,128)(2,1)S(1)}, bf16[272,256]{1,0:T(8,128)(2,1)S(1)}, u32[]{:S(2)}, u32[]{:S(2)}) collective-permute-start(bf16[272,256]{1,0:T(8,128)(2,1)S(1)} %get-tuple-element.31), channel_id=1, source_target_pairs={{0,0},{2,4},{4,2},{6,8},{8,6},{10,12},{12,10},{14,16},{16,14},{18,... | collective-permute-start | bytes 417800 | tf_op jit(solution)/shard_map/ppermute | solution.py:31
  6.7 2.8 %inner_rows.1 = (bf16[768,512]{1,0:T(8,128)(2,1)S(1)}, bf16[768,512]{1,0:T(8,128)(2,1)S(1)}, f32[1280,128]{1,0:T(8,128)S(1)}, f32[1,512]{1,0:T(1,128)S(1)}) custom-call(bf16[8,128,256]{2,1,0:T(8,128)(2,1)S(1)} %copy-done.2, bf16[2,8,256]{2,1,0:T(8,128)(2,1)S(1)} %get-tuple-element.32.left_ref, bf16[2,8,256]{2,1,0:T(8,128)(2,1)S(1)} %get-tuple-element.33.right_ref, ...), custom_call_target="tpu_custom_call" | custom-call | flops 2214592512 | bytes 6000000 | tf_op jit(solution)/shard_map/inner_rows/pallas_call | solution.py:521
  9.5 0.5 %collective-permute-done.1.even_ref = bf16[272,256]{1,0:T(8,128)(2,1)S(1)} collective-permute-done((bf16[272,256]{1,0:T(8,128)(2,1)S(1)}, bf16[272,256]{1,0:T(8,128)(2,1)S(1)}, u32[]{:S(2)}, u32[]{:S(2)}) %collective-permute-start.1) | collective-permute-done | bytes 139296 | tf_op jit(solution)/shard_map/ppermute | solution.py:31
  10.0 2.3 %outer_rows.1 = (bf16[544,512]{1,0:T(8,128)(2,1)S(1)}, bf16[544,512]{1,0:T(8,128)(2,1)S(1)}, bf16[640,128]{1,0:T(8,128)(2,1)S(1)}, f32[640,128]{1,0:T(8,128)S(1)}) custom-call(bf16[8,128,256]{2,1,0:T(8,128)(2,1)S(1)} %copy-done.2, bf16[272,256]{1,0:T(8,128)(2,1)S(1)} %collective-permute-done.1.even_ref, bf16[272,256]{1,0:T(8,128)(2,1)S(1)} %collective-permute-done.2.odd_ref, ...), custom_call_target="tpu_custom_call" | custom-call | tf_op jit(solution)/shard_map/outer_rows/pallas_call | solution.py:542
  12.3 0.1 collective-permute-start.3
  12.4 1.4 %collective-permute-done.3.got_ref = bf16[640,128]{1,0:T(8,128)(2,1)S(1)} collective-permute-done((bf16[640,128]{1,0:T(8,128)(2,1)S(1)}, bf16[640,128]{1,0:T(8,128)(2,1)S(1)}, u32[]{:S(2)}, u32[]{:S(2)}) %collective-permute-start.3) | collective-permute-done | bytes 163872 | tf_op jit(solution)/shard_map/ppermute | solution.py:47
  13.8 5.5 %collective-permute-start.4 = (bf16[320,128]{1,0:T(8,128)(2,1)S(1)}, bf16[320,128]{1,0:T(8,128)(2,1)S(1)}, u32[]{:S(2)}, u32[]{:S(2)}) collective-permute-start(bf16[320,128]{1,0:T(8,128)(2,1)S(1)} %get-tuple-element.39), channel_id=1, source_target_pairs={{0,3},{1,2},{2,1},{3,0},{4,7},{5,6},{6,5},{7,4},{8,11},{9,10},{10,... | collective-permute-start | bytes 245768 | tf_op jit(solution)/shard_map/ppermute | solution.py:47
  19.3 2.6 %collective-permute-start.10 = (bf16[1,16,512]{2,1,0:T(8,128)(2,1)S(1)}, bf16[1,16,512]{2,1,0:T(8,128)(2,1)S(1)}, u32[]{:S(2)}, u32[]{:S(2)}) collective-permute-start(bf16[1,16,512]{2,1,0:T(8,128)(2,1)S(1)} %get-tuple-element.43), channel_id=1, source_target_pairs={{0,17},{1,16},{2,19},{3,18},{4,21},{5,20},{6,23},{7,22},{8,25},{9,... | collective-permute-start | bytes 49160 | tf_op jit(solution)/shard_map/ppermute | solution.py:47
  21.9 2.0 %collective-permute-start.5 = (bf16[160,128]{1,0:T(8,128)(2,1)S(1)}, bf16[160,128]{1,0:T(8,128)(2,1)S(1)}, u32[]{:S(2)}, u32[]{:S(2)}) collective-permute-start(bf16[160,128]{1,0:T(8,128)(2,1)S(1)} %get-tuple-element.41), channel_id=1, source_target_pairs={{0,5},{1,4},{2,7},{3,6},{4,1},{5,0},{6,3},{7,2},{8,13},{9,12},{10,... | collective-permute-start | bytes 122888 | tf_op jit(solution)/shard_map/ppermute | solution.py:47
  23.9 1.6 %collective-permute-start.11 = (bf16[2,16,512]{2,1,0:T(8,128)(2,1)S(1)}, bf16[2,16,512]{2,1,0:T(8,128)(2,1)S(1)}, u32[]{:S(2)}, u32[]{:S(2)}) collective-permute-start(bf16[2,16,512]{2,1,0:T(8,128)(2,1)S(1)} %bitcast.39), channel_id=1, source_target_pairs={{0,9},{1,8},{2,11},{3,10},{4,13},{5,12},{6,15},{7,14},{8,1},{9,0},... | collective-permute-start | bytes 98312 | tf_op jit(solution)/shard_map/ppermute | solution.py:47
  25.5 0.1 collective-permute-done.5.got_ref
  25.6 3.1 %collective-permute-start.6 = (bf16[160,128]{1,0:T(8,128)(2,1)S(1)}, bf16[160,128]{1,0:T(8,128)(2,1)S(1)}, u32[]{:S(2)}, u32[]{:S(2)}) collective-permute-start(bf16[160,128]{1,0:T(8,128)(2,1)S(1)} %add.3.keep_ref), channel_id=1, source_target_pairs={{0,9},{1,8},{2,11},{3,10},{4,13},{5,12},{6,15},{7,14},{8,1},{9,0},... | collective-permute-start | bytes 122888 | tf_op jit(solution)/shard_map/ppermute | solution.py:47
  28.7 0.4 collective-permute-start.12
  29.1 1.4 %collective-permute-done.6.got_ref = bf16[160,128]{1,0:T(8,128)(2,1)S(1)} collective-permute-done((bf16[160,128]{1,0:T(8,128)(2,1)S(1)}, bf16[160,128]{1,0:T(8,128)(2,1)S(1)}, u32[]{:S(2)}, u32[]{:S(2)}) %collective-permute-start.6) | collective-permute-done | bytes 40992 | tf_op jit(solution)/shard_map/ppermute | solution.py:47
  30.5 2.7 %collective-permute-start.7 = (bf16[160,128]{1,0:T(8,128)(2,1)S(1)}, bf16[160,128]{1,0:T(8,128)(2,1)S(1)}, u32[]{:S(2)}, u32[]{:S(2)}) collective-permute-start(bf16[160,128]{1,0:T(8,128)(2,1)S(1)} %add.4.keep_ref), channel_id=1, source_target_pairs={{0,17},{1,16},{2,19},{3,18},{4,21},{5,20},{6,23},{7,22},{8,25},{9,... | collective-permute-start | bytes 122888 | tf_op jit(solution)/shard_map/ppermute | solution.py:47
  33.2 0.5 collective-permute-start.13
  33.7 1.3 %collective-permute-done.7.got_ref = bf16[160,128]{1,0:T(8,128)(2,1)S(1)} collective-permute-done((bf16[160,128]{1,0:T(8,128)(2,1)S(1)}, bf16[160,128]{1,0:T(8,128)(2,1)S(1)}, u32[]{:S(2)}, u32[]{:S(2)}) %collective-permute-start.7) | collective-permute-done | bytes 40992 | tf_op jit(solution)/shard_map/ppermute | solution.py:47
  35.0 0.6 %collective-permute-start.8 = (bf16[160,128]{1,0:T(8,128)(2,1)S(1)}, bf16[160,128]{1,0:T(8,128)(2,1)S(1)}, u32[]{:S(2)}, u32[]{:S(2)}) collective-permute-start(bf16[160,128]{1,0:T(8,128)(2,1)S(1)} %add.5), channel_id=1, source_target_pairs={{0,5},{1,4},{2,7},{3,6},{4,1},{5,0},{6,3},{7,2},{8,13},{9,12},{10,... | collective-permute-start | bytes 122888 | tf_op jit(solution)/shard_map/ppermute | solution.py:47
  35.6 3.1 %collective-permute-done.13 = bf16[8,16,512]{2,1,0:T(8,128)(2,1)S(1)} collective-permute-done((bf16[8,16,512]{2,1,0:T(8,128)(2,1)S(1)}, bf16[8,16,512]{2,1,0:T(8,128)(2,1)S(1)}, u32[]{:S(2)}, u32[]{:S(2)}) %collective-permute-start.13) | collective-permute-done | bytes 131104 | tf_op jit(solution)/shard_map/ppermute | solution.py:47
  38.8 0.2 collective-permute-start.14
  39.0 0.3 collective-permute-start.9
  39.4 1.0 %collective-permute-done.14.other_ref = bf16[16,16,512]{2,1,0:T(8,128)(2,1)S(1)} collective-permute-done((bf16[16,16,512]{2,1,0:T(8,128)(2,1)S(1)}, bf16[16,16,512]{2,1,0:T(8,128)(2,1)S(1)}, u32[]{:S(2)}, u32[]{:S(2)}) %collective-permute-start.14) | collective-permute-done | bytes 262176 | tf_op jit(solution)/shard_map/ppermute | solution.py:47
  40.4 0.1 join_cores.1
  40.5 1.0 %prepare.1 = (bf16[4608,256]{1,0:T(8,128)(2,1)S(1)}, f32[512,512]{1,0:T(8,128)S(1)}) custom-call(bf16[2304,512]{1,0:T(8,128)(2,1)S(1)} %bitcast.23, bf16[512,512]{1,0:T(8,128)(2,1)S(1)} %bitcast.44), custom_call_target="tpu_custom_call" | custom-call | flops 2000000000 | bytes 6000000 | tf_op jit(solution)/shard_map/prepare/pallas_call | solution.py:571
  41.4 1.9 %collective-permute-done.9 = bf16[320,128]{1,0:T(8,128)(2,1)S(1)} collective-permute-done((bf16[320,128]{1,0:T(8,128)(2,1)S(1)}, bf16[320,128]{1,0:T(8,128)(2,1)S(1)}, u32[]{:S(2)}, u32[]{:S(2)}) %collective-permute-start.9) | collective-permute-done | bytes 81952 | tf_op jit(solution)/shard_map/ppermute | solution.py:47
  43.4 0.3 collective-permute-start.15
  43.8 1.1 %collective-permute-done.15.other_ref = bf16[640,128]{1,0:T(8,128)(2,1)S(1)} collective-permute-done((bf16[640,128]{1,0:T(8,128)(2,1)S(1)}, bf16[640,128]{1,0:T(8,128)(2,1)S(1)}, u32[]{:S(2)}, u32[]{:S(2)}) %collective-permute-start.15) | collective-permute-done | bytes 163872 | tf_op jit(solution)/shard_map/ppermute | solution.py:47
  44.9 4.4 %grad_conv.1 = (f32[16,512]{1,0:T(8,128)}, bf16[1024,256]{1,0:T(8,128)(2,1)}) custom-call(bf16[640,128]{1,0:T(8,128)(2,1)S(1)} %bitcast.25, bf16[640,128]{1,0:T(8,128)(2,1)S(1)} %collective-permute-done.15.other_ref, f32[512,512]{1,0:T(8,128)S(1)} %get-tuple-element.50.both_ref, bf16[768,512]{1,0:T(8,128)(2,1)S(1)} %get-tuple-element.52.in_feat_ref, ...), custom_call_target="tpu_custom_call" | custom-call | tf_op jit(solution)/shard_map/grad_conv/pallas_call | solution.py:589
  (28 shorter events, 0.3 us)
Async XLA Ops:
  0.6 1.0 %copy-start.1 = (bf16[8,128,256]{2,1,0:T(8,128)(2,1)S(1)}, bf16[8,128,256]{2,1,0:T(8,128)(2,1)}, u32[]{:S(2)}) copy-start(bf16[8,128,256]{2,1,0:T(8,128)(2,1)} %own_ref.3) | copy-start | bytes 1572868
  1.7 1.4 %copy-start.3 = (f32[16,512]{1,0:T(8,128)S(1)}, f32[16,512]{1,0:T(8,128)}, u32[]{:S(2)}) copy-start(f32[16,512]{1,0:T(8,128)} %target_ref.1) | copy-start | bytes 98308
  1.7 5.0 %copy-start = (bf16[3,3,256,512]{3,2,1,0:T(8,128)(2,1)S(1)}, bf16[3,3,256,512]{3,2,1,0:T(8,128)(2,1)}, u32[]{:S(2)}) copy-start(bf16[3,3,256,512]{3,2,1,0:T(8,128)(2,1)} %param.5) | copy-start | bytes 7077892
  1.7 5.0 %copy-start.2 = (bf16[8,128,256]{2,1,0:T(8,128)(2,1)S(1)}, bf16[8,128,256]{2,1,0:T(8,128)(2,1)}, u32[]{:S(2)}) copy-start(bf16[8,128,256]{2,1,0:T(8,128)(2,1)} %own_ref.3) | copy-start | bytes 1572868
  1.7 5.0 %copy-start.4 = (bf16[512]{0:T(512)(128)(2,1)S(1)}, bf16[512]{0:T(512)(128)(2,1)}, u32[]{:S(2)}) copy-start(bf16[512]{0:T(512)(128)(2,1)} %bias_ref.1) | copy-start | bytes 3076
  1.7 1.3 %collective-permute-start = (bf16[2,8,256]{2,1,0:T(8,128)(2,1)S(1)}, bf16[2,8,256]{2,1,0:T(8,128)(2,1)S(1)}, u32[]{:S(2)}, u32[]{:S(2)}) collective-permute-start(bf16[2,8,256]{2,1,0:T(8,128)(2,1)S(1)} %column_rims.1), channel_id=1, source_target_pairs={{0,1},{1,0},{2,3},{3,2},{4,5},{5,4},{6,7},{7,6},{8,9},{9,8},{10,11... | collective-permute-start | bytes 24584 | tf_op jit(solution)/shard_map/ppermute | solution.py:501
  3.1 6.9 %collective-permute-start.1 = (bf16[272,256]{1,0:T(8,128)(2,1)S(1)}, bf16[272,256]{1,0:T(8,128)(2,1)S(1)}, u32[]{:S(2)}, u32[]{:S(2)}) collective-permute-start(bf16[272,256]{1,0:T(8,128)(2,1)S(1)} %get-tuple-element.30), channel_id=1, source_target_pairs={{0,2},{2,0},{4,6},{6,4},{8,10},{10,8},{12,14},{14,12},{16,18},{18,... | collective-permute-start | bytes 417800 | tf_op jit(solution)/shard_map/ppermute | solution.py:31
  6.0 4.0 %collective-permute-start.2 = (bf16[272,256]{1,0:T(8,128)(2,1)S(1)}, bf16[272,256]{1,0:T(8,128)(2,1)S(1)}, u32[]{:S(2)}, u32[]{:S(2)}) collective-permute-start(bf16[272,256]{1,0:T(8,128)(2,1)S(1)} %get-tuple-element.31), channel_id=1, source_target_pairs={{0,0},{2,4},{4,2},{6,8},{8,6},{10,12},{12,10},{14,16},{16,14},{18,... | collective-permute-start | bytes 417800 | tf_op jit(solution)/shard_map/ppermute | solution.py:31
  12.3 1.5 %collective-permute-start.3 = (bf16[640,128]{1,0:T(8,128)(2,1)S(1)}, bf16[640,128]{1,0:T(8,128)(2,1)S(1)}, u32[]{:S(2)}, u32[]{:S(2)}) collective-permute-start(bf16[640,128]{1,0:T(8,128)(2,1)S(1)} %get-tuple-element.37), channel_id=1, source_target_pairs={{0,1},{1,0},{2,3},{3,2},{4,5},{5,4},{6,7},{7,6},{8,9},{9,8},{10,11... | collective-permute-start | bytes 491528 | tf_op jit(solution)/shard_map/ppermute | solution.py:47
  13.8 8.0 %collective-permute-start.4 = (bf16[320,128]{1,0:T(8,128)(2,1)S(1)}, bf16[320,128]{1,0:T(8,128)(2,1)S(1)}, u32[]{:S(2)}, u32[]{:S(2)}) collective-permute-start(bf16[320,128]{1,0:T(8,128)(2,1)S(1)} %get-tuple-element.39), channel_id=1, source_target_pairs={{0,3},{1,2},{2,1},{3,0},{4,7},{5,6},{6,5},{7,4},{8,11},{9,10},{10,... | collective-permute-start | bytes 245768 | tf_op jit(solution)/shard_map/ppermute | solution.py:47
  19.3 4.6 %collective-permute-start.10 = (bf16[1,16,512]{2,1,0:T(8,128)(2,1)S(1)}, bf16[1,16,512]{2,1,0:T(8,128)(2,1)S(1)}, u32[]{:S(2)}, u32[]{:S(2)}) collective-permute-start(bf16[1,16,512]{2,1,0:T(8,128)(2,1)S(1)} %get-tuple-element.43), channel_id=1, source_target_pairs={{0,17},{1,16},{2,19},{3,18},{4,21},{5,20},{6,23},{7,22},{8,25},{9,... | collective-permute-start | bytes 49160 | tf_op jit(solution)/shard_map/ppermute | solution.py:47
  21.9 3.7 %collective-permute-start.5 = (bf16[160,128]{1,0:T(8,128)(2,1)S(1)}, bf16[160,128]{1,0:T(8,128)(2,1)S(1)}, u32[]{:S(2)}, u32[]{:S(2)}) collective-permute-start(bf16[160,128]{1,0:T(8,128)(2,1)S(1)} %get-tuple-element.41), channel_id=1, source_target_pairs={{0,5},{1,4},{2,7},{3,6},{4,1},{5,0},{6,3},{7,2},{8,13},{9,12},{10,... | collective-permute-start | bytes 122888 | tf_op jit(solution)/shard_map/ppermute | solution.py:47
  23.9 4.8 %collective-permute-start.11 = (bf16[2,16,512]{2,1,0:T(8,128)(2,1)S(1)}, bf16[2,16,512]{2,1,0:T(8,128)(2,1)S(1)}, u32[]{:S(2)}, u32[]{:S(2)}) collective-permute-start(bf16[2,16,512]{2,1,0:T(8,128)(2,1)S(1)} %bitcast.39), channel_id=1, source_target_pairs={{0,9},{1,8},{2,11},{3,10},{4,13},{5,12},{6,15},{7,14},{8,1},{9,0},... | collective-permute-start | bytes 98312 | tf_op jit(solution)/shard_map/ppermute | solution.py:47
  25.6 4.9 %collective-permute-start.6 = (bf16[160,128]{1,0:T(8,128)(2,1)S(1)}, bf16[160,128]{1,0:T(8,128)(2,1)S(1)}, u32[]{:S(2)}, u32[]{:S(2)}) collective-permute-start(bf16[160,128]{1,0:T(8,128)(2,1)S(1)} %add.3.keep_ref), channel_id=1, source_target_pairs={{0,9},{1,8},{2,11},{3,10},{4,13},{5,12},{6,15},{7,14},{8,1},{9,0},... | collective-permute-start | bytes 122888 | tf_op jit(solution)/shard_map/ppermute | solution.py:47
  28.7 4.5 %collective-permute-start.12 = (bf16[4,16,512]{2,1,0:T(8,128)(2,1)S(1)}, bf16[4,16,512]{2,1,0:T(8,128)(2,1)S(1)}, u32[]{:S(2)}, u32[]{:S(2)}) collective-permute-start(bf16[4,16,512]{2,1,0:T(8,128)(2,1)S(1)} %bitcast.34), channel_id=1, source_target_pairs={{0,5},{1,4},{2,7},{3,6},{4,1},{5,0},{6,3},{7,2},{8,13},{9,12},{10,... | collective-permute-start | bytes 196616 | tf_op jit(solution)/shard_map/ppermute | solution.py:47
  30.5 4.5 %collective-permute-start.7 = (bf16[160,128]{1,0:T(8,128)(2,1)S(1)}, bf16[160,128]{1,0:T(8,128)(2,1)S(1)}, u32[]{:S(2)}, u32[]{:S(2)}) collective-permute-start(bf16[160,128]{1,0:T(8,128)(2,1)S(1)} %add.4.keep_ref), channel_id=1, source_target_pairs={{0,17},{1,16},{2,19},{3,18},{4,21},{5,20},{6,23},{7,22},{8,25},{9,... | collective-permute-start | bytes 122888 | tf_op jit(solution)/shard_map/ppermute | solution.py:47
  33.2 5.5 %collective-permute-start.13 = (bf16[8,16,512]{2,1,0:T(8,128)(2,1)S(1)}, bf16[8,16,512]{2,1,0:T(8,128)(2,1)S(1)}, u32[]{:S(2)}, u32[]{:S(2)}) collective-permute-start(bf16[8,16,512]{2,1,0:T(8,128)(2,1)S(1)} %bitcast.28), channel_id=1, source_target_pairs={{0,3},{1,2},{2,1},{3,0},{4,7},{5,6},{6,5},{7,4},{8,11},{9,10},{10,... | collective-permute-start | bytes 393224 | tf_op jit(solution)/shard_map/ppermute | solution.py:47
  35.0 4.0 %collective-permute-start.8 = (bf16[160,128]{1,0:T(8,128)(2,1)S(1)}, bf16[160,128]{1,0:T(8,128)(2,1)S(1)}, u32[]{:S(2)}, u32[]{:S(2)}) collective-permute-start(bf16[160,128]{1,0:T(8,128)(2,1)S(1)} %add.5), channel_id=1, source_target_pairs={{0,5},{1,4},{2,7},{3,6},{4,1},{5,0},{6,3},{7,2},{8,13},{9,12},{10,... | collective-permute-start | bytes 122888 | tf_op jit(solution)/shard_map/ppermute | solution.py:47
  38.8 1.6 %collective-permute-start.14 = (bf16[16,16,512]{2,1,0:T(8,128)(2,1)S(1)}, bf16[16,16,512]{2,1,0:T(8,128)(2,1)S(1)}, u32[]{:S(2)}, u32[]{:S(2)}) collective-permute-start(bf16[16,16,512]{2,1,0:T(8,128)(2,1)S(1)} %bitcast.26), channel_id=1, source_target_pairs={{0,1},{1,0},{2,3},{3,2},{4,5},{5,4},{6,7},{7,6},{8,9},{9,8},{10,11... | collective-permute-start | bytes 786440 | tf_op jit(solution)/shard_map/ppermute | solution.py:47
  39.0 4.4 %collective-permute-start.9 = (bf16[320,128]{1,0:T(8,128)(2,1)S(1)}, bf16[320,128]{1,0:T(8,128)(2,1)S(1)}, u32[]{:S(2)}, u32[]{:S(2)}) collective-permute-start(bf16[320,128]{1,0:T(8,128)(2,1)S(1)} %bitcast.31), channel_id=1, source_target_pairs={{0,3},{1,2},{2,1},{3,0},{4,7},{5,6},{6,5},{7,4},{8,11},{9,10},{10,... | collective-permute-start | bytes 245768 | tf_op jit(solution)/shard_map/ppermute | solution.py:47
  43.4 1.5 %collective-permute-start.15 = (bf16[640,128]{1,0:T(8,128)(2,1)S(1)}, bf16[640,128]{1,0:T(8,128)(2,1)S(1)}, u32[]{:S(2)}, u32[]{:S(2)}) collective-permute-start(bf16[640,128]{1,0:T(8,128)(2,1)S(1)} %bitcast.24), channel_id=1, source_target_pairs={{0,1},{1,0},{2,3},{3,2},{4,5},{5,4},{6,7},{7,6},{8,9},{9,8},{10,11... | collective-permute-start | bytes 491528 | tf_op jit(solution)/shard_map/ppermute | solution.py:47

commit v3 on v2

--- a/solution.py
+++ b/solution.py
@@ -230,11 +230,12 @@
 
 
 def moved_rows(row, before, after):
-    cols, width = row.shape
+    cols = row.shape[0]
     wide = row.astype(f32)
-    place = lax.broadcasted_iota(jnp.int32, (cols, width), 0)
-    right = jnp.where(place == 0, before, pltpu.roll(wide, 1, 0))
-    left = jnp.where(place == cols - 1, after, pltpu.roll(wide, cols - 1, 0))
+    place = lax.broadcasted_iota(jnp.int32, (8, row.shape[1]), 0)
+    right, left = pltpu.roll(wide, 1, 0), pltpu.roll(wide, cols - 1, 0)
+    right = jnp.concatenate([jnp.where(place == 0, before, right[:8]), right[8:]], axis=0)
+    left = jnp.concatenate([left[:-8], jnp.where(place == 7, after, left[-8:])], axis=0)
     return right.astype(bf16), row.astype(bf16), left.astype(bf16)
 
 
@@ -242,14 +243,6 @@
     cols, width = row.shape
     for b, part in enumerate(moved_rows(row, before, after)):
         cat_ref[r * cols : (r + 1) * cols, b * width : (b + 1) * width] = part
-
-
-def fill_patches(cat_ref, spots, row, before, after):
-    cols, width = row.shape
-    for b, part in enumerate(moved_rows(row, before, after)):
-        for r, a in spots:
-            at = (3 * a + b) * width
-            cat_ref[r * cols : (r + 1) * cols, at : at + width] = part
 
 
 def gram_tiles(feat, gram_ref, base_ref=None):
@@ -274,7 +267,7 @@
 
 def inner_kernel(
     shape, own_ref, left_ref, right_ref, kernel_ref, bias_ref,
-    feat_ref, slope_ref, gram_ref, row_ref, cat_ref,
+    feat_ref, slope_ref, gram_ref, row_ref, part_ref, cat_ref,
 ):
     row_ref[...] = bias_ref[...].astype(f32).reshape(row_ref.shape)
     tile_rows, tile_cols, in_width, out_width, step = shape
@@ -284,24 +277,34 @@
     bias = row_ref[...]
     root = 1.0 / math.sqrt(out_width)
     span = 3 * in_width
+
+    def product(begin, count, a):
+        return jnp.dot(
+            cat_ref[begin * tile_cols : (begin + count) * tile_cols, :],
+            kernel_ref[a * span : (a + 1) * span, :],
+            preferred_element_type=f32,
+        )
+
     for h in range(0, tile_rows - 2, step):
         total = bias
         for a in range(3):
-            total = total + jnp.dot(
-                cat_ref[(h + a) * tile_cols : (h + a + step) * tile_cols, :],
-                kernel_ref[a * span : (a + 1) * span, :],
-                preferred_element_type=f32,
-            )
+            total = total + product(h + a, step, a)
         features, slope = gelu_pair(total)
         at = slice(h * tile_cols, (h + step) * tile_cols)
         feat_ref[at, :] = features.astype(bf16)
         slope_ref[at, :] = (slope * root).astype(bf16)
+    low, high = product(0, 2, 2), product(tile_rows - 2, 2, 0)
+    ends = product(0, 1, 1), product(tile_rows - 1, 1, 1)
+    part_ref[0:tile_cols, :] = low[:tile_cols] + bias
+    part_ref[tile_cols : 2 * tile_cols, :] = low[tile_cols:] + ends[0] + bias
+    part_ref[2 * tile_cols : 3 * tile_cols, :] = high[:tile_cols] + ends[1] + bias
+    part_ref[3 * tile_cols :, :] = high[tile_cols:] + bias
     gram_tiles(feat_ref[...], gram_ref)
 
 
 def outer_kernel(
-    shape, own_ref, even_ref, odd_ref, left_ref, right_ref, kernel_ref, bias_ref, base_ref,
-    feat_ref, slope_ref, send_ref, keep_ref, cat_ref, low_ref, high_ref, gram_ref,
+    shape, own_ref, even_ref, odd_ref, left_ref, right_ref, kernel_ref, bias_ref, base_ref, part_ref,
+    feat_ref, slope_ref, send_ref, keep_ref, cat_ref, edge_ref, low_ref, high_ref, gram_ref,
 ):
     tile_rows, tile_cols, in_width, out_width, step = shape
     odd = lax.rem(lax.axis_index("rows"), 2)
@@ -344,18 +347,11 @@
     rights = [
         ends(tile_cols - 1, own_end), sides(2, right_ref[0].astype(f32)), sides(3, right_ref[1].astype(f32))
     ]
-    lines = [0, 1, 2, 3, tile_rows, tile_rows + 1, tile_rows + 2, tile_rows + 3]
-    for r, line in enumerate(lines):
-        if line < 2:
-            row = low_ref[line * tile_cols : (line + 1) * tile_cols, :]
-        elif line < tile_rows + 2:
-            row = own_ref[line - 2]
-        else:
-            k = line - tile_rows - 2
-            row = high_ref[k * tile_cols : (k + 1) * tile_cols, :]
-        group, r = r // 4, r % 4
-        spots = [(2 * group + r - a, a) for a in range(3) if 0 <= r - a < 2]
-        fill_patches(cat_ref, spots, row, lefts[1][line : line + 1], rights[1][line : line + 1])
+    span = 3 * in_width
+    for r, line in enumerate([0, 1, tile_rows + 2, tile_rows + 3]):
+        source = low_ref if r < 2 else high_ref
+        row = source[r % 2 * tile_cols : (r % 2 + 1) * tile_cols, :]
+        fill_row(cat_ref, r, row, lefts[1][line : line + 1], rights[1][line : line + 1])
     blank = jnp.zeros((edge - tile_rows - 2, in_width), f32)
     for a in range(3):
         for b in range(3):
@@ -364,23 +360,35 @@
                 axis=0,
             )
             at = (3 * a + b) * in_width
-            cat_ref[2 * main :, at : at + in_width] = piece.astype(bf16)
+            edge_ref[:, at : at + in_width] = piece.astype(bf16)
     root = 1.0 / math.sqrt(out_width)
     line = lax.broadcasted_iota(jnp.int32, (2 * edge, out_width // 2), 0)
     weight = jnp.where(line < edge, left, right)
     weight = jnp.where(line % edge == 0, weight * first, weight)
     weight = jnp.where(line % edge == tile_rows + 1, weight * last, weight)
     for at in (slice(0, out_width // 2), slice(out_width // 2, out_width)):
-        total = bias_ref[:, at] + jnp.dot(
-            cat_ref[...], kernel_ref[:, at], preferred_element_type=f32
-        )
-        features, slope = gelu_pair(total)
-        slope = slope * root
-        feat_ref[:, at] = features.astype(bf16)
-        slope_ref[0:tile_cols, at] = (slope[:tile_cols] * first).astype(bf16)
-        slope_ref[tile_cols : 3 * tile_cols, at] = slope[tile_cols : 3 * tile_cols].astype(bf16)
-        slope_ref[3 * tile_cols : 2 * main, at] = (slope[3 * tile_cols : 2 * main] * last).astype(bf16)
-        slope_ref[2 * main :, at] = (slope[2 * main :] * weight).astype(bf16)
+        taps = [
+            jnp.dot(
+                cat_ref[a * tile_cols : (a + 2) * tile_cols, :],
+                kernel_ref[a * span : (a + 1) * span, at],
+                preferred_element_type=f32,
+            )
+            for a in range(3)
+        ]
+        totals = [
+            part_ref[0:tile_cols, at] + taps[0][:tile_cols] + taps[1][:tile_cols],
+            part_ref[tile_cols : 2 * tile_cols, at] + taps[0][tile_cols:],
+            part_ref[2 * tile_cols : 3 * tile_cols, at] + taps[2][:tile_cols],
+            part_ref[3 * tile_cols :, at] + taps[1][tile_cols:] + taps[2][tile_cols:],
+            bias_ref[:, at]
+            + jnp.dot(edge_ref[...], kernel_ref[:, at], preferred_element_type=f32),
+        ]
+        scales = [first * root, root, root, last * root, weight * root]
+        for n, (total, scale) in enumerate(zip(totals, scales)):
+            features, slope = gelu_pair(total)
+            rows = slice(n * tile_cols, n * tile_cols + total.shape[0])
+            feat_ref[rows, at] = features.astype(bf16)
+            slope_ref[rows, at] = (slope * scale).astype(bf16)
     gram_tiles(feat_ref[tile_cols : 3 * tile_cols, :], gram_ref, base_ref)
     half = send_ref.shape[0]
     side = side_of(0)
@@ -518,13 +526,14 @@
     gather = Gather(rows)
     far = list(reversed(range(3, bits)))
     inner = (tile_rows - 2) * tile_cols
-    in_feat, in_slope, in_gram, bias = pl.pallas_call(
+    in_feat, in_slope, in_gram, bias, part = pl.pallas_call(
         functools.partial(inner_kernel, shape),
         out_shape=(
             jax.ShapeDtypeStruct((inner, out_width), bf16),
             jax.ShapeDtypeStruct((inner, out_width), bf16),
             packed_shape,
             jax.ShapeDtypeStruct((1, out_width), f32),
+            jax.ShapeDtypeStruct((4 * tile_cols, out_width), f32),
         ),
         in_specs=[vmem] * 5,
         scratch_shapes=[pltpu.VMEM((tile_rows * tile_cols, 3 * in_width), bf16)],
@@ -547,24 +556,25 @@
             jax.ShapeDtypeStruct(half_gram, bf16),
             jax.ShapeDtypeStruct(half_gram, f32),
         ),
-        in_specs=[vmem] * 8,
+        in_specs=[vmem] * 9,
         scratch_shapes=[
-            pltpu.VMEM((outer, 9 * in_width), bf16),
+            pltpu.VMEM((4 * tile_cols, 3 * in_width), bf16),
+            pltpu.VMEM((2 * edge, 9 * in_width), bf16),
             pltpu.VMEM(payload_shape.shape, bf16),
             pltpu.VMEM(payload_shape.shape, bf16),
             pltpu.VMEM(packed_shape.shape, f32),
         ],
         compiler_params=params,
         name="outer_rows",
-    )(canvas, even, odd, left, right, kernel, bias, in_gram)
-
-    exchanges = {"halve 1": far[:1], "halve 2": far[1:], "add 3": [2], "add 4": [1], "join 2": [0]}
+    )(canvas, even, odd, left, right, kernel, bias, in_gram, part)
+
+    exchanges = {"cores": far[:1], "halve 1": far[1:], "halve 2": [1], "add 3": [2], "add 4": [0]}
     prepared = []
 
     def beside(name, sent, got):
         for bit in exchanges.get(name, []):
             gather.step(bit, sent)
-        if name != "join 1":
+        if name != "join 2":
             return got
         gather.settle(sent)
         prepared.extend(

time: 49.5 us -> 50 us (1.010)
  waiting for transfers between devices: 12.7 us -> 14.6 us
  starting transfers between devices: 24 us -> 22.5 us
    ppermute x13, waiting for transfers between devices: 11.3 us -> 13.8 us  [swap(): lax.ppermute(value, ('rows', 'cols'), [(i, i ^ (1 << bit | 1)) for i in r...]
    ppermute x13, starting transfers between devices: 19.9 us -> 18.4 us  [swap(): lax.ppermute(value, ('rows', 'cols'), [(i, i ^ (1 << bit | 1)) for i in r...]
    pallas_call x1, Pallas kernels: 2.79 us -> 3.38 us  [on_device(): pl.pallas_call(functools.partial(inner_kernel, shape), out_shape=(jax.Sha...]
    pallas_call x1, Pallas kernels: 2.3 us -> 1.76 us  [on_device(): pl.pallas_call(functools.partial(outer_kernel, shape), out_shape=(jax.Sha...]
    ppermute x2, waiting for transfers between devices: 0.51 us -> 0.01 us  [swap_rows(): lax.ppermute(value, 'rows', perm(low))]
  transfers between devices with their start and end apart: 16 -> 16, of which waited for: 10 -> 10; matrix products, arithmetic and copies ran while one was open for 0% -> 0% of each run, Pallas kernels for 8% -> 9%
where the time goes in v3:
time: 50 us; the launch traced here: 49.9 us
  starting transfers between devices  22.5 us (45%)
  waiting for transfers between devices  14.6 us (29%)
  Pallas kernels  10.9 us (22%)
  local copies, waits for them, and re-layouts  1.05 us (2%)
  between operations  0.79 us (2%)
    ppermute x13, starting transfers between devices, swap(): lax.ppermute(value, ('rows', 'cols'), [(i, i ^ (1 << bit | 1)) for i in r...  18.4 us
    ppermute x13, waiting for transfers between devices, swap(): lax.ppermute(value, ('rows', 'cols'), [(i, i ^ (1 << bit | 1)) for i in r...  13.8 us
    pallas_call x1, Pallas kernels, on_device(): pl.pallas_call(functools.partial(backward_kernel, shape, pixel_total), ou...  4.47 us
    ppermute x2, starting transfers between devices, swap_rows(): lax.ppermute(value, 'rows', perm(low))  3.55 us
    pallas_call x1, Pallas kernels, on_device(): pl.pallas_call(functools.partial(inner_kernel, shape), out_shape=(jax.Sha...  3.38 us
    pallas_call x1, Pallas kernels, on_device(): pl.pallas_call(functools.partial(outer_kernel, shape), out_shape=(jax.Sha...  1.76 us
    unnamed x10, local copies, waits for them, and re-layouts  1.05 us
  transfers between devices with their start and end apart: 16, of which 10 were waited for; matrix products, arithmetic and copies ran while one was open for 0% of the time, Pallas kernels for 9%

profile of v3, /device:TPU:0, one launch (start us, length us, event | category | flops | bytes accessed | tf_op | source)
XLA Modules:
  0.0 49.9 jit_solution(17995219512332602417)
XLA Ops:
  0.6 1.0 %copy-done.1 = bf16[8,128,256]{2,1,0:T(8,128)(2,1)S(1)} copy-done((bf16[8,128,256]{2,1,0:T(8,128)(2,1)S(1)}, bf16[8,128,256]{2,1,0:T(8,128)(2,1)}, u32[]{:S(2)}) %copy-start.1) | copy-done | bytes 524312
  1.7 0.5 %collective-permute-start = (bf16[2,8,256]{2,1,0:T(8,128)(2,1)S(1)}, bf16[2,8,256]{2,1,0:T(8,128)(2,1)S(1)}, u32[]{:S(2)}, u32[]{:S(2)}) collective-permute-start(bf16[2,8,256]{2,1,0:T(8,128)(2,1)S(1)} %column_rims.1), channel_id=1, source_target_pairs={{0,1},{1,0},{2,3},{3,2},{4,5},{5,4},{6,7},{7,6},{8,9},{9,8},{10,11... | collective-permute-start | bytes 24584 | tf_op jit(solution)/shard_map/ppermute | solution.py:509
  2.2 0.8 %collective-permute-done.refs_0_ = bf16[2,8,256]{2,1,0:T(8,128)(2,1)S(1)} collective-permute-done((bf16[2,8,256]{2,1,0:T(8,128)(2,1)S(1)}, bf16[2,8,256]{2,1,0:T(8,128)(2,1)S(1)}, u32[]{:S(2)}, u32[]{:S(2)}) %collective-permute-start) | collective-permute-done | bytes 8224 | tf_op jit(solution)/shard_map/ppermute | solution.py:509
  3.1 2.9 %collective-permute-start.1 = (bf16[272,256]{1,0:T(8,128)(2,1)S(1)}, bf16[272,256]{1,0:T(8,128)(2,1)S(1)}, u32[]{:S(2)}, u32[]{:S(2)}) collective-permute-start(bf16[272,256]{1,0:T(8,128)(2,1)S(1)} %get-tuple-element.31), channel_id=1, source_target_pairs={{0,2},{2,0},{4,6},{6,4},{8,10},{10,8},{12,14},{14,12},{16,18},{18,... | collective-permute-start | bytes 417800 | tf_op jit(solution)/shard_map/ppermute | solution.py:31
  6.0 0.7 %collective-permute-start.2 = (bf16[272,256]{1,0:T(8,128)(2,1)S(1)}, bf16[272,256]{1,0:T(8,128)(2,1)S(1)}, u32[]{:S(2)}, u32[]{:S(2)}) collective-permute-start(bf16[272,256]{1,0:T(8,128)(2,1)S(1)} %get-tuple-element.32), channel_id=1, source_target_pairs={{0,0},{2,4},{4,2},{6,8},{8,6},{10,12},{12,10},{14,16},{16,14},{18,... | collective-permute-start | bytes 417800 | tf_op jit(solution)/shard_map/ppermute | solution.py:31
  6.7 3.4 %inner_rows.1 = (bf16[768,512]{1,0:T(8,128)(2,1)S(1)}, bf16[768,512]{1,0:T(8,128)(2,1)S(1)}, f32[1280,128]{1,0:T(8,128)S(1)}, f32[1,512]{1,0:T(1,128)S(1)}, f32[512,512]{1,0:T(8,128)S(1)}) custom-call(bf16[8,128,256]{2,1,0:T(8,128)(2,1)S(1)} %copy-done.2, bf16[2,8,256]{2,1,0:T(8,128)(2,1)S(1)} %get-tuple-element.33.left_ref, ...), custom_call_target="tpu_custom_call" | custom-call | flops 2214592512 | bytes 6000000 | tf_op jit(solution)/shard_map/inner_rows/pallas_call | solution.py:529
  10.1 1.8 %outer_rows.1 = (bf16[544,512]{1,0:T(8,128)(2,1)S(1)}, bf16[544,512]{1,0:T(8,128)(2,1)S(1)}, bf16[640,128]{1,0:T(8,128)(2,1)S(1)}, f32[640,128]{1,0:T(8,128)S(1)}) custom-call(bf16[8,128,256]{2,1,0:T(8,128)(2,1)S(1)} %copy-done.2, bf16[272,256]{1,0:T(8,128)(2,1)S(1)} %collective-permute-done.1.even_ref, bf16[272,256]{1,0:T(8,128)(2,1)S(1)} %collective-permute-done.2.odd_ref, ...), custom_call_target="tpu_custom_call" | custom-call | tf_op jit(solution)/shard_map/outer_rows/pallas_call | solution.py:551
  11.9 0.1 collective-permute-start.3
  11.9 7.7 %collective-permute-start.9 = (bf16[1,16,512]{2,1,0:T(8,128)(2,1)S(1)}, bf16[1,16,512]{2,1,0:T(8,128)(2,1)S(1)}, u32[]{:S(2)}, u32[]{:S(2)}) collective-permute-start(bf16[1,16,512]{2,1,0:T(8,128)(2,1)S(1)} %get-tuple-element.45), channel_id=1, source_target_pairs={{0,17},{1,16},{2,19},{3,18},{4,21},{5,20},{6,23},{7,22},{8,25},{9,... | collective-permute-start | bytes 49160 | tf_op jit(solution)/shard_map/ppermute | solution.py:47
  19.7 0.3 collective-permute-start.4
  20.0 1.1 %collective-permute-done.9 = bf16[1,16,512]{2,1,0:T(8,128)(2,1)S(1)} collective-permute-done((bf16[1,16,512]{2,1,0:T(8,128)(2,1)S(1)}, bf16[1,16,512]{2,1,0:T(8,128)(2,1)S(1)}, u32[]{:S(2)}, u32[]{:S(2)}) %collective-permute-start.9) | collective-permute-done | bytes 16416 | tf_op jit(solution)/shard_map/ppermute | solution.py:47
  21.1 1.6 %collective-permute-start.10 = (bf16[2,16,512]{2,1,0:T(8,128)(2,1)S(1)}, bf16[2,16,512]{2,1,0:T(8,128)(2,1)S(1)}, u32[]{:S(2)}, u32[]{:S(2)}) collective-permute-start(bf16[2,16,512]{2,1,0:T(8,128)(2,1)S(1)} %bitcast.39), channel_id=1, source_target_pairs={{0,9},{1,8},{2,11},{3,10},{4,13},{5,12},{6,15},{7,14},{8,1},{9,0},... | collective-permute-start | bytes 98312 | tf_op jit(solution)/shard_map/ppermute | solution.py:47
  22.7 1.5 %collective-permute-done.4.got_ref = bf16[320,128]{1,0:T(8,128)(2,1)S(1)} collective-permute-done((bf16[320,128]{1,0:T(8,128)(2,1)S(1)}, bf16[320,128]{1,0:T(8,128)(2,1)S(1)}, u32[]{:S(2)}, u32[]{:S(2)}) %collective-permute-start.4) | collective-permute-done | bytes 81952 | tf_op jit(solution)/shard_map/ppermute | solution.py:47
  24.3 0.6 %collective-permute-start.5 = (bf16[160,128]{1,0:T(8,128)(2,1)S(1)}, bf16[160,128]{1,0:T(8,128)(2,1)S(1)}, u32[]{:S(2)}, u32[]{:S(2)}) collective-permute-start(bf16[160,128]{1,0:T(8,128)(2,1)S(1)} %get-tuple-element.43), channel_id=1, source_target_pairs={{0,5},{1,4},{2,7},{3,6},{4,1},{5,0},{6,3},{7,2},{8,13},{9,12},{10,... | collective-permute-start | bytes 122888 | tf_op jit(solution)/shard_map/ppermute | solution.py:47
  24.9 1.3 %collective-permute-start.11 = (bf16[4,16,512]{2,1,0:T(8,128)(2,1)S(1)}, bf16[4,16,512]{2,1,0:T(8,128)(2,1)S(1)}, u32[]{:S(2)}, u32[]{:S(2)}) collective-permute-start(bf16[4,16,512]{2,1,0:T(8,128)(2,1)S(1)} %bitcast.34), channel_id=1, source_target_pairs={{0,3},{1,2},{2,1},{3,0},{4,7},{5,6},{6,5},{7,4},{8,11},{9,10},{10,... | collective-permute-start | bytes 196616 | tf_op jit(solution)/shard_map/ppermute | solution.py:47
  26.2 1.6 %collective-permute-done.5.got_ref = bf16[160,128]{1,0:T(8,128)(2,1)S(1)} collective-permute-done((bf16[160,128]{1,0:T(8,128)(2,1)S(1)}, bf16[160,128]{1,0:T(8,128)(2,1)S(1)}, u32[]{:S(2)}, u32[]{:S(2)}) %collective-permute-start.5) | collective-permute-done | bytes 40992 | tf_op jit(solution)/shard_map/ppermute | solution.py:47
  27.8 1.8 %collective-permute-start.6 = (bf16[160,128]{1,0:T(8,128)(2,1)S(1)}, bf16[160,128]{1,0:T(8,128)(2,1)S(1)}, u32[]{:S(2)}, u32[]{:S(2)}) collective-permute-start(bf16[160,128]{1,0:T(8,128)(2,1)S(1)} %add.3.keep_ref), channel_id=1, source_target_pairs={{0,9},{1,8},{2,11},{3,10},{4,13},{5,12},{6,15},{7,14},{8,1},{9,0},... | collective-permute-start | bytes 122888 | tf_op jit(solution)/shard_map/ppermute | solution.py:47
  29.7 0.7 %collective-permute-start.12 = (bf16[8,16,512]{2,1,0:T(8,128)(2,1)S(1)}, bf16[8,16,512]{2,1,0:T(8,128)(2,1)S(1)}, u32[]{:S(2)}, u32[]{:S(2)}) collective-permute-start(bf16[8,16,512]{2,1,0:T(8,128)(2,1)S(1)} %bitcast.28), channel_id=1, source_target_pairs={{0,5},{1,4},{2,7},{3,6},{4,1},{5,0},{6,3},{7,2},{8,13},{9,12},{10,... | collective-permute-start | bytes 393224 | tf_op jit(solution)/shard_map/ppermute | solution.py:47
  30.3 1.0 %collective-permute-done.6.got_ref = bf16[160,128]{1,0:T(8,128)(2,1)S(1)} collective-permute-done((bf16[160,128]{1,0:T(8,128)(2,1)S(1)}, bf16[160,128]{1,0:T(8,128)(2,1)S(1)}, u32[]{:S(2)}, u32[]{:S(2)}) %collective-permute-start.6) | collective-permute-done | bytes 40992 | tf_op jit(solution)/shard_map/ppermute | solution.py:47
  31.3 1.2 %collective-permute-start.7 = (bf16[160,128]{1,0:T(8,128)(2,1)S(1)}, bf16[160,128]{1,0:T(8,128)(2,1)S(1)}, u32[]{:S(2)}, u32[]{:S(2)}) collective-permute-start(bf16[160,128]{1,0:T(8,128)(2,1)S(1)} %add.4.keep_ref), channel_id=1, source_target_pairs={{0,17},{1,16},{2,19},{3,18},{4,21},{5,20},{6,23},{7,22},{8,25},{9,... | collective-permute-start | bytes 122888 | tf_op jit(solution)/shard_map/ppermute | solution.py:47
  32.5 2.9 %collective-permute-done.12 = bf16[8,16,512]{2,1,0:T(8,128)(2,1)S(1)} collective-permute-done((bf16[8,16,512]{2,1,0:T(8,128)(2,1)S(1)}, bf16[8,16,512]{2,1,0:T(8,128)(2,1)S(1)}, u32[]{:S(2)}, u32[]{:S(2)}) %collective-permute-start.12) | collective-permute-done | bytes 131104 | tf_op jit(solution)/shard_map/ppermute | solution.py:47
  35.5 0.3 collective-permute-start.13
  35.8 0.6 %collective-permute-start.8 = (bf16[160,128]{1,0:T(8,128)(2,1)S(1)}, bf16[160,128]{1,0:T(8,128)(2,1)S(1)}, u32[]{:S(2)}, u32[]{:S(2)}) collective-permute-start(bf16[160,128]{1,0:T(8,128)(2,1)S(1)} %add.5), channel_id=1, source_target_pairs={{0,5},{1,4},{2,7},{3,6},{4,1},{5,0},{6,3},{7,2},{8,13},{9,12},{10,... | collective-permute-start | bytes 122888 | tf_op jit(solution)/shard_map/ppermute | solution.py:47
  36.4 0.7 %collective-permute-done.13.other_ref = bf16[16,16,512]{2,1,0:T(8,128)(2,1)S(1)} collective-permute-done((bf16[16,16,512]{2,1,0:T(8,128)(2,1)S(1)}, bf16[16,16,512]{2,1,0:T(8,128)(2,1)S(1)}, u32[]{:S(2)}, u32[]{:S(2)}) %collective-permute-start.13) | collective-permute-done | bytes 262176 | tf_op jit(solution)/shard_map/ppermute | solution.py:47
  37.1 0.1 join_cores.1
  37.2 1.0 %prepare.1 = (bf16[4608,256]{1,0:T(8,128)(2,1)S(1)}, f32[512,512]{1,0:T(8,128)S(1)}) custom-call(bf16[2304,512]{1,0:T(8,128)(2,1)S(1)} %bitcast.23, bf16[512,512]{1,0:T(8,128)(2,1)S(1)} %bitcast.44), custom_call_target="tpu_custom_call" | custom-call | flops 2000000000 | bytes 6000000 | tf_op jit(solution)/shard_map/prepare/pallas_call | solution.py:581
  38.1 1.1 %collective-permute-done.8 = bf16[160,128]{1,0:T(8,128)(2,1)S(1)} collective-permute-done((bf16[160,128]{1,0:T(8,128)(2,1)S(1)}, bf16[160,128]{1,0:T(8,128)(2,1)S(1)}, u32[]{:S(2)}, u32[]{:S(2)}) %collective-permute-start.8) | collective-permute-done | bytes 40992 | tf_op jit(solution)/shard_map/ppermute | solution.py:47
  39.3 1.1 %collective-permute-start.14 = (bf16[320,128]{1,0:T(8,128)(2,1)S(1)}, bf16[320,128]{1,0:T(8,128)(2,1)S(1)}, u32[]{:S(2)}, u32[]{:S(2)}) collective-permute-start(bf16[320,128]{1,0:T(8,128)(2,1)S(1)} %bitcast.31), channel_id=1, source_target_pairs={{0,3},{1,2},{2,1},{3,0},{4,7},{5,6},{6,5},{7,4},{8,11},{9,10},{10,... | collective-permute-start | bytes 245768 | tf_op jit(solution)/shard_map/ppermute | solution.py:47
  40.4 2.8 %collective-permute-done.14 = bf16[320,128]{1,0:T(8,128)(2,1)S(1)} collective-permute-done((bf16[320,128]{1,0:T(8,128)(2,1)S(1)}, bf16[320,128]{1,0:T(8,128)(2,1)S(1)}, u32[]{:S(2)}, u32[]{:S(2)}) %collective-permute-start.14) | collective-permute-done | bytes 81952 | tf_op jit(solution)/shard_map/ppermute | solution.py:47
  43.3 1.1 %collective-permute-start.15 = (bf16[640,128]{1,0:T(8,128)(2,1)S(1)}, bf16[640,128]{1,0:T(8,128)(2,1)S(1)}, u32[]{:S(2)}, u32[]{:S(2)}) collective-permute-start(bf16[640,128]{1,0:T(8,128)(2,1)S(1)} %bitcast.24), channel_id=1, source_target_pairs={{0,1},{1,0},{2,3},{3,2},{4,5},{5,4},{6,7},{7,6},{8,9},{9,8},{10,11... | collective-permute-start | bytes 491528 | tf_op jit(solution)/shard_map/ppermute | solution.py:47
  44.4 1.0 %collective-permute-done.15.other_ref = bf16[640,128]{1,0:T(8,128)(2,1)S(1)} collective-permute-done((bf16[640,128]{1,0:T(8,128)(2,1)S(1)}, bf16[640,128]{1,0:T(8,128)(2,1)S(1)}, u32[]{:S(2)}, u32[]{:S(2)}) %collective-permute-start.15) | collective-permute-done | bytes 163872 | tf_op jit(solution)/shard_map/ppermute | solution.py:47
  45.4 4.5 %grad_conv.1 = (f32[16,512]{1,0:T(8,128)}, bf16[1024,256]{1,0:T(8,128)(2,1)}) custom-call(bf16[640,128]{1,0:T(8,128)(2,1)S(1)} %bitcast.25, bf16[640,128]{1,0:T(8,128)(2,1)S(1)} %collective-permute-done.15.other_ref, f32[512,512]{1,0:T(8,128)S(1)} %get-tuple-element.52.both_ref, bf16[768,512]{1,0:T(8,128)(2,1)S(1)} %get-tuple-element.54.in_feat_ref, ...), custom_call_target="tpu_custom_call" | custom-call | tf_op jit(solution)/shard_map/grad_conv/pallas_call | solution.py:599
  (28 shorter events, 0.3 us)
Async XLA Ops:
  0.6 1.0 %copy-start.1 = (bf16[8,128,256]{2,1,0:T(8,128)(2,1)S(1)}, bf16[8,128,256]{2,1,0:T(8,128)(2,1)}, u32[]{:S(2)}) copy-start(bf16[8,128,256]{2,1,0:T(8,128)(2,1)} %own_ref.3) | copy-start | bytes 1572868
  1.7 1.4 %copy-start.3 = (f32[16,512]{1,0:T(8,128)S(1)}, f32[16,512]{1,0:T(8,128)}, u32[]{:S(2)}) copy-start(f32[16,512]{1,0:T(8,128)} %target_ref.1) | copy-start | bytes 98308
  1.7 5.0 %copy-start = (bf16[3,3,256,512]{3,2,1,0:T(8,128)(2,1)S(1)}, bf16[3,3,256,512]{3,2,1,0:T(8,128)(2,1)}, u32[]{:S(2)}) copy-start(bf16[3,3,256,512]{3,2,1,0:T(8,128)(2,1)} %param.5) | copy-start | bytes 7077892
  1.7 5.0 %copy-start.2 = (bf16[8,128,256]{2,1,0:T(8,128)(2,1)S(1)}, bf16[8,128,256]{2,1,0:T(8,128)(2,1)}, u32[]{:S(2)}) copy-start(bf16[8,128,256]{2,1,0:T(8,128)(2,1)} %own_ref.3) | copy-start | bytes 1572868
  1.7 5.0 %copy-start.4 = (bf16[512]{0:T(512)(128)(2,1)S(1)}, bf16[512]{0:T(512)(128)(2,1)}, u32[]{:S(2)}) copy-start(bf16[512]{0:T(512)(128)(2,1)} %bias_ref.1) | copy-start | bytes 3076
  1.7 1.3 %collective-permute-start = (bf16[2,8,256]{2,1,0:T(8,128)(2,1)S(1)}, bf16[2,8,256]{2,1,0:T(8,128)(2,1)S(1)}, u32[]{:S(2)}, u32[]{:S(2)}) collective-permute-start(bf16[2,8,256]{2,1,0:T(8,128)(2,1)S(1)} %column_rims.1), channel_id=1, source_target_pairs={{0,1},{1,0},{2,3},{3,2},{4,5},{5,4},{6,7},{7,6},{8,9},{9,8},{10,11... | collective-permute-start | bytes 24584 | tf_op jit(solution)/shard_map/ppermute | solution.py:509
  3.1 7.0 %collective-permute-start.1 = (bf16[272,256]{1,0:T(8,128)(2,1)S(1)}, bf16[272,256]{1,0:T(8,128)(2,1)S(1)}, u32[]{:S(2)}, u32[]{:S(2)}) collective-permute-start(bf16[272,256]{1,0:T(8,128)(2,1)S(1)} %get-tuple-element.31), channel_id=1, source_target_pairs={{0,2},{2,0},{4,6},{6,4},{8,10},{10,8},{12,14},{14,12},{16,18},{18,... | collective-permute-start | bytes 417800 | tf_op jit(solution)/shard_map/ppermute | solution.py:31
  6.0 4.1 %collective-permute-start.2 = (bf16[272,256]{1,0:T(8,128)(2,1)S(1)}, bf16[272,256]{1,0:T(8,128)(2,1)S(1)}, u32[]{:S(2)}, u32[]{:S(2)}) collective-permute-start(bf16[272,256]{1,0:T(8,128)(2,1)S(1)} %get-tuple-element.32), channel_id=1, source_target_pairs={{0,0},{2,4},{4,2},{6,8},{8,6},{10,12},{12,10},{14,16},{16,14},{18,... | collective-permute-start | bytes 417800 | tf_op jit(solution)/shard_map/ppermute | solution.py:31
  11.9 7.8 %collective-permute-start.3 = (bf16[640,128]{1,0:T(8,128)(2,1)S(1)}, bf16[640,128]{1,0:T(8,128)(2,1)S(1)}, u32[]{:S(2)}, u32[]{:S(2)}) collective-permute-start(bf16[640,128]{1,0:T(8,128)(2,1)S(1)} %get-tuple-element.39), channel_id=1, source_target_pairs={{0,1},{1,0},{2,3},{3,2},{4,5},{5,4},{6,7},{7,6},{8,9},{9,8},{10,11... | collective-permute-start | bytes 491528 | tf_op jit(solution)/shard_map/ppermute | solution.py:47
  11.9 9.2 %collective-permute-start.9 = (bf16[1,16,512]{2,1,0:T(8,128)(2,1)S(1)}, bf16[1,16,512]{2,1,0:T(8,128)(2,1)S(1)}, u32[]{:S(2)}, u32[]{:S(2)}) collective-permute-start(bf16[1,16,512]{2,1,0:T(8,128)(2,1)S(1)} %get-tuple-element.45), channel_id=1, source_target_pairs={{0,17},{1,16},{2,19},{3,18},{4,21},{5,20},{6,23},{7,22},{8,25},{9,... | collective-permute-start | bytes 49160 | tf_op jit(solution)/shard_map/ppermute | solution.py:47
  19.7 4.6 %collective-permute-start.4 = (bf16[320,128]{1,0:T(8,128)(2,1)S(1)}, bf16[320,128]{1,0:T(8,128)(2,1)S(1)}, u32[]{:S(2)}, u32[]{:S(2)}) collective-permute-start(bf16[320,128]{1,0:T(8,128)(2,1)S(1)} %get-tuple-element.41), channel_id=1, source_target_pairs={{0,3},{1,2},{2,1},{3,0},{4,7},{5,6},{6,5},{7,4},{8,11},{9,10},{10,... | collective-permute-start | bytes 245768 | tf_op jit(solution)/shard_map/ppermute | solution.py:47
  21.1 3.8 %collective-permute-start.10 = (bf16[2,16,512]{2,1,0:T(8,128)(2,1)S(1)}, bf16[2,16,512]{2,1,0:T(8,128)(2,1)S(1)}, u32[]{:S(2)}, u32[]{:S(2)}) collective-permute-start(bf16[2,16,512]{2,1,0:T(8,128)(2,1)S(1)} %bitcast.39), channel_id=1, source_target_pairs={{0,9},{1,8},{2,11},{3,10},{4,13},{5,12},{6,15},{7,14},{8,1},{9,0},... | collective-permute-start | bytes 98312 | tf_op jit(solution)/shard_map/ppermute | solution.py:47
  24.3 3.5 %collective-permute-start.5 = (bf16[160,128]{1,0:T(8,128)(2,1)S(1)}, bf16[160,128]{1,0:T(8,128)(2,1)S(1)}, u32[]{:S(2)}, u32[]{:S(2)}) collective-permute-start(bf16[160,128]{1,0:T(8,128)(2,1)S(1)} %get-tuple-element.43), channel_id=1, source_target_pairs={{0,5},{1,4},{2,7},{3,6},{4,1},{5,0},{6,3},{7,2},{8,13},{9,12},{10,... | collective-permute-start | bytes 122888 | tf_op jit(solution)/shard_map/ppermute | solution.py:47
  24.9 4.7 %collective-permute-start.11 = (bf16[4,16,512]{2,1,0:T(8,128)(2,1)S(1)}, bf16[4,16,512]{2,1,0:T(8,128)(2,1)S(1)}, u32[]{:S(2)}, u32[]{:S(2)}) collective-permute-start(bf16[4,16,512]{2,1,0:T(8,128)(2,1)S(1)} %bitcast.34), channel_id=1, source_target_pairs={{0,3},{1,2},{2,1},{3,0},{4,7},{5,6},{6,5},{7,4},{8,11},{9,10},{10,... | collective-permute-start | bytes 196616 | tf_op jit(solution)/shard_map/ppermute | solution.py:47
  27.8 3.5 %collective-permute-start.6 = (bf16[160,128]{1,0:T(8,128)(2,1)S(1)}, bf16[160,128]{1,0:T(8,128)(2,1)S(1)}, u32[]{:S(2)}, u32[]{:S(2)}) collective-permute-start(bf16[160,128]{1,0:T(8,128)(2,1)S(1)} %add.3.keep_ref), channel_id=1, source_target_pairs={{0,9},{1,8},{2,11},{3,10},{4,13},{5,12},{6,15},{7,14},{8,1},{9,0},... | collective-permute-start | bytes 122888 | tf_op jit(solution)/shard_map/ppermute | solution.py:47
  29.7 5.8 %collective-permute-start.12 = (bf16[8,16,512]{2,1,0:T(8,128)(2,1)S(1)}, bf16[8,16,512]{2,1,0:T(8,128)(2,1)S(1)}, u32[]{:S(2)}, u32[]{:S(2)}) collective-permute-start(bf16[8,16,512]{2,1,0:T(8,128)(2,1)S(1)} %bitcast.28), channel_id=1, source_target_pairs={{0,5},{1,4},{2,7},{3,6},{4,1},{5,0},{6,3},{7,2},{8,13},{9,12},{10,... | collective-permute-start | bytes 393224 | tf_op jit(solution)/shard_map/ppermute | solution.py:47
  31.3 4.4 %collective-permute-start.7 = (bf16[160,128]{1,0:T(8,128)(2,1)S(1)}, bf16[160,128]{1,0:T(8,128)(2,1)S(1)}, u32[]{:S(2)}, u32[]{:S(2)}) collective-permute-start(bf16[160,128]{1,0:T(8,128)(2,1)S(1)} %add.4.keep_ref), channel_id=1, source_target_pairs={{0,17},{1,16},{2,19},{3,18},{4,21},{5,20},{6,23},{7,22},{8,25},{9,... | collective-permute-start | bytes 122888 | tf_op jit(solution)/shard_map/ppermute | solution.py:47
  35.5 1.6 %collective-permute-start.13 = (bf16[16,16,512]{2,1,0:T(8,128)(2,1)S(1)}, bf16[16,16,512]{2,1,0:T(8,128)(2,1)S(1)}, u32[]{:S(2)}, u32[]{:S(2)}) collective-permute-start(bf16[16,16,512]{2,1,0:T(8,128)(2,1)S(1)} %bitcast.26), channel_id=1, source_target_pairs={{0,1},{1,0},{2,3},{3,2},{4,5},{5,4},{6,7},{7,6},{8,9},{9,8},{10,11... | collective-permute-start | bytes 786440 | tf_op jit(solution)/shard_map/ppermute | solution.py:47
  35.8 3.5 %collective-permute-start.8 = (bf16[160,128]{1,0:T(8,128)(2,1)S(1)}, bf16[160,128]{1,0:T(8,128)(2,1)S(1)}, u32[]{:S(2)}, u32[]{:S(2)}) collective-permute-start(bf16[160,128]{1,0:T(8,128)(2,1)S(1)} %add.5), channel_id=1, source_target_pairs={{0,5},{1,4},{2,7},{3,6},{4,1},{5,0},{6,3},{7,2},{8,13},{9,12},{10,... | collective-permute-start | bytes 122888 | tf_op jit(solution)/shard_map/ppermute | solution.py:47
  39.3 3.9 %collective-permute-start.14 = (bf16[320,128]{1,0:T(8,128)(2,1)S(1)}, bf16[320,128]{1,0:T(8,128)(2,1)S(1)}, u32[]{:S(2)}, u32[]{:S(2)}) collective-permute-start(bf16[320,128]{1,0:T(8,128)(2,1)S(1)} %bitcast.31), channel_id=1, source_target_pairs={{0,3},{1,2},{2,1},{3,0},{4,7},{5,6},{6,5},{7,4},{8,11},{9,10},{10,... | collective-permute-start | bytes 245768 | tf_op jit(solution)/shard_map/ppermute | solution.py:47
  43.3 2.1 %collective-permute-start.15 = (bf16[640,128]{1,0:T(8,128)(2,1)S(1)}, bf16[640,128]{1,0:T(8,128)(2,1)S(1)}, u32[]{:S(2)}, u32[]{:S(2)}) collective-permute-start(bf16[640,128]{1,0:T(8,128)(2,1)S(1)} %bitcast.24), channel_id=1, source_target_pairs={{0,1},{1,0},{2,3},{3,2},{4,5},{5,4},{6,7},{7,6},{8,9},{9,8},{10,11... | collective-permute-start | bytes 491528 | tf_op jit(solution)/shard_map/ppermute | solution.py:47

commit v4 on v3

--- a/solution.py
+++ b/solution.py
@@ -19,16 +19,10 @@
     return [(i, j) for i in range(count) for j in range(i, count)]
 
 
-def swap_rows(pairs, values):
+def swap_rows(low, value):
     count = lax.axis_size("rows")
-
-    def perm(low):
-        partner = {i: i for i in range(count)}
-        partner.update({i: i + 1 for i in low})
-        partner.update({i + 1: i for i in low})
-        return list(partner.items())
-
-    return [lax.ppermute(value, "rows", perm(low)) for low, value in zip(pairs, values)]
+    pairs = [(i, (i + 1) % count) for i in low]
+    return lax.ppermute(value, "rows", pairs + [(target, source) for source, target in pairs])
 
 
 def shift_cols(last, first):
@@ -302,13 +296,9 @@
     gram_tiles(feat_ref[...], gram_ref)
 
 
-def outer_kernel(
-    shape, own_ref, even_ref, odd_ref, left_ref, right_ref, kernel_ref, bias_ref, base_ref, part_ref,
-    feat_ref, slope_ref, send_ref, keep_ref, cat_ref, edge_ref, low_ref, high_ref, gram_ref,
-):
-    tile_rows, tile_cols, in_width, out_width, step = shape
-    odd = lax.rem(lax.axis_index("rows"), 2)
+def halo_rows(even_ref, odd_ref, low_ref, high_ref):
     row = lax.axis_index("rows")
+    odd = lax.rem(row, 2)
     low_ref[...] = jnp.where(odd == 0, odd_ref[...], even_ref[...])
     high_ref[...] = jnp.where(odd == 0, even_ref[...], odd_ref[...])
 
@@ -320,6 +310,49 @@
     def _():
         high_ref[...] = jnp.zeros_like(high_ref)
 
+
+def halves(width):
+    return slice(0, width // 2), slice(width // 2, width)
+
+
+def outer_kernel(
+    shape, even_ref, odd_ref, kernel_ref, base_ref, part_ref,
+    feat_ref, slope_ref, send_ref, keep_ref, low_ref, high_ref, cat_ref, gram_ref,
+):
+    tile_rows, tile_cols, in_width, out_width, step = shape
+    span, main = 3 * in_width, 2 * tile_cols
+    halo_rows(even_ref, odd_ref, low_ref, high_ref)
+    for n, (source, at) in enumerate([(low_ref, tile_cols), (high_ref, 0)]):
+        rim = source[main:, :].astype(f32)
+        k = 4 * (1 - n)
+        fill_row(cat_ref, n, source[at : at + tile_cols, :], rim[k + 1 : k + 2], rim[k + 2 : k + 3])
+    root = 1.0 / math.sqrt(out_width)
+    for at in halves(out_width):
+        for n, a in enumerate([0, 2]):
+            rows = slice(n * tile_cols, (n + 1) * tile_cols)
+            features, slope = gelu_pair(
+                part_ref[(n + 1) * tile_cols : (n + 2) * tile_cols, at]
+                + jnp.dot(
+                    cat_ref[rows, :],
+                    kernel_ref[a * span : (a + 1) * span, at],
+                    preferred_element_type=f32,
+                )
+            )
+            feat_ref[rows, at] = features.astype(bf16)
+            slope_ref[rows, at] = (slope * root).astype(bf16)
+    gram_tiles(feat_ref[...], gram_ref, base_ref)
+    half = send_ref.shape[0]
+    side = side_of(0)
+    send_ref[...] = gram_ref[rows_at(1 - side, half), :].astype(bf16)
+    keep_ref[...] = gram_ref[rows_at(side, half), :]
+
+
+def beyond_kernel(
+    shape, own_ref, even_ref, odd_ref, left_ref, right_ref, kernel_ref, bias_ref, part_ref,
+    feat_ref, slope_ref, low_ref, high_ref, cat_ref, edge_ref,
+):
+    tile_rows, tile_cols, in_width, out_width, step = shape
+    halo_rows(even_ref, odd_ref, low_ref, high_ref)
     first = (lax.axis_index("rows") > 0).astype(f32)
     last = (lax.axis_index("rows") < lax.axis_size("rows") - 1).astype(f32)
     left = (lax.axis_index("cols") > 0).astype(f32)
@@ -366,34 +399,26 @@
     weight = jnp.where(line < edge, left, right)
     weight = jnp.where(line % edge == 0, weight * first, weight)
     weight = jnp.where(line % edge == tile_rows + 1, weight * last, weight)
-    for at in (slice(0, out_width // 2), slice(out_width // 2, out_width)):
-        taps = [
-            jnp.dot(
-                cat_ref[a * tile_cols : (a + 2) * tile_cols, :],
+    for at in halves(out_width):
+
+        def product(begin, a):
+            return jnp.dot(
+                cat_ref[begin * tile_cols : (begin + 1) * tile_cols, :],
                 kernel_ref[a * span : (a + 1) * span, at],
                 preferred_element_type=f32,
             )
-            for a in range(3)
+
+        totals = [
+            part_ref[0:tile_cols, at] + product(0, 0) + product(1, 1),
+            part_ref[3 * tile_cols :, at] + product(2, 1) + product(3, 2),
+            bias_ref[:, at] + jnp.dot(edge_ref[...], kernel_ref[:, at], preferred_element_type=f32),
         ]
-        totals = [
-            part_ref[0:tile_cols, at] + taps[0][:tile_cols] + taps[1][:tile_cols],
-            part_ref[tile_cols : 2 * tile_cols, at] + taps[0][tile_cols:],
-            part_ref[2 * tile_cols : 3 * tile_cols, at] + taps[2][:tile_cols],
-            part_ref[3 * tile_cols :, at] + taps[1][tile_cols:] + taps[2][tile_cols:],
-            bias_ref[:, at]
-            + jnp.dot(edge_ref[...], kernel_ref[:, at], preferred_element_type=f32),
-        ]
-        scales = [first * root, root, root, last * root, weight * root]
+        scales = [first * root, last * root, weight * root]
         for n, (total, scale) in enumerate(zip(totals, scales)):
             features, slope = gelu_pair(total)
             rows = slice(n * tile_cols, n * tile_cols + total.shape[0])
             feat_ref[rows, at] = features.astype(bf16)
             slope_ref[rows, at] = (slope * scale).astype(bf16)
-    gram_tiles(feat_ref[tile_cols : 3 * tile_cols, :], gram_ref, base_ref)
-    half = send_ref.shape[0]
-    side = side_of(0)
-    send_ref[...] = gram_ref[rows_at(1 - side, half), :].astype(bf16)
-    keep_ref[...] = gram_ref[rows_at(side, half), :]
 
 
 def prepare_kernel(kernel_ref, target_ref, turned_ref, both_ref):
@@ -411,7 +436,7 @@
 
 def backward_kernel(
     shape, pixel_total, mine_ref, other_ref, both_ref, in_feat_ref, in_slope_ref, out_feat_ref, out_slope_ref,
-    turned_ref, own_gram_ref, out_ref, gram_ref, full_ref, sym_ref, cat_ref,
+    far_feat_ref, far_slope_ref, turned_ref, own_gram_ref, out_ref, gram_ref, full_ref, sym_ref, cat_ref,
 ):
     tile_rows, tile_cols, in_width, out_width, step = shape
     half = mine_ref.shape[0]
@@ -443,15 +468,24 @@
         return product * slope_ref[at, :].astype(f32)
 
     main = 2 * tile_cols
-    edges = grad_of(out_feat_ref, out_slope_ref, slice(2 * main, None))
-    lines = [(out_feat_ref, out_slope_ref, 0)]
-    lines += [(in_feat_ref, in_slope_ref, h * tile_cols) for h in range(0, tile_rows - 2, step)]
-    lines += [(out_feat_ref, out_slope_ref, main)]
+    edges = grad_of(far_feat_ref, far_slope_ref, slice(main, None))
+    near, far = (out_feat_ref, out_slope_ref), (far_feat_ref, far_slope_ref)
+    lines = [[(*far, 0), (*near, 0)]]
+    lines += [
+        [(in_feat_ref, in_slope_ref, k * tile_cols) for k in range(h, h + step)]
+        for h in range(0, tile_rows - 2, step)
+    ]
+    lines += [[(*near, tile_cols), (*far, tile_cols)]]
     grads = {}
 
     def upstream(c):
-        feat_ref, slope_ref, begin = lines[c]
-        grads[c] = grad_of(feat_ref, slope_ref, slice(begin, begin + step * tile_cols))
+        pieces = lines[c]
+        if pieces[0][0] is pieces[1][0]:
+            feat_ref, slope_ref, begin = pieces[0]
+            grads[c] = grad_of(feat_ref, slope_ref, slice(begin, begin + step * tile_cols))
+        else:
+            parts = [grad_of(feat, slope, slice(begin, begin + tile_cols)) for feat, slope, begin in pieces]
+            grads[c] = jnp.concatenate(parts, axis=0)
 
     def fill(c):
         for k in range(step):
@@ -520,7 +554,7 @@
         *beyond,
     )
     count = lax.axis_size("rows")
-    odd, even = swap_rows([range(1, count - 1, 2), range(0, count - 1, 2)], [odd, even])
+    even, odd = swap_rows(range(0, count, 2), even), swap_rows(range(1, count, 2), odd)
 
     bits = (lax.axis_size("rows") * lax.axis_size("cols")).bit_length() - 1
     gather = Gather(rows)
@@ -546,32 +580,49 @@
         ),
     )(canvas, left, right, kernel, conv_bias)
 
-    outer = 4 * tile_cols + 2 * edge
     half_gram = (packed_shape.shape[0] // 2, tile)
+    halo_scratch = [pltpu.VMEM(payload_shape.shape, bf16), pltpu.VMEM(payload_shape.shape, bf16)]
     out_feat, out_slope, send, keep = pl.pallas_call(
         functools.partial(outer_kernel, shape),
         out_shape=(
-            jax.ShapeDtypeStruct((outer, out_width), bf16),
-            jax.ShapeDtypeStruct((outer, out_width), bf16),
+            jax.ShapeDtypeStruct((2 * tile_cols, out_width), bf16),
+            jax.ShapeDtypeStruct((2 * tile_cols, out_width), bf16),
             jax.ShapeDtypeStruct(half_gram, bf16),
             jax.ShapeDtypeStruct(half_gram, f32),
         ),
-        in_specs=[vmem] * 9,
+        in_specs=[vmem] * 5,
         scratch_shapes=[
-            pltpu.VMEM((4 * tile_cols, 3 * in_width), bf16),
-            pltpu.VMEM((2 * edge, 9 * in_width), bf16),
-            pltpu.VMEM(payload_shape.shape, bf16),
-            pltpu.VMEM(payload_shape.shape, bf16),
+            *halo_scratch,
+            pltpu.VMEM((2 * tile_cols, 3 * in_width), bf16),
             pltpu.VMEM(packed_shape.shape, f32),
         ],
         compiler_params=params,
         name="outer_rows",
-    )(canvas, even, odd, left, right, kernel, bias, in_gram, part)
+    )(even, odd, kernel, in_gram, part)
 
     exchanges = {"cores": far[:1], "halve 1": far[1:], "halve 2": [1], "add 3": [2], "add 4": [0]}
-    prepared = []
+    prepared, far_pixels = [], []
 
     def beside(name, sent, got):
+        if name == "join 1":
+            outer = 2 * tile_cols + 2 * edge
+            rim_sums, _ = lax.optimization_barrier((part, sent))
+            far_pixels.extend(
+                pl.pallas_call(
+                    functools.partial(beyond_kernel, shape),
+                    out_shape=(jax.ShapeDtypeStruct((outer, out_width), bf16),) * 2,
+                    in_specs=[vmem] * 8,
+                    scratch_shapes=[
+                        *halo_scratch,
+                        pltpu.VMEM((4 * tile_cols, 3 * in_width), bf16),
+                        pltpu.VMEM((2 * edge, 9 * in_width), bf16),
+                    ],
+                    compiler_params=params,
+                    name="beyond",
+                    cost_estimate=chained,
+                )(canvas, even, odd, left, right, kernel, bias, rim_sums)
+            )
+            return lax.optimization_barrier((got, *far_pixels))[0]
         for bit in exchanges.get(name, []):
             gather.step(bit, sent)
         if name != "join 2":
@@ -596,13 +647,14 @@
 
     mine, other = sum_all(send, keep, beside)
     turned, both = prepared
+    far_feat, far_slope = far_pixels
     own_gram, grad = pl.pallas_call(
         functools.partial(backward_kernel, shape, pixel_total),
         out_shape=(
             jax.ShapeDtypeStruct(target_gram.shape, f32),
             jax.ShapeDtypeStruct((tile_rows * tile_cols, in_width), bf16),
         ),
-        in_specs=[vmem] * 8,
+        in_specs=[vmem] * 10,
         scratch_shapes=[
             pltpu.VMEM(packed_shape.shape, f32),
             pltpu.VMEM((out_width, out_width), f32),
@@ -611,7 +663,7 @@
         ],
         compiler_params=params,
         name="grad_conv",
-    )(mine, other, both, in_feat, in_slope, out_feat, out_slope, turned)
+    )(mine, other, both, in_feat, in_slope, out_feat, out_slope, far_feat, far_slope, turned)
     return own_gram, grad.reshape(tile_rows, tile_cols, in_width)
 
 

time: 50 us -> 48.9 us (0.978)
  starting transfers between devices: 22.5 us -> 20.7 us
  waiting for transfers between devices: 14.6 us -> 15.2 us
    ppermute x13, starting transfers between devices: 18.4 us -> 12.8 us  [swap(): lax.ppermute(value, ('rows', 'cols'), [(i, i ^ (1 << bit | 1)) for i in r...]
    ppermute x2, starting transfers between devices: 3.55 us -> 7.42 us  [swap_rows(): lax.ppermute(value, 'rows', pairs + [(target, source) for source, target...]
    ppermute x2, waiting for transfers between devices: 0.01 us -> 1.15 us  [swap_rows(): lax.ppermute(value, 'rows', pairs + [(target, source) for source, target...]
    pallas_call x0 -> x1, Pallas kernels: none -> 1.04 us  [beside(): pl.pallas_call(functools.partial(beyond_kernel, shape), out_shape=(jax.Sh...]
    pallas_call x1, Pallas kernels: 1.76 us -> 0.9 us  [on_device(): pl.pallas_call(functools.partial(outer_kernel, shape), out_shape=(jax.Sha...]
    ppermute x13, waiting for transfers between devices: 13.8 us -> 13.2 us  [swap(): lax.ppermute(value, ('rows', 'cols'), [(i, i ^ (1 << bit | 1)) for i in r...]
  transfers between devices with their start and end apart: 16 -> 16, of which waited for: 10 -> 14; matrix products, arithmetic and copies ran while one was open for 0% -> 0% of each run, Pallas kernels for 9% -> 11%
where the time goes in v4:
time: 48.9 us; the launch traced here: 48.7 us
  starting transfers between devices  20.7 us (42%)
  waiting for transfers between devices  15.2 us (31%)
  Pallas kernels  11 us (22%)
  local copies, waits for them, and re-layouts  1.05 us (2%)
  between operations  0.76 us (2%)
    ppermute x13, waiting for transfers between devices, swap(): lax.ppermute(value, ('rows', 'cols'), [(i, i ^ (1 << bit | 1)) for i in r...  13.2 us
    ppermute x13, starting transfers between devices, swap(): lax.ppermute(value, ('rows', 'cols'), [(i, i ^ (1 << bit | 1)) for i in r...  12.8 us
    ppermute x2, starting transfers between devices, swap_rows(): lax.ppermute(value, 'rows', pairs + [(target, source) for source, target...  7.42 us
    pallas_call x1, Pallas kernels, on_device(): pl.pallas_call(functools.partial(backward_kernel, shape, pixel_total), ou...  4.45 us
    pallas_call x1, Pallas kernels, on_device(): pl.pallas_call(functools.partial(inner_kernel, shape), out_shape=(jax.Sha...  3.36 us
    ppermute x2, waiting for transfers between devices, swap_rows(): lax.ppermute(value, 'rows', pairs + [(target, source) for source, target...  1.15 us
    unnamed x10, local copies, waits for them, and re-layouts  1.05 us
    pallas_call x1, Pallas kernels, beside(): pl.pallas_call(functools.partial(beyond_kernel, shape), out_shape=(jax.Sh...  1.04 us
  transfers between devices with their start and end apart: 16, of which 14 were waited for; matrix products, arithmetic and copies ran while one was open for 0% of the time, Pallas kernels for 11%

profile of v4, /device:TPU:0, one launch (start us, length us, event | category | flops | bytes accessed | tf_op | source)
XLA Modules:
  0.0 48.7 jit_solution(10080087312889641411)
XLA Ops:
  0.6 1.0 %copy-done.1 = bf16[8,128,256]{2,1,0:T(8,128)(2,1)S(1)} copy-done((bf16[8,128,256]{2,1,0:T(8,128)(2,1)S(1)}, bf16[8,128,256]{2,1,0:T(8,128)(2,1)}, u32[]{:S(2)}) %copy-start.1) | copy-done | bytes 524312
  1.7 0.5 %collective-permute-start = (bf16[2,8,256]{2,1,0:T(8,128)(2,1)S(1)}, bf16[2,8,256]{2,1,0:T(8,128)(2,1)S(1)}, u32[]{:S(2)}, u32[]{:S(2)}) collective-permute-start(bf16[2,8,256]{2,1,0:T(8,128)(2,1)S(1)} %column_rims.1), channel_id=1, source_target_pairs={{0,1},{1,0},{2,3},{3,2},{4,5},{5,4},{6,7},{7,6},{8,9},{9,8},{10,11... | collective-permute-start | bytes 24584 | tf_op jit(solution)/shard_map/ppermute | solution.py:543
  2.2 0.8 %collective-permute-done.refs_0_ = bf16[2,8,256]{2,1,0:T(8,128)(2,1)S(1)} collective-permute-done((bf16[2,8,256]{2,1,0:T(8,128)(2,1)S(1)}, bf16[2,8,256]{2,1,0:T(8,128)(2,1)S(1)}, u32[]{:S(2)}, u32[]{:S(2)}) %collective-permute-start) | collective-permute-done | bytes 8224 | tf_op jit(solution)/shard_map/ppermute | solution.py:543
  3.1 2.9 %collective-permute-start.1 = (bf16[272,256]{1,0:T(8,128)(2,1)S(1)}, bf16[272,256]{1,0:T(8,128)(2,1)S(1)}, u32[]{:S(2)}, u32[]{:S(2)}) collective-permute-start(bf16[272,256]{1,0:T(8,128)(2,1)S(1)} %get-tuple-element.35), channel_id=1, source_target_pairs={{0,2},{4,6},{8,10},{12,14},{16,18},{20,22},{24,26},{28,30},{2,0},{... | collective-permute-start | bytes 417800 | tf_op jit(solution)/shard_map/ppermute | solution.py:25
  6.0 4.5 %collective-permute-start.2 = (bf16[272,256]{1,0:T(8,128)(2,1)S(1)}, bf16[272,256]{1,0:T(8,128)(2,1)S(1)}, u32[]{:S(2)}, u32[]{:S(2)}) collective-permute-start(bf16[272,256]{1,0:T(8,128)(2,1)S(1)} %get-tuple-element.36), channel_id=1, source_target_pairs={{2,4},{6,8},{10,12},{14,16},{18,20},{22,24},{26,28},{30,0},{4,2},{... | collective-permute-start | bytes 417800 | tf_op jit(solution)/shard_map/ppermute | solution.py:25
  10.5 3.4 %inner_rows.1 = (bf16[768,512]{1,0:T(8,128)(2,1)S(1)}, bf16[768,512]{1,0:T(8,128)(2,1)S(1)}, f32[1280,128]{1,0:T(8,128)S(1)}, f32[1,512]{1,0:T(1,128)S(1)}, f32[512,512]{1,0:T(8,128)S(1)}) custom-call(bf16[8,128,256]{2,1,0:T(8,128)(2,1)S(1)} %copy-done.2, bf16[2,8,256]{2,1,0:T(8,128)(2,1)S(1)} %get-tuple-element.37.left_ref, ...), custom_call_target="tpu_custom_call" | custom-call | flops 2214592512 | bytes 6000000 | tf_op jit(solution)/shard_map/inner_rows/pallas_call | solution.py:563
  13.9 1.1 %collective-permute-done.2.odd_ref = bf16[272,256]{1,0:T(8,128)(2,1)S(1)} collective-permute-done((bf16[272,256]{1,0:T(8,128)(2,1)S(1)}, bf16[272,256]{1,0:T(8,128)(2,1)S(1)}, u32[]{:S(2)}, u32[]{:S(2)}) %collective-permute-start.2) | collective-permute-done | bytes 139296 | tf_op jit(solution)/shard_map/ppermute | solution.py:25
  15.1 0.9 %outer_rows.1 = (bf16[256,512]{1,0:T(8,128)(2,1)S(1)}, bf16[256,512]{1,0:T(8,128)(2,1)S(1)}, bf16[640,128]{1,0:T(8,128)(2,1)S(1)}, f32[640,128]{1,0:T(8,128)S(1)}) custom-call(bf16[272,256]{1,0:T(8,128)(2,1)S(1)} %collective-permute-done.1.even_ref, bf16[272,256]{1,0:T(8,128)(2,1)S(1)} %collective-permute-done.2.odd_ref, bf16[2304,512]{1,0:T(8,128)(2,1)S(1)} %bitcast.22, ...), custom_call_target="tpu_custom_call" | custom-call | tf_op jit(solution)/shard_map/outer_rows/pallas_call | solution.py:585
  16.0 1.0 %collective-permute-start.9 = (bf16[1,16,512]{2,1,0:T(8,128)(2,1)S(1)}, bf16[1,16,512]{2,1,0:T(8,128)(2,1)S(1)}, u32[]{:S(2)}, u32[]{:S(2)}) collective-permute-start(bf16[1,16,512]{2,1,0:T(8,128)(2,1)S(1)} %get-tuple-element.48), channel_id=1, source_target_pairs={{0,17},{1,16},{2,19},{3,18},{4,21},{5,20},{6,23},{7,22},{8,25},{9,... | collective-permute-start | bytes 49160 | tf_op jit(solution)/shard_map/ppermute | solution.py:41
  17.4 1.7 %collective-permute-start.4 = (bf16[320,128]{1,0:T(8,128)(2,1)S(1)}, bf16[320,128]{1,0:T(8,128)(2,1)S(1)}, u32[]{:S(2)}, u32[]{:S(2)}) collective-permute-start(bf16[320,128]{1,0:T(8,128)(2,1)S(1)} %get-tuple-element.44), channel_id=1, source_target_pairs={{0,3},{1,2},{2,1},{3,0},{4,7},{5,6},{6,5},{7,4},{8,11},{9,10},{10,... | collective-permute-start | bytes 245768 | tf_op jit(solution)/shard_map/ppermute | solution.py:41
  19.1 1.2 %collective-permute-done.9 = bf16[1,16,512]{2,1,0:T(8,128)(2,1)S(1)} collective-permute-done((bf16[1,16,512]{2,1,0:T(8,128)(2,1)S(1)}, bf16[1,16,512]{2,1,0:T(8,128)(2,1)S(1)}, u32[]{:S(2)}, u32[]{:S(2)}) %collective-permute-start.9) | collective-permute-done | bytes 16416 | tf_op jit(solution)/shard_map/ppermute | solution.py:41
  20.3 0.5 %collective-permute-start.10 = (bf16[2,16,512]{2,1,0:T(8,128)(2,1)S(1)}, bf16[2,16,512]{2,1,0:T(8,128)(2,1)S(1)}, u32[]{:S(2)}, u32[]{:S(2)}) collective-permute-start(bf16[2,16,512]{2,1,0:T(8,128)(2,1)S(1)} %bitcast.40), channel_id=1, source_target_pairs={{0,9},{1,8},{2,11},{3,10},{4,13},{5,12},{6,15},{7,14},{8,1},{9,0},... | collective-permute-start | bytes 98312 | tf_op jit(solution)/shard_map/ppermute | solution.py:41
  20.8 1.0 %collective-permute-done.4.got_ref = bf16[320,128]{1,0:T(8,128)(2,1)S(1)} collective-permute-done((bf16[320,128]{1,0:T(8,128)(2,1)S(1)}, bf16[320,128]{1,0:T(8,128)(2,1)S(1)}, u32[]{:S(2)}, u32[]{:S(2)}) %collective-permute-start.4) | collective-permute-done | bytes 81952 | tf_op jit(solution)/shard_map/ppermute | solution.py:41
  21.9 1.0 %collective-permute-start.5 = (bf16[160,128]{1,0:T(8,128)(2,1)S(1)}, bf16[160,128]{1,0:T(8,128)(2,1)S(1)}, u32[]{:S(2)}, u32[]{:S(2)}) collective-permute-start(bf16[160,128]{1,0:T(8,128)(2,1)S(1)} %get-tuple-element.46), channel_id=1, source_target_pairs={{0,5},{1,4},{2,7},{3,6},{4,1},{5,0},{6,3},{7,2},{8,13},{9,12},{10,... | collective-permute-start | bytes 122888 | tf_op jit(solution)/shard_map/ppermute | solution.py:41
  22.8 0.8 %collective-permute-done.10 = bf16[2,16,512]{2,1,0:T(8,128)(2,1)S(1)} collective-permute-done((bf16[2,16,512]{2,1,0:T(8,128)(2,1)S(1)}, bf16[2,16,512]{2,1,0:T(8,128)(2,1)S(1)}, u32[]{:S(2)}, u32[]{:S(2)}) %collective-permute-start.10) | collective-permute-done | bytes 32800 | tf_op jit(solution)/shard_map/ppermute | solution.py:41
  23.6 0.6 %collective-permute-start.11 = (bf16[4,16,512]{2,1,0:T(8,128)(2,1)S(1)}, bf16[4,16,512]{2,1,0:T(8,128)(2,1)S(1)}, u32[]{:S(2)}, u32[]{:S(2)}) collective-permute-start(bf16[4,16,512]{2,1,0:T(8,128)(2,1)S(1)} %bitcast.35), channel_id=1, source_target_pairs={{0,3},{1,2},{2,1},{3,0},{4,7},{5,6},{6,5},{7,4},{8,11},{9,10},{10,... | collective-permute-start | bytes 196616 | tf_op jit(solution)/shard_map/ppermute | solution.py:41
  24.3 1.2 %collective-permute-done.5.got_ref = bf16[160,128]{1,0:T(8,128)(2,1)S(1)} collective-permute-done((bf16[160,128]{1,0:T(8,128)(2,1)S(1)}, bf16[160,128]{1,0:T(8,128)(2,1)S(1)}, u32[]{:S(2)}, u32[]{:S(2)}) %collective-permute-start.5) | collective-permute-done | bytes 40992 | tf_op jit(solution)/shard_map/ppermute | solution.py:41
  25.5 1.5 %collective-permute-start.6 = (bf16[160,128]{1,0:T(8,128)(2,1)S(1)}, bf16[160,128]{1,0:T(8,128)(2,1)S(1)}, u32[]{:S(2)}, u32[]{:S(2)}) collective-permute-start(bf16[160,128]{1,0:T(8,128)(2,1)S(1)} %add.3.keep_ref), channel_id=1, source_target_pairs={{0,9},{1,8},{2,11},{3,10},{4,13},{5,12},{6,15},{7,14},{8,1},{9,0},... | collective-permute-start | bytes 122888 | tf_op jit(solution)/shard_map/ppermute | solution.py:41
  26.9 0.7 %collective-permute-done.11 = bf16[4,16,512]{2,1,0:T(8,128)(2,1)S(1)} collective-permute-done((bf16[4,16,512]{2,1,0:T(8,128)(2,1)S(1)}, bf16[4,16,512]{2,1,0:T(8,128)(2,1)S(1)}, u32[]{:S(2)}, u32[]{:S(2)}) %collective-permute-start.11) | collective-permute-done | bytes 65568 | tf_op jit(solution)/shard_map/ppermute | solution.py:41
  27.7 0.6 %collective-permute-start.12 = (bf16[8,16,512]{2,1,0:T(8,128)(2,1)S(1)}, bf16[8,16,512]{2,1,0:T(8,128)(2,1)S(1)}, u32[]{:S(2)}, u32[]{:S(2)}) collective-permute-start(bf16[8,16,512]{2,1,0:T(8,128)(2,1)S(1)} %bitcast.29), channel_id=1, source_target_pairs={{0,5},{1,4},{2,7},{3,6},{4,1},{5,0},{6,3},{7,2},{8,13},{9,12},{10,... | collective-permute-start | bytes 393224 | tf_op jit(solution)/shard_map/ppermute | solution.py:41
  28.3 0.8 %collective-permute-done.6.got_ref = bf16[160,128]{1,0:T(8,128)(2,1)S(1)} collective-permute-done((bf16[160,128]{1,0:T(8,128)(2,1)S(1)}, bf16[160,128]{1,0:T(8,128)(2,1)S(1)}, u32[]{:S(2)}, u32[]{:S(2)}) %collective-permute-start.6) | collective-permute-done | bytes 40992 | tf_op jit(solution)/shard_map/ppermute | solution.py:41
  29.1 1.7 %collective-permute-start.7 = (bf16[160,128]{1,0:T(8,128)(2,1)S(1)}, bf16[160,128]{1,0:T(8,128)(2,1)S(1)}, u32[]{:S(2)}, u32[]{:S(2)}) collective-permute-start(bf16[160,128]{1,0:T(8,128)(2,1)S(1)} %add.4.keep_ref), channel_id=1, source_target_pairs={{0,17},{1,16},{2,19},{3,18},{4,21},{5,20},{6,23},{7,22},{8,25},{9,... | collective-permute-start | bytes 122888 | tf_op jit(solution)/shard_map/ppermute | solution.py:41
  30.8 2.4 %collective-permute-done.12 = bf16[8,16,512]{2,1,0:T(8,128)(2,1)S(1)} collective-permute-done((bf16[8,16,512]{2,1,0:T(8,128)(2,1)S(1)}, bf16[8,16,512]{2,1,0:T(8,128)(2,1)S(1)}, u32[]{:S(2)}, u32[]{:S(2)}) %collective-permute-start.12) | collective-permute-done | bytes 131104 | tf_op jit(solution)/shard_map/ppermute | solution.py:41
  33.2 0.5 %collective-permute-start.13 = (bf16[16,16,512]{2,1,0:T(8,128)(2,1)S(1)}, bf16[16,16,512]{2,1,0:T(8,128)(2,1)S(1)}, u32[]{:S(2)}, u32[]{:S(2)}) collective-permute-start(bf16[16,16,512]{2,1,0:T(8,128)(2,1)S(1)} %bitcast.27), channel_id=1, source_target_pairs={{0,1},{1,0},{2,3},{3,2},{4,5},{5,4},{6,7},{7,6},{8,9},{9,8},{10,11... | collective-permute-start | bytes 786440 | tf_op jit(solution)/shard_map/ppermute | solution.py:41
  33.8 0.9 %collective-permute-start.8 = (bf16[160,128]{1,0:T(8,128)(2,1)S(1)}, bf16[160,128]{1,0:T(8,128)(2,1)S(1)}, u32[]{:S(2)}, u32[]{:S(2)}) collective-permute-start(bf16[160,128]{1,0:T(8,128)(2,1)S(1)} %add.5), channel_id=1, source_target_pairs={{0,5},{1,4},{2,7},{3,6},{4,1},{5,0},{6,3},{7,2},{8,13},{9,12},{10,... | collective-permute-start | bytes 122888 | tf_op jit(solution)/shard_map/ppermute | solution.py:41
  35.0 1.0 %prepare.1 = (bf16[4608,256]{1,0:T(8,128)(2,1)S(1)}, f32[512,512]{1,0:T(8,128)S(1)}) custom-call(bf16[2304,512]{1,0:T(8,128)(2,1)S(1)} %bitcast.23, bf16[512,512]{1,0:T(8,128)(2,1)S(1)} %bitcast.45), custom_call_target="tpu_custom_call" | custom-call | flops 2000000000 | bytes 6000000 | tf_op jit(solution)/shard_map/prepare/pallas_call | solution.py:632
  36.0 1.5 %collective-permute-done.8 = bf16[160,128]{1,0:T(8,128)(2,1)S(1)} collective-permute-done((bf16[160,128]{1,0:T(8,128)(2,1)S(1)}, bf16[160,128]{1,0:T(8,128)(2,1)S(1)}, u32[]{:S(2)}, u32[]{:S(2)}) %collective-permute-start.8) | collective-permute-done | bytes 40992 | tf_op jit(solution)/shard_map/ppermute | solution.py:41
  37.5 2.6 %collective-permute-start.14 = (bf16[320,128]{1,0:T(8,128)(2,1)S(1)}, bf16[320,128]{1,0:T(8,128)(2,1)S(1)}, u32[]{:S(2)}, u32[]{:S(2)}) collective-permute-start(bf16[320,128]{1,0:T(8,128)(2,1)S(1)} %bitcast.32), channel_id=1, source_target_pairs={{0,3},{1,2},{2,1},{3,0},{4,7},{5,6},{6,5},{7,4},{8,11},{9,10},{10,... | collective-permute-start | bytes 245768 | tf_op jit(solution)/shard_map/ppermute | solution.py:41
  40.1 1.0 %beyond.1 = (bf16[288,512]{1,0:T(8,128)(2,1)S(1)}, bf16[288,512]{1,0:T(8,128)(2,1)S(1)}) custom-call(bf16[8,128,256]{2,1,0:T(8,128)(2,1)S(1)} %copy-done.2, bf16[272,256]{1,0:T(8,128)(2,1)S(1)} %collective-permute-done.1.even_ref, bf16[272,256]{1,0:T(8,128)(2,1)S(1)} %collective-permute-done.2.odd_ref, bf16[2,8,256]{2,1,0:T(8,128)(2,1)S(1)} %get-tuple-element.37.left_ref, ...), custom_call_target="tpu_custom_call" | custom-call | flops 8000000000 | bytes 100000 | tf_op jit(solution)/shard_map/beyond/pallas_call | solution.py:611
  41.1 1.7 %collective-permute-done.14 = bf16[320,128]{1,0:T(8,128)(2,1)S(1)} collective-permute-done((bf16[320,128]{1,0:T(8,128)(2,1)S(1)}, bf16[320,128]{1,0:T(8,128)(2,1)S(1)}, u32[]{:S(2)}, u32[]{:S(2)}) %collective-permute-start.14) | collective-permute-done | bytes 81952 | tf_op jit(solution)/shard_map/ppermute | solution.py:41
  42.9 1.4 %collective-permute-done.15.other_ref = bf16[640,128]{1,0:T(8,128)(2,1)S(1)} collective-permute-done((bf16[640,128]{1,0:T(8,128)(2,1)S(1)}, bf16[640,128]{1,0:T(8,128)(2,1)S(1)}, u32[]{:S(2)}, u32[]{:S(2)}) %collective-permute-start.15) | collective-permute-done | bytes 163872 | tf_op jit(solution)/shard_map/ppermute | solution.py:41
  44.3 4.5 %grad_conv.1 = (f32[16,512]{1,0:T(8,128)}, bf16[1024,256]{1,0:T(8,128)(2,1)}) custom-call(bf16[640,128]{1,0:T(8,128)(2,1)S(1)} %bitcast.26, bf16[640,128]{1,0:T(8,128)(2,1)S(1)} %collective-permute-done.15.other_ref, f32[512,512]{1,0:T(8,128)S(1)} %get-tuple-element.55.both_ref, bf16[768,512]{1,0:T(8,128)(2,1)S(1)} %get-tuple-element.62.in_feat_ref, ...), custom_call_target="tpu_custom_call" | custom-call | tf_op jit(solution)/shard_map/grad_conv/pallas_call | solution.py:651
  (29 shorter events, 1.1 us)
Async XLA Ops:
  0.6 1.0 %copy-start.1 = (bf16[8,128,256]{2,1,0:T(8,128)(2,1)S(1)}, bf16[8,128,256]{2,1,0:T(8,128)(2,1)}, u32[]{:S(2)}) copy-start(bf16[8,128,256]{2,1,0:T(8,128)(2,1)} %own_ref.3) | copy-start | bytes 1572868
  1.7 1.4 %copy-start.3 = (f32[16,512]{1,0:T(8,128)S(1)}, f32[16,512]{1,0:T(8,128)}, u32[]{:S(2)}) copy-start(f32[16,512]{1,0:T(8,128)} %target_ref.1) | copy-start | bytes 98308
  1.7 8.9 %copy-start = (bf16[3,3,256,512]{3,2,1,0:T(8,128)(2,1)S(1)}, bf16[3,3,256,512]{3,2,1,0:T(8,128)(2,1)}, u32[]{:S(2)}) copy-start(bf16[3,3,256,512]{3,2,1,0:T(8,128)(2,1)} %param.5) | copy-start | bytes 7077892
  1.7 8.9 %copy-start.2 = (bf16[8,128,256]{2,1,0:T(8,128)(2,1)S(1)}, bf16[8,128,256]{2,1,0:T(8,128)(2,1)}, u32[]{:S(2)}) copy-start(bf16[8,128,256]{2,1,0:T(8,128)(2,1)} %own_ref.3) | copy-start | bytes 1572868
  1.7 8.9 %copy-start.4 = (bf16[512]{0:T(512)(128)(2,1)S(1)}, bf16[512]{0:T(512)(128)(2,1)}, u32[]{:S(2)}) copy-start(bf16[512]{0:T(512)(128)(2,1)} %bias_ref.1) | copy-start | bytes 3076
  1.7 1.3 %collective-permute-start = (bf16[2,8,256]{2,1,0:T(8,128)(2,1)S(1)}, bf16[2,8,256]{2,1,0:T(8,128)(2,1)S(1)}, u32[]{:S(2)}, u32[]{:S(2)}) collective-permute-start(bf16[2,8,256]{2,1,0:T(8,128)(2,1)S(1)} %column_rims.1), channel_id=1, source_target_pairs={{0,1},{1,0},{2,3},{3,2},{4,5},{5,4},{6,7},{7,6},{8,9},{9,8},{10,11... | collective-permute-start | bytes 24584 | tf_op jit(solution)/shard_map/ppermute | solution.py:543
  3.1 10.8 %collective-permute-start.1 = (bf16[272,256]{1,0:T(8,128)(2,1)S(1)}, bf16[272,256]{1,0:T(8,128)(2,1)S(1)}, u32[]{:S(2)}, u32[]{:S(2)}) collective-permute-start(bf16[272,256]{1,0:T(8,128)(2,1)S(1)} %get-tuple-element.35), channel_id=1, source_target_pairs={{0,2},{4,6},{8,10},{12,14},{16,18},{20,22},{24,26},{28,30},{2,0},{... | collective-permute-start | bytes 417800 | tf_op jit(solution)/shard_map/ppermute | solution.py:25
  6.0 9.1 %collective-permute-start.2 = (bf16[272,256]{1,0:T(8,128)(2,1)S(1)}, bf16[272,256]{1,0:T(8,128)(2,1)S(1)}, u32[]{:S(2)}, u32[]{:S(2)}) collective-permute-start(bf16[272,256]{1,0:T(8,128)(2,1)S(1)} %get-tuple-element.36), channel_id=1, source_target_pairs={{2,4},{6,8},{10,12},{14,16},{18,20},{22,24},{26,28},{30,0},{4,2},{... | collective-permute-start | bytes 417800 | tf_op jit(solution)/shard_map/ppermute | solution.py:25
  16.0 1.5 %collective-permute-start.3 = (bf16[640,128]{1,0:T(8,128)(2,1)S(1)}, bf16[640,128]{1,0:T(8,128)(2,1)S(1)}, u32[]{:S(2)}, u32[]{:S(2)}) collective-permute-start(bf16[640,128]{1,0:T(8,128)(2,1)S(1)} %get-tuple-element.42), channel_id=1, source_target_pairs={{0,1},{1,0},{2,3},{3,2},{4,5},{5,4},{6,7},{7,6},{8,9},{9,8},{10,11... | collective-permute-start | bytes 491528 | tf_op jit(solution)/shard_map/ppermute | solution.py:41
  16.0 4.2 %collective-permute-start.9 = (bf16[1,16,512]{2,1,0:T(8,128)(2,1)S(1)}, bf16[1,16,512]{2,1,0:T(8,128)(2,1)S(1)}, u32[]{:S(2)}, u32[]{:S(2)}) collective-permute-start(bf16[1,16,512]{2,1,0:T(8,128)(2,1)S(1)} %get-tuple-element.48), channel_id=1, source_target_pairs={{0,17},{1,16},{2,19},{3,18},{4,21},{5,20},{6,23},{7,22},{8,25},{9,... | collective-permute-start | bytes 49160 | tf_op jit(solution)/shard_map/ppermute | solution.py:41
  17.4 4.4 %collective-permute-start.4 = (bf16[320,128]{1,0:T(8,128)(2,1)S(1)}, bf16[320,128]{1,0:T(8,128)(2,1)S(1)}, u32[]{:S(2)}, u32[]{:S(2)}) collective-permute-start(bf16[320,128]{1,0:T(8,128)(2,1)S(1)} %get-tuple-element.44), channel_id=1, source_target_pairs={{0,3},{1,2},{2,1},{3,0},{4,7},{5,6},{6,5},{7,4},{8,11},{9,10},{10,... | collective-permute-start | bytes 245768 | tf_op jit(solution)/shard_map/ppermute | solution.py:41
  20.3 3.3 %collective-permute-start.10 = (bf16[2,16,512]{2,1,0:T(8,128)(2,1)S(1)}, bf16[2,16,512]{2,1,0:T(8,128)(2,1)S(1)}, u32[]{:S(2)}, u32[]{:S(2)}) collective-permute-start(bf16[2,16,512]{2,1,0:T(8,128)(2,1)S(1)} %bitcast.40), channel_id=1, source_target_pairs={{0,9},{1,8},{2,11},{3,10},{4,13},{5,12},{6,15},{7,14},{8,1},{9,0},... | collective-permute-start | bytes 98312 | tf_op jit(solution)/shard_map/ppermute | solution.py:41
  21.9 3.6 %collective-permute-start.5 = (bf16[160,128]{1,0:T(8,128)(2,1)S(1)}, bf16[160,128]{1,0:T(8,128)(2,1)S(1)}, u32[]{:S(2)}, u32[]{:S(2)}) collective-permute-start(bf16[160,128]{1,0:T(8,128)(2,1)S(1)} %get-tuple-element.46), channel_id=1, source_target_pairs={{0,5},{1,4},{2,7},{3,6},{4,1},{5,0},{6,3},{7,2},{8,13},{9,12},{10,... | collective-permute-start | bytes 122888 | tf_op jit(solution)/shard_map/ppermute | solution.py:41
  23.6 4.0 %collective-permute-start.11 = (bf16[4,16,512]{2,1,0:T(8,128)(2,1)S(1)}, bf16[4,16,512]{2,1,0:T(8,128)(2,1)S(1)}, u32[]{:S(2)}, u32[]{:S(2)}) collective-permute-start(bf16[4,16,512]{2,1,0:T(8,128)(2,1)S(1)} %bitcast.35), channel_id=1, source_target_pairs={{0,3},{1,2},{2,1},{3,0},{4,7},{5,6},{6,5},{7,4},{8,11},{9,10},{10,... | collective-permute-start | bytes 196616 | tf_op jit(solution)/shard_map/ppermute | solution.py:41
  25.5 3.6 %collective-permute-start.6 = (bf16[160,128]{1,0:T(8,128)(2,1)S(1)}, bf16[160,128]{1,0:T(8,128)(2,1)S(1)}, u32[]{:S(2)}, u32[]{:S(2)}) collective-permute-start(bf16[160,128]{1,0:T(8,128)(2,1)S(1)} %add.3.keep_ref), channel_id=1, source_target_pairs={{0,9},{1,8},{2,11},{3,10},{4,13},{5,12},{6,15},{7,14},{8,1},{9,0},... | collective-permute-start | bytes 122888 | tf_op jit(solution)/shard_map/ppermute | solution.py:41
  27.7 5.5 %collective-permute-start.12 = (bf16[8,16,512]{2,1,0:T(8,128)(2,1)S(1)}, bf16[8,16,512]{2,1,0:T(8,128)(2,1)S(1)}, u32[]{:S(2)}, u32[]{:S(2)}) collective-permute-start(bf16[8,16,512]{2,1,0:T(8,128)(2,1)S(1)} %bitcast.29), channel_id=1, source_target_pairs={{0,5},{1,4},{2,7},{3,6},{4,1},{5,0},{6,3},{7,2},{8,13},{9,12},{10,... | collective-permute-start | bytes 393224 | tf_op jit(solution)/shard_map/ppermute | solution.py:41
  29.1 4.7 %collective-permute-start.7 = (bf16[160,128]{1,0:T(8,128)(2,1)S(1)}, bf16[160,128]{1,0:T(8,128)(2,1)S(1)}, u32[]{:S(2)}, u32[]{:S(2)}) collective-permute-start(bf16[160,128]{1,0:T(8,128)(2,1)S(1)} %add.4.keep_ref), channel_id=1, source_target_pairs={{0,17},{1,16},{2,19},{3,18},{4,21},{5,20},{6,23},{7,22},{8,25},{9,... | collective-permute-start | bytes 122888 | tf_op jit(solution)/shard_map/ppermute | solution.py:41
  33.2 1.7 %collective-permute-start.13 = (bf16[16,16,512]{2,1,0:T(8,128)(2,1)S(1)}, bf16[16,16,512]{2,1,0:T(8,128)(2,1)S(1)}, u32[]{:S(2)}, u32[]{:S(2)}) collective-permute-start(bf16[16,16,512]{2,1,0:T(8,128)(2,1)S(1)} %bitcast.27), channel_id=1, source_target_pairs={{0,1},{1,0},{2,3},{3,2},{4,5},{5,4},{6,7},{7,6},{8,9},{9,8},{10,11... | collective-permute-start | bytes 786440 | tf_op jit(solution)/shard_map/ppermute | solution.py:41
  33.8 3.7 %collective-permute-start.8 = (bf16[160,128]{1,0:T(8,128)(2,1)S(1)}, bf16[160,128]{1,0:T(8,128)(2,1)S(1)}, u32[]{:S(2)}, u32[]{:S(2)}) collective-permute-start(bf16[160,128]{1,0:T(8,128)(2,1)S(1)} %add.5), channel_id=1, source_target_pairs={{0,5},{1,4},{2,7},{3,6},{4,1},{5,0},{6,3},{7,2},{8,13},{9,12},{10,... | collective-permute-start | bytes 122888 | tf_op jit(solution)/shard_map/ppermute | solution.py:41
  37.5 5.3 %collective-permute-start.14 = (bf16[320,128]{1,0:T(8,128)(2,1)S(1)}, bf16[320,128]{1,0:T(8,128)(2,1)S(1)}, u32[]{:S(2)}, u32[]{:S(2)}) collective-permute-start(bf16[320,128]{1,0:T(8,128)(2,1)S(1)} %bitcast.32), channel_id=1, source_target_pairs={{0,3},{1,2},{2,1},{3,0},{4,7},{5,6},{6,5},{7,4},{8,11},{9,10},{10,... | collective-permute-start | bytes 245768 | tf_op jit(solution)/shard_map/ppermute | solution.py:41
  42.8 1.5 %collective-permute-start.15 = (bf16[640,128]{1,0:T(8,128)(2,1)S(1)}, bf16[640,128]{1,0:T(8,128)(2,1)S(1)}, u32[]{:S(2)}, u32[]{:S(2)}) collective-permute-start(bf16[640,128]{1,0:T(8,128)(2,1)S(1)} %bitcast.25), channel_id=1, source_target_pairs={{0,1},{1,0},{2,3},{3,2},{4,5},{5,4},{6,7},{7,6},{8,9},{9,8},{10,11... | collective-permute-start | bytes 491528 | tf_op jit(solution)/shard_map/ppermute | solution.py:41

commit v5 on v4

--- a/solution.py
+++ b/solution.py
@@ -36,9 +36,10 @@
     return lax.axis_index("rows") * lax.axis_size("cols") + lax.axis_index("cols")
 
 
-def swap(value, bit):
+def swap(value, bit, other=None):
     total = lax.axis_size("rows") * lax.axis_size("cols")
-    return lax.ppermute(value, ("rows", "cols"), [(i, i ^ (1 << bit | 1)) for i in range(total)])
+    flip = lambda i: 1 << (other if other is not None and i.bit_count() % 2 else bit) | 1
+    return lax.ppermute(value, ("rows", "cols"), [(i, i ^ flip(i)) for i in range(total)])
 
 
 def local(body, out_shape, name, *operands, **kwargs):
@@ -52,10 +53,13 @@
     )(*operands)
 
 
-def side_of(bit):
+def side_of(bit, other=None):
     index = device_index()
     if bit > 0:
-        return lax.rem(index // (1 << bit), 2)
+        side = lax.rem(index // (1 << bit), 2)
+        if other is None:
+            return side
+        return jnp.where(side_of(0) == 0, side, lax.rem(index // (1 << other), 2))
     bits = (lax.axis_size("rows") * lax.axis_size("cols")).bit_length() - 1
     return lax.rem(sum(lax.rem(index // (1 << k), 2) for k in range(bits)), 2)
 
@@ -68,11 +72,11 @@
 chained = pl.CostEstimate(flops=8_000_000_000, bytes_accessed=100_000, transcendentals=0)
 
 
-def halve(keep, got, bit):
+def halve(keep, got, bit, other=None):
     half = keep.shape[0] // 2
 
     def body(keep_ref, got_ref, send_ref, stay_ref):
-        side = side_of(bit)
+        side = side_of(bit, other)
         away, here = rows_at(1 - side, half), rows_at(side, half)
         send_ref[...] = (keep_ref[away, :] + got_ref[away, :].astype(f32)).astype(bf16)
         stay_ref[...] = keep_ref[here, :] + got_ref[here, :].astype(f32)
@@ -95,14 +99,32 @@
     return local(body, jax.ShapeDtypeStruct(got.shape, bf16), "add", keep, got, cost_estimate=chained)
 
 
-def join(mine, other, bit, **kwargs):
-    def body(mine_ref, other_ref, both_ref):
-        side = side_of(bit)
+def join(mine, got, bit, other=None, **kwargs):
+    def body(mine_ref, got_ref, both_ref):
+        side = side_of(bit, other)
         both_ref[:, pl.ds(side, 1)] = mine_ref[...][:, None]
-        both_ref[:, pl.ds(1 - side, 1)] = other_ref[...][:, None]
+        both_ref[:, pl.ds(1 - side, 1)] = got_ref[...][:, None]
 
     shape = (mine.shape[0], 2, *mine.shape[1:])
-    return local(body, jax.ShapeDtypeStruct(shape, mine.dtype), "join", mine, other, **kwargs)
+    return local(body, jax.ShapeDtypeStruct(shape, mine.dtype), "join", mine, got, **kwargs)
+
+
+def join_second(mine, got, bit, other, **kwargs):
+    def body(mine_ref, got_ref, both_ref):
+        parity, side = side_of(0), side_of(bit, other)
+
+        @pl.when(parity == 0)
+        def _():
+            both_ref[:, pl.ds(side, 1)] = mine_ref[...][:, None]
+            both_ref[:, pl.ds(1 - side, 1)] = got_ref[...][:, None]
+
+        @pl.when(parity == 1)
+        def _():
+            both_ref[:, :, pl.ds(side, 1)] = mine_ref[...][:, :, None]
+            both_ref[:, :, pl.ds(1 - side, 1)] = got_ref[...][:, :, None]
+
+    shape = (mine.shape[0], 2, *mine.shape[1:])
+    return local(body, jax.ShapeDtypeStruct(shape, mine.dtype), "join_second", mine, got, **kwargs)
 
 
 def join_cores(mine, other, **kwargs):
@@ -119,7 +141,7 @@
 
 class Gather:
     def __init__(self, rows):
-        self.rows, self.got, self.done = rows, None, []
+        self.rows, self.got, self.last = rows, None, None
 
     def settle(self, after):
         if self.got is None:
@@ -127,40 +149,40 @@
             return
         share = self.rows.shape[-2:]
         got, _ = lax.optimization_barrier((self.got, after))
-        bit = self.done[-1]
-        if bit > 0:
-            lead = 1 << sum(other > bit for other in self.done)
-            mine, got = (part.reshape(lead, -1, *share) for part in (self.rows, got))
-            both = join(mine, got, bit, cost_estimate=waiting)
+        bit, other = self.last
+        if bit == 0:
+            both = join_cores(self.rows, got, cost_estimate=waiting)
+        elif other is None or bit < other:
+            mine, got = (part.reshape(-1, 1, *share) for part in (self.rows, got))
+            both = join(mine, got, bit, other, cost_estimate=waiting)
         else:
-            both = join_cores(self.rows, got, cost_estimate=waiting)
+            mine, got = (part.reshape(-1, 2, *share) for part in (self.rows, got))
+            both = join_second(mine, got, bit, other, cost_estimate=waiting)
         self.rows, self.got = both.reshape(-1, *share), None
 
-    def step(self, bit, after):
+    def step(self, after, bit, other=None):
         self.settle(after)
-        self.got = swap(self.rows, bit)
-        self.done.append(bit)
+        self.got, self.last = swap(self.rows, bit, other), (bit, other)
 
 
 def sum_all(send, keep, beside):
     bits = (lax.axis_size("rows") * lax.axis_size("cols")).bit_length() - 1
-    halving = list(range(1, min(3, bits)))
-
-    def step(value, bit, name):
-        got = swap(value, bit)
-        return beside(name, value, got)
-
-    got = step(send, 0, "cores")
-    for bit in halving:
-        send, keep = halve(keep, got, bit)
-        got = step(send, bit, f"halve {bit}")
+    halving = [(1, 2), (2, 1)]
+    adding = []
+    for bit in range(3, bits, 2):
+        adding += [(bit, bit + 1), (bit + 1, bit)] if bit + 1 < bits else [(bit, None)]
+
+    got = beside("cores", send, swap(send, 0))
+    for n, pair in enumerate(halving):
+        send, keep = halve(keep, got, *pair)
+        got = beside(f"halve {n}", send, swap(send, *pair))
     mine = add(keep, got)
-    for bit in range(len(halving) + 1, bits):
-        mine = add(mine, step(mine, bit, f"add {bit}"))
-    for bit in reversed(halving):
-        got = step(mine, bit, f"join {bit}")
-        mine = join(mine[None], got[None], bit, cost_estimate=chained).reshape(-1, mine.shape[1])
-    return mine, step(mine, 0, "halves")
+    for n, pair in enumerate(adding):
+        mine = add(mine, beside(f"add {n}", mine, swap(mine, *pair)))
+    for n, pair in enumerate(reversed(halving)):
+        got = beside(f"join {n}", mine, swap(mine, *pair))
+        mine = join(mine[None], got[None], *pair, cost_estimate=chained).reshape(-1, mine.shape[1])
+    return mine, beside("halves", mine, swap(mine, 0))
 
 
 def gelu_pair(value):
@@ -600,7 +622,13 @@
         name="outer_rows",
     )(even, odd, kernel, in_gram, part)
 
-    exchanges = {"cores": far[:1], "halve 1": far[1:], "halve 2": [1], "add 3": [2], "add 4": [0]}
+    exchanges = {
+        "cores": [(bit,) for bit in far[:1]],
+        "halve 0": [(bit,) for bit in far[1:]],
+        "halve 1": [(1, 2)],
+        "add 0": [(2, 1)],
+        "add 1": [(0,)],
+    }
     prepared, far_pixels = [], []
 
     def beside(name, sent, got):
@@ -624,8 +652,8 @@
             )
             return lax.optimization_barrier((got, *far_pixels))[0]
         for bit in exchanges.get(name, []):
-            gather.step(bit, sent)
-        if name != "join 2":
+            gather.step(sent, *bit)
+        if name != "join 0":
             return got
         gather.settle(sent)
         prepared.extend(

time: 48.9 us -> 46.8 us (0.957)
  waiting for transfers between devices: 15.2 us -> 12.7 us
    ppermute x13, waiting for transfers between devices: 13.2 us -> 10.7 us  [swap(): lax.ppermute(value, ('rows', 'cols'), [(i, i ^ flip(i)) for i in range(to...]
  transfers between devices with their start and end apart: 16 -> 16, of which waited for: 14 -> 14; matrix products, arithmetic and copies ran while one was open for 0% -> 0% of each run, Pallas kernels for 11% -> 12%
where the time goes in v5:
time: 46.8 us; the launch traced here: 46.6 us
  starting transfers between devices  21.1 us (45%)
  waiting for transfers between devices  12.7 us (27%)
  Pallas kernels  11 us (24%)
  local copies, waits for them, and re-layouts  1.05 us (2%)
  between operations  0.76 us (2%)
    ppermute x13, starting transfers between devices, swap(): lax.ppermute(value, ('rows', 'cols'), [(i, i ^ flip(i)) for i in range(to...  13.2 us
    ppermute x13, waiting for transfers between devices, swap(): lax.ppermute(value, ('rows', 'cols'), [(i, i ^ flip(i)) for i in range(to...  10.7 us
    ppermute x2, starting transfers between devices, swap_rows(): lax.ppermute(value, 'rows', pairs + [(target, source) for source, target...  7.42 us
    pallas_call x1, Pallas kernels, on_device(): pl.pallas_call(functools.partial(backward_kernel, shape, pixel_total), ou...  4.46 us
    pallas_call x1, Pallas kernels, on_device(): pl.pallas_call(functools.partial(inner_kernel, shape), out_shape=(jax.Sha...  3.36 us
    ppermute x2, waiting for transfers between devices, swap_rows(): lax.ppermute(value, 'rows', pairs + [(target, source) for source, target...  1.15 us
    unnamed x10, local copies, waits for them, and re-layouts  1.05 us
    pallas_call x1, Pallas kernels, beside(): pl.pallas_call(functools.partial(beyond_kernel, shape), out_shape=(jax.Sh...  1.04 us
  transfers between devices with their start and end apart: 16, of which 14 were waited for; matrix products, arithmetic and copies ran while one was open for 0% of the time, Pallas kernels for 12%

profile of v5, /device:TPU:0, one launch (start us, length us, event | category | flops | bytes accessed | tf_op | source)
XLA Modules:
  0.0 46.6 jit_solution(1412130729965681153)
XLA Ops:
  0.6 1.0 %copy-done.1 = bf16[8,128,256]{2,1,0:T(8,128)(2,1)S(1)} copy-done((bf16[8,128,256]{2,1,0:T(8,128)(2,1)S(1)}, bf16[8,128,256]{2,1,0:T(8,128)(2,1)}, u32[]{:S(2)}) %copy-start.1) | copy-done | bytes 524312
  1.7 0.5 %collective-permute-start = (bf16[2,8,256]{2,1,0:T(8,128)(2,1)S(1)}, bf16[2,8,256]{2,1,0:T(8,128)(2,1)S(1)}, u32[]{:S(2)}, u32[]{:S(2)}) collective-permute-start(bf16[2,8,256]{2,1,0:T(8,128)(2,1)S(1)} %column_rims.1), channel_id=1, source_target_pairs={{0,1},{1,0},{2,3},{3,2},{4,5},{5,4},{6,7},{7,6},{8,9},{9,8},{10,11... | collective-permute-start | bytes 24584 | tf_op jit(solution)/shard_map/ppermute | solution.py:565
  2.2 0.8 %collective-permute-done.refs_0_ = bf16[2,8,256]{2,1,0:T(8,128)(2,1)S(1)} collective-permute-done((bf16[2,8,256]{2,1,0:T(8,128)(2,1)S(1)}, bf16[2,8,256]{2,1,0:T(8,128)(2,1)S(1)}, u32[]{:S(2)}, u32[]{:S(2)}) %collective-permute-start) | collective-permute-done | bytes 8224 | tf_op jit(solution)/shard_map/ppermute | solution.py:565
  3.1 2.9 %collective-permute-start.1 = (bf16[272,256]{1,0:T(8,128)(2,1)S(1)}, bf16[272,256]{1,0:T(8,128)(2,1)S(1)}, u32[]{:S(2)}, u32[]{:S(2)}) collective-permute-start(bf16[272,256]{1,0:T(8,128)(2,1)S(1)} %get-tuple-element.35), channel_id=1, source_target_pairs={{0,2},{4,6},{8,10},{12,14},{16,18},{20,22},{24,26},{28,30},{2,0},{... | collective-permute-start | bytes 417800 | tf_op jit(solution)/shard_map/ppermute | solution.py:25
  6.0 4.5 %collective-permute-start.2 = (bf16[272,256]{1,0:T(8,128)(2,1)S(1)}, bf16[272,256]{1,0:T(8,128)(2,1)S(1)}, u32[]{:S(2)}, u32[]{:S(2)}) collective-permute-start(bf16[272,256]{1,0:T(8,128)(2,1)S(1)} %get-tuple-element.36), channel_id=1, source_target_pairs={{2,4},{6,8},{10,12},{14,16},{18,20},{22,24},{26,28},{30,0},{4,2},{... | collective-permute-start | bytes 417800 | tf_op jit(solution)/shard_map/ppermute | solution.py:25
  10.5 3.4 %inner_rows.1 = (bf16[768,512]{1,0:T(8,128)(2,1)S(1)}, bf16[768,512]{1,0:T(8,128)(2,1)S(1)}, f32[1280,128]{1,0:T(8,128)S(1)}, f32[1,512]{1,0:T(1,128)S(1)}, f32[512,512]{1,0:T(8,128)S(1)}) custom-call(bf16[8,128,256]{2,1,0:T(8,128)(2,1)S(1)} %copy-done.2, bf16[2,8,256]{2,1,0:T(8,128)(2,1)S(1)} %get-tuple-element.37.left_ref, ...), custom_call_target="tpu_custom_call" | custom-call | flops 2214592512 | bytes 6000000 | tf_op jit(solution)/shard_map/inner_rows/pallas_call | solution.py:585
  13.9 1.1 %collective-permute-done.2.odd_ref = bf16[272,256]{1,0:T(8,128)(2,1)S(1)} collective-permute-done((bf16[272,256]{1,0:T(8,128)(2,1)S(1)}, bf16[272,256]{1,0:T(8,128)(2,1)S(1)}, u32[]{:S(2)}, u32[]{:S(2)}) %collective-permute-start.2) | collective-permute-done | bytes 139296 | tf_op jit(solution)/shard_map/ppermute | solution.py:25
  15.1 0.9 %outer_rows.1 = (bf16[256,512]{1,0:T(8,128)(2,1)S(1)}, bf16[256,512]{1,0:T(8,128)(2,1)S(1)}, bf16[640,128]{1,0:T(8,128)(2,1)S(1)}, f32[640,128]{1,0:T(8,128)S(1)}) custom-call(bf16[272,256]{1,0:T(8,128)(2,1)S(1)} %collective-permute-done.1.even_ref, bf16[272,256]{1,0:T(8,128)(2,1)S(1)} %collective-permute-done.2.odd_ref, bf16[2304,512]{1,0:T(8,128)(2,1)S(1)} %bitcast.22, ...), custom_call_target="tpu_custom_call" | custom-call | tf_op jit(solution)/shard_map/outer_rows/pallas_call | solution.py:607
  16.0 1.0 %collective-permute-start.9 = (bf16[1,16,512]{2,1,0:T(8,128)(2,1)S(1)}, bf16[1,16,512]{2,1,0:T(8,128)(2,1)S(1)}, u32[]{:S(2)}, u32[]{:S(2)}) collective-permute-start(bf16[1,16,512]{2,1,0:T(8,128)(2,1)S(1)} %get-tuple-element.48), channel_id=1, source_target_pairs={{0,17},{1,16},{2,19},{3,18},{4,21},{5,20},{6,23},{7,22},{8,25},{9,... | collective-permute-start | bytes 49160 | tf_op jit(solution)/shard_map/ppermute | solution.py:42
  17.4 1.7 %collective-permute-start.4 = (bf16[320,128]{1,0:T(8,128)(2,1)S(1)}, bf16[320,128]{1,0:T(8,128)(2,1)S(1)}, u32[]{:S(2)}, u32[]{:S(2)}) collective-permute-start(bf16[320,128]{1,0:T(8,128)(2,1)S(1)} %get-tuple-element.44), channel_id=1, source_target_pairs={{0,3},{1,4},{2,7},{3,0},{4,1},{5,6},{6,5},{7,2},{8,13},{9,10},{10,... | collective-permute-start | bytes 245768 | tf_op jit(solution)/shard_map/ppermute | solution.py:42
  19.1 1.2 %collective-permute-done.9 = bf16[1,16,512]{2,1,0:T(8,128)(2,1)S(1)} collective-permute-done((bf16[1,16,512]{2,1,0:T(8,128)(2,1)S(1)}, bf16[1,16,512]{2,1,0:T(8,128)(2,1)S(1)}, u32[]{:S(2)}, u32[]{:S(2)}) %collective-permute-start.9) | collective-permute-done | bytes 16416 | tf_op jit(solution)/shard_map/ppermute | solution.py:42
  20.3 0.5 %collective-permute-start.10 = (bf16[2,16,512]{2,1,0:T(8,128)(2,1)S(1)}, bf16[2,16,512]{2,1,0:T(8,128)(2,1)S(1)}, u32[]{:S(2)}, u32[]{:S(2)}) collective-permute-start(bf16[2,16,512]{2,1,0:T(8,128)(2,1)S(1)} %bitcast.40), channel_id=1, source_target_pairs={{0,9},{1,8},{2,11},{3,10},{4,13},{5,12},{6,15},{7,14},{8,1},{9,0},... | collective-permute-start | bytes 98312 | tf_op jit(solution)/shard_map/ppermute | solution.py:42
  20.8 0.6 %collective-permute-done.4.got_ref = bf16[320,128]{1,0:T(8,128)(2,1)S(1)} collective-permute-done((bf16[320,128]{1,0:T(8,128)(2,1)S(1)}, bf16[320,128]{1,0:T(8,128)(2,1)S(1)}, u32[]{:S(2)}, u32[]{:S(2)}) %collective-permute-start.4) | collective-permute-done | bytes 81952 | tf_op jit(solution)/shard_map/ppermute | solution.py:42
  21.4 0.8 %collective-permute-start.5 = (bf16[160,128]{1,0:T(8,128)(2,1)S(1)}, bf16[160,128]{1,0:T(8,128)(2,1)S(1)}, u32[]{:S(2)}, u32[]{:S(2)}) collective-permute-start(bf16[160,128]{1,0:T(8,128)(2,1)S(1)} %get-tuple-element.46), channel_id=1, source_target_pairs={{0,5},{1,2},{2,1},{3,6},{4,7},{5,0},{6,3},{7,4},{8,11},{9,12},{10,... | collective-permute-start | bytes 122888 | tf_op jit(solution)/shard_map/ppermute | solution.py:42
  22.2 1.4 %collective-permute-done.10 = bf16[2,16,512]{2,1,0:T(8,128)(2,1)S(1)} collective-permute-done((bf16[2,16,512]{2,1,0:T(8,128)(2,1)S(1)}, bf16[2,16,512]{2,1,0:T(8,128)(2,1)S(1)}, u32[]{:S(2)}, u32[]{:S(2)}) %collective-permute-start.10) | collective-permute-done | bytes 32800 | tf_op jit(solution)/shard_map/ppermute | solution.py:42
  23.6 0.6 %collective-permute-start.11 = (bf16[4,16,512]{2,1,0:T(8,128)(2,1)S(1)}, bf16[4,16,512]{2,1,0:T(8,128)(2,1)S(1)}, u32[]{:S(2)}, u32[]{:S(2)}) collective-permute-start(bf16[4,16,512]{2,1,0:T(8,128)(2,1)S(1)} %bitcast.35), channel_id=1, source_target_pairs={{0,3},{1,4},{2,7},{3,0},{4,1},{5,6},{6,5},{7,2},{8,13},{9,10},{10,... | collective-permute-start | bytes 196616 | tf_op jit(solution)/shard_map/ppermute | solution.py:42
  24.3 0.6 %collective-permute-done.5.got_ref = bf16[160,128]{1,0:T(8,128)(2,1)S(1)} collective-permute-done((bf16[160,128]{1,0:T(8,128)(2,1)S(1)}, bf16[160,128]{1,0:T(8,128)(2,1)S(1)}, u32[]{:S(2)}, u32[]{:S(2)}) %collective-permute-start.5) | collective-permute-done | bytes 40992 | tf_op jit(solution)/shard_map/ppermute | solution.py:42
  24.9 1.6 %collective-permute-start.6 = (bf16[160,128]{1,0:T(8,128)(2,1)S(1)}, bf16[160,128]{1,0:T(8,128)(2,1)S(1)}, u32[]{:S(2)}, u32[]{:S(2)}) collective-permute-start(bf16[160,128]{1,0:T(8,128)(2,1)S(1)} %add.3.keep_ref), channel_id=1, source_target_pairs={{0,9},{1,16},{2,19},{3,10},{4,21},{5,12},{6,15},{7,22},{8,25},{9,0... | collective-permute-start | bytes 122888 | tf_op jit(solution)/shard_map/ppermute | solution.py:42
  26.5 0.9 %collective-permute-done.11 = bf16[4,16,512]{2,1,0:T(8,128)(2,1)S(1)} collective-permute-done((bf16[4,16,512]{2,1,0:T(8,128)(2,1)S(1)}, bf16[4,16,512]{2,1,0:T(8,128)(2,1)S(1)}, u32[]{:S(2)}, u32[]{:S(2)}) %collective-permute-start.11) | collective-permute-done | bytes 65568 | tf_op jit(solution)/shard_map/ppermute | solution.py:42
  27.7 0.7 %collective-permute-done.6.got_ref = bf16[160,128]{1,0:T(8,128)(2,1)S(1)} collective-permute-done((bf16[160,128]{1,0:T(8,128)(2,1)S(1)}, bf16[160,128]{1,0:T(8,128)(2,1)S(1)}, u32[]{:S(2)}, u32[]{:S(2)}) %collective-permute-start.6) | collective-permute-done | bytes 40992 | tf_op jit(solution)/shard_map/ppermute | solution.py:42
  28.4 2.2 %collective-permute-start.7 = (bf16[160,128]{1,0:T(8,128)(2,1)S(1)}, bf16[160,128]{1,0:T(8,128)(2,1)S(1)}, u32[]{:S(2)}, u32[]{:S(2)}) collective-permute-start(bf16[160,128]{1,0:T(8,128)(2,1)S(1)} %add.4.keep_ref), channel_id=1, source_target_pairs={{0,17},{1,8},{2,11},{3,18},{4,13},{5,20},{6,23},{7,14},{8,1},{9,24... | collective-permute-start | bytes 122888 | tf_op jit(solution)/shard_map/ppermute | solution.py:42
  30.6 1.2 %collective-permute-done.12 = bf16[8,16,512]{2,1,0:T(8,128)(2,1)S(1)} collective-permute-done((bf16[8,16,512]{2,1,0:T(8,128)(2,1)S(1)}, bf16[8,16,512]{2,1,0:T(8,128)(2,1)S(1)}, u32[]{:S(2)}, u32[]{:S(2)}) %collective-permute-start.12) | collective-permute-done | bytes 131104 | tf_op jit(solution)/shard_map/ppermute | solution.py:42
  31.9 0.7 %collective-permute-start.13 = (bf16[16,16,512]{2,1,0:T(8,128)(2,1)S(1)}, bf16[16,16,512]{2,1,0:T(8,128)(2,1)S(1)}, u32[]{:S(2)}, u32[]{:S(2)}) collective-permute-start(bf16[16,16,512]{2,1,0:T(8,128)(2,1)S(1)} %bitcast.27), channel_id=1, source_target_pairs={{0,1},{1,0},{2,3},{3,2},{4,5},{5,4},{6,7},{7,6},{8,9},{9,8},{10,11... | collective-permute-start | bytes 786440 | tf_op jit(solution)/shard_map/ppermute | solution.py:42
  32.8 1.0 %collective-permute-start.8 = (bf16[160,128]{1,0:T(8,128)(2,1)S(1)}, bf16[160,128]{1,0:T(8,128)(2,1)S(1)}, u32[]{:S(2)}, u32[]{:S(2)}) collective-permute-start(bf16[160,128]{1,0:T(8,128)(2,1)S(1)} %add.5), channel_id=1, source_target_pairs={{0,5},{1,2},{2,1},{3,6},{4,7},{5,0},{6,3},{7,4},{8,11},{9,12},{10,... | collective-permute-start | bytes 122888 | tf_op jit(solution)/shard_map/ppermute | solution.py:42
  33.9 1.0 %prepare.1 = (bf16[4608,256]{1,0:T(8,128)(2,1)S(1)}, f32[512,512]{1,0:T(8,128)S(1)}) custom-call(bf16[2304,512]{1,0:T(8,128)(2,1)S(1)} %bitcast.23, bf16[512,512]{1,0:T(8,128)(2,1)S(1)} %bitcast.45), custom_call_target="tpu_custom_call" | custom-call | flops 2000000000 | bytes 6000000 | tf_op jit(solution)/shard_map/prepare/pallas_call | solution.py:660
  34.9 1.4 %collective-permute-done.8 = bf16[160,128]{1,0:T(8,128)(2,1)S(1)} collective-permute-done((bf16[160,128]{1,0:T(8,128)(2,1)S(1)}, bf16[160,128]{1,0:T(8,128)(2,1)S(1)}, u32[]{:S(2)}, u32[]{:S(2)}) %collective-permute-start.8) | collective-permute-done | bytes 40992 | tf_op jit(solution)/shard_map/ppermute | solution.py:42
  36.3 2.1 %collective-permute-start.14 = (bf16[320,128]{1,0:T(8,128)(2,1)S(1)}, bf16[320,128]{1,0:T(8,128)(2,1)S(1)}, u32[]{:S(2)}, u32[]{:S(2)}) collective-permute-start(bf16[320,128]{1,0:T(8,128)(2,1)S(1)} %bitcast.32), channel_id=1, source_target_pairs={{0,3},{1,4},{2,7},{3,0},{4,1},{5,6},{6,5},{7,2},{8,13},{9,10},{10,... | collective-permute-start | bytes 245768 | tf_op jit(solution)/shard_map/ppermute | solution.py:42
  38.5 1.0 %beyond.1 = (bf16[288,512]{1,0:T(8,128)(2,1)S(1)}, bf16[288,512]{1,0:T(8,128)(2,1)S(1)}) custom-call(bf16[8,128,256]{2,1,0:T(8,128)(2,1)S(1)} %copy-done.2, bf16[272,256]{1,0:T(8,128)(2,1)S(1)} %collective-permute-done.1.even_ref, bf16[272,256]{1,0:T(8,128)(2,1)S(1)} %collective-permute-done.2.odd_ref, bf16[2,8,256]{2,1,0:T(8,128)(2,1)S(1)} %get-tuple-element.37.left_ref, ...), custom_call_target="tpu_custom_call" | custom-call | flops 8000000000 | bytes 100000 | tf_op jit(solution)/shard_map/beyond/pallas_call | solution.py:639
  39.5 1.1 %collective-permute-done.14 = bf16[320,128]{1,0:T(8,128)(2,1)S(1)} collective-permute-done((bf16[320,128]{1,0:T(8,128)(2,1)S(1)}, bf16[320,128]{1,0:T(8,128)(2,1)S(1)}, u32[]{:S(2)}, u32[]{:S(2)}) %collective-permute-start.14) | collective-permute-done | bytes 81952 | tf_op jit(solution)/shard_map/ppermute | solution.py:42
  40.6 0.5 %collective-permute-start.15 = (bf16[640,128]{1,0:T(8,128)(2,1)S(1)}, bf16[640,128]{1,0:T(8,128)(2,1)S(1)}, u32[]{:S(2)}, u32[]{:S(2)}) collective-permute-start(bf16[640,128]{1,0:T(8,128)(2,1)S(1)} %bitcast.25), channel_id=1, source_target_pairs={{0,1},{1,0},{2,3},{3,2},{4,5},{5,4},{6,7},{7,6},{8,9},{9,8},{10,11... | collective-permute-start | bytes 491528 | tf_op jit(solution)/shard_map/ppermute | solution.py:42
  41.1 1.0 %collective-permute-done.15.other_ref = bf16[640,128]{1,0:T(8,128)(2,1)S(1)} collective-permute-done((bf16[640,128]{1,0:T(8,128)(2,1)S(1)}, bf16[640,128]{1,0:T(8,128)(2,1)S(1)}, u32[]{:S(2)}, u32[]{:S(2)}) %collective-permute-start.15) | collective-permute-done | bytes 163872 | tf_op jit(solution)/shard_map/ppermute | solution.py:42
  42.2 4.5 %grad_conv.1 = (f32[16,512]{1,0:T(8,128)}, bf16[1024,256]{1,0:T(8,128)(2,1)}) custom-call(bf16[640,128]{1,0:T(8,128)(2,1)S(1)} %bitcast.26, bf16[640,128]{1,0:T(8,128)(2,1)S(1)} %collective-permute-done.15.other_ref, f32[512,512]{1,0:T(8,128)S(1)} %get-tuple-element.55.both_ref, bf16[768,512]{1,0:T(8,128)(2,1)S(1)} %get-tuple-element.62.in_feat_ref, ...), custom_call_target="tpu_custom_call" | custom-call | tf_op jit(solution)/shard_map/grad_conv/pallas_call | solution.py:679
  (29 shorter events, 1.3 us)
Async XLA Ops:
  0.6 1.0 %copy-start.1 = (bf16[8,128,256]{2,1,0:T(8,128)(2,1)S(1)}, bf16[8,128,256]{2,1,0:T(8,128)(2,1)}, u32[]{:S(2)}) copy-start(bf16[8,128,256]{2,1,0:T(8,128)(2,1)} %own_ref.3) | copy-start | bytes 1572868
  1.7 1.4 %copy-start.3 = (f32[16,512]{1,0:T(8,128)S(1)}, f32[16,512]{1,0:T(8,128)}, u32[]{:S(2)}) copy-start(f32[16,512]{1,0:T(8,128)} %target_ref.1) | copy-start | bytes 98308
  1.7 8.9 %copy-start = (bf16[3,3,256,512]{3,2,1,0:T(8,128)(2,1)S(1)}, bf16[3,3,256,512]{3,2,1,0:T(8,128)(2,1)}, u32[]{:S(2)}) copy-start(bf16[3,3,256,512]{3,2,1,0:T(8,128)(2,1)} %param.5) | copy-start | bytes 7077892
  1.7 8.9 %copy-start.2 = (bf16[8,128,256]{2,1,0:T(8,128)(2,1)S(1)}, bf16[8,128,256]{2,1,0:T(8,128)(2,1)}, u32[]{:S(2)}) copy-start(bf16[8,128,256]{2,1,0:T(8,128)(2,1)} %own_ref.3) | copy-start | bytes 1572868
  1.7 8.9 %copy-start.4 = (bf16[512]{0:T(512)(128)(2,1)S(1)}, bf16[512]{0:T(512)(128)(2,1)}, u32[]{:S(2)}) copy-start(bf16[512]{0:T(512)(128)(2,1)} %bias_ref.1) | copy-start | bytes 3076
  1.7 1.3 %collective-permute-start = (bf16[2,8,256]{2,1,0:T(8,128)(2,1)S(1)}, bf16[2,8,256]{2,1,0:T(8,128)(2,1)S(1)}, u32[]{:S(2)}, u32[]{:S(2)}) collective-permute-start(bf16[2,8,256]{2,1,0:T(8,128)(2,1)S(1)} %column_rims.1), channel_id=1, source_target_pairs={{0,1},{1,0},{2,3},{3,2},{4,5},{5,4},{6,7},{7,6},{8,9},{9,8},{10,11... | collective-permute-start | bytes 24584 | tf_op jit(solution)/shard_map/ppermute | solution.py:565
  3.1 10.8 %collective-permute-start.1 = (bf16[272,256]{1,0:T(8,128)(2,1)S(1)}, bf16[272,256]{1,0:T(8,128)(2,1)S(1)}, u32[]{:S(2)}, u32[]{:S(2)}) collective-permute-start(bf16[272,256]{1,0:T(8,128)(2,1)S(1)} %get-tuple-element.35), channel_id=1, source_target_pairs={{0,2},{4,6},{8,10},{12,14},{16,18},{20,22},{24,26},{28,30},{2,0},{... | collective-permute-start | bytes 417800 | tf_op jit(solution)/shard_map/ppermute | solution.py:25
  6.0 9.1 %collective-permute-start.2 = (bf16[272,256]{1,0:T(8,128)(2,1)S(1)}, bf16[272,256]{1,0:T(8,128)(2,1)S(1)}, u32[]{:S(2)}, u32[]{:S(2)}) collective-permute-start(bf16[272,256]{1,0:T(8,128)(2,1)S(1)} %get-tuple-element.36), channel_id=1, source_target_pairs={{2,4},{6,8},{10,12},{14,16},{18,20},{22,24},{26,28},{30,0},{4,2},{... | collective-permute-start | bytes 417800 | tf_op jit(solution)/shard_map/ppermute | solution.py:25
  16.0 1.5 %collective-permute-start.3 = (bf16[640,128]{1,0:T(8,128)(2,1)S(1)}, bf16[640,128]{1,0:T(8,128)(2,1)S(1)}, u32[]{:S(2)}, u32[]{:S(2)}) collective-permute-start(bf16[640,128]{1,0:T(8,128)(2,1)S(1)} %get-tuple-element.42), channel_id=1, source_target_pairs={{0,1},{1,0},{2,3},{3,2},{4,5},{5,4},{6,7},{7,6},{8,9},{9,8},{10,11... | collective-permute-start | bytes 491528 | tf_op jit(solution)/shard_map/ppermute | solution.py:42
  16.0 4.2 %collective-permute-start.9 = (bf16[1,16,512]{2,1,0:T(8,128)(2,1)S(1)}, bf16[1,16,512]{2,1,0:T(8,128)(2,1)S(1)}, u32[]{:S(2)}, u32[]{:S(2)}) collective-permute-start(bf16[1,16,512]{2,1,0:T(8,128)(2,1)S(1)} %get-tuple-element.48), channel_id=1, source_target_pairs={{0,17},{1,16},{2,19},{3,18},{4,21},{5,20},{6,23},{7,22},{8,25},{9,... | collective-permute-start | bytes 49160 | tf_op jit(solution)/shard_map/ppermute | solution.py:42
  17.4 3.9 %collective-permute-start.4 = (bf16[320,128]{1,0:T(8,128)(2,1)S(1)}, bf16[320,128]{1,0:T(8,128)(2,1)S(1)}, u32[]{:S(2)}, u32[]{:S(2)}) collective-permute-start(bf16[320,128]{1,0:T(8,128)(2,1)S(1)} %get-tuple-element.44), channel_id=1, source_target_pairs={{0,3},{1,4},{2,7},{3,0},{4,1},{5,6},{6,5},{7,2},{8,13},{9,10},{10,... | collective-permute-start | bytes 245768 | tf_op jit(solution)/shard_map/ppermute | solution.py:42
  20.3 3.3 %collective-permute-start.10 = (bf16[2,16,512]{2,1,0:T(8,128)(2,1)S(1)}, bf16[2,16,512]{2,1,0:T(8,128)(2,1)S(1)}, u32[]{:S(2)}, u32[]{:S(2)}) collective-permute-start(bf16[2,16,512]{2,1,0:T(8,128)(2,1)S(1)} %bitcast.40), channel_id=1, source_target_pairs={{0,9},{1,8},{2,11},{3,10},{4,13},{5,12},{6,15},{7,14},{8,1},{9,0},... | collective-permute-start | bytes 98312 | tf_op jit(solution)/shard_map/ppermute | solution.py:42
  21.4 3.5 %collective-permute-start.5 = (bf16[160,128]{1,0:T(8,128)(2,1)S(1)}, bf16[160,128]{1,0:T(8,128)(2,1)S(1)}, u32[]{:S(2)}, u32[]{:S(2)}) collective-permute-start(bf16[160,128]{1,0:T(8,128)(2,1)S(1)} %get-tuple-element.46), channel_id=1, source_target_pairs={{0,5},{1,2},{2,1},{3,6},{4,7},{5,0},{6,3},{7,4},{8,11},{9,12},{10,... | collective-permute-start | bytes 122888 | tf_op jit(solution)/shard_map/ppermute | solution.py:42
  23.6 3.8 %collective-permute-start.11 = (bf16[4,16,512]{2,1,0:T(8,128)(2,1)S(1)}, bf16[4,16,512]{2,1,0:T(8,128)(2,1)S(1)}, u32[]{:S(2)}, u32[]{:S(2)}) collective-permute-start(bf16[4,16,512]{2,1,0:T(8,128)(2,1)S(1)} %bitcast.35), channel_id=1, source_target_pairs={{0,3},{1,4},{2,7},{3,0},{4,1},{5,6},{6,5},{7,2},{8,13},{9,10},{10,... | collective-permute-start | bytes 196616 | tf_op jit(solution)/shard_map/ppermute | solution.py:42
  24.9 3.5 %collective-permute-start.6 = (bf16[160,128]{1,0:T(8,128)(2,1)S(1)}, bf16[160,128]{1,0:T(8,128)(2,1)S(1)}, u32[]{:S(2)}, u32[]{:S(2)}) collective-permute-start(bf16[160,128]{1,0:T(8,128)(2,1)S(1)} %add.3.keep_ref), channel_id=1, source_target_pairs={{0,9},{1,16},{2,19},{3,10},{4,21},{5,12},{6,15},{7,22},{8,25},{9,0... | collective-permute-start | bytes 122888 | tf_op jit(solution)/shard_map/ppermute | solution.py:42
  27.4 4.5 %collective-permute-start.12 = (bf16[8,16,512]{2,1,0:T(8,128)(2,1)S(1)}, bf16[8,16,512]{2,1,0:T(8,128)(2,1)S(1)}, u32[]{:S(2)}, u32[]{:S(2)}) collective-permute-start(bf16[8,16,512]{2,1,0:T(8,128)(2,1)S(1)} %bitcast.29), channel_id=1, source_target_pairs={{0,5},{1,2},{2,1},{3,6},{4,7},{5,0},{6,3},{7,4},{8,11},{9,12},{10,... | collective-permute-start | bytes 393224 | tf_op jit(solution)/shard_map/ppermute | solution.py:42
  28.4 4.4 %collective-permute-start.7 = (bf16[160,128]{1,0:T(8,128)(2,1)S(1)}, bf16[160,128]{1,0:T(8,128)(2,1)S(1)}, u32[]{:S(2)}, u32[]{:S(2)}) collective-permute-start(bf16[160,128]{1,0:T(8,128)(2,1)S(1)} %add.4.keep_ref), channel_id=1, source_target_pairs={{0,17},{1,8},{2,11},{3,18},{4,13},{5,20},{6,23},{7,14},{8,1},{9,24... | collective-permute-start | bytes 122888 | tf_op jit(solution)/shard_map/ppermute | solution.py:42
  31.9 2.0 %collective-permute-start.13 = (bf16[16,16,512]{2,1,0:T(8,128)(2,1)S(1)}, bf16[16,16,512]{2,1,0:T(8,128)(2,1)S(1)}, u32[]{:S(2)}, u32[]{:S(2)}) collective-permute-start(bf16[16,16,512]{2,1,0:T(8,128)(2,1)S(1)} %bitcast.27), channel_id=1, source_target_pairs={{0,1},{1,0},{2,3},{3,2},{4,5},{5,4},{6,7},{7,6},{8,9},{9,8},{10,11... | collective-permute-start | bytes 786440 | tf_op jit(solution)/shard_map/ppermute | solution.py:42
  32.8 3.5 %collective-permute-start.8 = (bf16[160,128]{1,0:T(8,128)(2,1)S(1)}, bf16[160,128]{1,0:T(8,128)(2,1)S(1)}, u32[]{:S(2)}, u32[]{:S(2)}) collective-permute-start(bf16[160,128]{1,0:T(8,128)(2,1)S(1)} %add.5), channel_id=1, source_target_pairs={{0,5},{1,2},{2,1},{3,6},{4,7},{5,0},{6,3},{7,4},{8,11},{9,12},{10,... | collective-permute-start | bytes 122888 | tf_op jit(solution)/shard_map/ppermute | solution.py:42
  36.3 4.3 %collective-permute-start.14 = (bf16[320,128]{1,0:T(8,128)(2,1)S(1)}, bf16[320,128]{1,0:T(8,128)(2,1)S(1)}, u32[]{:S(2)}, u32[]{:S(2)}) collective-permute-start(bf16[320,128]{1,0:T(8,128)(2,1)S(1)} %bitcast.32), channel_id=1, source_target_pairs={{0,3},{1,4},{2,7},{3,0},{4,1},{5,6},{6,5},{7,2},{8,13},{9,10},{10,... | collective-permute-start | bytes 245768 | tf_op jit(solution)/shard_map/ppermute | solution.py:42
  40.6 1.5 %collective-permute-start.15 = (bf16[640,128]{1,0:T(8,128)(2,1)S(1)}, bf16[640,128]{1,0:T(8,128)(2,1)S(1)}, u32[]{:S(2)}, u32[]{:S(2)}) collective-permute-start(bf16[640,128]{1,0:T(8,128)(2,1)S(1)} %bitcast.25), channel_id=1, source_target_pairs={{0,1},{1,0},{2,3},{3,2},{4,5},{5,4},{6,7},{7,6},{8,9},{9,8},{10,11... | collective-permute-start | bytes 491528 | tf_op jit(solution)/shard_map/ppermute | solution.py:42

commit v6 on v5

--- a/solution.py
+++ b/solution.py
@@ -213,10 +213,10 @@
 
 
 def payload_kernel(canvas_ref, target_ref, *refs):
-    even_ref, odd_ref, left_ref, right_ref, half_ref = refs[-5:]
+    payload_refs, (left_ref, right_ref, half_ref) = refs[-7:-3], refs[-3:]
     rows, cols, width = canvas_ref.shape
     half_ref[0] = target_ref[...].astype(bf16)
-    if len(refs) == 6:
+    if len(refs) == 8:
         here = lax.axis_index("cols")
         other = refs[0][...].astype(f32)
         left_ref[...] = jnp.where(here == 0, 0.0, other).astype(bf16)
@@ -226,23 +226,17 @@
     beyond = [ref[c].astype(f32) for ref in (left_ref, right_ref) for c in range(2)]
 
     def fill(ref, r):
-        for k in range(2):
-            ref[k * cols : (k + 1) * cols, :] = canvas_ref[r + k]
-        rim = [part[r + k : r + k + 1] for k in range(2) for part in beyond]
-        rim = jnp.concatenate([*rim, jnp.zeros((8, width), f32)], axis=0)
-        ref[2 * cols :, :] = rim.astype(bf16)
+        ref[0:cols, :] = canvas_ref[r]
+        rim = jnp.concatenate([*(part[r : r + 1] for part in beyond), jnp.zeros((12, width), f32)], axis=0)
+        ref[cols:, :] = rim.astype(bf16)
 
     odd = lax.rem(lax.axis_index("rows"), 2)
-
-    @pl.when(odd == 0)
-    def _():
-        fill(even_ref, rows - 2)
-        fill(odd_ref, 0)
-
-    @pl.when(odd == 1)
-    def _():
-        fill(even_ref, 0)
-        fill(odd_ref, rows - 2)
+    for case, order in ((0, [rows - 1, 0, rows - 2, 1]), (1, [0, rows - 1, 1, rows - 2])):
+
+        @pl.when(odd == case)
+        def _():
+            for ref, r in zip(payload_refs, order):
+                fill(ref, r)
 
 
 def moved_rows(row, before, after):
@@ -342,12 +336,11 @@
     feat_ref, slope_ref, send_ref, keep_ref, low_ref, high_ref, cat_ref, gram_ref,
 ):
     tile_rows, tile_cols, in_width, out_width, step = shape
-    span, main = 3 * in_width, 2 * tile_cols
+    span = 3 * in_width
     halo_rows(even_ref, odd_ref, low_ref, high_ref)
-    for n, (source, at) in enumerate([(low_ref, tile_cols), (high_ref, 0)]):
-        rim = source[main:, :].astype(f32)
-        k = 4 * (1 - n)
-        fill_row(cat_ref, n, source[at : at + tile_cols, :], rim[k + 1 : k + 2], rim[k + 2 : k + 3])
+    for n, source in enumerate([low_ref, high_ref]):
+        rim = source[tile_cols:, :].astype(f32)
+        fill_row(cat_ref, n, source[0:tile_cols, :], rim[1:2], rim[2:3])
     root = 1.0 / math.sqrt(out_width)
     for at in halves(out_width):
         for n, a in enumerate([0, 2]):
@@ -370,31 +363,29 @@
 
 
 def beyond_kernel(
-    shape, own_ref, even_ref, odd_ref, left_ref, right_ref, kernel_ref, bias_ref, part_ref,
-    feat_ref, slope_ref, low_ref, high_ref, cat_ref, edge_ref,
+    shape, own_ref, even_ref, odd_ref, far_even_ref, far_odd_ref, left_ref, right_ref, kernel_ref, bias_ref,
+    part_ref, feat_ref, slope_ref, low_ref, high_ref, far_low_ref, far_high_ref, cat_ref, edge_ref,
 ):
     tile_rows, tile_cols, in_width, out_width, step = shape
     halo_rows(even_ref, odd_ref, low_ref, high_ref)
+    halo_rows(far_even_ref, far_odd_ref, far_low_ref, far_high_ref)
     first = (lax.axis_index("rows") > 0).astype(f32)
     last = (lax.axis_index("rows") < lax.axis_size("rows") - 1).astype(f32)
     left = (lax.axis_index("cols") > 0).astype(f32)
     right = (lax.axis_index("cols") < lax.axis_size("cols") - 1).astype(f32)
-    main = 2 * tile_cols
-    low_rim, high_rim = low_ref[main:, :].astype(f32), high_ref[main:, :].astype(f32)
+    around = [far_low_ref, low_ref, high_ref, far_high_ref]
+    rims = [ref[tile_cols:, :].astype(f32) for ref in around]
     own_begin = column(own_ref[:, 0:16, :].astype(f32), 0)
     own_end = column(own_ref[:, tile_cols - 16 :, :].astype(f32), 15)
 
     def sides(c, own):
-        return jnp.concatenate(
-            [low_rim[c : c + 1], low_rim[4 + c : 5 + c], own, high_rim[c : c + 1], high_rim[4 + c : 5 + c]],
-            axis=0,
-        )
+        parts = [rim[c : c + 1] for rim in rims]
+        return jnp.concatenate([*parts[:2], own, *parts[2:]], axis=0)
 
     def ends(c, own):
         c16 = c // 16 * 16
-        piece = lambda ref, k: ref[k + c16 : k + c16 + 16, :].astype(f32)[c - c16 : c - c16 + 1]
-        rows = [piece(low_ref, 0), piece(low_ref, tile_cols), own]
-        return jnp.concatenate([*rows, piece(high_ref, 0), piece(high_ref, tile_cols)], axis=0)
+        parts = [ref[c16 : c16 + 16, :].astype(f32)[c - c16 : c - c16 + 1] for ref in around]
+        return jnp.concatenate([*parts[:2], own, *parts[2:]], axis=0)
 
     lefts = [
         sides(0, left_ref[0].astype(f32)), sides(1, left_ref[1].astype(f32)), ends(0, own_begin)
@@ -403,9 +394,8 @@
         ends(tile_cols - 1, own_end), sides(2, right_ref[0].astype(f32)), sides(3, right_ref[1].astype(f32))
     ]
     span = 3 * in_width
-    for r, line in enumerate([0, 1, tile_rows + 2, tile_rows + 3]):
-        source = low_ref if r < 2 else high_ref
-        row = source[r % 2 * tile_cols : (r % 2 + 1) * tile_cols, :]
+    for r, (source, line) in enumerate(zip(around, [0, 1, tile_rows + 2, tile_rows + 3])):
+        row = source[0:tile_cols, :]
         fill_row(cat_ref, r, row, lefts[1][line : line + 1], rights[1][line : line + 1])
     blank = jnp.zeros((edge - tile_rows - 2, in_width), f32)
     for a in range(3):
@@ -565,11 +555,11 @@
         beyond = [lax.ppermute(rims[0], "cols", [(0, 1), (1, 0)])]
     else:
         beyond = shift_cols(rims[1], rims[0])
-    payload_shape = jax.ShapeDtypeStruct((2 * tile_cols + edge, in_width), bf16)
+    payload_shape = jax.ShapeDtypeStruct((tile_cols + edge, in_width), bf16)
     half_shape = jax.ShapeDtypeStruct((1, *target_gram.shape), bf16)
-    even, odd, left, right, rows = local(
+    even, odd, far_even, far_odd, left, right, rows = local(
         payload_kernel,
-        (payload_shape, payload_shape, rim_shape, rim_shape, half_shape),
+        (*(payload_shape,) * 4, rim_shape, rim_shape, half_shape),
         "row_payload",
         canvas,
         target_gram,
@@ -629,9 +619,16 @@
         "add 0": [(2, 1)],
         "add 1": [(0,)],
     }
-    prepared, far_pixels = [], []
+    prepared, far_pixels, second_rows = [], [], []
 
     def beside(name, sent, got):
+        for bits in exchanges.get(name, []):
+            gather.step(sent, *bits)
+        if name == "join 0":
+            sends = lax.optimization_barrier((far_even, far_odd, sent))
+            second_rows.extend(swap_rows(range(k, count, 2), sends[k]) for k in range(2))
+            gather.settle(sent)
+            got, gather.rows = lax.optimization_barrier((got, gather.rows))
         if name == "join 1":
             outer = 2 * tile_cols + 2 * edge
             rim_sums, _ = lax.optimization_barrier((part, sent))
@@ -639,8 +636,9 @@
                 pl.pallas_call(
                     functools.partial(beyond_kernel, shape),
                     out_shape=(jax.ShapeDtypeStruct((outer, out_width), bf16),) * 2,
-                    in_specs=[vmem] * 8,
+                    in_specs=[vmem] * 10,
                     scratch_shapes=[
+                        *halo_scratch,
                         *halo_scratch,
                         pltpu.VMEM((4 * tile_cols, 3 * in_width), bf16),
                         pltpu.VMEM((2 * edge, 9 * in_width), bf16),
@@ -648,14 +646,12 @@
                     compiler_params=params,
                     name="beyond",
                     cost_estimate=chained,
-                )(canvas, even, odd, left, right, kernel, bias, rim_sums)
+                )(canvas, even, odd, *second_rows, left, right, kernel, bias, rim_sums)
             )
             return lax.optimization_barrier((got, *far_pixels))[0]
-        for bit in exchanges.get(name, []):
-            gather.step(sent, *bit)
-        if name != "join 0":
+        if name != "halves":
             return got
-        gather.settle(sent)
+        rows, _ = lax.optimization_barrier((gather.rows, sent))
         prepared.extend(
             pl.pallas_call(
                 prepare_kernel,
@@ -669,7 +665,7 @@
                 cost_estimate=pl.CostEstimate(
                     flops=2_000_000_000, bytes_accessed=6_000_000, transcendentals=0
                 ),
-            )(kernel, gather.rows.reshape(out_width, out_width))
+            )(kernel, rows.reshape(out_width, out_width))
         )
         return lax.optimization_barrier((got, *prepared))[0]
 

time: 46.8 us -> 49.7 us (1.062)
  waiting for transfers between devices: 12.7 us -> 16.1 us
  starting transfers between devices: 21.1 us -> 20.5 us
    ppermute x13, starting transfers between devices: 13.2 us -> 7.23 us  [swap(): lax.ppermute(value, ('rows', 'cols'), [(i, i ^ flip(i)) for i in range(to...]
    ppermute x2 -> x4, starting transfers between devices: 7.42 us -> 12.7 us  [swap_rows(): lax.ppermute(value, 'rows', pairs + [(target, source) for source, target...]
    ppermute x2 -> x4, waiting for transfers between devices: 1.15 us -> 3.85 us  [swap_rows(): lax.ppermute(value, 'rows', pairs + [(target, source) for source, target...]
    ppermute x13, waiting for transfers between devices: 10.7 us -> 11.5 us  [swap(): lax.ppermute(value, ('rows', 'cols'), [(i, i ^ flip(i)) for i in range(to...]
  transfers between devices with their start and end apart: 16 -> 18, of which waited for: 14 -> 12; matrix products, arithmetic and copies ran while one was open for 0% -> 0% of each run, Pallas kernels for 12% -> 11%
where the time goes in v6:
time: 49.7 us; the launch traced here: 49.6 us
  starting transfers between devices  20.5 us (41%)
  waiting for transfers between devices  16.1 us (32%)
  Pallas kernels  11.1 us (22%)
  local copies, waits for them, and re-layouts  1.05 us (2%)
  between operations  0.82 us (2%)
    ppermute x4, starting transfers between devices, swap_rows(): lax.ppermute(value, 'rows', pairs + [(target, source) for source, target...  12.7 us
    ppermute x13, waiting for transfers between devices, swap(): lax.ppermute(value, ('rows', 'cols'), [(i, i ^ flip(i)) for i in range(to...  11.5 us
    ppermute x13, starting transfers between devices, swap(): lax.ppermute(value, ('rows', 'cols'), [(i, i ^ flip(i)) for i in range(to...  7.23 us
    pallas_call x1, Pallas kernels, on_device(): pl.pallas_call(functools.partial(backward_kernel, shape, pixel_total), ou...  4.45 us
    ppermute x4, waiting for transfers between devices, swap_rows(): lax.ppermute(value, 'rows', pairs + [(target, source) for source, target...  3.85 us
    pallas_call x1, Pallas kernels, on_device(): pl.pallas_call(functools.partial(inner_kernel, shape), out_shape=(jax.Sha...  3.37 us
    unnamed x10, local copies, waits for them, and re-layouts  1.05 us
    pallas_call x1, Pallas kernels, beside(): pl.pallas_call(functools.partial(beyond_kernel, shape), out_shape=(jax.Sh...  1.04 us
  transfers between devices with their start and end apart: 18, of which 12 were waited for; matrix products, arithmetic and copies ran while one was open for 0% of the time, Pallas kernels for 11%

profile of v6, /device:TPU:0, one launch (start us, length us, event | category | flops | bytes accessed | tf_op | source)
XLA Modules:
  0.0 49.6 jit_solution(16260540827664841969)
XLA Ops:
  0.6 1.0 %copy-done.1 = bf16[8,128,256]{2,1,0:T(8,128)(2,1)S(1)} copy-done((bf16[8,128,256]{2,1,0:T(8,128)(2,1)S(1)}, bf16[8,128,256]{2,1,0:T(8,128)(2,1)}, u32[]{:S(2)}) %copy-start.1) | copy-done | bytes 524312
  1.7 0.5 %collective-permute-start = (bf16[2,8,256]{2,1,0:T(8,128)(2,1)S(1)}, bf16[2,8,256]{2,1,0:T(8,128)(2,1)S(1)}, u32[]{:S(2)}, u32[]{:S(2)}) collective-permute-start(bf16[2,8,256]{2,1,0:T(8,128)(2,1)S(1)} %column_rims.1), channel_id=1, source_target_pairs={{0,1},{1,0},{2,3},{3,2},{4,5},{5,4},{6,7},{7,6},{8,9},{9,8},{10,11... | collective-permute-start | bytes 24584 | tf_op jit(solution)/shard_map/ppermute | solution.py:555
  2.2 0.8 %collective-permute-done.refs_0_ = bf16[2,8,256]{2,1,0:T(8,128)(2,1)S(1)} collective-permute-done((bf16[2,8,256]{2,1,0:T(8,128)(2,1)S(1)}, bf16[2,8,256]{2,1,0:T(8,128)(2,1)S(1)}, u32[]{:S(2)}, u32[]{:S(2)}) %collective-permute-start) | collective-permute-done | bytes 8224 | tf_op jit(solution)/shard_map/ppermute | solution.py:555
  3.1 2.9 %collective-permute-start.1 = (bf16[144,256]{1,0:T(8,128)(2,1)S(1)}, bf16[144,256]{1,0:T(8,128)(2,1)S(1)}, u32[]{:S(2)}, u32[]{:S(2)}) collective-permute-start(bf16[144,256]{1,0:T(8,128)(2,1)S(1)} %get-tuple-element.42), channel_id=1, source_target_pairs={{0,2},{4,6},{8,10},{12,14},{16,18},{20,22},{24,26},{28,30},{2,0},{... | collective-permute-start | bytes 221192 | tf_op jit(solution)/shard_map/ppermute | solution.py:25
  6.0 4.5 %collective-permute-start.2 = (bf16[144,256]{1,0:T(8,128)(2,1)S(1)}, bf16[144,256]{1,0:T(8,128)(2,1)S(1)}, u32[]{:S(2)}, u32[]{:S(2)}) collective-permute-start(bf16[144,256]{1,0:T(8,128)(2,1)S(1)} %get-tuple-element.43), channel_id=1, source_target_pairs={{2,4},{6,8},{10,12},{14,16},{18,20},{22,24},{26,28},{30,0},{4,2},{... | collective-permute-start | bytes 221192 | tf_op jit(solution)/shard_map/ppermute | solution.py:25
  10.5 3.4 %inner_rows.1 = (bf16[768,512]{1,0:T(8,128)(2,1)S(1)}, bf16[768,512]{1,0:T(8,128)(2,1)S(1)}, f32[1280,128]{1,0:T(8,128)S(1)}, f32[1,512]{1,0:T(1,128)S(1)}, f32[512,512]{1,0:T(8,128)S(1)}) custom-call(bf16[8,128,256]{2,1,0:T(8,128)(2,1)S(1)} %copy-done.2, bf16[2,8,256]{2,1,0:T(8,128)(2,1)S(1)} %get-tuple-element.44.left_ref, ...), custom_call_target="tpu_custom_call" | custom-call | flops 2214592512 | bytes 6000000 | tf_op jit(solution)/shard_map/inner_rows/pallas_call | solution.py:575
  13.9 0.9 %outer_rows.1 = (bf16[256,512]{1,0:T(8,128)(2,1)S(1)}, bf16[256,512]{1,0:T(8,128)(2,1)S(1)}, bf16[640,128]{1,0:T(8,128)(2,1)S(1)}, f32[640,128]{1,0:T(8,128)S(1)}) custom-call(bf16[144,256]{1,0:T(8,128)(2,1)S(1)} %collective-permute-done.1.even_ref, bf16[144,256]{1,0:T(8,128)(2,1)S(1)} %collective-permute-done.2.odd_ref, bf16[2304,512]{1,0:T(8,128)(2,1)S(1)} %bitcast.23, ...), custom_call_target="tpu_custom_call" | custom-call | tf_op jit(solution)/shard_map/outer_rows/pallas_call | solution.py:597
  14.9 0.9 %collective-permute-start.9 = (bf16[1,16,512]{2,1,0:T(8,128)(2,1)S(1)}, bf16[1,16,512]{2,1,0:T(8,128)(2,1)S(1)}, u32[]{:S(2)}, u32[]{:S(2)}) collective-permute-start(bf16[1,16,512]{2,1,0:T(8,128)(2,1)S(1)} %get-tuple-element.55), channel_id=1, source_target_pairs={{0,17},{1,16},{2,19},{3,18},{4,21},{5,20},{6,23},{7,22},{8,25},{9,... | collective-permute-start | bytes 49160 | tf_op jit(solution)/shard_map/ppermute | solution.py:42
  15.8 0.5 collective-permute-done.3.got_ref
  16.3 0.1 collective-permute-start.4
  16.4 2.6 %collective-permute-done.9 = bf16[1,16,512]{2,1,0:T(8,128)(2,1)S(1)} collective-permute-done((bf16[1,16,512]{2,1,0:T(8,128)(2,1)S(1)}, bf16[1,16,512]{2,1,0:T(8,128)(2,1)S(1)}, u32[]{:S(2)}, u32[]{:S(2)}) %collective-permute-start.9) | collective-permute-done | bytes 16416 | tf_op jit(solution)/shard_map/ppermute | solution.py:42
  19.1 1.2 %collective-permute-done.4.got_ref = bf16[320,128]{1,0:T(8,128)(2,1)S(1)} collective-permute-done((bf16[320,128]{1,0:T(8,128)(2,1)S(1)}, bf16[320,128]{1,0:T(8,128)(2,1)S(1)}, u32[]{:S(2)}, u32[]{:S(2)}) %collective-permute-start.4) | collective-permute-done | bytes 81952 | tf_op jit(solution)/shard_map/ppermute | solution.py:42
  20.3 0.6 %collective-permute-start.5 = (bf16[160,128]{1,0:T(8,128)(2,1)S(1)}, bf16[160,128]{1,0:T(8,128)(2,1)S(1)}, u32[]{:S(2)}, u32[]{:S(2)}) collective-permute-start(bf16[160,128]{1,0:T(8,128)(2,1)S(1)} %get-tuple-element.53), channel_id=1, source_target_pairs={{0,5},{1,2},{2,1},{3,6},{4,7},{5,0},{6,3},{7,4},{8,11},{9,12},{10,... | collective-permute-start | bytes 122888 | tf_op jit(solution)/shard_map/ppermute | solution.py:42
  20.9 1.5 %collective-permute-done.10 = bf16[2,16,512]{2,1,0:T(8,128)(2,1)S(1)} collective-permute-done((bf16[2,16,512]{2,1,0:T(8,128)(2,1)S(1)}, bf16[2,16,512]{2,1,0:T(8,128)(2,1)S(1)}, u32[]{:S(2)}, u32[]{:S(2)}) %collective-permute-start.10) | collective-permute-done | bytes 32800 | tf_op jit(solution)/shard_map/ppermute | solution.py:42
  22.5 1.3 %collective-permute-done.5.got_ref = bf16[160,128]{1,0:T(8,128)(2,1)S(1)} collective-permute-done((bf16[160,128]{1,0:T(8,128)(2,1)S(1)}, bf16[160,128]{1,0:T(8,128)(2,1)S(1)}, u32[]{:S(2)}, u32[]{:S(2)}) %collective-permute-start.5) | collective-permute-done | bytes 40992 | tf_op jit(solution)/shard_map/ppermute | solution.py:42
  23.8 1.1 %collective-permute-start.6 = (bf16[160,128]{1,0:T(8,128)(2,1)S(1)}, bf16[160,128]{1,0:T(8,128)(2,1)S(1)}, u32[]{:S(2)}, u32[]{:S(2)}) collective-permute-start(bf16[160,128]{1,0:T(8,128)(2,1)S(1)} %add.3.keep_ref), channel_id=1, source_target_pairs={{0,9},{1,16},{2,19},{3,10},{4,21},{5,12},{6,15},{7,22},{8,25},{9,0... | collective-permute-start | bytes 122888 | tf_op jit(solution)/shard_map/ppermute | solution.py:42
  24.9 1.3 %collective-permute-done.11 = bf16[4,16,512]{2,1,0:T(8,128)(2,1)S(1)} collective-permute-done((bf16[4,16,512]{2,1,0:T(8,128)(2,1)S(1)}, bf16[4,16,512]{2,1,0:T(8,128)(2,1)S(1)}, u32[]{:S(2)}, u32[]{:S(2)}) %collective-permute-start.11) | collective-permute-done | bytes 65568 | tf_op jit(solution)/shard_map/ppermute | solution.py:42
  26.2 0.4 collective-permute-start.12
  26.6 0.7 %collective-permute-done.6.got_ref = bf16[160,128]{1,0:T(8,128)(2,1)S(1)} collective-permute-done((bf16[160,128]{1,0:T(8,128)(2,1)S(1)}, bf16[160,128]{1,0:T(8,128)(2,1)S(1)}, u32[]{:S(2)}, u32[]{:S(2)}) %collective-permute-start.6) | collective-permute-done | bytes 40992 | tf_op jit(solution)/shard_map/ppermute | solution.py:42
  27.3 1.6 %collective-permute-start.7 = (bf16[160,128]{1,0:T(8,128)(2,1)S(1)}, bf16[160,128]{1,0:T(8,128)(2,1)S(1)}, u32[]{:S(2)}, u32[]{:S(2)}) collective-permute-start(bf16[160,128]{1,0:T(8,128)(2,1)S(1)} %add.4.keep_ref), channel_id=1, source_target_pairs={{0,17},{1,8},{2,11},{3,18},{4,13},{5,20},{6,23},{7,14},{8,1},{9,24... | collective-permute-start | bytes 122888 | tf_op jit(solution)/shard_map/ppermute | solution.py:42
  28.9 1.7 %collective-permute-done.12 = bf16[8,16,512]{2,1,0:T(8,128)(2,1)S(1)} collective-permute-done((bf16[8,16,512]{2,1,0:T(8,128)(2,1)S(1)}, bf16[8,16,512]{2,1,0:T(8,128)(2,1)S(1)}, u32[]{:S(2)}, u32[]{:S(2)}) %collective-permute-start.12) | collective-permute-done | bytes 131104 | tf_op jit(solution)/shard_map/ppermute | solution.py:42
  30.7 0.8 %collective-permute-start.13 = (bf16[16,16,512]{2,1,0:T(8,128)(2,1)S(1)}, bf16[16,16,512]{2,1,0:T(8,128)(2,1)S(1)}, u32[]{:S(2)}, u32[]{:S(2)}) collective-permute-start(bf16[16,16,512]{2,1,0:T(8,128)(2,1)S(1)} %bitcast.28), channel_id=1, source_target_pairs={{0,1},{1,0},{2,3},{3,2},{4,5},{5,4},{6,7},{7,6},{8,9},{9,8},{10,11... | collective-permute-start | bytes 786440 | tf_op jit(solution)/shard_map/ppermute | solution.py:42
  31.5 0.2 collective-permute-done.7.got_ref
  31.7 1.5 %collective-permute-start.8 = (bf16[160,128]{1,0:T(8,128)(2,1)S(1)}, bf16[160,128]{1,0:T(8,128)(2,1)S(1)}, u32[]{:S(2)}, u32[]{:S(2)}) collective-permute-start(bf16[160,128]{1,0:T(8,128)(2,1)S(1)} %add.5), channel_id=1, source_target_pairs={{0,5},{1,2},{2,1},{3,6},{4,7},{5,0},{6,3},{7,4},{8,11},{9,12},{10,... | collective-permute-start | bytes 122888 | tf_op jit(solution)/shard_map/ppermute | solution.py:42
  33.2 0.5 collective-permute-start.15
  33.7 4.8 %collective-permute-start.16 = (bf16[144,256]{1,0:T(8,128)(2,1)S(1)}, bf16[144,256]{1,0:T(8,128)(2,1)S(1)}, u32[]{:S(2)}, u32[]{:S(2)}) collective-permute-start(bf16[144,256]{1,0:T(8,128)(2,1)S(1)} %get-tuple-element.65), channel_id=1, source_target_pairs={{2,4},{6,8},{10,12},{14,16},{18,20},{22,24},{26,28},{30,0},{4,2},{... | collective-permute-start | bytes 221192 | tf_op jit(solution)/shard_map/ppermute | solution.py:25
  38.7 3.8 %collective-permute-done.16.far_odd_ref = bf16[144,256]{1,0:T(8,128)(2,1)S(1)} collective-permute-done((bf16[144,256]{1,0:T(8,128)(2,1)S(1)}, bf16[144,256]{1,0:T(8,128)(2,1)S(1)}, u32[]{:S(2)}, u32[]{:S(2)}) %collective-permute-start.16) | collective-permute-done | bytes 73760 | tf_op jit(solution)/shard_map/ppermute | solution.py:25
  42.6 1.0 %beyond.1 = (bf16[288,512]{1,0:T(8,128)(2,1)S(1)}, bf16[288,512]{1,0:T(8,128)(2,1)S(1)}) custom-call(bf16[8,128,256]{2,1,0:T(8,128)(2,1)S(1)} %copy-done.2, bf16[144,256]{1,0:T(8,128)(2,1)S(1)} %collective-permute-done.1.even_ref, bf16[144,256]{1,0:T(8,128)(2,1)S(1)} %collective-permute-done.2.odd_ref, ...), custom_call_target="tpu_custom_call" | custom-call | flops 8000000000 | bytes 100000 | tf_op jit(solution)/shard_map/beyond/pallas_call | solution.py:636
  43.7 0.1 collective-permute-start.17
  43.7 1.0 %prepare.1 = (bf16[4608,256]{1,0:T(8,128)(2,1)S(1)}, f32[512,512]{1,0:T(8,128)S(1)}) custom-call(bf16[2304,512]{1,0:T(8,128)(2,1)S(1)} %bitcast.25, bf16[512,512]{1,0:T(8,128)(2,1)S(1)} %bitcast.46), custom_call_target="tpu_custom_call" | custom-call | flops 2000000000 | bytes 6000000 | tf_op jit(solution)/shard_map/prepare/pallas_call | solution.py:656
  44.7 0.4 collective-permute-done.17.other_ref
  45.1 4.5 %grad_conv.1 = (f32[16,512]{1,0:T(8,128)}, bf16[1024,256]{1,0:T(8,128)(2,1)}) custom-call(bf16[640,128]{1,0:T(8,128)(2,1)S(1)} %bitcast.27, bf16[640,128]{1,0:T(8,128)(2,1)S(1)} %collective-permute-done.17.other_ref, f32[512,512]{1,0:T(8,128)S(1)} %get-tuple-element.74.both_ref, bf16[768,512]{1,0:T(8,128)(2,1)S(1)} %get-tuple-element.76.in_feat_ref, ...), custom_call_target="tpu_custom_call" | custom-call | tf_op jit(solution)/shard_map/grad_conv/pallas_call | solution.py:675
  (33 shorter events, 0.6 us)
Async XLA Ops:
  0.6 1.0 %copy-start.1 = (bf16[8,128,256]{2,1,0:T(8,128)(2,1)S(1)}, bf16[8,128,256]{2,1,0:T(8,128)(2,1)}, u32[]{:S(2)}) copy-start(bf16[8,128,256]{2,1,0:T(8,128)(2,1)} %own_ref.3) | copy-start | bytes 1572868
  1.7 1.4 %copy-start.3 = (f32[16,512]{1,0:T(8,128)S(1)}, f32[16,512]{1,0:T(8,128)}, u32[]{:S(2)}) copy-start(f32[16,512]{1,0:T(8,128)} %target_ref.1) | copy-start | bytes 98308
  1.7 8.9 %copy-start = (bf16[3,3,256,512]{3,2,1,0:T(8,128)(2,1)S(1)}, bf16[3,3,256,512]{3,2,1,0:T(8,128)(2,1)}, u32[]{:S(2)}) copy-start(bf16[3,3,256,512]{3,2,1,0:T(8,128)(2,1)} %param.5) | copy-start | bytes 7077892
  1.7 8.9 %copy-start.2 = (bf16[8,128,256]{2,1,0:T(8,128)(2,1)S(1)}, bf16[8,128,256]{2,1,0:T(8,128)(2,1)}, u32[]{:S(2)}) copy-start(bf16[8,128,256]{2,1,0:T(8,128)(2,1)} %own_ref.3) | copy-start | bytes 1572868
  1.7 8.9 %copy-start.4 = (bf16[512]{0:T(512)(128)(2,1)S(1)}, bf16[512]{0:T(512)(128)(2,1)}, u32[]{:S(2)}) copy-start(bf16[512]{0:T(512)(128)(2,1)} %bias_ref.1) | copy-start | bytes 3076
  1.7 1.3 %collective-permute-start = (bf16[2,8,256]{2,1,0:T(8,128)(2,1)S(1)}, bf16[2,8,256]{2,1,0:T(8,128)(2,1)S(1)}, u32[]{:S(2)}, u32[]{:S(2)}) collective-permute-start(bf16[2,8,256]{2,1,0:T(8,128)(2,1)S(1)} %column_rims.1), channel_id=1, source_target_pairs={{0,1},{1,0},{2,3},{3,2},{4,5},{5,4},{6,7},{7,6},{8,9},{9,8},{10,11... | collective-permute-start | bytes 24584 | tf_op jit(solution)/shard_map/ppermute | solution.py:555
  3.1 10.8 %collective-permute-start.1 = (bf16[144,256]{1,0:T(8,128)(2,1)S(1)}, bf16[144,256]{1,0:T(8,128)(2,1)S(1)}, u32[]{:S(2)}, u32[]{:S(2)}) collective-permute-start(bf16[144,256]{1,0:T(8,128)(2,1)S(1)} %get-tuple-element.42), channel_id=1, source_target_pairs={{0,2},{4,6},{8,10},{12,14},{16,18},{20,22},{24,26},{28,30},{2,0},{... | collective-permute-start | bytes 221192 | tf_op jit(solution)/shard_map/ppermute | solution.py:25
  6.0 7.9 %collective-permute-start.2 = (bf16[144,256]{1,0:T(8,128)(2,1)S(1)}, bf16[144,256]{1,0:T(8,128)(2,1)S(1)}, u32[]{:S(2)}, u32[]{:S(2)}) collective-permute-start(bf16[144,256]{1,0:T(8,128)(2,1)S(1)} %get-tuple-element.43), channel_id=1, source_target_pairs={{2,4},{6,8},{10,12},{14,16},{18,20},{22,24},{26,28},{30,0},{4,2},{... | collective-permute-start | bytes 221192 | tf_op jit(solution)/shard_map/ppermute | solution.py:25
  14.8 1.5 %collective-permute-start.3 = (bf16[640,128]{1,0:T(8,128)(2,1)S(1)}, bf16[640,128]{1,0:T(8,128)(2,1)S(1)}, u32[]{:S(2)}, u32[]{:S(2)}) collective-permute-start(bf16[640,128]{1,0:T(8,128)(2,1)S(1)} %get-tuple-element.49), channel_id=1, source_target_pairs={{0,1},{1,0},{2,3},{3,2},{4,5},{5,4},{6,7},{7,6},{8,9},{9,8},{10,11... | collective-permute-start | bytes 491528 | tf_op jit(solution)/shard_map/ppermute | solution.py:42
  14.9 4.1 %collective-permute-start.9 = (bf16[1,16,512]{2,1,0:T(8,128)(2,1)S(1)}, bf16[1,16,512]{2,1,0:T(8,128)(2,1)S(1)}, u32[]{:S(2)}, u32[]{:S(2)}) collective-permute-start(bf16[1,16,512]{2,1,0:T(8,128)(2,1)S(1)} %get-tuple-element.55), channel_id=1, source_target_pairs={{0,17},{1,16},{2,19},{3,18},{4,21},{5,20},{6,23},{7,22},{8,25},{9,... | collective-permute-start | bytes 49160 | tf_op jit(solution)/shard_map/ppermute | solution.py:42
  16.3 3.9 %collective-permute-start.4 = (bf16[320,128]{1,0:T(8,128)(2,1)S(1)}, bf16[320,128]{1,0:T(8,128)(2,1)S(1)}, u32[]{:S(2)}, u32[]{:S(2)}) collective-permute-start(bf16[320,128]{1,0:T(8,128)(2,1)S(1)} %get-tuple-element.51), channel_id=1, source_target_pairs={{0,3},{1,4},{2,7},{3,0},{4,1},{5,6},{6,5},{7,2},{8,13},{9,10},{10,... | collective-permute-start | bytes 245768 | tf_op jit(solution)/shard_map/ppermute | solution.py:42
  19.1 3.3 %collective-permute-start.10 = (bf16[2,16,512]{2,1,0:T(8,128)(2,1)S(1)}, bf16[2,16,512]{2,1,0:T(8,128)(2,1)S(1)}, u32[]{:S(2)}, u32[]{:S(2)}) collective-permute-start(bf16[2,16,512]{2,1,0:T(8,128)(2,1)S(1)} %bitcast.41), channel_id=1, source_target_pairs={{0,9},{1,8},{2,11},{3,10},{4,13},{5,12},{6,15},{7,14},{8,1},{9,0},... | collective-permute-start | bytes 98312 | tf_op jit(solution)/shard_map/ppermute | solution.py:42
  20.3 3.5 %collective-permute-start.5 = (bf16[160,128]{1,0:T(8,128)(2,1)S(1)}, bf16[160,128]{1,0:T(8,128)(2,1)S(1)}, u32[]{:S(2)}, u32[]{:S(2)}) collective-permute-start(bf16[160,128]{1,0:T(8,128)(2,1)S(1)} %get-tuple-element.53), channel_id=1, source_target_pairs={{0,5},{1,2},{2,1},{3,6},{4,7},{5,0},{6,3},{7,4},{8,11},{9,12},{10,... | collective-permute-start | bytes 122888 | tf_op jit(solution)/shard_map/ppermute | solution.py:42
  22.4 3.8 %collective-permute-start.11 = (bf16[4,16,512]{2,1,0:T(8,128)(2,1)S(1)}, bf16[4,16,512]{2,1,0:T(8,128)(2,1)S(1)}, u32[]{:S(2)}, u32[]{:S(2)}) collective-permute-start(bf16[4,16,512]{2,1,0:T(8,128)(2,1)S(1)} %bitcast.36), channel_id=1, source_target_pairs={{0,3},{1,4},{2,7},{3,0},{4,1},{5,6},{6,5},{7,2},{8,13},{9,10},{10,... | collective-permute-start | bytes 196616 | tf_op jit(solution)/shard_map/ppermute | solution.py:42
  23.8 3.5 %collective-permute-start.6 = (bf16[160,128]{1,0:T(8,128)(2,1)S(1)}, bf16[160,128]{1,0:T(8,128)(2,1)S(1)}, u32[]{:S(2)}, u32[]{:S(2)}) collective-permute-start(bf16[160,128]{1,0:T(8,128)(2,1)S(1)} %add.3.keep_ref), channel_id=1, source_target_pairs={{0,9},{1,16},{2,19},{3,10},{4,21},{5,12},{6,15},{7,22},{8,25},{9,0... | collective-permute-start | bytes 122888 | tf_op jit(solution)/shard_map/ppermute | solution.py:42
  26.2 4.5 %collective-permute-start.12 = (bf16[8,16,512]{2,1,0:T(8,128)(2,1)S(1)}, bf16[8,16,512]{2,1,0:T(8,128)(2,1)S(1)}, u32[]{:S(2)}, u32[]{:S(2)}) collective-permute-start(bf16[8,16,512]{2,1,0:T(8,128)(2,1)S(1)} %bitcast.30), channel_id=1, source_target_pairs={{0,5},{1,2},{2,1},{3,6},{4,7},{5,0},{6,3},{7,4},{8,11},{9,12},{10,... | collective-permute-start | bytes 393224 | tf_op jit(solution)/shard_map/ppermute | solution.py:42
  27.3 4.4 %collective-permute-start.7 = (bf16[160,128]{1,0:T(8,128)(2,1)S(1)}, bf16[160,128]{1,0:T(8,128)(2,1)S(1)}, u32[]{:S(2)}, u32[]{:S(2)}) collective-permute-start(bf16[160,128]{1,0:T(8,128)(2,1)S(1)} %add.4.keep_ref), channel_id=1, source_target_pairs={{0,17},{1,8},{2,11},{3,18},{4,13},{5,20},{6,23},{7,14},{8,1},{9,24... | collective-permute-start | bytes 122888 | tf_op jit(solution)/shard_map/ppermute | solution.py:42
  30.7 7.8 %collective-permute-start.13 = (bf16[16,16,512]{2,1,0:T(8,128)(2,1)S(1)}, bf16[16,16,512]{2,1,0:T(8,128)(2,1)S(1)}, u32[]{:S(2)}, u32[]{:S(2)}) collective-permute-start(bf16[16,16,512]{2,1,0:T(8,128)(2,1)S(1)} %bitcast.28), channel_id=1, source_target_pairs={{0,1},{1,0},{2,3},{3,2},{4,5},{5,4},{6,7},{7,6},{8,9},{9,8},{10,11... | collective-permute-start | bytes 786440 | tf_op jit(solution)/shard_map/ppermute | solution.py:42
  31.7 6.9 %collective-permute-start.8 = (bf16[160,128]{1,0:T(8,128)(2,1)S(1)}, bf16[160,128]{1,0:T(8,128)(2,1)S(1)}, u32[]{:S(2)}, u32[]{:S(2)}) collective-permute-start(bf16[160,128]{1,0:T(8,128)(2,1)S(1)} %add.5), channel_id=1, source_target_pairs={{0,5},{1,2},{2,1},{3,6},{4,7},{5,0},{6,3},{7,4},{8,11},{9,12},{10,... | collective-permute-start | bytes 122888 | tf_op jit(solution)/shard_map/ppermute | solution.py:42
  33.2 5.5 %collective-permute-start.15 = (bf16[144,256]{1,0:T(8,128)(2,1)S(1)}, bf16[144,256]{1,0:T(8,128)(2,1)S(1)}, u32[]{:S(2)}, u32[]{:S(2)}) collective-permute-start(bf16[144,256]{1,0:T(8,128)(2,1)S(1)} %get-tuple-element.64), channel_id=1, source_target_pairs={{0,2},{4,6},{8,10},{12,14},{16,18},{20,22},{24,26},{28,30},{2,0},{... | collective-permute-start | bytes 221192 | tf_op jit(solution)/shard_map/ppermute | solution.py:25
  33.7 8.9 %collective-permute-start.16 = (bf16[144,256]{1,0:T(8,128)(2,1)S(1)}, bf16[144,256]{1,0:T(8,128)(2,1)S(1)}, u32[]{:S(2)}, u32[]{:S(2)}) collective-permute-start(bf16[144,256]{1,0:T(8,128)(2,1)S(1)} %get-tuple-element.65), channel_id=1, source_target_pairs={{2,4},{6,8},{10,12},{14,16},{18,20},{22,24},{26,28},{30,0},{4,2},{... | collective-permute-start | bytes 221192 | tf_op jit(solution)/shard_map/ppermute | solution.py:25
  38.6 5.0 %collective-permute-start.14 = (bf16[320,128]{1,0:T(8,128)(2,1)S(1)}, bf16[320,128]{1,0:T(8,128)(2,1)S(1)}, u32[]{:S(2)}, u32[]{:S(2)}) collective-permute-start(bf16[320,128]{1,0:T(8,128)(2,1)S(1)} %bitcast.33), channel_id=1, source_target_pairs={{0,3},{1,4},{2,7},{3,0},{4,1},{5,6},{6,5},{7,2},{8,13},{9,10},{10,... | collective-permute-start | bytes 245768 | tf_op jit(solution)/shard_map/ppermute | solution.py:42
  43.7 1.5 %collective-permute-start.17 = (bf16[640,128]{1,0:T(8,128)(2,1)S(1)}, bf16[640,128]{1,0:T(8,128)(2,1)S(1)}, u32[]{:S(2)}, u32[]{:S(2)}) collective-permute-start(bf16[640,128]{1,0:T(8,128)(2,1)S(1)} %bitcast.26), channel_id=1, source_target_pairs={{0,1},{1,0},{2,3},{3,2},{4,5},{5,4},{6,7},{7,6},{8,9},{9,8},{10,11... | collective-permute-start | bytes 491528 | tf_op jit(solution)/shard_map/ppermute | solution.py:42

commit v7 on v5

--- a/solution.py
+++ b/solution.py
@@ -623,11 +623,11 @@
     )(even, odd, kernel, in_gram, part)
 
     exchanges = {
-        "cores": [(bit,) for bit in far[:1]],
-        "halve 0": [(bit,) for bit in far[1:]],
-        "halve 1": [(1, 2)],
-        "add 0": [(2, 1)],
-        "add 1": [(0,)],
+        "halve 0": [(bit,) for bit in far[:1]],
+        "halve 1": [(bit,) for bit in far[1:]],
+        "add 0": [(1, 2)],
+        "add 1": [(2, 1)],
+        "join 0": [(0,)],
     }
     prepared, far_pixels = [], []
 
@@ -650,10 +650,14 @@
                     cost_estimate=chained,
                 )(canvas, even, odd, left, right, kernel, bias, rim_sums)
             )
-            return lax.optimization_barrier((got, *far_pixels))[0]
+            gather.settle(sent)
+            got, gather.rows, *_ = lax.optimization_barrier((got, gather.rows, *far_pixels))
+            return got
         for bit in exchanges.get(name, []):
             gather.step(sent, *bit)
-        if name != "join 0":
+        if name == "join 0":
+            got, gather.rows = lax.optimization_barrier((got, gather.rows))
+        if name != "halves":
             return got
         gather.settle(sent)
         prepared.extend(

time: 46.8 us -> 46.6 us (level)
  starting transfers between devices: 21.1 us -> 20 us
  waiting for transfers between devices: 12.7 us -> 13.6 us
    ppermute x13, starting transfers between devices: 13.2 us -> 12 us  [swap(): lax.ppermute(value, ('rows', 'cols'), [(i, i ^ flip(i)) for i in range(to...]
    ppermute x13, waiting for transfers between devices: 10.7 us -> 11.6 us  [swap(): lax.ppermute(value, ('rows', 'cols'), [(i, i ^ flip(i)) for i in range(to...]
where the time goes in v7:
time: 46.6 us; the launch traced here: 46.4 us
  starting transfers between devices  20 us (43%)
  waiting for transfers between devices  13.6 us (29%)
  Pallas kernels  11.1 us (24%)
  local copies, waits for them, and re-layouts  1.05 us (2%)
  between operations  0.77 us (2%)
    ppermute x13, starting transfers between devices, swap(): lax.ppermute(value, ('rows', 'cols'), [(i, i ^ flip(i)) for i in range(to...  12 us
    ppermute x13, waiting for transfers between devices, swap(): lax.ppermute(value, ('rows', 'cols'), [(i, i ^ flip(i)) for i in range(to...  11.6 us
    ppermute x2, starting transfers between devices, swap_rows(): lax.ppermute(value, 'rows', pairs + [(target, source) for source, target...  7.42 us
    pallas_call x1, Pallas kernels, on_device(): pl.pallas_call(functools.partial(backward_kernel, shape, pixel_total), ou...  4.46 us
    pallas_call x1, Pallas kernels, on_device(): pl.pallas_call(functools.partial(inner_kernel, shape), out_shape=(jax.Sha...  3.36 us
    ppermute x2, waiting for transfers between devices, swap_rows(): lax.ppermute(value, 'rows', pairs + [(target, source) for source, target...  1.14 us
    unnamed x10, local copies, waits for them, and re-layouts  1.05 us
    pallas_call x1, Pallas kernels, beside(): pl.pallas_call(functools.partial(beyond_kernel, shape), out_shape=(jax.Sh...  1.03 us
  transfers between devices with their start and end apart: 16, of which 14 were waited for; matrix products, arithmetic and copies ran while one was open for 0% of the time, Pallas kernels for 12%

profile of v7, /device:TPU:0, one launch (start us, length us, event | category | flops | bytes accessed | tf_op | source)
XLA Modules:
  0.0 46.4 jit_solution(14909292375091049567)
XLA Ops:
  0.6 1.0 %copy-done.1 = bf16[8,128,256]{2,1,0:T(8,128)(2,1)S(1)} copy-done((bf16[8,128,256]{2,1,0:T(8,128)(2,1)S(1)}, bf16[8,128,256]{2,1,0:T(8,128)(2,1)}, u32[]{:S(2)}) %copy-start.1) | copy-done | bytes 524312
  1.7 0.5 %collective-permute-start = (bf16[2,8,256]{2,1,0:T(8,128)(2,1)S(1)}, bf16[2,8,256]{2,1,0:T(8,128)(2,1)S(1)}, u32[]{:S(2)}, u32[]{:S(2)}) collective-permute-start(bf16[2,8,256]{2,1,0:T(8,128)(2,1)S(1)} %column_rims.1), channel_id=1, source_target_pairs={{0,1},{1,0},{2,3},{3,2},{4,5},{5,4},{6,7},{7,6},{8,9},{9,8},{10,11... | collective-permute-start | bytes 24584 | tf_op jit(solution)/shard_map/ppermute | solution.py:565
  2.2 0.8 %collective-permute-done.refs_0_ = bf16[2,8,256]{2,1,0:T(8,128)(2,1)S(1)} collective-permute-done((bf16[2,8,256]{2,1,0:T(8,128)(2,1)S(1)}, bf16[2,8,256]{2,1,0:T(8,128)(2,1)S(1)}, u32[]{:S(2)}, u32[]{:S(2)}) %collective-permute-start) | collective-permute-done | bytes 8224 | tf_op jit(solution)/shard_map/ppermute | solution.py:565
  3.1 2.9 %collective-permute-start.1 = (bf16[272,256]{1,0:T(8,128)(2,1)S(1)}, bf16[272,256]{1,0:T(8,128)(2,1)S(1)}, u32[]{:S(2)}, u32[]{:S(2)}) collective-permute-start(bf16[272,256]{1,0:T(8,128)(2,1)S(1)} %get-tuple-element.39), channel_id=1, source_target_pairs={{0,2},{4,6},{8,10},{12,14},{16,18},{20,22},{24,26},{28,30},{2,0},{... | collective-permute-start | bytes 417800 | tf_op jit(solution)/shard_map/ppermute | solution.py:25
  6.0 4.5 %collective-permute-start.2 = (bf16[272,256]{1,0:T(8,128)(2,1)S(1)}, bf16[272,256]{1,0:T(8,128)(2,1)S(1)}, u32[]{:S(2)}, u32[]{:S(2)}) collective-permute-start(bf16[272,256]{1,0:T(8,128)(2,1)S(1)} %get-tuple-element.40), channel_id=1, source_target_pairs={{2,4},{6,8},{10,12},{14,16},{18,20},{22,24},{26,28},{30,0},{4,2},{... | collective-permute-start | bytes 417800 | tf_op jit(solution)/shard_map/ppermute | solution.py:25
  10.5 3.4 %inner_rows.1 = (bf16[768,512]{1,0:T(8,128)(2,1)S(1)}, bf16[768,512]{1,0:T(8,128)(2,1)S(1)}, f32[1280,128]{1,0:T(8,128)S(1)}, f32[1,512]{1,0:T(1,128)S(1)}, f32[512,512]{1,0:T(8,128)S(1)}) custom-call(bf16[8,128,256]{2,1,0:T(8,128)(2,1)S(1)} %copy-done.2, bf16[2,8,256]{2,1,0:T(8,128)(2,1)S(1)} %get-tuple-element.41.left_ref, ...), custom_call_target="tpu_custom_call" | custom-call | flops 2214592512 | bytes 6000000 | tf_op jit(solution)/shard_map/inner_rows/pallas_call | solution.py:585
  13.9 1.1 %collective-permute-done.2.odd_ref = bf16[272,256]{1,0:T(8,128)(2,1)S(1)} collective-permute-done((bf16[272,256]{1,0:T(8,128)(2,1)S(1)}, bf16[272,256]{1,0:T(8,128)(2,1)S(1)}, u32[]{:S(2)}, u32[]{:S(2)}) %collective-permute-start.2) | collective-permute-done | bytes 139296 | tf_op jit(solution)/shard_map/ppermute | solution.py:25
  15.1 0.9 %outer_rows.1 = (bf16[256,512]{1,0:T(8,128)(2,1)S(1)}, bf16[256,512]{1,0:T(8,128)(2,1)S(1)}, bf16[640,128]{1,0:T(8,128)(2,1)S(1)}, f32[640,128]{1,0:T(8,128)S(1)}) custom-call(bf16[272,256]{1,0:T(8,128)(2,1)S(1)} %collective-permute-done.1.even_ref, bf16[272,256]{1,0:T(8,128)(2,1)S(1)} %collective-permute-done.2.odd_ref, bf16[2304,512]{1,0:T(8,128)(2,1)S(1)} %bitcast.23, ...), custom_call_target="tpu_custom_call" | custom-call | tf_op jit(solution)/shard_map/outer_rows/pallas_call | solution.py:607
  16.0 1.4 %collective-permute-done.3.got_ref = bf16[640,128]{1,0:T(8,128)(2,1)S(1)} collective-permute-done((bf16[640,128]{1,0:T(8,128)(2,1)S(1)}, bf16[640,128]{1,0:T(8,128)(2,1)S(1)}, u32[]{:S(2)}, u32[]{:S(2)}) %collective-permute-start.3) | collective-permute-done | bytes 163872 | tf_op jit(solution)/shard_map/ppermute | solution.py:42
  17.4 0.4 collective-permute-start.4
  17.9 2.6 %collective-permute-start.9 = (bf16[1,16,512]{2,1,0:T(8,128)(2,1)S(1)}, bf16[1,16,512]{2,1,0:T(8,128)(2,1)S(1)}, u32[]{:S(2)}, u32[]{:S(2)}) collective-permute-start(bf16[1,16,512]{2,1,0:T(8,128)(2,1)S(1)} %get-tuple-element.52), channel_id=1, source_target_pairs={{0,17},{1,16},{2,19},{3,18},{4,21},{5,20},{6,23},{7,22},{8,25},{9,... | collective-permute-start | bytes 49160 | tf_op jit(solution)/shard_map/ppermute | solution.py:42
  20.4 0.9 %collective-permute-done.4.got_ref = bf16[320,128]{1,0:T(8,128)(2,1)S(1)} collective-permute-done((bf16[320,128]{1,0:T(8,128)(2,1)S(1)}, bf16[320,128]{1,0:T(8,128)(2,1)S(1)}, u32[]{:S(2)}, u32[]{:S(2)}) %collective-permute-start.4) | collective-permute-done | bytes 81952 | tf_op jit(solution)/shard_map/ppermute | solution.py:42
  21.5 0.8 %collective-permute-done.9 = bf16[1,16,512]{2,1,0:T(8,128)(2,1)S(1)} collective-permute-done((bf16[1,16,512]{2,1,0:T(8,128)(2,1)S(1)}, bf16[1,16,512]{2,1,0:T(8,128)(2,1)S(1)}, u32[]{:S(2)}, u32[]{:S(2)}) %collective-permute-start.9) | collective-permute-done | bytes 16416 | tf_op jit(solution)/shard_map/ppermute | solution.py:42
  22.3 1.2 %collective-permute-start.10 = (bf16[2,16,512]{2,1,0:T(8,128)(2,1)S(1)}, bf16[2,16,512]{2,1,0:T(8,128)(2,1)S(1)}, u32[]{:S(2)}, u32[]{:S(2)}) collective-permute-start(bf16[2,16,512]{2,1,0:T(8,128)(2,1)S(1)} %bitcast.41), channel_id=1, source_target_pairs={{0,9},{1,8},{2,11},{3,10},{4,13},{5,12},{6,15},{7,14},{8,1},{9,0},... | collective-permute-start | bytes 98312 | tf_op jit(solution)/shard_map/ppermute | solution.py:42
  23.5 1.4 %collective-permute-done.5.got_ref = bf16[160,128]{1,0:T(8,128)(2,1)S(1)} collective-permute-done((bf16[160,128]{1,0:T(8,128)(2,1)S(1)}, bf16[160,128]{1,0:T(8,128)(2,1)S(1)}, u32[]{:S(2)}, u32[]{:S(2)}) %collective-permute-start.5) | collective-permute-done | bytes 40992 | tf_op jit(solution)/shard_map/ppermute | solution.py:42
  24.9 0.5 collective-permute-start.6
  25.4 0.3 collective-permute-done.10
  25.7 1.3 %collective-permute-start.11 = (bf16[4,16,512]{2,1,0:T(8,128)(2,1)S(1)}, bf16[4,16,512]{2,1,0:T(8,128)(2,1)S(1)}, u32[]{:S(2)}, u32[]{:S(2)}) collective-permute-start(bf16[4,16,512]{2,1,0:T(8,128)(2,1)S(1)} %bitcast.36), channel_id=1, source_target_pairs={{0,3},{1,4},{2,7},{3,0},{4,1},{5,6},{6,5},{7,2},{8,13},{9,10},{10,... | collective-permute-start | bytes 196616 | tf_op jit(solution)/shard_map/ppermute | solution.py:42
  27.0 1.4 %collective-permute-done.6.got_ref = bf16[160,128]{1,0:T(8,128)(2,1)S(1)} collective-permute-done((bf16[160,128]{1,0:T(8,128)(2,1)S(1)}, bf16[160,128]{1,0:T(8,128)(2,1)S(1)}, u32[]{:S(2)}, u32[]{:S(2)}) %collective-permute-start.6) | collective-permute-done | bytes 40992 | tf_op jit(solution)/shard_map/ppermute | solution.py:42
  28.4 1.3 %collective-permute-start.7 = (bf16[160,128]{1,0:T(8,128)(2,1)S(1)}, bf16[160,128]{1,0:T(8,128)(2,1)S(1)}, u32[]{:S(2)}, u32[]{:S(2)}) collective-permute-start(bf16[160,128]{1,0:T(8,128)(2,1)S(1)} %add.4.keep_ref), channel_id=1, source_target_pairs={{0,17},{1,8},{2,11},{3,18},{4,13},{5,20},{6,23},{7,14},{8,1},{9,24... | collective-permute-start | bytes 122888 | tf_op jit(solution)/shard_map/ppermute | solution.py:42
  29.7 1.3 %collective-permute-start.12 = (bf16[8,16,512]{2,1,0:T(8,128)(2,1)S(1)}, bf16[8,16,512]{2,1,0:T(8,128)(2,1)S(1)}, u32[]{:S(2)}, u32[]{:S(2)}) collective-permute-start(bf16[8,16,512]{2,1,0:T(8,128)(2,1)S(1)} %bitcast.30), channel_id=1, source_target_pairs={{0,5},{1,2},{2,1},{3,6},{4,7},{5,0},{6,3},{7,4},{8,11},{9,12},{10,... | collective-permute-start | bytes 393224 | tf_op jit(solution)/shard_map/ppermute | solution.py:42
  31.1 1.8 %collective-permute-done.7.got_ref = bf16[160,128]{1,0:T(8,128)(2,1)S(1)} collective-permute-done((bf16[160,128]{1,0:T(8,128)(2,1)S(1)}, bf16[160,128]{1,0:T(8,128)(2,1)S(1)}, u32[]{:S(2)}, u32[]{:S(2)}) %collective-permute-start.7) | collective-permute-done | bytes 40992 | tf_op jit(solution)/shard_map/ppermute | solution.py:42
  32.8 1.2 %collective-permute-start.8 = (bf16[160,128]{1,0:T(8,128)(2,1)S(1)}, bf16[160,128]{1,0:T(8,128)(2,1)S(1)}, u32[]{:S(2)}, u32[]{:S(2)}) collective-permute-start(bf16[160,128]{1,0:T(8,128)(2,1)S(1)} %add.5), channel_id=1, source_target_pairs={{0,5},{1,2},{2,1},{3,6},{4,7},{5,0},{6,3},{7,4},{8,11},{9,12},{10,... | collective-permute-start | bytes 122888 | tf_op jit(solution)/shard_map/ppermute | solution.py:42
  34.0 0.2 collective-permute-done.12
  34.2 2.1 %collective-permute-done.8 = bf16[160,128]{1,0:T(8,128)(2,1)S(1)} collective-permute-done((bf16[160,128]{1,0:T(8,128)(2,1)S(1)}, bf16[160,128]{1,0:T(8,128)(2,1)S(1)}, u32[]{:S(2)}, u32[]{:S(2)}) %collective-permute-start.8) | collective-permute-done | bytes 40992 | tf_op jit(solution)/shard_map/ppermute | solution.py:42
  36.3 1.6 %collective-permute-start.13 = (bf16[320,128]{1,0:T(8,128)(2,1)S(1)}, bf16[320,128]{1,0:T(8,128)(2,1)S(1)}, u32[]{:S(2)}, u32[]{:S(2)}) collective-permute-start(bf16[320,128]{1,0:T(8,128)(2,1)S(1)} %bitcast.33), channel_id=1, source_target_pairs={{0,3},{1,4},{2,7},{3,0},{4,1},{5,6},{6,5},{7,2},{8,13},{9,10},{10,... | collective-permute-start | bytes 245768 | tf_op jit(solution)/shard_map/ppermute | solution.py:42
  37.9 1.0 %beyond.1 = (bf16[288,512]{1,0:T(8,128)(2,1)S(1)}, bf16[288,512]{1,0:T(8,128)(2,1)S(1)}) custom-call(bf16[8,128,256]{2,1,0:T(8,128)(2,1)S(1)} %copy-done.2, bf16[272,256]{1,0:T(8,128)(2,1)S(1)} %collective-permute-done.1.even_ref, bf16[272,256]{1,0:T(8,128)(2,1)S(1)} %collective-permute-done.2.odd_ref, bf16[2,8,256]{2,1,0:T(8,128)(2,1)S(1)} %get-tuple-element.41.left_ref, ...), custom_call_target="tpu_custom_call" | custom-call | flops 8000000000 | bytes 100000 | tf_op jit(solution)/shard_map/beyond/pallas_call | solution.py:639
  38.9 0.5 %collective-permute-done.14.other_ref = bf16[16,16,512]{2,1,0:T(8,128)(2,1)S(1)} collective-permute-done((bf16[16,16,512]{2,1,0:T(8,128)(2,1)S(1)}, bf16[16,16,512]{2,1,0:T(8,128)(2,1)S(1)}, u32[]{:S(2)}, u32[]{:S(2)}) %collective-permute-start.14) | collective-permute-done | bytes 262176 | tf_op jit(solution)/shard_map/ppermute | solution.py:42
  39.5 0.8 %collective-permute-done.13 = bf16[320,128]{1,0:T(8,128)(2,1)S(1)} collective-permute-done((bf16[320,128]{1,0:T(8,128)(2,1)S(1)}, bf16[320,128]{1,0:T(8,128)(2,1)S(1)}, u32[]{:S(2)}, u32[]{:S(2)}) %collective-permute-start.13) | collective-permute-done | bytes 81952 | tf_op jit(solution)/shard_map/ppermute | solution.py:42
  40.3 0.6 %collective-permute-start.15 = (bf16[640,128]{1,0:T(8,128)(2,1)S(1)}, bf16[640,128]{1,0:T(8,128)(2,1)S(1)}, u32[]{:S(2)}, u32[]{:S(2)}) collective-permute-start(bf16[640,128]{1,0:T(8,128)(2,1)S(1)} %bitcast.26), channel_id=1, source_target_pairs={{0,1},{1,0},{2,3},{3,2},{4,5},{5,4},{6,7},{7,6},{8,9},{9,8},{10,11... | collective-permute-start | bytes 491528 | tf_op jit(solution)/shard_map/ppermute | solution.py:42
  40.9 1.0 %prepare.1 = (bf16[4608,256]{1,0:T(8,128)(2,1)S(1)}, f32[512,512]{1,0:T(8,128)S(1)}) custom-call(bf16[2304,512]{1,0:T(8,128)(2,1)S(1)} %bitcast.25, bf16[512,512]{1,0:T(8,128)(2,1)S(1)} %bitcast.46), custom_call_target="tpu_custom_call" | custom-call | flops 2000000000 | bytes 6000000 | tf_op jit(solution)/shard_map/prepare/pallas_call | solution.py:664
  42.0 4.5 %grad_conv.1 = (f32[16,512]{1,0:T(8,128)}, bf16[1024,256]{1,0:T(8,128)(2,1)}) custom-call(bf16[640,128]{1,0:T(8,128)(2,1)S(1)} %bitcast.27, bf16[640,128]{1,0:T(8,128)(2,1)S(1)} %collective-permute-done.15.other_ref, f32[512,512]{1,0:T(8,128)S(1)} %get-tuple-element.68.both_ref, bf16[768,512]{1,0:T(8,128)(2,1)S(1)} %get-tuple-element.70.in_feat_ref, ...), custom_call_target="tpu_custom_call" | custom-call | tf_op jit(solution)/shard_map/grad_conv/pallas_call | solution.py:683
  (29 shorter events, 0.6 us)
Async XLA Ops:
  0.6 1.0 %copy-start.1 = (bf16[8,128,256]{2,1,0:T(8,128)(2,1)S(1)}, bf16[8,128,256]{2,1,0:T(8,128)(2,1)}, u32[]{:S(2)}) copy-start(bf16[8,128,256]{2,1,0:T(8,128)(2,1)} %own_ref.3) | copy-start | bytes 1572868
  1.7 1.4 %copy-start.3 = (f32[16,512]{1,0:T(8,128)S(1)}, f32[16,512]{1,0:T(8,128)}, u32[]{:S(2)}) copy-start(f32[16,512]{1,0:T(8,128)} %target_ref.1) | copy-start | bytes 98308
  1.7 8.9 %copy-start = (bf16[3,3,256,512]{3,2,1,0:T(8,128)(2,1)S(1)}, bf16[3,3,256,512]{3,2,1,0:T(8,128)(2,1)}, u32[]{:S(2)}) copy-start(bf16[3,3,256,512]{3,2,1,0:T(8,128)(2,1)} %param.5) | copy-start | bytes 7077892
  1.7 8.9 %copy-start.2 = (bf16[8,128,256]{2,1,0:T(8,128)(2,1)S(1)}, bf16[8,128,256]{2,1,0:T(8,128)(2,1)}, u32[]{:S(2)}) copy-start(bf16[8,128,256]{2,1,0:T(8,128)(2,1)} %own_ref.3) | copy-start | bytes 1572868
  1.7 8.9 %copy-start.4 = (bf16[512]{0:T(512)(128)(2,1)S(1)}, bf16[512]{0:T(512)(128)(2,1)}, u32[]{:S(2)}) copy-start(bf16[512]{0:T(512)(128)(2,1)} %bias_ref.1) | copy-start | bytes 3076
  1.7 1.3 %collective-permute-start = (bf16[2,8,256]{2,1,0:T(8,128)(2,1)S(1)}, bf16[2,8,256]{2,1,0:T(8,128)(2,1)S(1)}, u32[]{:S(2)}, u32[]{:S(2)}) collective-permute-start(bf16[2,8,256]{2,1,0:T(8,128)(2,1)S(1)} %column_rims.1), channel_id=1, source_target_pairs={{0,1},{1,0},{2,3},{3,2},{4,5},{5,4},{6,7},{7,6},{8,9},{9,8},{10,11... | collective-permute-start | bytes 24584 | tf_op jit(solution)/shard_map/ppermute | solution.py:565
  3.1 10.8 %collective-permute-start.1 = (bf16[272,256]{1,0:T(8,128)(2,1)S(1)}, bf16[272,256]{1,0:T(8,128)(2,1)S(1)}, u32[]{:S(2)}, u32[]{:S(2)}) collective-permute-start(bf16[272,256]{1,0:T(8,128)(2,1)S(1)} %get-tuple-element.39), channel_id=1, source_target_pairs={{0,2},{4,6},{8,10},{12,14},{16,18},{20,22},{24,26},{28,30},{2,0},{... | collective-permute-start | bytes 417800 | tf_op jit(solution)/shard_map/ppermute | solution.py:25
  6.0 9.1 %collective-permute-start.2 = (bf16[272,256]{1,0:T(8,128)(2,1)S(1)}, bf16[272,256]{1,0:T(8,128)(2,1)S(1)}, u32[]{:S(2)}, u32[]{:S(2)}) collective-permute-start(bf16[272,256]{1,0:T(8,128)(2,1)S(1)} %get-tuple-element.40), channel_id=1, source_target_pairs={{2,4},{6,8},{10,12},{14,16},{18,20},{22,24},{26,28},{30,0},{4,2},{... | collective-permute-start | bytes 417800 | tf_op jit(solution)/shard_map/ppermute | solution.py:25
  16.0 1.5 %collective-permute-start.3 = (bf16[640,128]{1,0:T(8,128)(2,1)S(1)}, bf16[640,128]{1,0:T(8,128)(2,1)S(1)}, u32[]{:S(2)}, u32[]{:S(2)}) collective-permute-start(bf16[640,128]{1,0:T(8,128)(2,1)S(1)} %get-tuple-element.46), channel_id=1, source_target_pairs={{0,1},{1,0},{2,3},{3,2},{4,5},{5,4},{6,7},{7,6},{8,9},{9,8},{10,11... | collective-permute-start | bytes 491528 | tf_op jit(solution)/shard_map/ppermute | solution.py:42
  17.4 3.9 %collective-permute-start.4 = (bf16[320,128]{1,0:T(8,128)(2,1)S(1)}, bf16[320,128]{1,0:T(8,128)(2,1)S(1)}, u32[]{:S(2)}, u32[]{:S(2)}) collective-permute-start(bf16[320,128]{1,0:T(8,128)(2,1)S(1)} %get-tuple-element.48), channel_id=1, source_target_pairs={{0,3},{1,4},{2,7},{3,0},{4,1},{5,6},{6,5},{7,2},{8,13},{9,10},{10,... | collective-permute-start | bytes 245768 | tf_op jit(solution)/shard_map/ppermute | solution.py:42
  17.9 4.4 %collective-permute-start.9 = (bf16[1,16,512]{2,1,0:T(8,128)(2,1)S(1)}, bf16[1,16,512]{2,1,0:T(8,128)(2,1)S(1)}, u32[]{:S(2)}, u32[]{:S(2)}) collective-permute-start(bf16[1,16,512]{2,1,0:T(8,128)(2,1)S(1)} %get-tuple-element.52), channel_id=1, source_target_pairs={{0,17},{1,16},{2,19},{3,18},{4,21},{5,20},{6,23},{7,22},{8,25},{9,... | collective-permute-start | bytes 49160 | tf_op jit(solution)/shard_map/ppermute | solution.py:42
  21.4 3.5 %collective-permute-start.5 = (bf16[160,128]{1,0:T(8,128)(2,1)S(1)}, bf16[160,128]{1,0:T(8,128)(2,1)S(1)}, u32[]{:S(2)}, u32[]{:S(2)}) collective-permute-start(bf16[160,128]{1,0:T(8,128)(2,1)S(1)} %get-tuple-element.50), channel_id=1, source_target_pairs={{0,5},{1,2},{2,1},{3,6},{4,7},{5,0},{6,3},{7,4},{8,11},{9,12},{10,... | collective-permute-start | bytes 122888 | tf_op jit(solution)/shard_map/ppermute | solution.py:42
  22.3 3.4 %collective-permute-start.10 = (bf16[2,16,512]{2,1,0:T(8,128)(2,1)S(1)}, bf16[2,16,512]{2,1,0:T(8,128)(2,1)S(1)}, u32[]{:S(2)}, u32[]{:S(2)}) collective-permute-start(bf16[2,16,512]{2,1,0:T(8,128)(2,1)S(1)} %bitcast.41), channel_id=1, source_target_pairs={{0,9},{1,8},{2,11},{3,10},{4,13},{5,12},{6,15},{7,14},{8,1},{9,0},... | collective-permute-start | bytes 98312 | tf_op jit(solution)/shard_map/ppermute | solution.py:42
  24.9 3.5 %collective-permute-start.6 = (bf16[160,128]{1,0:T(8,128)(2,1)S(1)}, bf16[160,128]{1,0:T(8,128)(2,1)S(1)}, u32[]{:S(2)}, u32[]{:S(2)}) collective-permute-start(bf16[160,128]{1,0:T(8,128)(2,1)S(1)} %add.3.keep_ref), channel_id=1, source_target_pairs={{0,9},{1,16},{2,19},{3,10},{4,21},{5,12},{6,15},{7,22},{8,25},{9,0... | collective-permute-start | bytes 122888 | tf_op jit(solution)/shard_map/ppermute | solution.py:42
  25.7 4.0 %collective-permute-start.11 = (bf16[4,16,512]{2,1,0:T(8,128)(2,1)S(1)}, bf16[4,16,512]{2,1,0:T(8,128)(2,1)S(1)}, u32[]{:S(2)}, u32[]{:S(2)}) collective-permute-start(bf16[4,16,512]{2,1,0:T(8,128)(2,1)S(1)} %bitcast.36), channel_id=1, source_target_pairs={{0,3},{1,4},{2,7},{3,0},{4,1},{5,6},{6,5},{7,2},{8,13},{9,10},{10,... | collective-permute-start | bytes 196616 | tf_op jit(solution)/shard_map/ppermute | solution.py:42
  28.4 4.4 %collective-permute-start.7 = (bf16[160,128]{1,0:T(8,128)(2,1)S(1)}, bf16[160,128]{1,0:T(8,128)(2,1)S(1)}, u32[]{:S(2)}, u32[]{:S(2)}) collective-permute-start(bf16[160,128]{1,0:T(8,128)(2,1)S(1)} %add.4.keep_ref), channel_id=1, source_target_pairs={{0,17},{1,8},{2,11},{3,18},{4,13},{5,20},{6,23},{7,14},{8,1},{9,24... | collective-permute-start | bytes 122888 | tf_op jit(solution)/shard_map/ppermute | solution.py:42
  29.7 4.5 %collective-permute-start.12 = (bf16[8,16,512]{2,1,0:T(8,128)(2,1)S(1)}, bf16[8,16,512]{2,1,0:T(8,128)(2,1)S(1)}, u32[]{:S(2)}, u32[]{:S(2)}) collective-permute-start(bf16[8,16,512]{2,1,0:T(8,128)(2,1)S(1)} %bitcast.30), channel_id=1, source_target_pairs={{0,5},{1,2},{2,1},{3,6},{4,7},{5,0},{6,3},{7,4},{8,11},{9,12},{10,... | collective-permute-start | bytes 393224 | tf_op jit(solution)/shard_map/ppermute | solution.py:42
  32.8 3.5 %collective-permute-start.8 = (bf16[160,128]{1,0:T(8,128)(2,1)S(1)}, bf16[160,128]{1,0:T(8,128)(2,1)S(1)}, u32[]{:S(2)}, u32[]{:S(2)}) collective-permute-start(bf16[160,128]{1,0:T(8,128)(2,1)S(1)} %add.5), channel_id=1, source_target_pairs={{0,5},{1,2},{2,1},{3,6},{4,7},{5,0},{6,3},{7,4},{8,11},{9,12},{10,... | collective-permute-start | bytes 122888 | tf_op jit(solution)/shard_map/ppermute | solution.py:42
  36.3 3.9 %collective-permute-start.13 = (bf16[320,128]{1,0:T(8,128)(2,1)S(1)}, bf16[320,128]{1,0:T(8,128)(2,1)S(1)}, u32[]{:S(2)}, u32[]{:S(2)}) collective-permute-start(bf16[320,128]{1,0:T(8,128)(2,1)S(1)} %bitcast.33), channel_id=1, source_target_pairs={{0,3},{1,4},{2,7},{3,0},{4,1},{5,6},{6,5},{7,2},{8,13},{9,10},{10,... | collective-permute-start | bytes 245768 | tf_op jit(solution)/shard_map/ppermute | solution.py:42
  37.9 1.5 %collective-permute-start.14 = (bf16[16,16,512]{2,1,0:T(8,128)(2,1)S(1)}, bf16[16,16,512]{2,1,0:T(8,128)(2,1)S(1)}, u32[]{:S(2)}, u32[]{:S(2)}) collective-permute-start(bf16[16,16,512]{2,1,0:T(8,128)(2,1)S(1)} %bitcast.28), channel_id=1, source_target_pairs={{0,1},{1,0},{2,3},{3,2},{4,5},{5,4},{6,7},{7,6},{8,9},{9,8},{10,11... | collective-permute-start | bytes 786440 | tf_op jit(solution)/shard_map/ppermute | solution.py:42
  40.3 1.6 %collective-permute-start.15 = (bf16[640,128]{1,0:T(8,128)(2,1)S(1)}, bf16[640,128]{1,0:T(8,128)(2,1)S(1)}, u32[]{:S(2)}, u32[]{:S(2)}) collective-permute-start(bf16[640,128]{1,0:T(8,128)(2,1)S(1)} %bitcast.26), channel_id=1, source_target_pairs={{0,1},{1,0},{2,3},{3,2},{4,5},{5,4},{6,7},{7,6},{8,9},{9,8},{10,11... | collective-permute-start | bytes 491528 | tf_op jit(solution)/shard_map/ppermute | solution.py:42

commit v8 on v7

--- a/solution.py
+++ b/solution.py
@@ -201,20 +201,28 @@
 
 
 def rim_kernel(canvas_ref, *out_refs):
-    cols = canvas_ref.shape[1]
+    even_ref, odd_ref = out_refs[-2:]
+    rows, cols, _ = canvas_ref.shape
     begin = canvas_ref[:, 0:16, :].astype(f32)
     end = canvas_ref[:, cols - 16 :, :].astype(f32)
     for c in range(2):
         pair = column(begin, c), column(end, 14 + c)
-        if len(out_refs) == 1:
+        if len(out_refs) == 3:
             out_refs[0][c] = jnp.where(lax.axis_index("cols") == 0, pair[1], pair[0]).astype(bf16)
         else:
             out_refs[0][c], out_refs[1][c] = pair[0].astype(bf16), pair[1].astype(bf16)
-
-
-def payload_kernel(canvas_ref, target_ref, *refs):
+    odd = lax.rem(lax.axis_index("rows"), 2)
+    for case, low_ref, high_ref in ((0, odd_ref, even_ref), (1, even_ref, odd_ref)):
+
+        @pl.when(odd == case)
+        def _():
+            for k in range(2):
+                at = slice(k * cols, (k + 1) * cols)
+                low_ref[at, :], high_ref[at, :] = canvas_ref[k], canvas_ref[rows - 2 + k]
+
+
+def payload_kernel(target_ref, *refs):
     even_ref, odd_ref, left_ref, right_ref, half_ref = refs[-5:]
-    rows, cols, width = canvas_ref.shape
     half_ref[0] = target_ref[...].astype(bf16)
     if len(refs) == 6:
         here = lax.axis_index("cols")
@@ -224,25 +232,18 @@
     else:
         left_ref[...], right_ref[...] = refs[0][...], refs[1][...]
     beyond = [ref[c].astype(f32) for ref in (left_ref, right_ref) for c in range(2)]
-
-    def fill(ref, r):
-        for k in range(2):
-            ref[k * cols : (k + 1) * cols, :] = canvas_ref[r + k]
-        rim = [part[r + k : r + k + 1] for k in range(2) for part in beyond]
-        rim = jnp.concatenate([*rim, jnp.zeros((8, width), f32)], axis=0)
-        ref[2 * cols :, :] = rim.astype(bf16)
+    rows, width = beyond[0].shape
+
+    def rim(r):
+        parts = [part[r + k : r + k + 1] for k in range(2) for part in beyond]
+        return jnp.concatenate([*parts, jnp.zeros((8, width), f32)], axis=0).astype(bf16)
 
     odd = lax.rem(lax.axis_index("rows"), 2)
-
-    @pl.when(odd == 0)
-    def _():
-        fill(even_ref, rows - 2)
-        fill(odd_ref, 0)
-
-    @pl.when(odd == 1)
-    def _():
-        fill(even_ref, 0)
-        fill(odd_ref, rows - 2)
+    for case, low_ref, high_ref in ((0, odd_ref, even_ref), (1, even_ref, odd_ref)):
+
+        @pl.when(odd == case)
+        def _():
+            low_ref[...], high_ref[...] = rim(0), rim(rows - 2)
 
 
 def moved_rows(row, before, after):
@@ -318,11 +319,15 @@
     gram_tiles(feat_ref[...], gram_ref)
 
 
-def halo_rows(even_ref, odd_ref, low_ref, high_ref):
+def halo_rows(halo_refs, low_ref, high_ref):
+    even_ref, odd_ref, even_rim_ref, odd_rim_ref = halo_refs
     row = lax.axis_index("rows")
     odd = lax.rem(row, 2)
-    low_ref[...] = jnp.where(odd == 0, odd_ref[...], even_ref[...])
-    high_ref[...] = jnp.where(odd == 0, even_ref[...], odd_ref[...])
+    main = even_ref.shape[0]
+    low_ref[0:main, :] = jnp.where(odd == 0, odd_ref[...], even_ref[...])
+    high_ref[0:main, :] = jnp.where(odd == 0, even_ref[...], odd_ref[...])
+    low_ref[main:, :] = jnp.where(odd == 0, odd_rim_ref[...], even_rim_ref[...])
+    high_ref[main:, :] = jnp.where(odd == 0, even_rim_ref[...], odd_rim_ref[...])
 
     @pl.when(row == 0)
     def _():
@@ -338,12 +343,12 @@
 
 
 def outer_kernel(
-    shape, even_ref, odd_ref, kernel_ref, base_ref, part_ref,
+    shape, even_ref, odd_ref, even_rim_ref, odd_rim_ref, kernel_ref, base_ref, part_ref,
     feat_ref, slope_ref, send_ref, keep_ref, low_ref, high_ref, cat_ref, gram_ref,
 ):
     tile_rows, tile_cols, in_width, out_width, step = shape
     span, main = 3 * in_width, 2 * tile_cols
-    halo_rows(even_ref, odd_ref, low_ref, high_ref)
+    halo_rows((even_ref, odd_ref, even_rim_ref, odd_rim_ref), low_ref, high_ref)
     for n, (source, at) in enumerate([(low_ref, tile_cols), (high_ref, 0)]):
         rim = source[main:, :].astype(f32)
         k = 4 * (1 - n)
@@ -370,11 +375,11 @@
 
 
 def beyond_kernel(
-    shape, own_ref, even_ref, odd_ref, left_ref, right_ref, kernel_ref, bias_ref, part_ref,
-    feat_ref, slope_ref, low_ref, high_ref, cat_ref, edge_ref,
+    shape, own_ref, even_ref, odd_ref, even_rim_ref, odd_rim_ref, left_ref, right_ref, kernel_ref, bias_ref,
+    part_ref, feat_ref, slope_ref, low_ref, high_ref, cat_ref, edge_ref,
 ):
     tile_rows, tile_cols, in_width, out_width, step = shape
-    halo_rows(even_ref, odd_ref, low_ref, high_ref)
+    halo_rows((even_ref, odd_ref, even_rim_ref, odd_rim_ref), low_ref, high_ref)
     first = (lax.axis_index("rows") > 0).astype(f32)
     last = (lax.axis_index("rows") < lax.axis_size("rows") - 1).astype(f32)
     left = (lax.axis_index("cols") > 0).astype(f32)
@@ -554,10 +559,12 @@
 
     rim_shape = jax.ShapeDtypeStruct((2, tile_rows, in_width), bf16)
     two = lax.axis_size("cols") == 2
-    rims = local(
+    count = lax.axis_size("rows")
+    main_shape = jax.ShapeDtypeStruct((2 * tile_cols, in_width), bf16)
+    *rims, even, odd = local(
         rim_kernel,
-        (rim_shape,) * (1 if two else 2),
-        "column_rims",
+        (*(rim_shape,) * (1 if two else 2), main_shape, main_shape),
+        "rims",
         canvas,
         cost_estimate=pl.CostEstimate(flops=4_000_000_000, bytes_accessed=600_000, transcendentals=0),
     )
@@ -565,19 +572,19 @@
         beyond = [lax.ppermute(rims[0], "cols", [(0, 1), (1, 0)])]
     else:
         beyond = shift_cols(rims[1], rims[0])
+    evens, odds = range(0, count, 2), range(1, count, 2)
+    even, odd = swap_rows(evens, even), swap_rows(odds, odd)
     payload_shape = jax.ShapeDtypeStruct((2 * tile_cols + edge, in_width), bf16)
+    end_shape = jax.ShapeDtypeStruct((edge, in_width), bf16)
     half_shape = jax.ShapeDtypeStruct((1, *target_gram.shape), bf16)
-    even, odd, left, right, rows = local(
+    even_rim, odd_rim, left, right, rows = local(
         payload_kernel,
-        (payload_shape, payload_shape, rim_shape, rim_shape, half_shape),
-        "row_payload",
-        canvas,
+        (end_shape, end_shape, rim_shape, rim_shape, half_shape),
+        "row_rims",
         target_gram,
         *beyond,
     )
-    count = lax.axis_size("rows")
-    even, odd = swap_rows(range(0, count, 2), even), swap_rows(range(1, count, 2), odd)
-
+    halo = [even, odd, swap_rows(evens, even_rim), swap_rows(odds, odd_rim)]
     bits = (lax.axis_size("rows") * lax.axis_size("cols")).bit_length() - 1
     gather = Gather(rows)
     far = list(reversed(range(3, bits)))
@@ -612,7 +619,7 @@
             jax.ShapeDtypeStruct(half_gram, bf16),
             jax.ShapeDtypeStruct(half_gram, f32),
         ),
-        in_specs=[vmem] * 5,
+        in_specs=[vmem] * 7,
         scratch_shapes=[
             *halo_scratch,
             pltpu.VMEM((2 * tile_cols, 3 * in_width), bf16),
@@ -620,7 +627,7 @@
         ],
         compiler_params=params,
         name="outer_rows",
-    )(even, odd, kernel, in_gram, part)
+    )(*halo, kernel, in_gram, part)
 
     exchanges = {
         "halve 0": [(bit,) for bit in far[:1]],
@@ -639,7 +646,7 @@
                 pl.pallas_call(
                     functools.partial(beyond_kernel, shape),
                     out_shape=(jax.ShapeDtypeStruct((outer, out_width), bf16),) * 2,
-                    in_specs=[vmem] * 8,
+                    in_specs=[vmem] * 10,
                     scratch_shapes=[
                         *halo_scratch,
                         pltpu.VMEM((4 * tile_cols, 3 * in_width), bf16),
@@ -648,7 +655,7 @@
                     compiler_params=params,
                     name="beyond",
                     cost_estimate=chained,
-                )(canvas, even, odd, left, right, kernel, bias, rim_sums)
+                )(canvas, *halo, left, right, kernel, bias, rim_sums)
             )
             gather.settle(sent)
             got, gather.rows, *_ = lax.optimization_barrier((got, gather.rows, *far_pixels))

time: 46.6 us -> 48.3 us (1.036)
  waiting for transfers between devices: 13.6 us -> 19.8 us
  starting transfers between devices: 20 us -> 15.4 us
    ppermute x13, starting transfers between devices: 12 us -> 5.79 us  [swap(): lax.ppermute(value, ('rows', 'cols'), [(i, i ^ flip(i)) for i in range(to...]
    ppermute x13, waiting for transfers between devices: 11.6 us -> 17.8 us  [swap(): lax.ppermute(value, ('rows', 'cols'), [(i, i ^ flip(i)) for i in range(to...]
    ppermute x2 -> x4, starting transfers between devices: 7.42 us -> 9.12 us  [swap_rows(): lax.ppermute(value, 'rows', pairs + [(target, source) for source, target...]
    ppermute x2 -> x4, waiting for transfers between devices: 1.14 us -> 1.98 us  [swap_rows(): lax.ppermute(value, 'rows', pairs + [(target, source) for source, target...]
    ppermute x1, waiting for transfers between devices: 0.83 us -> 0.01 us  [on_device(): beyond = [lax.ppermute(rims[0], 'cols', [(0, 1), (1, 0)])]]
  transfers between devices with their start and end apart: 16 -> 18, of which waited for: 14 -> 12; matrix products, arithmetic and copies ran while one was open for 0% -> 0% of each run, Pallas kernels for 12% -> 12%
where the time goes in v8:
time: 48.3 us; the launch traced here: 48.2 us
  waiting for transfers between devices  19.8 us (41%)
  starting transfers between devices  15.4 us (32%)
  Pallas kernels  11 us (23%)
  local copies, waits for them, and re-layouts  1.06 us (2%)
  between operations  0.81 us (2%)
    ppermute x13, waiting for transfers between devices, swap(): lax.ppermute(value, ('rows', 'cols'), [(i, i ^ flip(i)) for i in range(to...  17.8 us
    ppermute x4, starting transfers between devices, swap_rows(): lax.ppermute(value, 'rows', pairs + [(target, source) for source, target...  9.12 us
    ppermute x13, starting transfers between devices, swap(): lax.ppermute(value, ('rows', 'cols'), [(i, i ^ flip(i)) for i in range(to...  5.79 us
    pallas_call x1, Pallas kernels, on_device(): pl.pallas_call(functools.partial(backward_kernel, shape, pixel_total), ou...  4.45 us
    pallas_call x1, Pallas kernels, on_device(): pl.pallas_call(functools.partial(inner_kernel, shape), out_shape=(jax.Sha...  3.36 us
    ppermute x4, waiting for transfers between devices, swap_rows(): lax.ppermute(value, 'rows', pairs + [(target, source) for source, target...  1.98 us
    unnamed x10, local copies, waits for them, and re-layouts  1.06 us
    pallas_call x1, Pallas kernels, beside(): pl.pallas_call(functools.partial(beyond_kernel, shape), out_shape=(jax.Sh...  1.04 us
  transfers between devices with their start and end apart: 18, of which 12 were waited for; matrix products, arithmetic and copies ran while one was open for 0% of the time, Pallas kernels for 12%

profile of v8, /device:TPU:0, one launch (start us, length us, event | category | flops | bytes accessed | tf_op | source)
XLA Modules:
  0.0 48.2 jit_solution(10524869349885275990)
XLA Ops:
  0.7 1.0 %copy-done.2 = bf16[8,128,256]{2,1,0:T(8,128)(2,1)S(1)} copy-done((bf16[8,128,256]{2,1,0:T(8,128)(2,1)S(1)}, bf16[8,128,256]{2,1,0:T(8,128)(2,1)}, u32[]{:S(2)}) %copy-start.2) | copy-done | bytes 524312
  1.7 0.5 %collective-permute-start.2 = (bf16[2,8,256]{2,1,0:T(8,128)(2,1)S(1)}, bf16[2,8,256]{2,1,0:T(8,128)(2,1)S(1)}, u32[]{:S(2)}, u32[]{:S(2)}) collective-permute-start(bf16[2,8,256]{2,1,0:T(8,128)(2,1)S(1)} %get-tuple-element.44), channel_id=1, source_target_pairs={{0,1},{1,0},{2,3},{3,2},{4,5},{5,4},{6,7},{7,6},{8,9},{9,8},{10,11... | collective-permute-start | bytes 24584 | tf_op jit(solution)/shard_map/ppermute | solution.py:572
  2.3 2.6 %collective-permute-start = (bf16[256,256]{1,0:T(8,128)(2,1)S(1)}, bf16[256,256]{1,0:T(8,128)(2,1)S(1)}, u32[]{:S(2)}, u32[]{:S(2)}) collective-permute-start(bf16[256,256]{1,0:T(8,128)(2,1)S(1)} %get-tuple-element.42), channel_id=1, source_target_pairs={{0,2},{4,6},{8,10},{12,14},{16,18},{20,22},{24,26},{28,30},{2,0},{... | collective-permute-start | bytes 393224 | tf_op jit(solution)/shard_map/ppermute | solution.py:25
  4.8 4.5 %collective-permute-start.1 = (bf16[256,256]{1,0:T(8,128)(2,1)S(1)}, bf16[256,256]{1,0:T(8,128)(2,1)S(1)}, u32[]{:S(2)}, u32[]{:S(2)}) collective-permute-start(bf16[256,256]{1,0:T(8,128)(2,1)S(1)} %get-tuple-element.43), channel_id=1, source_target_pairs={{2,4},{6,8},{10,12},{14,16},{18,20},{22,24},{26,28},{30,0},{4,2},{... | collective-permute-start | bytes 393224 | tf_op jit(solution)/shard_map/ppermute | solution.py:25
  9.4 0.1 collective-permute-start.3
  9.5 2.0 %collective-permute-start.4 = (bf16[16,256]{1,0:T(8,128)(2,1)S(1)}, bf16[16,256]{1,0:T(8,128)(2,1)S(1)}, u32[]{:S(2)}, u32[]{:S(2)}) collective-permute-start(bf16[16,256]{1,0:T(8,128)(2,1)S(1)} %get-tuple-element.46), channel_id=1, source_target_pairs={{2,4},{6,8},{10,12},{14,16},{18,20},{22,24},{26,28},{30,0},{4,2},{... | collective-permute-start | bytes 24584 | tf_op jit(solution)/shard_map/ppermute | solution.py:25
  11.4 3.4 %inner_rows.1 = (bf16[768,512]{1,0:T(8,128)(2,1)S(1)}, bf16[768,512]{1,0:T(8,128)(2,1)S(1)}, f32[1280,128]{1,0:T(8,128)S(1)}, f32[1,512]{1,0:T(1,128)S(1)}, f32[512,512]{1,0:T(8,128)S(1)}) custom-call(bf16[8,128,256]{2,1,0:T(8,128)(2,1)S(1)} %copy-done.3, bf16[2,8,256]{2,1,0:T(8,128)(2,1)S(1)} %get-tuple-element.47.left_ref, ...), custom_call_target="tpu_custom_call" | custom-call | flops 2214592512 | bytes 6000000 | tf_op jit(solution)/shard_map/inner_rows/pallas_call | solution.py:592
  14.8 2.0 %collective-permute-done.4.odd_rim_ref = bf16[16,256]{1,0:T(8,128)(2,1)S(1)} collective-permute-done((bf16[16,256]{1,0:T(8,128)(2,1)S(1)}, bf16[16,256]{1,0:T(8,128)(2,1)S(1)}, u32[]{:S(2)}, u32[]{:S(2)}) %collective-permute-start.4) | collective-permute-done | bytes 8224 | tf_op jit(solution)/shard_map/ppermute | solution.py:25
  16.8 0.9 %outer_rows.1 = (bf16[256,512]{1,0:T(8,128)(2,1)S(1)}, bf16[256,512]{1,0:T(8,128)(2,1)S(1)}, bf16[640,128]{1,0:T(8,128)(2,1)S(1)}, f32[640,128]{1,0:T(8,128)S(1)}) custom-call(bf16[256,256]{1,0:T(8,128)(2,1)S(1)} %collective-permute-done.even_ref, bf16[256,256]{1,0:T(8,128)(2,1)S(1)} %collective-permute-done.1.odd_ref, ...), custom_call_target="tpu_custom_call" | custom-call | tf_op jit(solution)/shard_map/outer_rows/pallas_call | solution.py:614
  17.8 1.4 %collective-permute-done.5.got_ref = bf16[640,128]{1,0:T(8,128)(2,1)S(1)} collective-permute-done((bf16[640,128]{1,0:T(8,128)(2,1)S(1)}, bf16[640,128]{1,0:T(8,128)(2,1)S(1)}, u32[]{:S(2)}, u32[]{:S(2)}) %collective-permute-start.5) | collective-permute-done | bytes 163872 | tf_op jit(solution)/shard_map/ppermute | solution.py:42
  19.2 0.1 collective-permute-start.6
  19.3 0.3 collective-permute-start.11
  19.6 3.6 %collective-permute-done.6.got_ref = bf16[320,128]{1,0:T(8,128)(2,1)S(1)} collective-permute-done((bf16[320,128]{1,0:T(8,128)(2,1)S(1)}, bf16[320,128]{1,0:T(8,128)(2,1)S(1)}, u32[]{:S(2)}, u32[]{:S(2)}) %collective-permute-start.6) | collective-permute-done | bytes 81952 | tf_op jit(solution)/shard_map/ppermute | solution.py:42
  23.1 0.1 collective-permute-start.7
  23.2 0.2 collective-permute-done.11
  23.4 3.2 %collective-permute-done.7.got_ref = bf16[160,128]{1,0:T(8,128)(2,1)S(1)} collective-permute-done((bf16[160,128]{1,0:T(8,128)(2,1)S(1)}, bf16[160,128]{1,0:T(8,128)(2,1)S(1)}, u32[]{:S(2)}, u32[]{:S(2)}) %collective-permute-start.7) | collective-permute-done | bytes 40992 | tf_op jit(solution)/shard_map/ppermute | solution.py:42
  26.8 1.7 %collective-permute-start.13 = (bf16[4,16,512]{2,1,0:T(8,128)(2,1)S(1)}, bf16[4,16,512]{2,1,0:T(8,128)(2,1)S(1)}, u32[]{:S(2)}, u32[]{:S(2)}) collective-permute-start(bf16[4,16,512]{2,1,0:T(8,128)(2,1)S(1)} %bitcast.36), channel_id=1, source_target_pairs={{0,3},{1,4},{2,7},{3,0},{4,1},{5,6},{6,5},{7,2},{8,13},{9,10},{10,... | collective-permute-start | bytes 196616 | tf_op jit(solution)/shard_map/ppermute | solution.py:42
  28.5 1.7 %collective-permute-done.8.got_ref = bf16[160,128]{1,0:T(8,128)(2,1)S(1)} collective-permute-done((bf16[160,128]{1,0:T(8,128)(2,1)S(1)}, bf16[160,128]{1,0:T(8,128)(2,1)S(1)}, u32[]{:S(2)}, u32[]{:S(2)}) %collective-permute-start.8) | collective-permute-done | bytes 40992 | tf_op jit(solution)/shard_map/ppermute | solution.py:42
  30.1 0.1 collective-permute-start.9
  30.2 0.3 collective-permute-done.13
  30.5 1.7 %collective-permute-start.14 = (bf16[8,16,512]{2,1,0:T(8,128)(2,1)S(1)}, bf16[8,16,512]{2,1,0:T(8,128)(2,1)S(1)}, u32[]{:S(2)}, u32[]{:S(2)}) collective-permute-start(bf16[8,16,512]{2,1,0:T(8,128)(2,1)S(1)} %bitcast.30), channel_id=1, source_target_pairs={{0,5},{1,2},{2,1},{3,6},{4,7},{5,0},{6,3},{7,4},{8,11},{9,12},{10,... | collective-permute-start | bytes 393224 | tf_op jit(solution)/shard_map/ppermute | solution.py:42
  32.2 2.3 %collective-permute-done.9.got_ref = bf16[160,128]{1,0:T(8,128)(2,1)S(1)} collective-permute-done((bf16[160,128]{1,0:T(8,128)(2,1)S(1)}, bf16[160,128]{1,0:T(8,128)(2,1)S(1)}, u32[]{:S(2)}, u32[]{:S(2)}) %collective-permute-start.9) | collective-permute-done | bytes 40992 | tf_op jit(solution)/shard_map/ppermute | solution.py:42
  34.6 0.4 collective-permute-start.10
  35.0 3.0 %collective-permute-done.10 = bf16[160,128]{1,0:T(8,128)(2,1)S(1)} collective-permute-done((bf16[160,128]{1,0:T(8,128)(2,1)S(1)}, bf16[160,128]{1,0:T(8,128)(2,1)S(1)}, u32[]{:S(2)}, u32[]{:S(2)}) %collective-permute-start.10) | collective-permute-done | bytes 40992 | tf_op jit(solution)/shard_map/ppermute | solution.py:42
  38.1 0.4 collective-permute-start.15
  38.5 0.3 collective-permute-start.16
  38.8 1.0 %beyond.1 = (bf16[288,512]{1,0:T(8,128)(2,1)S(1)}, bf16[288,512]{1,0:T(8,128)(2,1)S(1)}) custom-call(bf16[8,128,256]{2,1,0:T(8,128)(2,1)S(1)} %copy-done.3, bf16[256,256]{1,0:T(8,128)(2,1)S(1)} %collective-permute-done.even_ref, bf16[256,256]{1,0:T(8,128)(2,1)S(1)} %collective-permute-done.1.odd_ref, ...), custom_call_target="tpu_custom_call" | custom-call | flops 8000000000 | bytes 100000 | tf_op jit(solution)/shard_map/beyond/pallas_call | solution.py:646
  39.8 0.2 collective-permute-done.16.other_ref
  40.1 1.9 %collective-permute-done.15 = bf16[320,128]{1,0:T(8,128)(2,1)S(1)} collective-permute-done((bf16[320,128]{1,0:T(8,128)(2,1)S(1)}, bf16[320,128]{1,0:T(8,128)(2,1)S(1)}, u32[]{:S(2)}, u32[]{:S(2)}) %collective-permute-start.15) | collective-permute-done | bytes 81952 | tf_op jit(solution)/shard_map/ppermute | solution.py:42
  42.0 0.6 %collective-permute-start.17 = (bf16[640,128]{1,0:T(8,128)(2,1)S(1)}, bf16[640,128]{1,0:T(8,128)(2,1)S(1)}, u32[]{:S(2)}, u32[]{:S(2)}) collective-permute-start(bf16[640,128]{1,0:T(8,128)(2,1)S(1)} %bitcast.26), channel_id=1, source_target_pairs={{0,1},{1,0},{2,3},{3,2},{4,5},{5,4},{6,7},{7,6},{8,9},{9,8},{10,11... | collective-permute-start | bytes 491528 | tf_op jit(solution)/shard_map/ppermute | solution.py:42
  42.7 1.0 %prepare.1 = (bf16[4608,256]{1,0:T(8,128)(2,1)S(1)}, f32[512,512]{1,0:T(8,128)S(1)}) custom-call(bf16[2304,512]{1,0:T(8,128)(2,1)S(1)} %bitcast.25, bf16[512,512]{1,0:T(8,128)(2,1)S(1)} %bitcast.46), custom_call_target="tpu_custom_call" | custom-call | flops 2000000000 | bytes 6000000 | tf_op jit(solution)/shard_map/prepare/pallas_call | solution.py:671
  43.7 4.5 %grad_conv.1 = (f32[16,512]{1,0:T(8,128)}, bf16[1024,256]{1,0:T(8,128)(2,1)}) custom-call(bf16[640,128]{1,0:T(8,128)(2,1)S(1)} %bitcast.27, bf16[640,128]{1,0:T(8,128)(2,1)S(1)} %collective-permute-done.17.other_ref, f32[512,512]{1,0:T(8,128)S(1)} %get-tuple-element.74.both_ref, bf16[768,512]{1,0:T(8,128)(2,1)S(1)} %get-tuple-element.76.in_feat_ref, ...), custom_call_target="tpu_custom_call" | custom-call | tf_op jit(solution)/shard_map/grad_conv/pallas_call | solution.py:690
  (33 shorter events, 0.6 us)
Async XLA Ops:
  0.6 8.7 %copy-start.1 = (f32[16,512]{1,0:T(8,128)S(1)}, f32[16,512]{1,0:T(8,128)}, u32[]{:S(2)}) copy-start(f32[16,512]{1,0:T(8,128)} %target_ref.1) | copy-start | bytes 98308
  0.6 1.0 %copy-start.2 = (bf16[8,128,256]{2,1,0:T(8,128)(2,1)S(1)}, bf16[8,128,256]{2,1,0:T(8,128)(2,1)}, u32[]{:S(2)}) copy-start(bf16[8,128,256]{2,1,0:T(8,128)(2,1)} %own_ref.3) | copy-start | bytes 1572868
  1.7 9.7 %copy-start = (bf16[3,3,256,512]{3,2,1,0:T(8,128)(2,1)S(1)}, bf16[3,3,256,512]{3,2,1,0:T(8,128)(2,1)}, u32[]{:S(2)}) copy-start(bf16[3,3,256,512]{3,2,1,0:T(8,128)(2,1)} %param.5) | copy-start | bytes 7077892
  1.7 9.7 %copy-start.3 = (bf16[8,128,256]{2,1,0:T(8,128)(2,1)S(1)}, bf16[8,128,256]{2,1,0:T(8,128)(2,1)}, u32[]{:S(2)}) copy-start(bf16[8,128,256]{2,1,0:T(8,128)(2,1)} %own_ref.3) | copy-start | bytes 1572868
  1.7 9.7 %copy-start.4 = (bf16[512]{0:T(512)(128)(2,1)S(1)}, bf16[512]{0:T(512)(128)(2,1)}, u32[]{:S(2)}) copy-start(bf16[512]{0:T(512)(128)(2,1)} %bias_ref.1) | copy-start | bytes 3076
  1.7 7.6 %collective-permute-start.2 = (bf16[2,8,256]{2,1,0:T(8,128)(2,1)S(1)}, bf16[2,8,256]{2,1,0:T(8,128)(2,1)S(1)}, u32[]{:S(2)}, u32[]{:S(2)}) collective-permute-start(bf16[2,8,256]{2,1,0:T(8,128)(2,1)S(1)} %get-tuple-element.44), channel_id=1, source_target_pairs={{0,1},{1,0},{2,3},{3,2},{4,5},{5,4},{6,7},{7,6},{8,9},{9,8},{10,11... | collective-permute-start | bytes 24584 | tf_op jit(solution)/shard_map/ppermute | solution.py:572
  2.3 14.5 %collective-permute-start = (bf16[256,256]{1,0:T(8,128)(2,1)S(1)}, bf16[256,256]{1,0:T(8,128)(2,1)S(1)}, u32[]{:S(2)}, u32[]{:S(2)}) collective-permute-start(bf16[256,256]{1,0:T(8,128)(2,1)S(1)} %get-tuple-element.42), channel_id=1, source_target_pairs={{0,2},{4,6},{8,10},{12,14},{16,18},{20,22},{24,26},{28,30},{2,0},{... | collective-permute-start | bytes 393224 | tf_op jit(solution)/shard_map/ppermute | solution.py:25
  4.8 12.0 %collective-permute-start.1 = (bf16[256,256]{1,0:T(8,128)(2,1)S(1)}, bf16[256,256]{1,0:T(8,128)(2,1)S(1)}, u32[]{:S(2)}, u32[]{:S(2)}) collective-permute-start(bf16[256,256]{1,0:T(8,128)(2,1)S(1)} %get-tuple-element.43), channel_id=1, source_target_pairs={{2,4},{6,8},{10,12},{14,16},{18,20},{22,24},{26,28},{30,0},{4,2},{... | collective-permute-start | bytes 393224 | tf_op jit(solution)/shard_map/ppermute | solution.py:25
  9.4 5.4 %collective-permute-start.3 = (bf16[16,256]{1,0:T(8,128)(2,1)S(1)}, bf16[16,256]{1,0:T(8,128)(2,1)S(1)}, u32[]{:S(2)}, u32[]{:S(2)}) collective-permute-start(bf16[16,256]{1,0:T(8,128)(2,1)S(1)} %get-tuple-element.45), channel_id=1, source_target_pairs={{0,2},{4,6},{8,10},{12,14},{16,18},{20,22},{24,26},{28,30},{2,0},{... | collective-permute-start | bytes 24584 | tf_op jit(solution)/shard_map/ppermute | solution.py:25
  9.5 7.3 %collective-permute-start.4 = (bf16[16,256]{1,0:T(8,128)(2,1)S(1)}, bf16[16,256]{1,0:T(8,128)(2,1)S(1)}, u32[]{:S(2)}, u32[]{:S(2)}) collective-permute-start(bf16[16,256]{1,0:T(8,128)(2,1)S(1)} %get-tuple-element.46), channel_id=1, source_target_pairs={{2,4},{6,8},{10,12},{14,16},{18,20},{22,24},{26,28},{30,0},{4,2},{... | collective-permute-start | bytes 24584 | tf_op jit(solution)/shard_map/ppermute | solution.py:25
  17.7 1.5 %collective-permute-start.5 = (bf16[640,128]{1,0:T(8,128)(2,1)S(1)}, bf16[640,128]{1,0:T(8,128)(2,1)S(1)}, u32[]{:S(2)}, u32[]{:S(2)}) collective-permute-start(bf16[640,128]{1,0:T(8,128)(2,1)S(1)} %get-tuple-element.52), channel_id=1, source_target_pairs={{0,1},{1,0},{2,3},{3,2},{4,5},{5,4},{6,7},{7,6},{8,9},{9,8},{10,11... | collective-permute-start | bytes 491528 | tf_op jit(solution)/shard_map/ppermute | solution.py:42
  19.2 3.9 %collective-permute-start.6 = (bf16[320,128]{1,0:T(8,128)(2,1)S(1)}, bf16[320,128]{1,0:T(8,128)(2,1)S(1)}, u32[]{:S(2)}, u32[]{:S(2)}) collective-permute-start(bf16[320,128]{1,0:T(8,128)(2,1)S(1)} %get-tuple-element.54), channel_id=1, source_target_pairs={{0,3},{1,4},{2,7},{3,0},{4,1},{5,6},{6,5},{7,2},{8,13},{9,10},{10,... | collective-permute-start | bytes 245768 | tf_op jit(solution)/shard_map/ppermute | solution.py:42
  19.3 4.1 %collective-permute-start.11 = (bf16[1,16,512]{2,1,0:T(8,128)(2,1)S(1)}, bf16[1,16,512]{2,1,0:T(8,128)(2,1)S(1)}, u32[]{:S(2)}, u32[]{:S(2)}) collective-permute-start(bf16[1,16,512]{2,1,0:T(8,128)(2,1)S(1)} %get-tuple-element.58), channel_id=1, source_target_pairs={{0,17},{1,16},{2,19},{3,18},{4,21},{5,20},{6,23},{7,22},{8,25},{9,... | collective-permute-start | bytes 49160 | tf_op jit(solution)/shard_map/ppermute | solution.py:42
  23.1 3.5 %collective-permute-start.7 = (bf16[160,128]{1,0:T(8,128)(2,1)S(1)}, bf16[160,128]{1,0:T(8,128)(2,1)S(1)}, u32[]{:S(2)}, u32[]{:S(2)}) collective-permute-start(bf16[160,128]{1,0:T(8,128)(2,1)S(1)} %get-tuple-element.56), channel_id=1, source_target_pairs={{0,5},{1,2},{2,1},{3,6},{4,7},{5,0},{6,3},{7,4},{8,11},{9,12},{10,... | collective-permute-start | bytes 122888 | tf_op jit(solution)/shard_map/ppermute | solution.py:42
  23.4 3.3 %collective-permute-start.12 = (bf16[2,16,512]{2,1,0:T(8,128)(2,1)S(1)}, bf16[2,16,512]{2,1,0:T(8,128)(2,1)S(1)}, u32[]{:S(2)}, u32[]{:S(2)}) collective-permute-start(bf16[2,16,512]{2,1,0:T(8,128)(2,1)S(1)} %bitcast.41), channel_id=1, source_target_pairs={{0,9},{1,8},{2,11},{3,10},{4,13},{5,12},{6,15},{7,14},{8,1},{9,0},... | collective-permute-start | bytes 98312 | tf_op jit(solution)/shard_map/ppermute | solution.py:42
  26.6 3.5 %collective-permute-start.8 = (bf16[160,128]{1,0:T(8,128)(2,1)S(1)}, bf16[160,128]{1,0:T(8,128)(2,1)S(1)}, u32[]{:S(2)}, u32[]{:S(2)}) collective-permute-start(bf16[160,128]{1,0:T(8,128)(2,1)S(1)} %add.3.keep_ref), channel_id=1, source_target_pairs={{0,9},{1,16},{2,19},{3,10},{4,21},{5,12},{6,15},{7,22},{8,25},{9,0... | collective-permute-start | bytes 122888 | tf_op jit(solution)/shard_map/ppermute | solution.py:42
  26.8 3.8 %collective-permute-start.13 = (bf16[4,16,512]{2,1,0:T(8,128)(2,1)S(1)}, bf16[4,16,512]{2,1,0:T(8,128)(2,1)S(1)}, u32[]{:S(2)}, u32[]{:S(2)}) collective-permute-start(bf16[4,16,512]{2,1,0:T(8,128)(2,1)S(1)} %bitcast.36), channel_id=1, source_target_pairs={{0,3},{1,4},{2,7},{3,0},{4,1},{5,6},{6,5},{7,2},{8,13},{9,10},{10,... | collective-permute-start | bytes 196616 | tf_op jit(solution)/shard_map/ppermute | solution.py:42
  30.1 4.4 %collective-permute-start.9 = (bf16[160,128]{1,0:T(8,128)(2,1)S(1)}, bf16[160,128]{1,0:T(8,128)(2,1)S(1)}, u32[]{:S(2)}, u32[]{:S(2)}) collective-permute-start(bf16[160,128]{1,0:T(8,128)(2,1)S(1)} %add.4.keep_ref), channel_id=1, source_target_pairs={{0,17},{1,8},{2,11},{3,18},{4,13},{5,20},{6,23},{7,14},{8,1},{9,24... | collective-permute-start | bytes 122888 | tf_op jit(solution)/shard_map/ppermute | solution.py:42
  30.5 4.5 %collective-permute-start.14 = (bf16[8,16,512]{2,1,0:T(8,128)(2,1)S(1)}, bf16[8,16,512]{2,1,0:T(8,128)(2,1)S(1)}, u32[]{:S(2)}, u32[]{:S(2)}) collective-permute-start(bf16[8,16,512]{2,1,0:T(8,128)(2,1)S(1)} %bitcast.30), channel_id=1, source_target_pairs={{0,5},{1,2},{2,1},{3,6},{4,7},{5,0},{6,3},{7,4},{8,11},{9,12},{10,... | collective-permute-start | bytes 393224 | tf_op jit(solution)/shard_map/ppermute | solution.py:42
  34.6 3.5 %collective-permute-start.10 = (bf16[160,128]{1,0:T(8,128)(2,1)S(1)}, bf16[160,128]{1,0:T(8,128)(2,1)S(1)}, u32[]{:S(2)}, u32[]{:S(2)}) collective-permute-start(bf16[160,128]{1,0:T(8,128)(2,1)S(1)} %add.5), channel_id=1, source_target_pairs={{0,5},{1,2},{2,1},{3,6},{4,7},{5,0},{6,3},{7,4},{8,11},{9,12},{10,... | collective-permute-start | bytes 122888 | tf_op jit(solution)/shard_map/ppermute | solution.py:42
  38.1 3.9 %collective-permute-start.15 = (bf16[320,128]{1,0:T(8,128)(2,1)S(1)}, bf16[320,128]{1,0:T(8,128)(2,1)S(1)}, u32[]{:S(2)}, u32[]{:S(2)}) collective-permute-start(bf16[320,128]{1,0:T(8,128)(2,1)S(1)} %bitcast.33), channel_id=1, source_target_pairs={{0,3},{1,4},{2,7},{3,0},{4,1},{5,6},{6,5},{7,2},{8,13},{9,10},{10,... | collective-permute-start | bytes 245768 | tf_op jit(solution)/shard_map/ppermute | solution.py:42
  38.5 1.5 %collective-permute-start.16 = (bf16[16,16,512]{2,1,0:T(8,128)(2,1)S(1)}, bf16[16,16,512]{2,1,0:T(8,128)(2,1)S(1)}, u32[]{:S(2)}, u32[]{:S(2)}) collective-permute-start(bf16[16,16,512]{2,1,0:T(8,128)(2,1)S(1)} %bitcast.28), channel_id=1, source_target_pairs={{0,1},{1,0},{2,3},{3,2},{4,5},{5,4},{6,7},{7,6},{8,9},{9,8},{10,11... | collective-permute-start | bytes 786440 | tf_op jit(solution)/shard_map/ppermute | solution.py:42
  42.0 1.7 %collective-permute-start.17 = (bf16[640,128]{1,0:T(8,128)(2,1)S(1)}, bf16[640,128]{1,0:T(8,128)(2,1)S(1)}, u32[]{:S(2)}, u32[]{:S(2)}) collective-permute-start(bf16[640,128]{1,0:T(8,128)(2,1)S(1)} %bitcast.26), channel_id=1, source_target_pairs={{0,1},{1,0},{2,3},{3,2},{4,5},{5,4},{6,7},{7,6},{8,9},{9,8},{10,11... | collective-permute-start | bytes 491528 | tf_op jit(solution)/shard_map/ppermute | solution.py:42

commit v9 on v8

--- a/solution.py
+++ b/solution.py
@@ -20,9 +20,15 @@
 
 
 def swap_rows(low, value):
-    count = lax.axis_size("rows")
-    pairs = [(i, (i + 1) % count) for i in low]
-    return lax.ppermute(value, "rows", pairs + [(target, source) for source, target in pairs])
+    count, cols = lax.axis_size("rows"), lax.axis_size("cols")
+    partner = {i: i + 1 for i in low if i + 1 < count}
+    partner.update({i + 1: i for i in low if i + 1 < count})
+    perm = [
+        (r * cols + c, partner[r] * cols + c if r in partner else r * cols + (c ^ 1))
+        for r in range(count)
+        for c in range(cols)
+    ]
+    return lax.ppermute(value, ("rows", "cols"), perm)
 
 
 def shift_cols(last, first):

time: 48.3 us -> 45.1 us (0.934)
  waiting for transfers between devices: 19.8 us -> 9.42 us
  starting transfers between devices: 15.4 us -> 22.6 us
    ppermute x13, starting transfers between devices: 5.79 us -> 16.5 us  [swap(): lax.ppermute(value, ('rows', 'cols'), [(i, i ^ flip(i)) for i in range(to...]
    ppermute x13, waiting for transfers between devices: 17.8 us -> 8.73 us  [swap(): lax.ppermute(value, ('rows', 'cols'), [(i, i ^ flip(i)) for i in range(to...]
    ppermute x4, starting transfers between devices: 9.12 us -> 5.62 us  [swap_rows(): return lax.ppermute(value, ('rows', 'cols'), perm)]
    ppermute x4, waiting for transfers between devices: 1.98 us -> 0.69 us  [swap_rows(): return lax.ppermute(value, ('rows', 'cols'), perm)]
  transfers between devices with their start and end apart: 18 -> 18, of which waited for: 12 -> 11; matrix products, arithmetic and copies ran while one was open for 0% -> 0% of each run, Pallas kernels for 12% -> 12%
where the time goes in v9:
time: 45.1 us; the launch traced here: 44.9 us
  starting transfers between devices  22.6 us (50%)
  Pallas kernels  11.1 us (25%)
  waiting for transfers between devices  9.42 us (21%)
  local copies, waits for them, and re-layouts  1.06 us (2%)
  between operations  0.78 us (2%)
    ppermute x13, starting transfers between devices, swap(): lax.ppermute(value, ('rows', 'cols'), [(i, i ^ flip(i)) for i in range(to...  16.5 us
    ppermute x13, waiting for transfers between devices, swap(): lax.ppermute(value, ('rows', 'cols'), [(i, i ^ flip(i)) for i in range(to...  8.73 us
    ppermute x4, starting transfers between devices, swap_rows(): return lax.ppermute(value, ('rows', 'cols'), perm)  5.62 us
    pallas_call x1, Pallas kernels, on_device(): pl.pallas_call(functools.partial(backward_kernel, shape, pixel_total), ou...  4.45 us
    pallas_call x1, Pallas kernels, on_device(): pl.pallas_call(functools.partial(inner_kernel, shape), out_shape=(jax.Sha...  3.36 us
    unnamed x10, local copies, waits for them, and re-layouts  1.06 us
    pallas_call x1, Pallas kernels, beside(): pl.pallas_call(functools.partial(beyond_kernel, shape), out_shape=(jax.Sh...  1.03 us
    pallas_call x1, Pallas kernels, beside(): pl.pallas_call(prepare_kernel, out_shape=(jax.ShapeDtypeStruct((9 * out_w...  0.97 us
  transfers between devices with their start and end apart: 18, of which 11 were waited for; matrix products, arithmetic and copies ran while one was open for 0% of the time, Pallas kernels for 12%

profile of v9, /device:TPU:0, one launch (start us, length us, event | category | flops | bytes accessed | tf_op | source)
XLA Modules:
  0.0 44.9 jit_solution(4229373213339099215)
XLA Ops:
  0.7 1.0 %copy-done.2 = bf16[8,128,256]{2,1,0:T(8,128)(2,1)S(1)} copy-done((bf16[8,128,256]{2,1,0:T(8,128)(2,1)S(1)}, bf16[8,128,256]{2,1,0:T(8,128)(2,1)}, u32[]{:S(2)}) %copy-start.2) | copy-done | bytes 524312
  1.7 0.5 %collective-permute-start.2 = (bf16[2,8,256]{2,1,0:T(8,128)(2,1)S(1)}, bf16[2,8,256]{2,1,0:T(8,128)(2,1)S(1)}, u32[]{:S(2)}, u32[]{:S(2)}) collective-permute-start(bf16[2,8,256]{2,1,0:T(8,128)(2,1)S(1)} %get-tuple-element.44), channel_id=1, source_target_pairs={{0,1},{1,0},{2,3},{3,2},{4,5},{5,4},{6,7},{7,6},{8,9},{9,8},{10,11... | collective-permute-start | bytes 24584 | tf_op jit(solution)/shard_map/ppermute | solution.py:578
  2.3 2.6 %collective-permute-start = (bf16[256,256]{1,0:T(8,128)(2,1)S(1)}, bf16[256,256]{1,0:T(8,128)(2,1)S(1)}, u32[]{:S(2)}, u32[]{:S(2)}) collective-permute-start(bf16[256,256]{1,0:T(8,128)(2,1)S(1)} %get-tuple-element.42), channel_id=1, source_target_pairs={{0,2},{1,3},{2,0},{3,1},{4,6},{5,7},{6,4},{7,5},{8,10},{9,11},{10,... | collective-permute-start | bytes 393224 | tf_op jit(solution)/shard_map/ppermute | solution.py:31
  4.8 0.2 collective-permute-start.1
  5.0 2.9 %collective-permute-start.3 = (bf16[16,256]{1,0:T(8,128)(2,1)S(1)}, bf16[16,256]{1,0:T(8,128)(2,1)S(1)}, u32[]{:S(2)}, u32[]{:S(2)}) collective-permute-start(bf16[16,256]{1,0:T(8,128)(2,1)S(1)} %get-tuple-element.45), channel_id=1, source_target_pairs={{0,2},{1,3},{2,0},{3,1},{4,6},{5,7},{6,4},{7,5},{8,10},{9,11},{10,... | collective-permute-start | bytes 24584 | tf_op jit(solution)/shard_map/ppermute | solution.py:31
  7.9 3.4 %inner_rows.1 = (bf16[768,512]{1,0:T(8,128)(2,1)S(1)}, bf16[768,512]{1,0:T(8,128)(2,1)S(1)}, f32[1280,128]{1,0:T(8,128)S(1)}, f32[1,512]{1,0:T(1,128)S(1)}, f32[512,512]{1,0:T(8,128)S(1)}) custom-call(bf16[8,128,256]{2,1,0:T(8,128)(2,1)S(1)} %copy-done.3, bf16[2,8,256]{2,1,0:T(8,128)(2,1)S(1)} %get-tuple-element.47.left_ref, ...), custom_call_target="tpu_custom_call" | custom-call | flops 2214592512 | bytes 6000000 | tf_op jit(solution)/shard_map/inner_rows/pallas_call | solution.py:598
  11.3 0.7 %collective-permute-done.3.even_rim_ref = bf16[16,256]{1,0:T(8,128)(2,1)S(1)} collective-permute-done((bf16[16,256]{1,0:T(8,128)(2,1)S(1)}, bf16[16,256]{1,0:T(8,128)(2,1)S(1)}, u32[]{:S(2)}, u32[]{:S(2)}) %collective-permute-start.3) | collective-permute-done | bytes 8224 | tf_op jit(solution)/shard_map/ppermute | solution.py:31
  12.0 0.9 %outer_rows.1 = (bf16[256,512]{1,0:T(8,128)(2,1)S(1)}, bf16[256,512]{1,0:T(8,128)(2,1)S(1)}, bf16[640,128]{1,0:T(8,128)(2,1)S(1)}, f32[640,128]{1,0:T(8,128)S(1)}) custom-call(bf16[256,256]{1,0:T(8,128)(2,1)S(1)} %collective-permute-done.even_ref, bf16[256,256]{1,0:T(8,128)(2,1)S(1)} %collective-permute-done.1.odd_ref, ...), custom_call_target="tpu_custom_call" | custom-call | tf_op jit(solution)/shard_map/outer_rows/pallas_call | solution.py:620
  13.0 1.4 %collective-permute-done.5.got_ref = bf16[640,128]{1,0:T(8,128)(2,1)S(1)} collective-permute-done((bf16[640,128]{1,0:T(8,128)(2,1)S(1)}, bf16[640,128]{1,0:T(8,128)(2,1)S(1)}, u32[]{:S(2)}, u32[]{:S(2)}) %collective-permute-start.5) | collective-permute-done | bytes 163872 | tf_op jit(solution)/shard_map/ppermute | solution.py:48
  14.4 2.6 %collective-permute-start.6 = (bf16[320,128]{1,0:T(8,128)(2,1)S(1)}, bf16[320,128]{1,0:T(8,128)(2,1)S(1)}, u32[]{:S(2)}, u32[]{:S(2)}) collective-permute-start(bf16[320,128]{1,0:T(8,128)(2,1)S(1)} %get-tuple-element.54), channel_id=1, source_target_pairs={{0,3},{1,4},{2,7},{3,0},{4,1},{5,6},{6,5},{7,2},{8,13},{9,10},{10,... | collective-permute-start | bytes 245768 | tf_op jit(solution)/shard_map/ppermute | solution.py:48
  17.0 2.6 %collective-permute-start.11 = (bf16[1,16,512]{2,1,0:T(8,128)(2,1)S(1)}, bf16[1,16,512]{2,1,0:T(8,128)(2,1)S(1)}, u32[]{:S(2)}, u32[]{:S(2)}) collective-permute-start(bf16[1,16,512]{2,1,0:T(8,128)(2,1)S(1)} %get-tuple-element.58), channel_id=1, source_target_pairs={{0,17},{1,16},{2,19},{3,18},{4,21},{5,20},{6,23},{7,22},{8,25},{9,... | collective-permute-start | bytes 49160 | tf_op jit(solution)/shard_map/ppermute | solution.py:48
  19.6 0.9 %collective-permute-start.7 = (bf16[160,128]{1,0:T(8,128)(2,1)S(1)}, bf16[160,128]{1,0:T(8,128)(2,1)S(1)}, u32[]{:S(2)}, u32[]{:S(2)}) collective-permute-start(bf16[160,128]{1,0:T(8,128)(2,1)S(1)} %get-tuple-element.56), channel_id=1, source_target_pairs={{0,5},{1,2},{2,1},{3,6},{4,7},{5,0},{6,3},{7,4},{8,11},{9,12},{10,... | collective-permute-start | bytes 122888 | tf_op jit(solution)/shard_map/ppermute | solution.py:48
  20.4 0.6 %collective-permute-done.11 = bf16[1,16,512]{2,1,0:T(8,128)(2,1)S(1)} collective-permute-done((bf16[1,16,512]{2,1,0:T(8,128)(2,1)S(1)}, bf16[1,16,512]{2,1,0:T(8,128)(2,1)S(1)}, u32[]{:S(2)}, u32[]{:S(2)}) %collective-permute-start.11) | collective-permute-done | bytes 16416 | tf_op jit(solution)/shard_map/ppermute | solution.py:48
  21.1 1.6 %collective-permute-start.12 = (bf16[2,16,512]{2,1,0:T(8,128)(2,1)S(1)}, bf16[2,16,512]{2,1,0:T(8,128)(2,1)S(1)}, u32[]{:S(2)}, u32[]{:S(2)}) collective-permute-start(bf16[2,16,512]{2,1,0:T(8,128)(2,1)S(1)} %bitcast.41), channel_id=1, source_target_pairs={{0,9},{1,8},{2,11},{3,10},{4,13},{5,12},{6,15},{7,14},{8,1},{9,0},... | collective-permute-start | bytes 98312 | tf_op jit(solution)/shard_map/ppermute | solution.py:48
  22.6 0.5 %collective-permute-done.7.got_ref = bf16[160,128]{1,0:T(8,128)(2,1)S(1)} collective-permute-done((bf16[160,128]{1,0:T(8,128)(2,1)S(1)}, bf16[160,128]{1,0:T(8,128)(2,1)S(1)}, u32[]{:S(2)}, u32[]{:S(2)}) %collective-permute-start.7) | collective-permute-done | bytes 40992 | tf_op jit(solution)/shard_map/ppermute | solution.py:48
  23.1 1.8 %collective-permute-start.8 = (bf16[160,128]{1,0:T(8,128)(2,1)S(1)}, bf16[160,128]{1,0:T(8,128)(2,1)S(1)}, u32[]{:S(2)}, u32[]{:S(2)}) collective-permute-start(bf16[160,128]{1,0:T(8,128)(2,1)S(1)} %add.3.keep_ref), channel_id=1, source_target_pairs={{0,9},{1,16},{2,19},{3,10},{4,21},{5,12},{6,15},{7,22},{8,25},{9,0... | collective-permute-start | bytes 122888 | tf_op jit(solution)/shard_map/ppermute | solution.py:48
  24.9 1.2 %collective-permute-start.13 = (bf16[4,16,512]{2,1,0:T(8,128)(2,1)S(1)}, bf16[4,16,512]{2,1,0:T(8,128)(2,1)S(1)}, u32[]{:S(2)}, u32[]{:S(2)}) collective-permute-start(bf16[4,16,512]{2,1,0:T(8,128)(2,1)S(1)} %bitcast.36), channel_id=1, source_target_pairs={{0,3},{1,4},{2,7},{3,0},{4,1},{5,6},{6,5},{7,2},{8,13},{9,10},{10,... | collective-permute-start | bytes 196616 | tf_op jit(solution)/shard_map/ppermute | solution.py:48
  26.1 0.5 %collective-permute-done.8.got_ref = bf16[160,128]{1,0:T(8,128)(2,1)S(1)} collective-permute-done((bf16[160,128]{1,0:T(8,128)(2,1)S(1)}, bf16[160,128]{1,0:T(8,128)(2,1)S(1)}, u32[]{:S(2)}, u32[]{:S(2)}) %collective-permute-start.8) | collective-permute-done | bytes 40992 | tf_op jit(solution)/shard_map/ppermute | solution.py:48
  26.6 3.1 %collective-permute-start.9 = (bf16[160,128]{1,0:T(8,128)(2,1)S(1)}, bf16[160,128]{1,0:T(8,128)(2,1)S(1)}, u32[]{:S(2)}, u32[]{:S(2)}) collective-permute-start(bf16[160,128]{1,0:T(8,128)(2,1)S(1)} %add.4.keep_ref), channel_id=1, source_target_pairs={{0,17},{1,8},{2,11},{3,18},{4,13},{5,20},{6,23},{7,14},{8,1},{9,24... | collective-permute-start | bytes 122888 | tf_op jit(solution)/shard_map/ppermute | solution.py:48
  29.8 0.2 collective-permute-start.14
  30.0 1.5 %collective-permute-done.9.got_ref = bf16[160,128]{1,0:T(8,128)(2,1)S(1)} collective-permute-done((bf16[160,128]{1,0:T(8,128)(2,1)S(1)}, bf16[160,128]{1,0:T(8,128)(2,1)S(1)}, u32[]{:S(2)}, u32[]{:S(2)}) %collective-permute-start.9) | collective-permute-done | bytes 40992 | tf_op jit(solution)/shard_map/ppermute | solution.py:48
  31.5 1.1 %collective-permute-start.10 = (bf16[160,128]{1,0:T(8,128)(2,1)S(1)}, bf16[160,128]{1,0:T(8,128)(2,1)S(1)}, u32[]{:S(2)}, u32[]{:S(2)}) collective-permute-start(bf16[160,128]{1,0:T(8,128)(2,1)S(1)} %add.5), channel_id=1, source_target_pairs={{0,5},{1,2},{2,1},{3,6},{4,7},{5,0},{6,3},{7,4},{8,11},{9,12},{10,... | collective-permute-start | bytes 122888 | tf_op jit(solution)/shard_map/ppermute | solution.py:48
  32.6 1.6 %collective-permute-done.14 = bf16[8,16,512]{2,1,0:T(8,128)(2,1)S(1)} collective-permute-done((bf16[8,16,512]{2,1,0:T(8,128)(2,1)S(1)}, bf16[8,16,512]{2,1,0:T(8,128)(2,1)S(1)}, u32[]{:S(2)}, u32[]{:S(2)}) %collective-permute-start.14) | collective-permute-done | bytes 131104 | tf_op jit(solution)/shard_map/ppermute | solution.py:48
  34.3 0.8 %collective-permute-done.10 = bf16[160,128]{1,0:T(8,128)(2,1)S(1)} collective-permute-done((bf16[160,128]{1,0:T(8,128)(2,1)S(1)}, bf16[160,128]{1,0:T(8,128)(2,1)S(1)}, u32[]{:S(2)}, u32[]{:S(2)}) %collective-permute-start.10) | collective-permute-done | bytes 40992 | tf_op jit(solution)/shard_map/ppermute | solution.py:48
  35.0 1.2 %collective-permute-start.15 = (bf16[320,128]{1,0:T(8,128)(2,1)S(1)}, bf16[320,128]{1,0:T(8,128)(2,1)S(1)}, u32[]{:S(2)}, u32[]{:S(2)}) collective-permute-start(bf16[320,128]{1,0:T(8,128)(2,1)S(1)} %bitcast.33), channel_id=1, source_target_pairs={{0,3},{1,4},{2,7},{3,0},{4,1},{5,6},{6,5},{7,2},{8,13},{9,10},{10,... | collective-permute-start | bytes 245768 | tf_op jit(solution)/shard_map/ppermute | solution.py:48
  36.3 1.0 %beyond.1 = (bf16[288,512]{1,0:T(8,128)(2,1)S(1)}, bf16[288,512]{1,0:T(8,128)(2,1)S(1)}) custom-call(bf16[8,128,256]{2,1,0:T(8,128)(2,1)S(1)} %copy-done.3, bf16[256,256]{1,0:T(8,128)(2,1)S(1)} %collective-permute-done.even_ref, bf16[256,256]{1,0:T(8,128)(2,1)S(1)} %collective-permute-done.1.odd_ref, ...), custom_call_target="tpu_custom_call" | custom-call | flops 8000000000 | bytes 100000 | tf_op jit(solution)/shard_map/beyond/pallas_call | solution.py:652
  37.3 0.5 %collective-permute-done.16.other_ref = bf16[16,16,512]{2,1,0:T(8,128)(2,1)S(1)} collective-permute-done((bf16[16,16,512]{2,1,0:T(8,128)(2,1)S(1)}, bf16[16,16,512]{2,1,0:T(8,128)(2,1)S(1)}, u32[]{:S(2)}, u32[]{:S(2)}) %collective-permute-start.16) | collective-permute-done | bytes 262176 | tf_op jit(solution)/shard_map/ppermute | solution.py:48
  37.9 1.1 %collective-permute-done.15 = bf16[320,128]{1,0:T(8,128)(2,1)S(1)} collective-permute-done((bf16[320,128]{1,0:T(8,128)(2,1)S(1)}, bf16[320,128]{1,0:T(8,128)(2,1)S(1)}, u32[]{:S(2)}, u32[]{:S(2)}) %collective-permute-start.15) | collective-permute-done | bytes 81952 | tf_op jit(solution)/shard_map/ppermute | solution.py:48
  39.0 0.2 collective-permute-start.17
  39.2 1.0 %prepare.1 = (bf16[4608,256]{1,0:T(8,128)(2,1)S(1)}, f32[512,512]{1,0:T(8,128)S(1)}) custom-call(bf16[2304,512]{1,0:T(8,128)(2,1)S(1)} %bitcast.25, bf16[512,512]{1,0:T(8,128)(2,1)S(1)} %bitcast.46), custom_call_target="tpu_custom_call" | custom-call | flops 2000000000 | bytes 6000000 | tf_op jit(solution)/shard_map/prepare/pallas_call | solution.py:677
  40.2 0.3 collective-permute-done.17.other_ref
  40.5 4.5 %grad_conv.1 = (f32[16,512]{1,0:T(8,128)}, bf16[1024,256]{1,0:T(8,128)(2,1)}) custom-call(bf16[640,128]{1,0:T(8,128)(2,1)S(1)} %bitcast.27, bf16[640,128]{1,0:T(8,128)(2,1)S(1)} %collective-permute-done.17.other_ref, f32[512,512]{1,0:T(8,128)S(1)} %get-tuple-element.74.both_ref, bf16[768,512]{1,0:T(8,128)(2,1)S(1)} %get-tuple-element.76.in_feat_ref, ...), custom_call_target="tpu_custom_call" | custom-call | tf_op jit(solution)/shard_map/grad_conv/pallas_call | solution.py:696
  (33 shorter events, 0.4 us)
Async XLA Ops:
  0.6 4.4 %copy-start.1 = (f32[16,512]{1,0:T(8,128)S(1)}, f32[16,512]{1,0:T(8,128)}, u32[]{:S(2)}) copy-start(f32[16,512]{1,0:T(8,128)} %target_ref.1) | copy-start | bytes 98308
  0.6 1.0 %copy-start.2 = (bf16[8,128,256]{2,1,0:T(8,128)(2,1)S(1)}, bf16[8,128,256]{2,1,0:T(8,128)(2,1)}, u32[]{:S(2)}) copy-start(bf16[8,128,256]{2,1,0:T(8,128)(2,1)} %own_ref.3) | copy-start | bytes 1572868
  1.7 6.2 %copy-start = (bf16[3,3,256,512]{3,2,1,0:T(8,128)(2,1)S(1)}, bf16[3,3,256,512]{3,2,1,0:T(8,128)(2,1)}, u32[]{:S(2)}) copy-start(bf16[3,3,256,512]{3,2,1,0:T(8,128)(2,1)} %param.5) | copy-start | bytes 7077892
  1.7 6.2 %copy-start.3 = (bf16[8,128,256]{2,1,0:T(8,128)(2,1)S(1)}, bf16[8,128,256]{2,1,0:T(8,128)(2,1)}, u32[]{:S(2)}) copy-start(bf16[8,128,256]{2,1,0:T(8,128)(2,1)} %own_ref.3) | copy-start | bytes 1572868
  1.7 6.2 %copy-start.4 = (bf16[512]{0:T(512)(128)(2,1)S(1)}, bf16[512]{0:T(512)(128)(2,1)}, u32[]{:S(2)}) copy-start(bf16[512]{0:T(512)(128)(2,1)} %bias_ref.1) | copy-start | bytes 3076
  1.7 3.3 %collective-permute-start.2 = (bf16[2,8,256]{2,1,0:T(8,128)(2,1)S(1)}, bf16[2,8,256]{2,1,0:T(8,128)(2,1)S(1)}, u32[]{:S(2)}, u32[]{:S(2)}) collective-permute-start(bf16[2,8,256]{2,1,0:T(8,128)(2,1)S(1)} %get-tuple-element.44), channel_id=1, source_target_pairs={{0,1},{1,0},{2,3},{3,2},{4,5},{5,4},{6,7},{7,6},{8,9},{9,8},{10,11... | collective-permute-start | bytes 24584 | tf_op jit(solution)/shard_map/ppermute | solution.py:578
  2.3 9.7 %collective-permute-start = (bf16[256,256]{1,0:T(8,128)(2,1)S(1)}, bf16[256,256]{1,0:T(8,128)(2,1)S(1)}, u32[]{:S(2)}, u32[]{:S(2)}) collective-permute-start(bf16[256,256]{1,0:T(8,128)(2,1)S(1)} %get-tuple-element.42), channel_id=1, source_target_pairs={{0,2},{1,3},{2,0},{3,1},{4,6},{5,7},{6,4},{7,5},{8,10},{9,11},{10,... | collective-permute-start | bytes 393224 | tf_op jit(solution)/shard_map/ppermute | solution.py:31
  4.8 7.2 %collective-permute-start.1 = (bf16[256,256]{1,0:T(8,128)(2,1)S(1)}, bf16[256,256]{1,0:T(8,128)(2,1)S(1)}, u32[]{:S(2)}, u32[]{:S(2)}) collective-permute-start(bf16[256,256]{1,0:T(8,128)(2,1)S(1)} %get-tuple-element.43), channel_id=1, source_target_pairs={{0,1},{1,0},{2,4},{3,5},{4,2},{5,3},{6,8},{7,9},{8,6},{9,7},{10,12... | collective-permute-start | bytes 393224 | tf_op jit(solution)/shard_map/ppermute | solution.py:31
  5.0 7.0 %collective-permute-start.3 = (bf16[16,256]{1,0:T(8,128)(2,1)S(1)}, bf16[16,256]{1,0:T(8,128)(2,1)S(1)}, u32[]{:S(2)}, u32[]{:S(2)}) collective-permute-start(bf16[16,256]{1,0:T(8,128)(2,1)S(1)} %get-tuple-element.45), channel_id=1, source_target_pairs={{0,2},{1,3},{2,0},{3,1},{4,6},{5,7},{6,4},{7,5},{8,10},{9,11},{10,... | collective-permute-start | bytes 24584 | tf_op jit(solution)/shard_map/ppermute | solution.py:31
  7.9 4.1 %collective-permute-start.4 = (bf16[16,256]{1,0:T(8,128)(2,1)S(1)}, bf16[16,256]{1,0:T(8,128)(2,1)S(1)}, u32[]{:S(2)}, u32[]{:S(2)}) collective-permute-start(bf16[16,256]{1,0:T(8,128)(2,1)S(1)} %get-tuple-element.46), channel_id=1, source_target_pairs={{0,1},{1,0},{2,4},{3,5},{4,2},{5,3},{6,8},{7,9},{8,6},{9,7},{10,12... | collective-permute-start | bytes 24584 | tf_op jit(solution)/shard_map/ppermute | solution.py:31
  12.9 1.5 %collective-permute-start.5 = (bf16[640,128]{1,0:T(8,128)(2,1)S(1)}, bf16[640,128]{1,0:T(8,128)(2,1)S(1)}, u32[]{:S(2)}, u32[]{:S(2)}) collective-permute-start(bf16[640,128]{1,0:T(8,128)(2,1)S(1)} %get-tuple-element.52), channel_id=1, source_target_pairs={{0,1},{1,0},{2,3},{3,2},{4,5},{5,4},{6,7},{7,6},{8,9},{9,8},{10,11... | collective-permute-start | bytes 491528 | tf_op jit(solution)/shard_map/ppermute | solution.py:48
  14.4 5.2 %collective-permute-start.6 = (bf16[320,128]{1,0:T(8,128)(2,1)S(1)}, bf16[320,128]{1,0:T(8,128)(2,1)S(1)}, u32[]{:S(2)}, u32[]{:S(2)}) collective-permute-start(bf16[320,128]{1,0:T(8,128)(2,1)S(1)} %get-tuple-element.54), channel_id=1, source_target_pairs={{0,3},{1,4},{2,7},{3,0},{4,1},{5,6},{6,5},{7,2},{8,13},{9,10},{10,... | collective-permute-start | bytes 245768 | tf_op jit(solution)/shard_map/ppermute | solution.py:48
  17.0 4.1 %collective-permute-start.11 = (bf16[1,16,512]{2,1,0:T(8,128)(2,1)S(1)}, bf16[1,16,512]{2,1,0:T(8,128)(2,1)S(1)}, u32[]{:S(2)}, u32[]{:S(2)}) collective-permute-start(bf16[1,16,512]{2,1,0:T(8,128)(2,1)S(1)} %get-tuple-element.58), channel_id=1, source_target_pairs={{0,17},{1,16},{2,19},{3,18},{4,21},{5,20},{6,23},{7,22},{8,25},{9,... | collective-permute-start | bytes 49160 | tf_op jit(solution)/shard_map/ppermute | solution.py:48
  19.6 3.5 %collective-permute-start.7 = (bf16[160,128]{1,0:T(8,128)(2,1)S(1)}, bf16[160,128]{1,0:T(8,128)(2,1)S(1)}, u32[]{:S(2)}, u32[]{:S(2)}) collective-permute-start(bf16[160,128]{1,0:T(8,128)(2,1)S(1)} %get-tuple-element.56), channel_id=1, source_target_pairs={{0,5},{1,2},{2,1},{3,6},{4,7},{5,0},{6,3},{7,4},{8,11},{9,12},{10,... | collective-permute-start | bytes 122888 | tf_op jit(solution)/shard_map/ppermute | solution.py:48
  21.1 3.8 %collective-permute-start.12 = (bf16[2,16,512]{2,1,0:T(8,128)(2,1)S(1)}, bf16[2,16,512]{2,1,0:T(8,128)(2,1)S(1)}, u32[]{:S(2)}, u32[]{:S(2)}) collective-permute-start(bf16[2,16,512]{2,1,0:T(8,128)(2,1)S(1)} %bitcast.41), channel_id=1, source_target_pairs={{0,9},{1,8},{2,11},{3,10},{4,13},{5,12},{6,15},{7,14},{8,1},{9,0},... | collective-permute-start | bytes 98312 | tf_op jit(solution)/shard_map/ppermute | solution.py:48
  23.1 3.5 %collective-permute-start.8 = (bf16[160,128]{1,0:T(8,128)(2,1)S(1)}, bf16[160,128]{1,0:T(8,128)(2,1)S(1)}, u32[]{:S(2)}, u32[]{:S(2)}) collective-permute-start(bf16[160,128]{1,0:T(8,128)(2,1)S(1)} %add.3.keep_ref), channel_id=1, source_target_pairs={{0,9},{1,16},{2,19},{3,10},{4,21},{5,12},{6,15},{7,22},{8,25},{9,0... | collective-permute-start | bytes 122888 | tf_op jit(solution)/shard_map/ppermute | solution.py:48
  24.9 4.8 %collective-permute-start.13 = (bf16[4,16,512]{2,1,0:T(8,128)(2,1)S(1)}, bf16[4,16,512]{2,1,0:T(8,128)(2,1)S(1)}, u32[]{:S(2)}, u32[]{:S(2)}) collective-permute-start(bf16[4,16,512]{2,1,0:T(8,128)(2,1)S(1)} %bitcast.36), channel_id=1, source_target_pairs={{0,3},{1,4},{2,7},{3,0},{4,1},{5,6},{6,5},{7,2},{8,13},{9,10},{10,... | collective-permute-start | bytes 196616 | tf_op jit(solution)/shard_map/ppermute | solution.py:48
  26.6 4.9 %collective-permute-start.9 = (bf16[160,128]{1,0:T(8,128)(2,1)S(1)}, bf16[160,128]{1,0:T(8,128)(2,1)S(1)}, u32[]{:S(2)}, u32[]{:S(2)}) collective-permute-start(bf16[160,128]{1,0:T(8,128)(2,1)S(1)} %add.4.keep_ref), channel_id=1, source_target_pairs={{0,17},{1,8},{2,11},{3,18},{4,13},{5,20},{6,23},{7,14},{8,1},{9,24... | collective-permute-start | bytes 122888 | tf_op jit(solution)/shard_map/ppermute | solution.py:48
  29.8 4.5 %collective-permute-start.14 = (bf16[8,16,512]{2,1,0:T(8,128)(2,1)S(1)}, bf16[8,16,512]{2,1,0:T(8,128)(2,1)S(1)}, u32[]{:S(2)}, u32[]{:S(2)}) collective-permute-start(bf16[8,16,512]{2,1,0:T(8,128)(2,1)S(1)} %bitcast.30), channel_id=1, source_target_pairs={{0,5},{1,2},{2,1},{3,6},{4,7},{5,0},{6,3},{7,4},{8,11},{9,12},{10,... | collective-permute-start | bytes 393224 | tf_op jit(solution)/shard_map/ppermute | solution.py:48
  31.5 3.5 %collective-permute-start.10 = (bf16[160,128]{1,0:T(8,128)(2,1)S(1)}, bf16[160,128]{1,0:T(8,128)(2,1)S(1)}, u32[]{:S(2)}, u32[]{:S(2)}) collective-permute-start(bf16[160,128]{1,0:T(8,128)(2,1)S(1)} %add.5), channel_id=1, source_target_pairs={{0,5},{1,2},{2,1},{3,6},{4,7},{5,0},{6,3},{7,4},{8,11},{9,12},{10,... | collective-permute-start | bytes 122888 | tf_op jit(solution)/shard_map/ppermute | solution.py:48
  35.0 3.9 %collective-permute-start.15 = (bf16[320,128]{1,0:T(8,128)(2,1)S(1)}, bf16[320,128]{1,0:T(8,128)(2,1)S(1)}, u32[]{:S(2)}, u32[]{:S(2)}) collective-permute-start(bf16[320,128]{1,0:T(8,128)(2,1)S(1)} %bitcast.33), channel_id=1, source_target_pairs={{0,3},{1,4},{2,7},{3,0},{4,1},{5,6},{6,5},{7,2},{8,13},{9,10},{10,... | collective-permute-start | bytes 245768 | tf_op jit(solution)/shard_map/ppermute | solution.py:48
  36.3 1.5 %collective-permute-start.16 = (bf16[16,16,512]{2,1,0:T(8,128)(2,1)S(1)}, bf16[16,16,512]{2,1,0:T(8,128)(2,1)S(1)}, u32[]{:S(2)}, u32[]{:S(2)}) collective-permute-start(bf16[16,16,512]{2,1,0:T(8,128)(2,1)S(1)} %bitcast.28), channel_id=1, source_target_pairs={{0,1},{1,0},{2,3},{3,2},{4,5},{5,4},{6,7},{7,6},{8,9},{9,8},{10,11... | collective-permute-start | bytes 786440 | tf_op jit(solution)/shard_map/ppermute | solution.py:48
  39.0 1.5 %collective-permute-start.17 = (bf16[640,128]{1,0:T(8,128)(2,1)S(1)}, bf16[640,128]{1,0:T(8,128)(2,1)S(1)}, u32[]{:S(2)}, u32[]{:S(2)}) collective-permute-start(bf16[640,128]{1,0:T(8,128)(2,1)S(1)} %bitcast.26), channel_id=1, source_target_pairs={{0,1},{1,0},{2,3},{3,2},{4,5},{5,4},{6,7},{7,6},{8,9},{9,8},{10,11... | collective-permute-start | bytes 491528 | tf_op jit(solution)/shard_map/ppermute | solution.py:48

commit v10 on v9

--- a/solution.py
+++ b/solution.py
@@ -227,8 +227,11 @@
                 low_ref[at, :], high_ref[at, :] = canvas_ref[k], canvas_ref[rows - 2 + k]
 
 
-def payload_kernel(target_ref, *refs):
-    even_ref, odd_ref, left_ref, right_ref, half_ref = refs[-5:]
+def payload_kernel(target_ref, rows_ref, *refs):
+    even_ref, payload_ref, left_ref, right_ref, half_ref = refs[-5:]
+    main = rows_ref.shape[0]
+    payload_ref[0:main, :] = rows_ref[...]
+    odd_ref = payload_ref.at[main:]
     half_ref[0] = target_ref[...].astype(bf16)
     if len(refs) == 6:
         here = lax.axis_index("cols")
@@ -326,14 +329,13 @@
 
 
 def halo_rows(halo_refs, low_ref, high_ref):
-    even_ref, odd_ref, even_rim_ref, odd_rim_ref = halo_refs
+    even_ref, odd_ref, even_rim_ref = halo_refs
     row = lax.axis_index("rows")
     odd = lax.rem(row, 2)
     main = even_ref.shape[0]
-    low_ref[0:main, :] = jnp.where(odd == 0, odd_ref[...], even_ref[...])
-    high_ref[0:main, :] = jnp.where(odd == 0, even_ref[...], odd_ref[...])
-    low_ref[main:, :] = jnp.where(odd == 0, odd_rim_ref[...], even_rim_ref[...])
-    high_ref[main:, :] = jnp.where(odd == 0, even_rim_ref[...], odd_rim_ref[...])
+    for at, even in ((slice(0, main), even_ref), (slice(main, None), even_rim_ref)):
+        low_ref[at, :] = jnp.where(odd == 0, odd_ref[at, :], even[...])
+        high_ref[at, :] = jnp.where(odd == 0, even[...], odd_ref[at, :])
 
     @pl.when(row == 0)
     def _():
@@ -349,12 +351,12 @@
 
 
 def outer_kernel(
-    shape, even_ref, odd_ref, even_rim_ref, odd_rim_ref, kernel_ref, base_ref, part_ref,
+    shape, even_ref, odd_ref, even_rim_ref, kernel_ref, base_ref, part_ref,
     feat_ref, slope_ref, send_ref, keep_ref, low_ref, high_ref, cat_ref, gram_ref,
 ):
     tile_rows, tile_cols, in_width, out_width, step = shape
     span, main = 3 * in_width, 2 * tile_cols
-    halo_rows((even_ref, odd_ref, even_rim_ref, odd_rim_ref), low_ref, high_ref)
+    halo_rows((even_ref, odd_ref, even_rim_ref), low_ref, high_ref)
     for n, (source, at) in enumerate([(low_ref, tile_cols), (high_ref, 0)]):
         rim = source[main:, :].astype(f32)
         k = 4 * (1 - n)
@@ -381,11 +383,11 @@
 
 
 def beyond_kernel(
-    shape, own_ref, even_ref, odd_ref, even_rim_ref, odd_rim_ref, left_ref, right_ref, kernel_ref, bias_ref,
+    shape, own_ref, even_ref, odd_ref, even_rim_ref, left_ref, right_ref, kernel_ref, bias_ref,
     part_ref, feat_ref, slope_ref, low_ref, high_ref, cat_ref, edge_ref,
 ):
     tile_rows, tile_cols, in_width, out_width, step = shape
-    halo_rows((even_ref, odd_ref, even_rim_ref, odd_rim_ref), low_ref, high_ref)
+    halo_rows((even_ref, odd_ref, even_rim_ref), low_ref, high_ref)
     first = (lax.axis_index("rows") > 0).astype(f32)
     last = (lax.axis_index("rows") < lax.axis_size("rows") - 1).astype(f32)
     left = (lax.axis_index("cols") > 0).astype(f32)
@@ -579,18 +581,19 @@
     else:
         beyond = shift_cols(rims[1], rims[0])
     evens, odds = range(0, count, 2), range(1, count, 2)
-    even, odd = swap_rows(evens, even), swap_rows(odds, odd)
+    even = swap_rows(evens, even)
     payload_shape = jax.ShapeDtypeStruct((2 * tile_cols + edge, in_width), bf16)
     end_shape = jax.ShapeDtypeStruct((edge, in_width), bf16)
     half_shape = jax.ShapeDtypeStruct((1, *target_gram.shape), bf16)
-    even_rim, odd_rim, left, right, rows = local(
+    even_rim, odd, left, right, rows = local(
         payload_kernel,
-        (end_shape, end_shape, rim_shape, rim_shape, half_shape),
+        (end_shape, payload_shape, rim_shape, rim_shape, half_shape),
         "row_rims",
         target_gram,
+        odd,
         *beyond,
     )
-    halo = [even, odd, swap_rows(evens, even_rim), swap_rows(odds, odd_rim)]
+    halo = [even, swap_rows(odds, odd), swap_rows(evens, even_rim)]
     bits = (lax.axis_size("rows") * lax.axis_size("cols")).bit_length() - 1
     gather = Gather(rows)
     far = list(reversed(range(3, bits)))
@@ -625,7 +628,7 @@
             jax.ShapeDtypeStruct(half_gram, bf16),
             jax.ShapeDtypeStruct(half_gram, f32),
         ),
-        in_specs=[vmem] * 7,
+        in_specs=[vmem] * 6,
         scratch_shapes=[
             *halo_scratch,
             pltpu.VMEM((2 * tile_cols, 3 * in_width), bf16),
@@ -652,7 +655,7 @@
                 pl.pallas_call(
                     functools.partial(beyond_kernel, shape),
                     out_shape=(jax.ShapeDtypeStruct((outer, out_width), bf16),) * 2,
-                    in_specs=[vmem] * 10,
+                    in_specs=[vmem] * 9,
                     scratch_shapes=[
                         *halo_scratch,
                         pltpu.VMEM((4 * tile_cols, 3 * in_width), bf16),

time: 45.1 us -> 45 us (level)
  waiting for transfers between devices: 9.42 us -> 8.15 us
  starting transfers between devices: 22.6 us -> 23.8 us
    ppermute x13, starting transfers between devices: 16.5 us -> 19.5 us  [swap(): lax.ppermute(value, ('rows', 'cols'), [(i, i ^ flip(i)) for i in range(to...]
    ppermute x4 -> x3, starting transfers between devices: 5.62 us -> 3.73 us  [swap_rows(): return lax.ppermute(value, ('rows', 'cols'), perm)]
    ppermute x4 -> x3, waiting for transfers between devices: 0.69 us -> 0.01 us  [swap_rows(): return lax.ppermute(value, ('rows', 'cols'), perm)]
    ppermute x13, waiting for transfers between devices: 8.73 us -> 8.14 us  [swap(): lax.ppermute(value, ('rows', 'cols'), [(i, i ^ flip(i)) for i in range(to...]
  transfers between devices with their start and end apart: 18 -> 17, of which waited for: 11 -> 10; matrix products, arithmetic and copies ran while one was open for 0% -> 0% of each run, Pallas kernels for 12% -> 12%
where the time goes in v10:
time: 45 us; the launch traced here: 44.9 us
  starting transfers between devices  23.8 us (53%)
  Pallas kernels  11.1 us (25%)
  waiting for transfers between devices  8.15 us (18%)
  local copies, waits for them, and re-layouts  1.06 us (2%)
  between operations  0.79 us (2%)
    ppermute x13, starting transfers between devices, swap(): lax.ppermute(value, ('rows', 'cols'), [(i, i ^ flip(i)) for i in range(to...  19.5 us
    ppermute x13, waiting for transfers between devices, swap(): lax.ppermute(value, ('rows', 'cols'), [(i, i ^ flip(i)) for i in range(to...  8.14 us
    pallas_call x1, Pallas kernels, on_device(): pl.pallas_call(functools.partial(backward_kernel, shape, pixel_total), ou...  4.46 us
    ppermute x3, starting transfers between devices, swap_rows(): return lax.ppermute(value, ('rows', 'cols'), perm)  3.73 us
    pallas_call x1, Pallas kernels, on_device(): pl.pallas_call(functools.partial(inner_kernel, shape), out_shape=(jax.Sha...  3.37 us
    unnamed x10, local copies, waits for them, and re-layouts  1.06 us
    pallas_call x1, Pallas kernels, beside(): pl.pallas_call(functools.partial(beyond_kernel, shape), out_shape=(jax.Sh...  1.03 us
    pallas_call x1, Pallas kernels, beside(): pl.pallas_call(prepare_kernel, out_shape=(jax.ShapeDtypeStruct((9 * out_w...  0.97 us
  transfers between devices with their start and end apart: 17, of which 10 were waited for; matrix products, arithmetic and copies ran while one was open for 0% of the time, Pallas kernels for 12%

profile of v10, /device:TPU:0, one launch (start us, length us, event | category | flops | bytes accessed | tf_op | source)
XLA Modules:
  0.0 44.9 jit_solution(12311441788410092632)
XLA Ops:
  0.7 1.0 %copy-done.2 = bf16[8,128,256]{2,1,0:T(8,128)(2,1)S(1)} copy-done((bf16[8,128,256]{2,1,0:T(8,128)(2,1)S(1)}, bf16[8,128,256]{2,1,0:T(8,128)(2,1)}, u32[]{:S(2)}) %copy-start.2) | copy-done | bytes 524312
  1.7 0.5 %collective-permute-start.1 = (bf16[2,8,256]{2,1,0:T(8,128)(2,1)S(1)}, bf16[2,8,256]{2,1,0:T(8,128)(2,1)S(1)}, u32[]{:S(2)}, u32[]{:S(2)}) collective-permute-start(bf16[2,8,256]{2,1,0:T(8,128)(2,1)S(1)} %get-tuple-element.44), channel_id=1, source_target_pairs={{0,1},{1,0},{2,3},{3,2},{4,5},{5,4},{6,7},{7,6},{8,9},{9,8},{10,11... | collective-permute-start | bytes 24584 | tf_op jit(solution)/shard_map/ppermute | solution.py:580
  2.3 2.6 %collective-permute-start = (bf16[256,256]{1,0:T(8,128)(2,1)S(1)}, bf16[256,256]{1,0:T(8,128)(2,1)S(1)}, u32[]{:S(2)}, u32[]{:S(2)}) collective-permute-start(bf16[256,256]{1,0:T(8,128)(2,1)S(1)} %get-tuple-element.42), channel_id=1, source_target_pairs={{0,2},{1,3},{2,0},{3,1},{4,6},{5,7},{6,4},{7,5},{8,10},{9,11},{10,... | collective-permute-start | bytes 393224 | tf_op jit(solution)/shard_map/ppermute | solution.py:31
  4.9 1.2 %collective-permute-start.3 = (bf16[16,256]{1,0:T(8,128)(2,1)S(1)}, bf16[16,256]{1,0:T(8,128)(2,1)S(1)}, u32[]{:S(2)}, u32[]{:S(2)}) collective-permute-start(bf16[16,256]{1,0:T(8,128)(2,1)S(1)} %get-tuple-element.46), channel_id=1, source_target_pairs={{0,2},{1,3},{2,0},{3,1},{4,6},{5,7},{6,4},{7,5},{8,10},{9,11},{10,... | collective-permute-start | bytes 24584 | tf_op jit(solution)/shard_map/ppermute | solution.py:31
  6.0 3.4 %inner_rows.1 = (bf16[768,512]{1,0:T(8,128)(2,1)S(1)}, bf16[768,512]{1,0:T(8,128)(2,1)S(1)}, f32[1280,128]{1,0:T(8,128)S(1)}, f32[1,512]{1,0:T(1,128)S(1)}, f32[512,512]{1,0:T(8,128)S(1)}) custom-call(bf16[8,128,256]{2,1,0:T(8,128)(2,1)S(1)} %copy-done.3, bf16[2,8,256]{2,1,0:T(8,128)(2,1)S(1)} %get-tuple-element.47.left_ref, ...), custom_call_target="tpu_custom_call" | custom-call | flops 2214592512 | bytes 6000000 | tf_op jit(solution)/shard_map/inner_rows/pallas_call | solution.py:601
  9.4 0.9 %outer_rows.1 = (bf16[256,512]{1,0:T(8,128)(2,1)S(1)}, bf16[256,512]{1,0:T(8,128)(2,1)S(1)}, bf16[640,128]{1,0:T(8,128)(2,1)S(1)}, f32[640,128]{1,0:T(8,128)S(1)}) custom-call(bf16[256,256]{1,0:T(8,128)(2,1)S(1)} %collective-permute-done.even_ref, bf16[272,256]{1,0:T(8,128)(2,1)S(1)} %collective-permute-done.2.odd_ref, ...), custom_call_target="tpu_custom_call" | custom-call | tf_op jit(solution)/shard_map/outer_rows/pallas_call | solution.py:623
  10.4 0.6 %collective-permute-start.4 = (bf16[640,128]{1,0:T(8,128)(2,1)S(1)}, bf16[640,128]{1,0:T(8,128)(2,1)S(1)}, u32[]{:S(2)}, u32[]{:S(2)}) collective-permute-start(bf16[640,128]{1,0:T(8,128)(2,1)S(1)} %get-tuple-element.52), channel_id=1, source_target_pairs={{0,1},{1,0},{2,3},{3,2},{4,5},{5,4},{6,7},{7,6},{8,9},{9,8},{10,11... | collective-permute-start | bytes 491528 | tf_op jit(solution)/shard_map/ppermute | solution.py:48
  10.9 1.0 %collective-permute-done.4.got_ref = bf16[640,128]{1,0:T(8,128)(2,1)S(1)} collective-permute-done((bf16[640,128]{1,0:T(8,128)(2,1)S(1)}, bf16[640,128]{1,0:T(8,128)(2,1)S(1)}, u32[]{:S(2)}, u32[]{:S(2)}) %collective-permute-start.4) | collective-permute-done | bytes 163872 | tf_op jit(solution)/shard_map/ppermute | solution.py:48
  12.0 5.0 %collective-permute-start.5 = (bf16[320,128]{1,0:T(8,128)(2,1)S(1)}, bf16[320,128]{1,0:T(8,128)(2,1)S(1)}, u32[]{:S(2)}, u32[]{:S(2)}) collective-permute-start(bf16[320,128]{1,0:T(8,128)(2,1)S(1)} %get-tuple-element.54), channel_id=1, source_target_pairs={{0,3},{1,4},{2,7},{3,0},{4,1},{5,6},{6,5},{7,2},{8,13},{9,10},{10,... | collective-permute-start | bytes 245768 | tf_op jit(solution)/shard_map/ppermute | solution.py:48
  17.0 2.6 %collective-permute-start.10 = (bf16[1,16,512]{2,1,0:T(8,128)(2,1)S(1)}, bf16[1,16,512]{2,1,0:T(8,128)(2,1)S(1)}, u32[]{:S(2)}, u32[]{:S(2)}) collective-permute-start(bf16[1,16,512]{2,1,0:T(8,128)(2,1)S(1)} %get-tuple-element.58), channel_id=1, source_target_pairs={{0,17},{1,16},{2,19},{3,18},{4,21},{5,20},{6,23},{7,22},{8,25},{9,... | collective-permute-start | bytes 49160 | tf_op jit(solution)/shard_map/ppermute | solution.py:48
  19.6 0.8 %collective-permute-start.6 = (bf16[160,128]{1,0:T(8,128)(2,1)S(1)}, bf16[160,128]{1,0:T(8,128)(2,1)S(1)}, u32[]{:S(2)}, u32[]{:S(2)}) collective-permute-start(bf16[160,128]{1,0:T(8,128)(2,1)S(1)} %get-tuple-element.56), channel_id=1, source_target_pairs={{0,5},{1,2},{2,1},{3,6},{4,7},{5,0},{6,3},{7,4},{8,11},{9,12},{10,... | collective-permute-start | bytes 122888 | tf_op jit(solution)/shard_map/ppermute | solution.py:48
  20.3 0.7 %collective-permute-done.10 = bf16[1,16,512]{2,1,0:T(8,128)(2,1)S(1)} collective-permute-done((bf16[1,16,512]{2,1,0:T(8,128)(2,1)S(1)}, bf16[1,16,512]{2,1,0:T(8,128)(2,1)S(1)}, u32[]{:S(2)}, u32[]{:S(2)}) %collective-permute-start.10) | collective-permute-done | bytes 16416 | tf_op jit(solution)/shard_map/ppermute | solution.py:48
  21.1 1.5 %collective-permute-start.11 = (bf16[2,16,512]{2,1,0:T(8,128)(2,1)S(1)}, bf16[2,16,512]{2,1,0:T(8,128)(2,1)S(1)}, u32[]{:S(2)}, u32[]{:S(2)}) collective-permute-start(bf16[2,16,512]{2,1,0:T(8,128)(2,1)S(1)} %bitcast.41), channel_id=1, source_target_pairs={{0,9},{1,8},{2,11},{3,10},{4,13},{5,12},{6,15},{7,14},{8,1},{9,0},... | collective-permute-start | bytes 98312 | tf_op jit(solution)/shard_map/ppermute | solution.py:48
  22.6 0.5 %collective-permute-done.6.got_ref = bf16[160,128]{1,0:T(8,128)(2,1)S(1)} collective-permute-done((bf16[160,128]{1,0:T(8,128)(2,1)S(1)}, bf16[160,128]{1,0:T(8,128)(2,1)S(1)}, u32[]{:S(2)}, u32[]{:S(2)}) %collective-permute-start.6) | collective-permute-done | bytes 40992 | tf_op jit(solution)/shard_map/ppermute | solution.py:48
  23.1 1.7 %collective-permute-start.7 = (bf16[160,128]{1,0:T(8,128)(2,1)S(1)}, bf16[160,128]{1,0:T(8,128)(2,1)S(1)}, u32[]{:S(2)}, u32[]{:S(2)}) collective-permute-start(bf16[160,128]{1,0:T(8,128)(2,1)S(1)} %add.3.keep_ref), channel_id=1, source_target_pairs={{0,9},{1,16},{2,19},{3,10},{4,21},{5,12},{6,15},{7,22},{8,25},{9,0... | collective-permute-start | bytes 122888 | tf_op jit(solution)/shard_map/ppermute | solution.py:48
  24.8 1.2 %collective-permute-start.12 = (bf16[4,16,512]{2,1,0:T(8,128)(2,1)S(1)}, bf16[4,16,512]{2,1,0:T(8,128)(2,1)S(1)}, u32[]{:S(2)}, u32[]{:S(2)}) collective-permute-start(bf16[4,16,512]{2,1,0:T(8,128)(2,1)S(1)} %bitcast.36), channel_id=1, source_target_pairs={{0,3},{1,4},{2,7},{3,0},{4,1},{5,6},{6,5},{7,2},{8,13},{9,10},{10,... | collective-permute-start | bytes 196616 | tf_op jit(solution)/shard_map/ppermute | solution.py:48
  26.1 0.5 %collective-permute-done.7.got_ref = bf16[160,128]{1,0:T(8,128)(2,1)S(1)} collective-permute-done((bf16[160,128]{1,0:T(8,128)(2,1)S(1)}, bf16[160,128]{1,0:T(8,128)(2,1)S(1)}, u32[]{:S(2)}, u32[]{:S(2)}) %collective-permute-start.7) | collective-permute-done | bytes 40992 | tf_op jit(solution)/shard_map/ppermute | solution.py:48
  26.6 3.0 %collective-permute-start.8 = (bf16[160,128]{1,0:T(8,128)(2,1)S(1)}, bf16[160,128]{1,0:T(8,128)(2,1)S(1)}, u32[]{:S(2)}, u32[]{:S(2)}) collective-permute-start(bf16[160,128]{1,0:T(8,128)(2,1)S(1)} %add.4.keep_ref), channel_id=1, source_target_pairs={{0,17},{1,8},{2,11},{3,18},{4,13},{5,20},{6,23},{7,14},{8,1},{9,24... | collective-permute-start | bytes 122888 | tf_op jit(solution)/shard_map/ppermute | solution.py:48
  29.7 0.2 collective-permute-start.13
  29.9 1.5 %collective-permute-done.8.got_ref = bf16[160,128]{1,0:T(8,128)(2,1)S(1)} collective-permute-done((bf16[160,128]{1,0:T(8,128)(2,1)S(1)}, bf16[160,128]{1,0:T(8,128)(2,1)S(1)}, u32[]{:S(2)}, u32[]{:S(2)}) %collective-permute-start.8) | collective-permute-done | bytes 40992 | tf_op jit(solution)/shard_map/ppermute | solution.py:48
  31.4 1.1 %collective-permute-start.9 = (bf16[160,128]{1,0:T(8,128)(2,1)S(1)}, bf16[160,128]{1,0:T(8,128)(2,1)S(1)}, u32[]{:S(2)}, u32[]{:S(2)}) collective-permute-start(bf16[160,128]{1,0:T(8,128)(2,1)S(1)} %add.5), channel_id=1, source_target_pairs={{0,5},{1,2},{2,1},{3,6},{4,7},{5,0},{6,3},{7,4},{8,11},{9,12},{10,... | collective-permute-start | bytes 122888 | tf_op jit(solution)/shard_map/ppermute | solution.py:48
  32.5 1.6 %collective-permute-done.13 = bf16[8,16,512]{2,1,0:T(8,128)(2,1)S(1)} collective-permute-done((bf16[8,16,512]{2,1,0:T(8,128)(2,1)S(1)}, bf16[8,16,512]{2,1,0:T(8,128)(2,1)S(1)}, u32[]{:S(2)}, u32[]{:S(2)}) %collective-permute-start.13) | collective-permute-done | bytes 131104 | tf_op jit(solution)/shard_map/ppermute | solution.py:48
  34.2 0.8 %collective-permute-done.9 = bf16[160,128]{1,0:T(8,128)(2,1)S(1)} collective-permute-done((bf16[160,128]{1,0:T(8,128)(2,1)S(1)}, bf16[160,128]{1,0:T(8,128)(2,1)S(1)}, u32[]{:S(2)}, u32[]{:S(2)}) %collective-permute-start.9) | collective-permute-done | bytes 40992 | tf_op jit(solution)/shard_map/ppermute | solution.py:48
  34.9 1.3 %collective-permute-start.14 = (bf16[320,128]{1,0:T(8,128)(2,1)S(1)}, bf16[320,128]{1,0:T(8,128)(2,1)S(1)}, u32[]{:S(2)}, u32[]{:S(2)}) collective-permute-start(bf16[320,128]{1,0:T(8,128)(2,1)S(1)} %bitcast.33), channel_id=1, source_target_pairs={{0,3},{1,4},{2,7},{3,0},{4,1},{5,6},{6,5},{7,2},{8,13},{9,10},{10,... | collective-permute-start | bytes 245768 | tf_op jit(solution)/shard_map/ppermute | solution.py:48
  36.3 0.2 collective-permute-start.15
  36.5 1.0 %beyond.1 = (bf16[288,512]{1,0:T(8,128)(2,1)S(1)}, bf16[288,512]{1,0:T(8,128)(2,1)S(1)}) custom-call(bf16[8,128,256]{2,1,0:T(8,128)(2,1)S(1)} %copy-done.3, bf16[256,256]{1,0:T(8,128)(2,1)S(1)} %collective-permute-done.even_ref, bf16[272,256]{1,0:T(8,128)(2,1)S(1)} %collective-permute-done.2.odd_ref, ...), custom_call_target="tpu_custom_call" | custom-call | flops 8000000000 | bytes 100000 | tf_op jit(solution)/shard_map/beyond/pallas_call | solution.py:655
  37.5 0.3 collective-permute-done.15.other_ref
  37.9 1.0 %collective-permute-done.14 = bf16[320,128]{1,0:T(8,128)(2,1)S(1)} collective-permute-done((bf16[320,128]{1,0:T(8,128)(2,1)S(1)}, bf16[320,128]{1,0:T(8,128)(2,1)S(1)}, u32[]{:S(2)}, u32[]{:S(2)}) %collective-permute-start.14) | collective-permute-done | bytes 81952 | tf_op jit(solution)/shard_map/ppermute | solution.py:48
  38.9 0.3 collective-permute-start.16
  39.2 1.0 %prepare.1 = (bf16[4608,256]{1,0:T(8,128)(2,1)S(1)}, f32[512,512]{1,0:T(8,128)S(1)}) custom-call(bf16[2304,512]{1,0:T(8,128)(2,1)S(1)} %bitcast.25, bf16[512,512]{1,0:T(8,128)(2,1)S(1)} %bitcast.46), custom_call_target="tpu_custom_call" | custom-call | flops 2000000000 | bytes 6000000 | tf_op jit(solution)/shard_map/prepare/pallas_call | solution.py:680
  40.2 0.2 collective-permute-done.16.other_ref
  40.4 4.5 %grad_conv.1 = (f32[16,512]{1,0:T(8,128)}, bf16[1024,256]{1,0:T(8,128)(2,1)}) custom-call(bf16[640,128]{1,0:T(8,128)(2,1)S(1)} %bitcast.27, bf16[640,128]{1,0:T(8,128)(2,1)S(1)} %collective-permute-done.16.other_ref, f32[512,512]{1,0:T(8,128)S(1)} %get-tuple-element.74.both_ref, bf16[768,512]{1,0:T(8,128)(2,1)S(1)} %get-tuple-element.76.in_feat_ref, ...), custom_call_target="tpu_custom_call" | custom-call | tf_op jit(solution)/shard_map/grad_conv/pallas_call | solution.py:699
  (31 shorter events, 0.4 us)
Async XLA Ops:
  0.6 4.2 %copy-start.1 = (f32[16,512]{1,0:T(8,128)S(1)}, f32[16,512]{1,0:T(8,128)}, u32[]{:S(2)}) copy-start(f32[16,512]{1,0:T(8,128)} %target_ref.1) | copy-start | bytes 98308
  0.6 1.0 %copy-start.2 = (bf16[8,128,256]{2,1,0:T(8,128)(2,1)S(1)}, bf16[8,128,256]{2,1,0:T(8,128)(2,1)}, u32[]{:S(2)}) copy-start(bf16[8,128,256]{2,1,0:T(8,128)(2,1)} %own_ref.3) | copy-start | bytes 1572868
  1.7 4.3 %copy-start = (bf16[3,3,256,512]{3,2,1,0:T(8,128)(2,1)S(1)}, bf16[3,3,256,512]{3,2,1,0:T(8,128)(2,1)}, u32[]{:S(2)}) copy-start(bf16[3,3,256,512]{3,2,1,0:T(8,128)(2,1)} %param.5) | copy-start | bytes 7077892
  1.7 4.3 %copy-start.3 = (bf16[8,128,256]{2,1,0:T(8,128)(2,1)S(1)}, bf16[8,128,256]{2,1,0:T(8,128)(2,1)}, u32[]{:S(2)}) copy-start(bf16[8,128,256]{2,1,0:T(8,128)(2,1)} %own_ref.3) | copy-start | bytes 1572868
  1.7 4.3 %copy-start.4 = (bf16[512]{0:T(512)(128)(2,1)S(1)}, bf16[512]{0:T(512)(128)(2,1)}, u32[]{:S(2)}) copy-start(bf16[512]{0:T(512)(128)(2,1)} %bias_ref.1) | copy-start | bytes 3076
  1.7 3.1 %collective-permute-start.1 = (bf16[2,8,256]{2,1,0:T(8,128)(2,1)S(1)}, bf16[2,8,256]{2,1,0:T(8,128)(2,1)S(1)}, u32[]{:S(2)}, u32[]{:S(2)}) collective-permute-start(bf16[2,8,256]{2,1,0:T(8,128)(2,1)S(1)} %get-tuple-element.44), channel_id=1, source_target_pairs={{0,1},{1,0},{2,3},{3,2},{4,5},{5,4},{6,7},{7,6},{8,9},{9,8},{10,11... | collective-permute-start | bytes 24584 | tf_op jit(solution)/shard_map/ppermute | solution.py:580
  2.3 7.2 %collective-permute-start = (bf16[256,256]{1,0:T(8,128)(2,1)S(1)}, bf16[256,256]{1,0:T(8,128)(2,1)S(1)}, u32[]{:S(2)}, u32[]{:S(2)}) collective-permute-start(bf16[256,256]{1,0:T(8,128)(2,1)S(1)} %get-tuple-element.42), channel_id=1, source_target_pairs={{0,2},{1,3},{2,0},{3,1},{4,6},{5,7},{6,4},{7,5},{8,10},{9,11},{10,... | collective-permute-start | bytes 393224 | tf_op jit(solution)/shard_map/ppermute | solution.py:31
  4.9 4.6 %collective-permute-start.3 = (bf16[16,256]{1,0:T(8,128)(2,1)S(1)}, bf16[16,256]{1,0:T(8,128)(2,1)S(1)}, u32[]{:S(2)}, u32[]{:S(2)}) collective-permute-start(bf16[16,256]{1,0:T(8,128)(2,1)S(1)} %get-tuple-element.46), channel_id=1, source_target_pairs={{0,2},{1,3},{2,0},{3,1},{4,6},{5,7},{6,4},{7,5},{8,10},{9,11},{10,... | collective-permute-start | bytes 24584 | tf_op jit(solution)/shard_map/ppermute | solution.py:31
  6.0 3.4 %collective-permute-start.2 = (bf16[272,256]{1,0:T(8,128)(2,1)S(1)}, bf16[272,256]{1,0:T(8,128)(2,1)S(1)}, u32[]{:S(2)}, u32[]{:S(2)}) collective-permute-start(bf16[272,256]{1,0:T(8,128)(2,1)S(1)} %get-tuple-element.45), channel_id=1, source_target_pairs={{0,1},{1,0},{2,4},{3,5},{4,2},{5,3},{6,8},{7,9},{8,6},{9,7},{10,12... | collective-permute-start | bytes 417800 | tf_op jit(solution)/shard_map/ppermute | solution.py:31
  10.4 1.6 %collective-permute-start.4 = (bf16[640,128]{1,0:T(8,128)(2,1)S(1)}, bf16[640,128]{1,0:T(8,128)(2,1)S(1)}, u32[]{:S(2)}, u32[]{:S(2)}) collective-permute-start(bf16[640,128]{1,0:T(8,128)(2,1)S(1)} %get-tuple-element.52), channel_id=1, source_target_pairs={{0,1},{1,0},{2,3},{3,2},{4,5},{5,4},{6,7},{7,6},{8,9},{9,8},{10,11... | collective-permute-start | bytes 491528 | tf_op jit(solution)/shard_map/ppermute | solution.py:48
  12.0 7.6 %collective-permute-start.5 = (bf16[320,128]{1,0:T(8,128)(2,1)S(1)}, bf16[320,128]{1,0:T(8,128)(2,1)S(1)}, u32[]{:S(2)}, u32[]{:S(2)}) collective-permute-start(bf16[320,128]{1,0:T(8,128)(2,1)S(1)} %get-tuple-element.54), channel_id=1, source_target_pairs={{0,3},{1,4},{2,7},{3,0},{4,1},{5,6},{6,5},{7,2},{8,13},{9,10},{10,... | collective-permute-start | bytes 245768 | tf_op jit(solution)/shard_map/ppermute | solution.py:48
  17.0 4.1 %collective-permute-start.10 = (bf16[1,16,512]{2,1,0:T(8,128)(2,1)S(1)}, bf16[1,16,512]{2,1,0:T(8,128)(2,1)S(1)}, u32[]{:S(2)}, u32[]{:S(2)}) collective-permute-start(bf16[1,16,512]{2,1,0:T(8,128)(2,1)S(1)} %get-tuple-element.58), channel_id=1, source_target_pairs={{0,17},{1,16},{2,19},{3,18},{4,21},{5,20},{6,23},{7,22},{8,25},{9,... | collective-permute-start | bytes 49160 | tf_op jit(solution)/shard_map/ppermute | solution.py:48
  19.6 3.5 %collective-permute-start.6 = (bf16[160,128]{1,0:T(8,128)(2,1)S(1)}, bf16[160,128]{1,0:T(8,128)(2,1)S(1)}, u32[]{:S(2)}, u32[]{:S(2)}) collective-permute-start(bf16[160,128]{1,0:T(8,128)(2,1)S(1)} %get-tuple-element.56), channel_id=1, source_target_pairs={{0,5},{1,2},{2,1},{3,6},{4,7},{5,0},{6,3},{7,4},{8,11},{9,12},{10,... | collective-permute-start | bytes 122888 | tf_op jit(solution)/shard_map/ppermute | solution.py:48
  21.1 3.8 %collective-permute-start.11 = (bf16[2,16,512]{2,1,0:T(8,128)(2,1)S(1)}, bf16[2,16,512]{2,1,0:T(8,128)(2,1)S(1)}, u32[]{:S(2)}, u32[]{:S(2)}) collective-permute-start(bf16[2,16,512]{2,1,0:T(8,128)(2,1)S(1)} %bitcast.41), channel_id=1, source_target_pairs={{0,9},{1,8},{2,11},{3,10},{4,13},{5,12},{6,15},{7,14},{8,1},{9,0},... | collective-permute-start | bytes 98312 | tf_op jit(solution)/shard_map/ppermute | solution.py:48
  23.1 3.5 %collective-permute-start.7 = (bf16[160,128]{1,0:T(8,128)(2,1)S(1)}, bf16[160,128]{1,0:T(8,128)(2,1)S(1)}, u32[]{:S(2)}, u32[]{:S(2)}) collective-permute-start(bf16[160,128]{1,0:T(8,128)(2,1)S(1)} %add.3.keep_ref), channel_id=1, source_target_pairs={{0,9},{1,16},{2,19},{3,10},{4,21},{5,12},{6,15},{7,22},{8,25},{9,0... | collective-permute-start | bytes 122888 | tf_op jit(solution)/shard_map/ppermute | solution.py:48
  24.8 4.8 %collective-permute-start.12 = (bf16[4,16,512]{2,1,0:T(8,128)(2,1)S(1)}, bf16[4,16,512]{2,1,0:T(8,128)(2,1)S(1)}, u32[]{:S(2)}, u32[]{:S(2)}) collective-permute-start(bf16[4,16,512]{2,1,0:T(8,128)(2,1)S(1)} %bitcast.36), channel_id=1, source_target_pairs={{0,3},{1,4},{2,7},{3,0},{4,1},{5,6},{6,5},{7,2},{8,13},{9,10},{10,... | collective-permute-start | bytes 196616 | tf_op jit(solution)/shard_map/ppermute | solution.py:48
  26.6 4.8 %collective-permute-start.8 = (bf16[160,128]{1,0:T(8,128)(2,1)S(1)}, bf16[160,128]{1,0:T(8,128)(2,1)S(1)}, u32[]{:S(2)}, u32[]{:S(2)}) collective-permute-start(bf16[160,128]{1,0:T(8,128)(2,1)S(1)} %add.4.keep_ref), channel_id=1, source_target_pairs={{0,17},{1,8},{2,11},{3,18},{4,13},{5,20},{6,23},{7,14},{8,1},{9,24... | collective-permute-start | bytes 122888 | tf_op jit(solution)/shard_map/ppermute | solution.py:48
  29.7 4.5 %collective-permute-start.13 = (bf16[8,16,512]{2,1,0:T(8,128)(2,1)S(1)}, bf16[8,16,512]{2,1,0:T(8,128)(2,1)S(1)}, u32[]{:S(2)}, u32[]{:S(2)}) collective-permute-start(bf16[8,16,512]{2,1,0:T(8,128)(2,1)S(1)} %bitcast.30), channel_id=1, source_target_pairs={{0,5},{1,2},{2,1},{3,6},{4,7},{5,0},{6,3},{7,4},{8,11},{9,12},{10,... | collective-permute-start | bytes 393224 | tf_op jit(solution)/shard_map/ppermute | solution.py:48
  31.4 3.5 %collective-permute-start.9 = (bf16[160,128]{1,0:T(8,128)(2,1)S(1)}, bf16[160,128]{1,0:T(8,128)(2,1)S(1)}, u32[]{:S(2)}, u32[]{:S(2)}) collective-permute-start(bf16[160,128]{1,0:T(8,128)(2,1)S(1)} %add.5), channel_id=1, source_target_pairs={{0,5},{1,2},{2,1},{3,6},{4,7},{5,0},{6,3},{7,4},{8,11},{9,12},{10,... | collective-permute-start | bytes 122888 | tf_op jit(solution)/shard_map/ppermute | solution.py:48
  34.9 3.9 %collective-permute-start.14 = (bf16[320,128]{1,0:T(8,128)(2,1)S(1)}, bf16[320,128]{1,0:T(8,128)(2,1)S(1)}, u32[]{:S(2)}, u32[]{:S(2)}) collective-permute-start(bf16[320,128]{1,0:T(8,128)(2,1)S(1)} %bitcast.33), channel_id=1, source_target_pairs={{0,3},{1,4},{2,7},{3,0},{4,1},{5,6},{6,5},{7,2},{8,13},{9,10},{10,... | collective-permute-start | bytes 245768 | tf_op jit(solution)/shard_map/ppermute | solution.py:48
  36.3 1.5 %collective-permute-start.15 = (bf16[16,16,512]{2,1,0:T(8,128)(2,1)S(1)}, bf16[16,16,512]{2,1,0:T(8,128)(2,1)S(1)}, u32[]{:S(2)}, u32[]{:S(2)}) collective-permute-start(bf16[16,16,512]{2,1,0:T(8,128)(2,1)S(1)} %bitcast.28), channel_id=1, source_target_pairs={{0,1},{1,0},{2,3},{3,2},{4,5},{5,4},{6,7},{7,6},{8,9},{9,8},{10,11... | collective-permute-start | bytes 786440 | tf_op jit(solution)/shard_map/ppermute | solution.py:48
  38.9 1.5 %collective-permute-start.16 = (bf16[640,128]{1,0:T(8,128)(2,1)S(1)}, bf16[640,128]{1,0:T(8,128)(2,1)S(1)}, u32[]{:S(2)}, u32[]{:S(2)}) collective-permute-start(bf16[640,128]{1,0:T(8,128)(2,1)S(1)} %bitcast.26), channel_id=1, source_target_pairs={{0,1},{1,0},{2,3},{3,2},{4,5},{5,4},{6,7},{7,6},{8,9},{9,8},{10,11... | collective-permute-start | bytes 491528 | tf_op jit(solution)/shard_map/ppermute | solution.py:48

commit v11 on v10

--- a/solution.py
+++ b/solution.py
@@ -174,9 +174,7 @@
 def sum_all(send, keep, beside):
     bits = (lax.axis_size("rows") * lax.axis_size("cols")).bit_length() - 1
     halving = [(1, 2), (2, 1)]
-    adding = []
-    for bit in range(3, bits, 2):
-        adding += [(bit, bit + 1), (bit + 1, bit)] if bit + 1 < bits else [(bit, None)]
+    adding = [(bit,) for bit in range(3, bits)]
 
     got = beside("cores", send, swap(send, 0))
     for n, pair in enumerate(halving):
@@ -456,12 +454,15 @@
             slope_ref[rows, at] = (slope * scale).astype(bf16)
 
 
-def prepare_kernel(kernel_ref, target_ref, turned_ref, both_ref):
+def turn_kernel(kernel_ref, turned_ref):
     taps, in_width, out_width = 9, kernel_ref.shape[0] // 9, kernel_ref.shape[1]
     for n in range(taps):
         to = (n // 3 * 3 + 2 - n % 3) * out_width
         turned_ref[to : to + out_width, :] = kernel_ref[n * in_width : (n + 1) * in_width, :].T
-    for i, j in tile_pairs(out_width):
+
+
+def prepare_kernel(target_ref, both_ref):
+    for i, j in tile_pairs(target_ref.shape[0]):
         at_i, at_j = slice(i * tile, (i + 1) * tile), slice(j * tile, (j + 1) * tile)
         both = target_ref[at_i, at_j].astype(f32) + target_ref[at_j, at_i].astype(f32).T
         both_ref[at_i, at_j] = both
@@ -618,6 +619,15 @@
         ),
     )(canvas, left, right, kernel, conv_bias)
 
+    weights, in_gram = lax.optimization_barrier((kernel, in_gram))
+    turned = local(
+        turn_kernel,
+        jax.ShapeDtypeStruct((9 * out_width, in_width), bf16),
+        "turn",
+        weights,
+        cost_estimate=waiting,
+    )
+    in_gram, turned = lax.optimization_barrier((in_gram, turned))
     half_gram = (packed_shape.shape[0] // 2, tile)
     halo_scratch = [pltpu.VMEM(payload_shape.shape, bf16), pltpu.VMEM(payload_shape.shape, bf16)]
     out_feat, out_slope, send, keep = pl.pallas_call(
@@ -676,25 +686,19 @@
         if name != "halves":
             return got
         gather.settle(sent)
-        prepared.extend(
-            pl.pallas_call(
+        prepared.append(
+            local(
                 prepare_kernel,
-                out_shape=(
-                    jax.ShapeDtypeStruct((9 * out_width, in_width), bf16),
-                    jax.ShapeDtypeStruct((out_width, out_width), f32),
-                ),
-                in_specs=[vmem] * 2,
-                compiler_params=params,
-                name="prepare",
-                cost_estimate=pl.CostEstimate(
-                    flops=2_000_000_000, bytes_accessed=6_000_000, transcendentals=0
-                ),
-            )(kernel, gather.rows.reshape(out_width, out_width))
+                jax.ShapeDtypeStruct((out_width, out_width), f32),
+                "prepare",
+                gather.rows.reshape(out_width, out_width),
+                cost_estimate=waiting,
+            )
         )
         return lax.optimization_barrier((got, *prepared))[0]
 
     mine, other = sum_all(send, keep, beside)
-    turned, both = prepared
+    (both,) = prepared
     far_feat, far_slope = far_pixels
     own_gram, grad = pl.pallas_call(
         functools.partial(backward_kernel, shape, pixel_total),

time: 45 us -> 44.8 us (level)
  starting transfers between devices: 23.8 us -> 22.6 us
  waiting for transfers between devices: 8.15 us -> 9.15 us
    ppermute x13, starting transfers between devices: 19.5 us -> 18.3 us  [swap(): lax.ppermute(value, ('rows', 'cols'), [(i, i ^ flip(i)) for i in range(to...]
    ppermute x13, waiting for transfers between devices: 8.14 us -> 9.14 us  [swap(): lax.ppermute(value, ('rows', 'cols'), [(i, i ^ flip(i)) for i in range(to...]
    pallas_call x14 -> x16, Pallas kernels: 0.35 us -> 1.34 us  [local(): pl.pallas_call(body, out_shape=out_shape, in_specs=[pl.BlockSpec(memory_s...]
    pallas_call x1 -> x0, Pallas kernels: 0.97 us -> none  [beside(): pl.pallas_call(prepare_kernel, out_shape=(jax.ShapeDtypeStruct((9 * out_w...]
  transfers between devices with their start and end apart: 17 -> 17, of which waited for: 10 -> 10; matrix products, arithmetic and copies ran while one was open for 0% -> 0% of each run, Pallas kernels for 12% -> 13%
where the time goes in v11:
time: 44.8 us; the launch traced here: 44.7 us
  starting transfers between devices  22.6 us (50%)
  Pallas kernels  11.1 us (25%)
  waiting for transfers between devices  9.15 us (20%)
  local copies, waits for them, and re-layouts  1.06 us (2%)
  between operations  0.79 us (2%)
    ppermute x13, starting transfers between devices, swap(): lax.ppermute(value, ('rows', 'cols'), [(i, i ^ flip(i)) for i in range(to...  18.3 us
    ppermute x13, waiting for transfers between devices, swap(): lax.ppermute(value, ('rows', 'cols'), [(i, i ^ flip(i)) for i in range(to...  9.14 us
    pallas_call x1, Pallas kernels, on_device(): pl.pallas_call(functools.partial(backward_kernel, shape, pixel_total), ou...  4.44 us
    ppermute x3, starting transfers between devices, swap_rows(): return lax.ppermute(value, ('rows', 'cols'), perm)  3.73 us
    pallas_call x1, Pallas kernels, on_device(): pl.pallas_call(functools.partial(inner_kernel, shape), out_shape=(jax.Sha...  3.36 us
    pallas_call x16, Pallas kernels, local(): pl.pallas_call(body, out_shape=out_shape, in_specs=[pl.BlockSpec(memory_s...  1.34 us
    unnamed x10, local copies, waits for them, and re-layouts  1.06 us
    pallas_call x1, Pallas kernels, beside(): pl.pallas_call(functools.partial(beyond_kernel, shape), out_shape=(jax.Sh...  1.04 us
  transfers between devices with their start and end apart: 17, of which 10 were waited for; matrix products, arithmetic and copies ran while one was open for 0% of the time, Pallas kernels for 13%

profile of v11, /device:TPU:0, one launch (start us, length us, event | category | flops | bytes accessed | tf_op | source)
XLA Modules:
  0.0 44.7 jit_solution(15033067627064653876)
XLA Ops:
  0.7 1.0 %copy-done.2 = bf16[8,128,256]{2,1,0:T(8,128)(2,1)S(1)} copy-done((bf16[8,128,256]{2,1,0:T(8,128)(2,1)S(1)}, bf16[8,128,256]{2,1,0:T(8,128)(2,1)}, u32[]{:S(2)}) %copy-start.2) | copy-done | bytes 524312
  1.7 0.5 %collective-permute-start.1 = (bf16[2,8,256]{2,1,0:T(8,128)(2,1)S(1)}, bf16[2,8,256]{2,1,0:T(8,128)(2,1)S(1)}, u32[]{:S(2)}, u32[]{:S(2)}) collective-permute-start(bf16[2,8,256]{2,1,0:T(8,128)(2,1)S(1)} %get-tuple-element.46), channel_id=1, source_target_pairs={{0,1},{1,0},{2,3},{3,2},{4,5},{5,4},{6,7},{7,6},{8,9},{9,8},{10,11... | collective-permute-start | bytes 24584 | tf_op jit(solution)/shard_map/ppermute | solution.py:581
  2.3 2.6 %collective-permute-start = (bf16[256,256]{1,0:T(8,128)(2,1)S(1)}, bf16[256,256]{1,0:T(8,128)(2,1)S(1)}, u32[]{:S(2)}, u32[]{:S(2)}) collective-permute-start(bf16[256,256]{1,0:T(8,128)(2,1)S(1)} %get-tuple-element.44), channel_id=1, source_target_pairs={{0,2},{1,3},{2,0},{3,1},{4,6},{5,7},{6,4},{7,5},{8,10},{9,11},{10,... | collective-permute-start | bytes 393224 | tf_op jit(solution)/shard_map/ppermute | solution.py:31
  4.9 1.2 %collective-permute-start.3 = (bf16[16,256]{1,0:T(8,128)(2,1)S(1)}, bf16[16,256]{1,0:T(8,128)(2,1)S(1)}, u32[]{:S(2)}, u32[]{:S(2)}) collective-permute-start(bf16[16,256]{1,0:T(8,128)(2,1)S(1)} %get-tuple-element.48), channel_id=1, source_target_pairs={{0,2},{1,3},{2,0},{3,1},{4,6},{5,7},{6,4},{7,5},{8,10},{9,11},{10,... | collective-permute-start | bytes 24584 | tf_op jit(solution)/shard_map/ppermute | solution.py:31
  6.0 3.4 %inner_rows.1 = (bf16[768,512]{1,0:T(8,128)(2,1)S(1)}, bf16[768,512]{1,0:T(8,128)(2,1)S(1)}, f32[1280,128]{1,0:T(8,128)S(1)}, f32[1,512]{1,0:T(1,128)S(1)}, f32[512,512]{1,0:T(8,128)S(1)}) custom-call(bf16[8,128,256]{2,1,0:T(8,128)(2,1)S(1)} %copy-done.3, bf16[2,8,256]{2,1,0:T(8,128)(2,1)S(1)} %get-tuple-element.49.left_ref, ...), custom_call_target="tpu_custom_call" | custom-call | flops 2214592512 | bytes 6000000 | tf_op jit(solution)/shard_map/inner_rows/pallas_call | solution.py:602
  9.4 0.7 %turn.1.turned_ref = bf16[4608,256]{1,0:T(8,128)(2,1)S(1)} custom-call(bf16[2304,512]{1,0:T(8,128)(2,1)S(1)} %bitcast.23), custom_call_target="tpu_custom_call" | custom-call | flops 1500000000 | bytes 100000 | tf_op jit(solution)/shard_map/turn/pallas_call | solution.py:52
  10.1 0.9 %outer_rows.1 = (bf16[256,512]{1,0:T(8,128)(2,1)S(1)}, bf16[256,512]{1,0:T(8,128)(2,1)S(1)}, bf16[640,128]{1,0:T(8,128)(2,1)S(1)}, f32[640,128]{1,0:T(8,128)S(1)}) custom-call(bf16[256,256]{1,0:T(8,128)(2,1)S(1)} %collective-permute-done.even_ref, bf16[272,256]{1,0:T(8,128)(2,1)S(1)} %collective-permute-done.2.odd_ref, ...), custom_call_target="tpu_custom_call" | custom-call | tf_op jit(solution)/shard_map/outer_rows/pallas_call | solution.py:633
  11.0 0.6 %collective-permute-start.4 = (bf16[640,128]{1,0:T(8,128)(2,1)S(1)}, bf16[640,128]{1,0:T(8,128)(2,1)S(1)}, u32[]{:S(2)}, u32[]{:S(2)}) collective-permute-start(bf16[640,128]{1,0:T(8,128)(2,1)S(1)} %get-tuple-element.57), channel_id=1, source_target_pairs={{0,1},{1,0},{2,3},{3,2},{4,5},{5,4},{6,7},{7,6},{8,9},{9,8},{10,11... | collective-permute-start | bytes 491528 | tf_op jit(solution)/shard_map/ppermute | solution.py:48
  11.6 1.0 %collective-permute-done.4.got_ref = bf16[640,128]{1,0:T(8,128)(2,1)S(1)} collective-permute-done((bf16[640,128]{1,0:T(8,128)(2,1)S(1)}, bf16[640,128]{1,0:T(8,128)(2,1)S(1)}, u32[]{:S(2)}, u32[]{:S(2)}) %collective-permute-start.4) | collective-permute-done | bytes 163872 | tf_op jit(solution)/shard_map/ppermute | solution.py:48
  12.6 4.3 %collective-permute-start.5 = (bf16[320,128]{1,0:T(8,128)(2,1)S(1)}, bf16[320,128]{1,0:T(8,128)(2,1)S(1)}, u32[]{:S(2)}, u32[]{:S(2)}) collective-permute-start(bf16[320,128]{1,0:T(8,128)(2,1)S(1)} %get-tuple-element.59), channel_id=1, source_target_pairs={{0,3},{1,4},{2,7},{3,0},{4,1},{5,6},{6,5},{7,2},{8,13},{9,10},{10,... | collective-permute-start | bytes 245768 | tf_op jit(solution)/shard_map/ppermute | solution.py:48
  17.0 2.6 %collective-permute-start.10 = (bf16[1,16,512]{2,1,0:T(8,128)(2,1)S(1)}, bf16[1,16,512]{2,1,0:T(8,128)(2,1)S(1)}, u32[]{:S(2)}, u32[]{:S(2)}) collective-permute-start(bf16[1,16,512]{2,1,0:T(8,128)(2,1)S(1)} %get-tuple-element.63), channel_id=1, source_target_pairs={{0,17},{1,16},{2,19},{3,18},{4,21},{5,20},{6,23},{7,22},{8,25},{9,... | collective-permute-start | bytes 49160 | tf_op jit(solution)/shard_map/ppermute | solution.py:48
  19.6 0.8 %collective-permute-start.6 = (bf16[160,128]{1,0:T(8,128)(2,1)S(1)}, bf16[160,128]{1,0:T(8,128)(2,1)S(1)}, u32[]{:S(2)}, u32[]{:S(2)}) collective-permute-start(bf16[160,128]{1,0:T(8,128)(2,1)S(1)} %get-tuple-element.61), channel_id=1, source_target_pairs={{0,5},{1,2},{2,1},{3,6},{4,7},{5,0},{6,3},{7,4},{8,11},{9,12},{10,... | collective-permute-start | bytes 122888 | tf_op jit(solution)/shard_map/ppermute | solution.py:48
  20.3 0.7 %collective-permute-done.10 = bf16[1,16,512]{2,1,0:T(8,128)(2,1)S(1)} collective-permute-done((bf16[1,16,512]{2,1,0:T(8,128)(2,1)S(1)}, bf16[1,16,512]{2,1,0:T(8,128)(2,1)S(1)}, u32[]{:S(2)}, u32[]{:S(2)}) %collective-permute-start.10) | collective-permute-done | bytes 16416 | tf_op jit(solution)/shard_map/ppermute | solution.py:48
  21.1 1.5 %collective-permute-start.11 = (bf16[2,16,512]{2,1,0:T(8,128)(2,1)S(1)}, bf16[2,16,512]{2,1,0:T(8,128)(2,1)S(1)}, u32[]{:S(2)}, u32[]{:S(2)}) collective-permute-start(bf16[2,16,512]{2,1,0:T(8,128)(2,1)S(1)} %bitcast.41), channel_id=1, source_target_pairs={{0,9},{1,8},{2,11},{3,10},{4,13},{5,12},{6,15},{7,14},{8,1},{9,0},... | collective-permute-start | bytes 98312 | tf_op jit(solution)/shard_map/ppermute | solution.py:48
  22.6 0.5 %collective-permute-done.6.got_ref = bf16[160,128]{1,0:T(8,128)(2,1)S(1)} collective-permute-done((bf16[160,128]{1,0:T(8,128)(2,1)S(1)}, bf16[160,128]{1,0:T(8,128)(2,1)S(1)}, u32[]{:S(2)}, u32[]{:S(2)}) %collective-permute-start.6) | collective-permute-done | bytes 40992 | tf_op jit(solution)/shard_map/ppermute | solution.py:48
  23.1 1.7 %collective-permute-start.7 = (bf16[160,128]{1,0:T(8,128)(2,1)S(1)}, bf16[160,128]{1,0:T(8,128)(2,1)S(1)}, u32[]{:S(2)}, u32[]{:S(2)}) collective-permute-start(bf16[160,128]{1,0:T(8,128)(2,1)S(1)} %add.3.keep_ref), channel_id=1, source_target_pairs={{0,9},{1,8},{2,11},{3,10},{4,13},{5,12},{6,15},{7,14},{8,1},{9,0},... | collective-permute-start | bytes 122888 | tf_op jit(solution)/shard_map/ppermute | solution.py:48
  24.8 1.2 %collective-permute-start.12 = (bf16[4,16,512]{2,1,0:T(8,128)(2,1)S(1)}, bf16[4,16,512]{2,1,0:T(8,128)(2,1)S(1)}, u32[]{:S(2)}, u32[]{:S(2)}) collective-permute-start(bf16[4,16,512]{2,1,0:T(8,128)(2,1)S(1)} %bitcast.36), channel_id=1, source_target_pairs={{0,3},{1,4},{2,7},{3,0},{4,1},{5,6},{6,5},{7,2},{8,13},{9,10},{10,... | collective-permute-start | bytes 196616 | tf_op jit(solution)/shard_map/ppermute | solution.py:48
  26.1 0.6 %collective-permute-done.7.got_ref = bf16[160,128]{1,0:T(8,128)(2,1)S(1)} collective-permute-done((bf16[160,128]{1,0:T(8,128)(2,1)S(1)}, bf16[160,128]{1,0:T(8,128)(2,1)S(1)}, u32[]{:S(2)}, u32[]{:S(2)}) %collective-permute-start.7) | collective-permute-done | bytes 40992 | tf_op jit(solution)/shard_map/ppermute | solution.py:48
  26.7 2.6 %collective-permute-start.8 = (bf16[160,128]{1,0:T(8,128)(2,1)S(1)}, bf16[160,128]{1,0:T(8,128)(2,1)S(1)}, u32[]{:S(2)}, u32[]{:S(2)}) collective-permute-start(bf16[160,128]{1,0:T(8,128)(2,1)S(1)} %add.4.keep_ref), channel_id=1, source_target_pairs={{0,17},{1,16},{2,19},{3,18},{4,21},{5,20},{6,23},{7,22},{8,25},{9,... | collective-permute-start | bytes 122888 | tf_op jit(solution)/shard_map/ppermute | solution.py:48
  29.4 0.5 %collective-permute-start.13 = (bf16[8,16,512]{2,1,0:T(8,128)(2,1)S(1)}, bf16[8,16,512]{2,1,0:T(8,128)(2,1)S(1)}, u32[]{:S(2)}, u32[]{:S(2)}) collective-permute-start(bf16[8,16,512]{2,1,0:T(8,128)(2,1)S(1)} %bitcast.30), channel_id=1, source_target_pairs={{0,5},{1,2},{2,1},{3,6},{4,7},{5,0},{6,3},{7,4},{8,11},{9,12},{10,... | collective-permute-start | bytes 393224 | tf_op jit(solution)/shard_map/ppermute | solution.py:48
  29.9 1.4 %collective-permute-done.8.got_ref = bf16[160,128]{1,0:T(8,128)(2,1)S(1)} collective-permute-done((bf16[160,128]{1,0:T(8,128)(2,1)S(1)}, bf16[160,128]{1,0:T(8,128)(2,1)S(1)}, u32[]{:S(2)}, u32[]{:S(2)}) %collective-permute-start.8) | collective-permute-done | bytes 40992 | tf_op jit(solution)/shard_map/ppermute | solution.py:48
  31.3 0.5 %collective-permute-start.9 = (bf16[160,128]{1,0:T(8,128)(2,1)S(1)}, bf16[160,128]{1,0:T(8,128)(2,1)S(1)}, u32[]{:S(2)}, u32[]{:S(2)}) collective-permute-start(bf16[160,128]{1,0:T(8,128)(2,1)S(1)} %add.5), channel_id=1, source_target_pairs={{0,5},{1,2},{2,1},{3,6},{4,7},{5,0},{6,3},{7,4},{8,11},{9,12},{10,... | collective-permute-start | bytes 122888 | tf_op jit(solution)/shard_map/ppermute | solution.py:48
  31.8 2.1 %collective-permute-done.13 = bf16[8,16,512]{2,1,0:T(8,128)(2,1)S(1)} collective-permute-done((bf16[8,16,512]{2,1,0:T(8,128)(2,1)S(1)}, bf16[8,16,512]{2,1,0:T(8,128)(2,1)S(1)}, u32[]{:S(2)}, u32[]{:S(2)}) %collective-permute-start.13) | collective-permute-done | bytes 131104 | tf_op jit(solution)/shard_map/ppermute | solution.py:48
  33.9 0.9 %collective-permute-done.9 = bf16[160,128]{1,0:T(8,128)(2,1)S(1)} collective-permute-done((bf16[160,128]{1,0:T(8,128)(2,1)S(1)}, bf16[160,128]{1,0:T(8,128)(2,1)S(1)}, u32[]{:S(2)}, u32[]{:S(2)}) %collective-permute-start.9) | collective-permute-done | bytes 40992 | tf_op jit(solution)/shard_map/ppermute | solution.py:48
  34.8 1.7 %collective-permute-start.14 = (bf16[320,128]{1,0:T(8,128)(2,1)S(1)}, bf16[320,128]{1,0:T(8,128)(2,1)S(1)}, u32[]{:S(2)}, u32[]{:S(2)}) collective-permute-start(bf16[320,128]{1,0:T(8,128)(2,1)S(1)} %bitcast.33), channel_id=1, source_target_pairs={{0,3},{1,4},{2,7},{3,0},{4,1},{5,6},{6,5},{7,2},{8,13},{9,10},{10,... | collective-permute-start | bytes 245768 | tf_op jit(solution)/shard_map/ppermute | solution.py:48
  36.5 1.0 %beyond.1 = (bf16[288,512]{1,0:T(8,128)(2,1)S(1)}, bf16[288,512]{1,0:T(8,128)(2,1)S(1)}) custom-call(bf16[8,128,256]{2,1,0:T(8,128)(2,1)S(1)} %copy-done.3, bf16[256,256]{1,0:T(8,128)(2,1)S(1)} %collective-permute-done.even_ref, bf16[272,256]{1,0:T(8,128)(2,1)S(1)} %collective-permute-done.2.odd_ref, ...), custom_call_target="tpu_custom_call" | custom-call | flops 8000000000 | bytes 100000 | tf_op jit(solution)/shard_map/beyond/pallas_call | solution.py:665
  37.5 0.5 %collective-permute-done.15.other_ref = bf16[16,16,512]{2,1,0:T(8,128)(2,1)S(1)} collective-permute-done((bf16[16,16,512]{2,1,0:T(8,128)(2,1)S(1)}, bf16[16,16,512]{2,1,0:T(8,128)(2,1)S(1)}, u32[]{:S(2)}, u32[]{:S(2)}) %collective-permute-start.15) | collective-permute-done | bytes 262176 | tf_op jit(solution)/shard_map/ppermute | solution.py:48
  38.1 0.6 %collective-permute-done.14 = bf16[320,128]{1,0:T(8,128)(2,1)S(1)} collective-permute-done((bf16[320,128]{1,0:T(8,128)(2,1)S(1)}, bf16[320,128]{1,0:T(8,128)(2,1)S(1)}, u32[]{:S(2)}, u32[]{:S(2)}) %collective-permute-start.14) | collective-permute-done | bytes 81952 | tf_op jit(solution)/shard_map/ppermute | solution.py:48
  38.8 0.3 collective-permute-start.16
  39.1 0.3 prepare.1.both_ref
  39.4 0.8 %collective-permute-done.16.other_ref = bf16[640,128]{1,0:T(8,128)(2,1)S(1)} collective-permute-done((bf16[640,128]{1,0:T(8,128)(2,1)S(1)}, bf16[640,128]{1,0:T(8,128)(2,1)S(1)}, u32[]{:S(2)}, u32[]{:S(2)}) %collective-permute-start.16) | collective-permute-done | bytes 163872 | tf_op jit(solution)/shard_map/ppermute | solution.py:48
  40.2 4.4 %grad_conv.1 = (f32[16,512]{1,0:T(8,128)}, bf16[1024,256]{1,0:T(8,128)(2,1)}) custom-call(bf16[640,128]{1,0:T(8,128)(2,1)S(1)} %bitcast.27, bf16[640,128]{1,0:T(8,128)(2,1)S(1)} %collective-permute-done.16.other_ref, f32[512,512]{1,0:T(8,128)S(1)} %prepare.1.both_ref, bf16[768,512]{1,0:T(8,128)(2,1)S(1)} %get-tuple-element.79.in_feat_ref, ...), custom_call_target="tpu_custom_call" | custom-call | tf_op jit(solution)/shard_map/grad_conv/pallas_call | solution.py:703
  (32 shorter events, 0.4 us)
Async XLA Ops:
  0.6 4.2 %copy-start.1 = (f32[16,512]{1,0:T(8,128)S(1)}, f32[16,512]{1,0:T(8,128)}, u32[]{:S(2)}) copy-start(f32[16,512]{1,0:T(8,128)} %target_ref.1) | copy-start | bytes 98308
  0.6 1.0 %copy-start.2 = (bf16[8,128,256]{2,1,0:T(8,128)(2,1)S(1)}, bf16[8,128,256]{2,1,0:T(8,128)(2,1)}, u32[]{:S(2)}) copy-start(bf16[8,128,256]{2,1,0:T(8,128)(2,1)} %own_ref.3) | copy-start | bytes 1572868
  1.7 4.3 %copy-start = (bf16[3,3,256,512]{3,2,1,0:T(8,128)(2,1)S(1)}, bf16[3,3,256,512]{3,2,1,0:T(8,128)(2,1)}, u32[]{:S(2)}) copy-start(bf16[3,3,256,512]{3,2,1,0:T(8,128)(2,1)} %param.5) | copy-start | bytes 7077892
  1.7 4.3 %copy-start.3 = (bf16[8,128,256]{2,1,0:T(8,128)(2,1)S(1)}, bf16[8,128,256]{2,1,0:T(8,128)(2,1)}, u32[]{:S(2)}) copy-start(bf16[8,128,256]{2,1,0:T(8,128)(2,1)} %own_ref.3) | copy-start | bytes 1572868
  1.7 4.3 %copy-start.4 = (bf16[512]{0:T(512)(128)(2,1)S(1)}, bf16[512]{0:T(512)(128)(2,1)}, u32[]{:S(2)}) copy-start(bf16[512]{0:T(512)(128)(2,1)} %bias_ref.1) | copy-start | bytes 3076
  1.7 3.1 %collective-permute-start.1 = (bf16[2,8,256]{2,1,0:T(8,128)(2,1)S(1)}, bf16[2,8,256]{2,1,0:T(8,128)(2,1)S(1)}, u32[]{:S(2)}, u32[]{:S(2)}) collective-permute-start(bf16[2,8,256]{2,1,0:T(8,128)(2,1)S(1)} %get-tuple-element.46), channel_id=1, source_target_pairs={{0,1},{1,0},{2,3},{3,2},{4,5},{5,4},{6,7},{7,6},{8,9},{9,8},{10,11... | collective-permute-start | bytes 24584 | tf_op jit(solution)/shard_map/ppermute | solution.py:581
  2.3 7.8 %collective-permute-start = (bf16[256,256]{1,0:T(8,128)(2,1)S(1)}, bf16[256,256]{1,0:T(8,128)(2,1)S(1)}, u32[]{:S(2)}, u32[]{:S(2)}) collective-permute-start(bf16[256,256]{1,0:T(8,128)(2,1)S(1)} %get-tuple-element.44), channel_id=1, source_target_pairs={{0,2},{1,3},{2,0},{3,1},{4,6},{5,7},{6,4},{7,5},{8,10},{9,11},{10,... | collective-permute-start | bytes 393224 | tf_op jit(solution)/shard_map/ppermute | solution.py:31
  4.9 5.2 %collective-permute-start.3 = (bf16[16,256]{1,0:T(8,128)(2,1)S(1)}, bf16[16,256]{1,0:T(8,128)(2,1)S(1)}, u32[]{:S(2)}, u32[]{:S(2)}) collective-permute-start(bf16[16,256]{1,0:T(8,128)(2,1)S(1)} %get-tuple-element.48), channel_id=1, source_target_pairs={{0,2},{1,3},{2,0},{3,1},{4,6},{5,7},{6,4},{7,5},{8,10},{9,11},{10,... | collective-permute-start | bytes 24584 | tf_op jit(solution)/shard_map/ppermute | solution.py:31
  6.0 4.1 %collective-permute-start.2 = (bf16[272,256]{1,0:T(8,128)(2,1)S(1)}, bf16[272,256]{1,0:T(8,128)(2,1)S(1)}, u32[]{:S(2)}, u32[]{:S(2)}) collective-permute-start(bf16[272,256]{1,0:T(8,128)(2,1)S(1)} %get-tuple-element.47), channel_id=1, source_target_pairs={{0,1},{1,0},{2,4},{3,5},{4,2},{5,3},{6,8},{7,9},{8,6},{9,7},{10,12... | collective-permute-start | bytes 417800 | tf_op jit(solution)/shard_map/ppermute | solution.py:31
  11.0 1.6 %collective-permute-start.4 = (bf16[640,128]{1,0:T(8,128)(2,1)S(1)}, bf16[640,128]{1,0:T(8,128)(2,1)S(1)}, u32[]{:S(2)}, u32[]{:S(2)}) collective-permute-start(bf16[640,128]{1,0:T(8,128)(2,1)S(1)} %get-tuple-element.57), channel_id=1, source_target_pairs={{0,1},{1,0},{2,3},{3,2},{4,5},{5,4},{6,7},{7,6},{8,9},{9,8},{10,11... | collective-permute-start | bytes 491528 | tf_op jit(solution)/shard_map/ppermute | solution.py:48
  12.6 6.9 %collective-permute-start.5 = (bf16[320,128]{1,0:T(8,128)(2,1)S(1)}, bf16[320,128]{1,0:T(8,128)(2,1)S(1)}, u32[]{:S(2)}, u32[]{:S(2)}) collective-permute-start(bf16[320,128]{1,0:T(8,128)(2,1)S(1)} %get-tuple-element.59), channel_id=1, source_target_pairs={{0,3},{1,4},{2,7},{3,0},{4,1},{5,6},{6,5},{7,2},{8,13},{9,10},{10,... | collective-permute-start | bytes 245768 | tf_op jit(solution)/shard_map/ppermute | solution.py:48
  17.0 4.1 %collective-permute-start.10 = (bf16[1,16,512]{2,1,0:T(8,128)(2,1)S(1)}, bf16[1,16,512]{2,1,0:T(8,128)(2,1)S(1)}, u32[]{:S(2)}, u32[]{:S(2)}) collective-permute-start(bf16[1,16,512]{2,1,0:T(8,128)(2,1)S(1)} %get-tuple-element.63), channel_id=1, source_target_pairs={{0,17},{1,16},{2,19},{3,18},{4,21},{5,20},{6,23},{7,22},{8,25},{9,... | collective-permute-start | bytes 49160 | tf_op jit(solution)/shard_map/ppermute | solution.py:48
  19.6 3.5 %collective-permute-start.6 = (bf16[160,128]{1,0:T(8,128)(2,1)S(1)}, bf16[160,128]{1,0:T(8,128)(2,1)S(1)}, u32[]{:S(2)}, u32[]{:S(2)}) collective-permute-start(bf16[160,128]{1,0:T(8,128)(2,1)S(1)} %get-tuple-element.61), channel_id=1, source_target_pairs={{0,5},{1,2},{2,1},{3,6},{4,7},{5,0},{6,3},{7,4},{8,11},{9,12},{10,... | collective-permute-start | bytes 122888 | tf_op jit(solution)/shard_map/ppermute | solution.py:48
  21.1 3.8 %collective-permute-start.11 = (bf16[2,16,512]{2,1,0:T(8,128)(2,1)S(1)}, bf16[2,16,512]{2,1,0:T(8,128)(2,1)S(1)}, u32[]{:S(2)}, u32[]{:S(2)}) collective-permute-start(bf16[2,16,512]{2,1,0:T(8,128)(2,1)S(1)} %bitcast.41), channel_id=1, source_target_pairs={{0,9},{1,8},{2,11},{3,10},{4,13},{5,12},{6,15},{7,14},{8,1},{9,0},... | collective-permute-start | bytes 98312 | tf_op jit(solution)/shard_map/ppermute | solution.py:48
  23.1 3.6 %collective-permute-start.7 = (bf16[160,128]{1,0:T(8,128)(2,1)S(1)}, bf16[160,128]{1,0:T(8,128)(2,1)S(1)}, u32[]{:S(2)}, u32[]{:S(2)}) collective-permute-start(bf16[160,128]{1,0:T(8,128)(2,1)S(1)} %add.3.keep_ref), channel_id=1, source_target_pairs={{0,9},{1,8},{2,11},{3,10},{4,13},{5,12},{6,15},{7,14},{8,1},{9,0},... | collective-permute-start | bytes 122888 | tf_op jit(solution)/shard_map/ppermute | solution.py:48
  24.8 4.5 %collective-permute-start.12 = (bf16[4,16,512]{2,1,0:T(8,128)(2,1)S(1)}, bf16[4,16,512]{2,1,0:T(8,128)(2,1)S(1)}, u32[]{:S(2)}, u32[]{:S(2)}) collective-permute-start(bf16[4,16,512]{2,1,0:T(8,128)(2,1)S(1)} %bitcast.36), channel_id=1, source_target_pairs={{0,3},{1,4},{2,7},{3,0},{4,1},{5,6},{6,5},{7,2},{8,13},{9,10},{10,... | collective-permute-start | bytes 196616 | tf_op jit(solution)/shard_map/ppermute | solution.py:48
  26.7 4.5 %collective-permute-start.8 = (bf16[160,128]{1,0:T(8,128)(2,1)S(1)}, bf16[160,128]{1,0:T(8,128)(2,1)S(1)}, u32[]{:S(2)}, u32[]{:S(2)}) collective-permute-start(bf16[160,128]{1,0:T(8,128)(2,1)S(1)} %add.4.keep_ref), channel_id=1, source_target_pairs={{0,17},{1,16},{2,19},{3,18},{4,21},{5,20},{6,23},{7,22},{8,25},{9,... | collective-permute-start | bytes 122888 | tf_op jit(solution)/shard_map/ppermute | solution.py:48
  29.4 4.5 %collective-permute-start.13 = (bf16[8,16,512]{2,1,0:T(8,128)(2,1)S(1)}, bf16[8,16,512]{2,1,0:T(8,128)(2,1)S(1)}, u32[]{:S(2)}, u32[]{:S(2)}) collective-permute-start(bf16[8,16,512]{2,1,0:T(8,128)(2,1)S(1)} %bitcast.30), channel_id=1, source_target_pairs={{0,5},{1,2},{2,1},{3,6},{4,7},{5,0},{6,3},{7,4},{8,11},{9,12},{10,... | collective-permute-start | bytes 393224 | tf_op jit(solution)/shard_map/ppermute | solution.py:48
  31.3 3.5 %collective-permute-start.9 = (bf16[160,128]{1,0:T(8,128)(2,1)S(1)}, bf16[160,128]{1,0:T(8,128)(2,1)S(1)}, u32[]{:S(2)}, u32[]{:S(2)}) collective-permute-start(bf16[160,128]{1,0:T(8,128)(2,1)S(1)} %add.5), channel_id=1, source_target_pairs={{0,5},{1,2},{2,1},{3,6},{4,7},{5,0},{6,3},{7,4},{8,11},{9,12},{10,... | collective-permute-start | bytes 122888 | tf_op jit(solution)/shard_map/ppermute | solution.py:48
  34.8 3.9 %collective-permute-start.14 = (bf16[320,128]{1,0:T(8,128)(2,1)S(1)}, bf16[320,128]{1,0:T(8,128)(2,1)S(1)}, u32[]{:S(2)}, u32[]{:S(2)}) collective-permute-start(bf16[320,128]{1,0:T(8,128)(2,1)S(1)} %bitcast.33), channel_id=1, source_target_pairs={{0,3},{1,4},{2,7},{3,0},{4,1},{5,6},{6,5},{7,2},{8,13},{9,10},{10,... | collective-permute-start | bytes 245768 | tf_op jit(solution)/shard_map/ppermute | solution.py:48
  36.5 1.5 %collective-permute-start.15 = (bf16[16,16,512]{2,1,0:T(8,128)(2,1)S(1)}, bf16[16,16,512]{2,1,0:T(8,128)(2,1)S(1)}, u32[]{:S(2)}, u32[]{:S(2)}) collective-permute-start(bf16[16,16,512]{2,1,0:T(8,128)(2,1)S(1)} %bitcast.28), channel_id=1, source_target_pairs={{0,1},{1,0},{2,3},{3,2},{4,5},{5,4},{6,7},{7,6},{8,9},{9,8},{10,11... | collective-permute-start | bytes 786440 | tf_op jit(solution)/shard_map/ppermute | solution.py:48
  38.8 1.5 %collective-permute-start.16 = (bf16[640,128]{1,0:T(8,128)(2,1)S(1)}, bf16[640,128]{1,0:T(8,128)(2,1)S(1)}, u32[]{:S(2)}, u32[]{:S(2)}) collective-permute-start(bf16[640,128]{1,0:T(8,128)(2,1)S(1)} %bitcast.26), channel_id=1, source_target_pairs={{0,1},{1,0},{2,3},{3,2},{4,5},{5,4},{6,7},{7,6},{8,9},{9,8},{10,11... | collective-permute-start | bytes 491528 | tf_op jit(solution)/shard_map/ppermute | solution.py:48

commit v12 on v11

--- a/solution.py
+++ b/solution.py
@@ -226,10 +226,10 @@
 
 
 def payload_kernel(target_ref, rows_ref, *refs):
-    even_ref, payload_ref, left_ref, right_ref, half_ref = refs[-5:]
+    odd_ref, payload_ref, left_ref, right_ref, half_ref = refs[-5:]
     main = rows_ref.shape[0]
     payload_ref[0:main, :] = rows_ref[...]
-    odd_ref = payload_ref.at[main:]
+    even_ref = payload_ref.at[main:]
     half_ref[0] = target_ref[...].astype(bf16)
     if len(refs) == 6:
         here = lax.axis_index("cols")
@@ -327,13 +327,13 @@
 
 
 def halo_rows(halo_refs, low_ref, high_ref):
-    even_ref, odd_ref, even_rim_ref = halo_refs
+    even_ref, odd_ref, odd_rim_ref = halo_refs
     row = lax.axis_index("rows")
     odd = lax.rem(row, 2)
-    main = even_ref.shape[0]
-    for at, even in ((slice(0, main), even_ref), (slice(main, None), even_rim_ref)):
-        low_ref[at, :] = jnp.where(odd == 0, odd_ref[at, :], even[...])
-        high_ref[at, :] = jnp.where(odd == 0, even[...], odd_ref[at, :])
+    main = odd_ref.shape[0]
+    for at, part in ((slice(0, main), odd_ref), (slice(main, None), odd_rim_ref)):
+        low_ref[at, :] = jnp.where(odd == 0, part[...], even_ref[at, :])
+        high_ref[at, :] = jnp.where(odd == 0, even_ref[at, :], part[...])
 
     @pl.when(row == 0)
     def _():
@@ -349,12 +349,12 @@
 
 
 def outer_kernel(
-    shape, even_ref, odd_ref, even_rim_ref, kernel_ref, base_ref, part_ref,
+    shape, even_ref, odd_ref, odd_rim_ref, kernel_ref, base_ref, part_ref,
     feat_ref, slope_ref, send_ref, keep_ref, low_ref, high_ref, cat_ref, gram_ref,
 ):
     tile_rows, tile_cols, in_width, out_width, step = shape
     span, main = 3 * in_width, 2 * tile_cols
-    halo_rows((even_ref, odd_ref, even_rim_ref), low_ref, high_ref)
+    halo_rows((even_ref, odd_ref, odd_rim_ref), low_ref, high_ref)
     for n, (source, at) in enumerate([(low_ref, tile_cols), (high_ref, 0)]):
         rim = source[main:, :].astype(f32)
         k = 4 * (1 - n)
@@ -381,11 +381,11 @@
 
 
 def beyond_kernel(
-    shape, own_ref, even_ref, odd_ref, even_rim_ref, left_ref, right_ref, kernel_ref, bias_ref,
+    shape, own_ref, even_ref, odd_ref, odd_rim_ref, left_ref, right_ref, kernel_ref, bias_ref,
     part_ref, feat_ref, slope_ref, low_ref, high_ref, cat_ref, edge_ref,
 ):
     tile_rows, tile_cols, in_width, out_width, step = shape
-    halo_rows((even_ref, odd_ref, even_rim_ref), low_ref, high_ref)
+    halo_rows((even_ref, odd_ref, odd_rim_ref), low_ref, high_ref)
     first = (lax.axis_index("rows") > 0).astype(f32)
     last = (lax.axis_index("rows") < lax.axis_size("rows") - 1).astype(f32)
     left = (lax.axis_index("cols") > 0).astype(f32)
@@ -582,19 +582,19 @@
     else:
         beyond = shift_cols(rims[1], rims[0])
     evens, odds = range(0, count, 2), range(1, count, 2)
-    even = swap_rows(evens, even)
+    odd = swap_rows(odds, odd)
     payload_shape = jax.ShapeDtypeStruct((2 * tile_cols + edge, in_width), bf16)
     end_shape = jax.ShapeDtypeStruct((edge, in_width), bf16)
     half_shape = jax.ShapeDtypeStruct((1, *target_gram.shape), bf16)
-    even_rim, odd, left, right, rows = local(
+    odd_rim, even, left, right, rows = local(
         payload_kernel,
         (end_shape, payload_shape, rim_shape, rim_shape, half_shape),
         "row_rims",
         target_gram,
-        odd,
+        even,
         *beyond,
     )
-    halo = [even, swap_rows(odds, odd), swap_rows(evens, even_rim)]
+    halo = [swap_rows(evens, even), odd, swap_rows(odds, odd_rim)]
     bits = (lax.axis_size("rows") * lax.axis_size("cols")).bit_length() - 1
     gather = Gather(rows)
     far = list(reversed(range(3, bits)))

time: 44.8 us -> 46.3 us (1.033)
  waiting for transfers between devices: 9.15 us -> 13.2 us
  starting transfers between devices: 22.6 us -> 20.1 us
    ppermute x13, starting transfers between devices: 18.3 us -> 14.8 us  [swap(): lax.ppermute(value, ('rows', 'cols'), [(i, i ^ flip(i)) for i in range(to...]
    ppermute x13, waiting for transfers between devices: 9.14 us -> 11 us  [swap(): lax.ppermute(value, ('rows', 'cols'), [(i, i ^ flip(i)) for i in range(to...]
    ppermute x3, waiting for transfers between devices: 0.01 us -> 1.38 us  [swap_rows(): return lax.ppermute(value, ('rows', 'cols'), perm)]
    ppermute x3, starting transfers between devices: 3.73 us -> 4.81 us  [swap_rows(): return lax.ppermute(value, ('rows', 'cols'), perm)]
    ppermute x1, waiting for transfers between devices: 0.01 us -> 0.75 us  [on_device(): beyond = [lax.ppermute(rims[0], 'cols', [(0, 1), (1, 0)])]]
  transfers between devices with their start and end apart: 17 -> 17, of which waited for: 10 -> 12; matrix products, arithmetic and copies ran while one was open for 0% -> 0% of each run, Pallas kernels for 13% -> 12%
where the time goes in v12:
time: 46.3 us; the launch traced here: 46.2 us
  starting transfers between devices  20.1 us (43%)
  waiting for transfers between devices  13.2 us (29%)
  Pallas kernels  11.1 us (24%)
  local copies, waits for them, and re-layouts  1.06 us (2%)
  between operations  0.79 us (2%)
    ppermute x13, starting transfers between devices, swap(): lax.ppermute(value, ('rows', 'cols'), [(i, i ^ flip(i)) for i in range(to...  14.8 us
    ppermute x13, waiting for transfers between devices, swap(): lax.ppermute(value, ('rows', 'cols'), [(i, i ^ flip(i)) for i in range(to...  11 us
    ppermute x3, starting transfers between devices, swap_rows(): return lax.ppermute(value, ('rows', 'cols'), perm)  4.81 us
    pallas_call x1, Pallas kernels, on_device(): pl.pallas_call(functools.partial(backward_kernel, shape, pixel_total), ou...  4.44 us
    pallas_call x1, Pallas kernels, on_device(): pl.pallas_call(functools.partial(inner_kernel, shape), out_shape=(jax.Sha...  3.36 us
    ppermute x3, waiting for transfers between devices, swap_rows(): return lax.ppermute(value, ('rows', 'cols'), perm)  1.38 us
    pallas_call x16, Pallas kernels, local(): pl.pallas_call(body, out_shape=out_shape, in_specs=[pl.BlockSpec(memory_s...  1.34 us
    unnamed x10, local copies, waits for them, and re-layouts  1.06 us
  transfers between devices with their start and end apart: 17, of which 12 were waited for; matrix products, arithmetic and copies ran while one was open for 0% of the time, Pallas kernels for 12%

profile of v12, /device:TPU:0, one launch (start us, length us, event | category | flops | bytes accessed | tf_op | source)
XLA Modules:
  0.0 46.2 jit_solution(14688878915473814404)
XLA Ops:
  0.7 1.0 %copy-done.2 = bf16[8,128,256]{2,1,0:T(8,128)(2,1)S(1)} copy-done((bf16[8,128,256]{2,1,0:T(8,128)(2,1)S(1)}, bf16[8,128,256]{2,1,0:T(8,128)(2,1)}, u32[]{:S(2)}) %copy-start.2) | copy-done | bytes 524312
  1.7 0.5 %collective-permute-start = (bf16[2,8,256]{2,1,0:T(8,128)(2,1)S(1)}, bf16[2,8,256]{2,1,0:T(8,128)(2,1)S(1)}, u32[]{:S(2)}, u32[]{:S(2)}) collective-permute-start(bf16[2,8,256]{2,1,0:T(8,128)(2,1)S(1)} %get-tuple-element.45), channel_id=1, source_target_pairs={{0,1},{1,0},{2,3},{3,2},{4,5},{5,4},{6,7},{7,6},{8,9},{9,8},{10,11... | collective-permute-start | bytes 24584 | tf_op jit(solution)/shard_map/ppermute | solution.py:581
  2.3 0.7 %collective-permute-done.refs_0_ = bf16[2,8,256]{2,1,0:T(8,128)(2,1)S(1)} collective-permute-done((bf16[2,8,256]{2,1,0:T(8,128)(2,1)S(1)}, bf16[2,8,256]{2,1,0:T(8,128)(2,1)S(1)}, u32[]{:S(2)}, u32[]{:S(2)}) %collective-permute-start) | collective-permute-done | bytes 8224 | tf_op jit(solution)/shard_map/ppermute | solution.py:581
  3.1 0.4 collective-permute-start.3
  3.5 4.3 %collective-permute-start.1 = (bf16[272,256]{1,0:T(8,128)(2,1)S(1)}, bf16[272,256]{1,0:T(8,128)(2,1)S(1)}, u32[]{:S(2)}, u32[]{:S(2)}) collective-permute-start(bf16[272,256]{1,0:T(8,128)(2,1)S(1)} %get-tuple-element.46), channel_id=1, source_target_pairs={{0,2},{1,3},{2,0},{3,1},{4,6},{5,7},{6,4},{7,5},{8,10},{9,11},{10,... | collective-permute-start | bytes 417800 | tf_op jit(solution)/shard_map/ppermute | solution.py:31
  7.9 3.4 %inner_rows.1 = (bf16[768,512]{1,0:T(8,128)(2,1)S(1)}, bf16[768,512]{1,0:T(8,128)(2,1)S(1)}, f32[1280,128]{1,0:T(8,128)S(1)}, f32[1,512]{1,0:T(1,128)S(1)}, f32[512,512]{1,0:T(8,128)S(1)}) custom-call(bf16[8,128,256]{2,1,0:T(8,128)(2,1)S(1)} %copy-done.3, bf16[2,8,256]{2,1,0:T(8,128)(2,1)S(1)} %get-tuple-element.49.left_ref, ...), custom_call_target="tpu_custom_call" | custom-call | flops 2214592512 | bytes 6000000 | tf_op jit(solution)/shard_map/inner_rows/pallas_call | solution.py:602
  11.2 0.7 %turn.1.turned_ref = bf16[4608,256]{1,0:T(8,128)(2,1)S(1)} custom-call(bf16[2304,512]{1,0:T(8,128)(2,1)S(1)} %bitcast.23), custom_call_target="tpu_custom_call" | custom-call | flops 1500000000 | bytes 100000 | tf_op jit(solution)/shard_map/turn/pallas_call | solution.py:52
  11.9 1.4 %collective-permute-done.1.even_ref = bf16[272,256]{1,0:T(8,128)(2,1)S(1)} collective-permute-done((bf16[272,256]{1,0:T(8,128)(2,1)S(1)}, bf16[272,256]{1,0:T(8,128)(2,1)S(1)}, u32[]{:S(2)}, u32[]{:S(2)}) %collective-permute-start.1) | collective-permute-done | bytes 139296 | tf_op jit(solution)/shard_map/ppermute | solution.py:31
  13.3 0.9 %outer_rows.1 = (bf16[256,512]{1,0:T(8,128)(2,1)S(1)}, bf16[256,512]{1,0:T(8,128)(2,1)S(1)}, bf16[640,128]{1,0:T(8,128)(2,1)S(1)}, f32[640,128]{1,0:T(8,128)S(1)}) custom-call(bf16[272,256]{1,0:T(8,128)(2,1)S(1)} %collective-permute-done.1.even_ref, bf16[256,256]{1,0:T(8,128)(2,1)S(1)} %collective-permute-done.2.odd_ref, ...), custom_call_target="tpu_custom_call" | custom-call | tf_op jit(solution)/shard_map/outer_rows/pallas_call | solution.py:633
  14.3 1.4 %collective-permute-done.4.got_ref = bf16[640,128]{1,0:T(8,128)(2,1)S(1)} collective-permute-done((bf16[640,128]{1,0:T(8,128)(2,1)S(1)}, bf16[640,128]{1,0:T(8,128)(2,1)S(1)}, u32[]{:S(2)}, u32[]{:S(2)}) %collective-permute-start.4) | collective-permute-done | bytes 163872 | tf_op jit(solution)/shard_map/ppermute | solution.py:48
  15.7 2.2 %collective-permute-start.5 = (bf16[320,128]{1,0:T(8,128)(2,1)S(1)}, bf16[320,128]{1,0:T(8,128)(2,1)S(1)}, u32[]{:S(2)}, u32[]{:S(2)}) collective-permute-start(bf16[320,128]{1,0:T(8,128)(2,1)S(1)} %get-tuple-element.59), channel_id=1, source_target_pairs={{0,3},{1,4},{2,7},{3,0},{4,1},{5,6},{6,5},{7,2},{8,13},{9,10},{10,... | collective-permute-start | bytes 245768 | tf_op jit(solution)/shard_map/ppermute | solution.py:48
  17.9 2.6 %collective-permute-start.10 = (bf16[1,16,512]{2,1,0:T(8,128)(2,1)S(1)}, bf16[1,16,512]{2,1,0:T(8,128)(2,1)S(1)}, u32[]{:S(2)}, u32[]{:S(2)}) collective-permute-start(bf16[1,16,512]{2,1,0:T(8,128)(2,1)S(1)} %get-tuple-element.63), channel_id=1, source_target_pairs={{0,17},{1,16},{2,19},{3,18},{4,21},{5,20},{6,23},{7,22},{8,25},{9,... | collective-permute-start | bytes 49160 | tf_op jit(solution)/shard_map/ppermute | solution.py:48
  20.5 1.6 %collective-permute-done.10 = bf16[1,16,512]{2,1,0:T(8,128)(2,1)S(1)} collective-permute-done((bf16[1,16,512]{2,1,0:T(8,128)(2,1)S(1)}, bf16[1,16,512]{2,1,0:T(8,128)(2,1)S(1)}, u32[]{:S(2)}, u32[]{:S(2)}) %collective-permute-start.10) | collective-permute-done | bytes 16416 | tf_op jit(solution)/shard_map/ppermute | solution.py:48
  22.1 1.4 %collective-permute-start.11 = (bf16[2,16,512]{2,1,0:T(8,128)(2,1)S(1)}, bf16[2,16,512]{2,1,0:T(8,128)(2,1)S(1)}, u32[]{:S(2)}, u32[]{:S(2)}) collective-permute-start(bf16[2,16,512]{2,1,0:T(8,128)(2,1)S(1)} %bitcast.41), channel_id=1, source_target_pairs={{0,9},{1,8},{2,11},{3,10},{4,13},{5,12},{6,15},{7,14},{8,1},{9,0},... | collective-permute-start | bytes 98312 | tf_op jit(solution)/shard_map/ppermute | solution.py:48
  23.5 0.5 collective-permute-done.6.got_ref
  24.0 1.5 %collective-permute-start.7 = (bf16[160,128]{1,0:T(8,128)(2,1)S(1)}, bf16[160,128]{1,0:T(8,128)(2,1)S(1)}, u32[]{:S(2)}, u32[]{:S(2)}) collective-permute-start(bf16[160,128]{1,0:T(8,128)(2,1)S(1)} %add.3.keep_ref), channel_id=1, source_target_pairs={{0,9},{1,8},{2,11},{3,10},{4,13},{5,12},{6,15},{7,14},{8,1},{9,0},... | collective-permute-start | bytes 122888 | tf_op jit(solution)/shard_map/ppermute | solution.py:48
  25.5 1.5 %collective-permute-start.12 = (bf16[4,16,512]{2,1,0:T(8,128)(2,1)S(1)}, bf16[4,16,512]{2,1,0:T(8,128)(2,1)S(1)}, u32[]{:S(2)}, u32[]{:S(2)}) collective-permute-start(bf16[4,16,512]{2,1,0:T(8,128)(2,1)S(1)} %bitcast.36), channel_id=1, source_target_pairs={{0,3},{1,4},{2,7},{3,0},{4,1},{5,6},{6,5},{7,2},{8,13},{9,10},{10,... | collective-permute-start | bytes 196616 | tf_op jit(solution)/shard_map/ppermute | solution.py:48
  27.0 0.6 %collective-permute-done.7.got_ref = bf16[160,128]{1,0:T(8,128)(2,1)S(1)} collective-permute-done((bf16[160,128]{1,0:T(8,128)(2,1)S(1)}, bf16[160,128]{1,0:T(8,128)(2,1)S(1)}, u32[]{:S(2)}, u32[]{:S(2)}) %collective-permute-start.7) | collective-permute-done | bytes 40992 | tf_op jit(solution)/shard_map/ppermute | solution.py:48
  27.6 2.4 %collective-permute-start.8 = (bf16[160,128]{1,0:T(8,128)(2,1)S(1)}, bf16[160,128]{1,0:T(8,128)(2,1)S(1)}, u32[]{:S(2)}, u32[]{:S(2)}) collective-permute-start(bf16[160,128]{1,0:T(8,128)(2,1)S(1)} %add.4.keep_ref), channel_id=1, source_target_pairs={{0,17},{1,16},{2,19},{3,18},{4,21},{5,20},{6,23},{7,22},{8,25},{9,... | collective-permute-start | bytes 122888 | tf_op jit(solution)/shard_map/ppermute | solution.py:48
  30.0 0.6 %collective-permute-start.13 = (bf16[8,16,512]{2,1,0:T(8,128)(2,1)S(1)}, bf16[8,16,512]{2,1,0:T(8,128)(2,1)S(1)}, u32[]{:S(2)}, u32[]{:S(2)}) collective-permute-start(bf16[8,16,512]{2,1,0:T(8,128)(2,1)S(1)} %bitcast.30), channel_id=1, source_target_pairs={{0,5},{1,2},{2,1},{3,6},{4,7},{5,0},{6,3},{7,4},{8,11},{9,12},{10,... | collective-permute-start | bytes 393224 | tf_op jit(solution)/shard_map/ppermute | solution.py:48
  30.7 1.5 %collective-permute-done.8.got_ref = bf16[160,128]{1,0:T(8,128)(2,1)S(1)} collective-permute-done((bf16[160,128]{1,0:T(8,128)(2,1)S(1)}, bf16[160,128]{1,0:T(8,128)(2,1)S(1)}, u32[]{:S(2)}, u32[]{:S(2)}) %collective-permute-start.8) | collective-permute-done | bytes 40992 | tf_op jit(solution)/shard_map/ppermute | solution.py:48
  32.2 0.1 collective-permute-start.9
  32.3 2.2 %collective-permute-done.13 = bf16[8,16,512]{2,1,0:T(8,128)(2,1)S(1)} collective-permute-done((bf16[8,16,512]{2,1,0:T(8,128)(2,1)S(1)}, bf16[8,16,512]{2,1,0:T(8,128)(2,1)S(1)}, u32[]{:S(2)}, u32[]{:S(2)}) %collective-permute-start.13) | collective-permute-done | bytes 131104 | tf_op jit(solution)/shard_map/ppermute | solution.py:48
  34.5 1.1 %collective-permute-done.9 = bf16[160,128]{1,0:T(8,128)(2,1)S(1)} collective-permute-done((bf16[160,128]{1,0:T(8,128)(2,1)S(1)}, bf16[160,128]{1,0:T(8,128)(2,1)S(1)}, u32[]{:S(2)}, u32[]{:S(2)}) %collective-permute-start.9) | collective-permute-done | bytes 40992 | tf_op jit(solution)/shard_map/ppermute | solution.py:48
  35.7 1.3 %collective-permute-start.14 = (bf16[320,128]{1,0:T(8,128)(2,1)S(1)}, bf16[320,128]{1,0:T(8,128)(2,1)S(1)}, u32[]{:S(2)}, u32[]{:S(2)}) collective-permute-start(bf16[320,128]{1,0:T(8,128)(2,1)S(1)} %bitcast.33), channel_id=1, source_target_pairs={{0,3},{1,4},{2,7},{3,0},{4,1},{5,6},{6,5},{7,2},{8,13},{9,10},{10,... | collective-permute-start | bytes 245768 | tf_op jit(solution)/shard_map/ppermute | solution.py:48
  37.0 1.0 %beyond.1 = (bf16[288,512]{1,0:T(8,128)(2,1)S(1)}, bf16[288,512]{1,0:T(8,128)(2,1)S(1)}) custom-call(bf16[8,128,256]{2,1,0:T(8,128)(2,1)S(1)} %copy-done.3, bf16[272,256]{1,0:T(8,128)(2,1)S(1)} %collective-permute-done.1.even_ref, bf16[256,256]{1,0:T(8,128)(2,1)S(1)} %collective-permute-done.2.odd_ref, ...), custom_call_target="tpu_custom_call" | custom-call | flops 8000000000 | bytes 100000 | tf_op jit(solution)/shard_map/beyond/pallas_call | solution.py:665
  38.1 0.5 %collective-permute-done.15.other_ref = bf16[16,16,512]{2,1,0:T(8,128)(2,1)S(1)} collective-permute-done((bf16[16,16,512]{2,1,0:T(8,128)(2,1)S(1)}, bf16[16,16,512]{2,1,0:T(8,128)(2,1)S(1)}, u32[]{:S(2)}, u32[]{:S(2)}) %collective-permute-start.15) | collective-permute-done | bytes 262176 | tf_op jit(solution)/shard_map/ppermute | solution.py:48
  38.6 1.0 %collective-permute-done.14 = bf16[320,128]{1,0:T(8,128)(2,1)S(1)} collective-permute-done((bf16[320,128]{1,0:T(8,128)(2,1)S(1)}, bf16[320,128]{1,0:T(8,128)(2,1)S(1)}, u32[]{:S(2)}, u32[]{:S(2)}) %collective-permute-start.14) | collective-permute-done | bytes 81952 | tf_op jit(solution)/shard_map/ppermute | solution.py:48
  39.7 1.1 %collective-permute-start.16 = (bf16[640,128]{1,0:T(8,128)(2,1)S(1)}, bf16[640,128]{1,0:T(8,128)(2,1)S(1)}, u32[]{:S(2)}, u32[]{:S(2)}) collective-permute-start(bf16[640,128]{1,0:T(8,128)(2,1)S(1)} %bitcast.26), channel_id=1, source_target_pairs={{0,1},{1,0},{2,3},{3,2},{4,5},{5,4},{6,7},{7,6},{8,9},{9,8},{10,11... | collective-permute-start | bytes 491528 | tf_op jit(solution)/shard_map/ppermute | solution.py:48
  40.7 0.3 prepare.1.both_ref
  41.1 0.7 %collective-permute-done.16.other_ref = bf16[640,128]{1,0:T(8,128)(2,1)S(1)} collective-permute-done((bf16[640,128]{1,0:T(8,128)(2,1)S(1)}, bf16[640,128]{1,0:T(8,128)(2,1)S(1)}, u32[]{:S(2)}, u32[]{:S(2)}) %collective-permute-start.16) | collective-permute-done | bytes 163872 | tf_op jit(solution)/shard_map/ppermute | solution.py:48
  41.8 4.4 %grad_conv.1 = (f32[16,512]{1,0:T(8,128)}, bf16[1024,256]{1,0:T(8,128)(2,1)}) custom-call(bf16[640,128]{1,0:T(8,128)(2,1)S(1)} %bitcast.27, bf16[640,128]{1,0:T(8,128)(2,1)S(1)} %collective-permute-done.16.other_ref, f32[512,512]{1,0:T(8,128)S(1)} %prepare.1.both_ref, bf16[768,512]{1,0:T(8,128)(2,1)S(1)} %get-tuple-element.79.in_feat_ref, ...), custom_call_target="tpu_custom_call" | custom-call | tf_op jit(solution)/shard_map/grad_conv/pallas_call | solution.py:703
  (32 shorter events, 0.6 us)
Async XLA Ops:
  0.6 2.5 %copy-start.1 = (f32[16,512]{1,0:T(8,128)S(1)}, f32[16,512]{1,0:T(8,128)}, u32[]{:S(2)}) copy-start(f32[16,512]{1,0:T(8,128)} %target_ref.1) | copy-start | bytes 98308
  0.6 1.0 %copy-start.2 = (bf16[8,128,256]{2,1,0:T(8,128)(2,1)S(1)}, bf16[8,128,256]{2,1,0:T(8,128)(2,1)}, u32[]{:S(2)}) copy-start(bf16[8,128,256]{2,1,0:T(8,128)(2,1)} %own_ref.3) | copy-start | bytes 1572868
  1.7 6.2 %copy-start = (bf16[3,3,256,512]{3,2,1,0:T(8,128)(2,1)S(1)}, bf16[3,3,256,512]{3,2,1,0:T(8,128)(2,1)}, u32[]{:S(2)}) copy-start(bf16[3,3,256,512]{3,2,1,0:T(8,128)(2,1)} %param.5) | copy-start | bytes 7077892
  1.7 6.2 %copy-start.3 = (bf16[8,128,256]{2,1,0:T(8,128)(2,1)S(1)}, bf16[8,128,256]{2,1,0:T(8,128)(2,1)}, u32[]{:S(2)}) copy-start(bf16[8,128,256]{2,1,0:T(8,128)(2,1)} %own_ref.3) | copy-start | bytes 1572868
  1.7 6.2 %copy-start.4 = (bf16[512]{0:T(512)(128)(2,1)S(1)}, bf16[512]{0:T(512)(128)(2,1)}, u32[]{:S(2)}) copy-start(bf16[512]{0:T(512)(128)(2,1)} %bias_ref.1) | copy-start | bytes 3076
  1.7 1.3 %collective-permute-start = (bf16[2,8,256]{2,1,0:T(8,128)(2,1)S(1)}, bf16[2,8,256]{2,1,0:T(8,128)(2,1)S(1)}, u32[]{:S(2)}, u32[]{:S(2)}) collective-permute-start(bf16[2,8,256]{2,1,0:T(8,128)(2,1)S(1)} %get-tuple-element.45), channel_id=1, source_target_pairs={{0,1},{1,0},{2,3},{3,2},{4,5},{5,4},{6,7},{7,6},{8,9},{9,8},{10,11... | collective-permute-start | bytes 24584 | tf_op jit(solution)/shard_map/ppermute | solution.py:581
  2.3 9.7 %collective-permute-start.2 = (bf16[256,256]{1,0:T(8,128)(2,1)S(1)}, bf16[256,256]{1,0:T(8,128)(2,1)S(1)}, u32[]{:S(2)}, u32[]{:S(2)}) collective-permute-start(bf16[256,256]{1,0:T(8,128)(2,1)S(1)} %get-tuple-element.47), channel_id=1, source_target_pairs={{0,1},{1,0},{2,4},{3,5},{4,2},{5,3},{6,8},{7,9},{8,6},{9,7},{10,12... | collective-permute-start | bytes 393224 | tf_op jit(solution)/shard_map/ppermute | solution.py:31
  3.1 8.8 %collective-permute-start.3 = (bf16[16,256]{1,0:T(8,128)(2,1)S(1)}, bf16[16,256]{1,0:T(8,128)(2,1)S(1)}, u32[]{:S(2)}, u32[]{:S(2)}) collective-permute-start(bf16[16,256]{1,0:T(8,128)(2,1)S(1)} %get-tuple-element.48), channel_id=1, source_target_pairs={{0,1},{1,0},{2,4},{3,5},{4,2},{5,3},{6,8},{7,9},{8,6},{9,7},{10,12... | collective-permute-start | bytes 24584 | tf_op jit(solution)/shard_map/ppermute | solution.py:31
  3.5 9.8 %collective-permute-start.1 = (bf16[272,256]{1,0:T(8,128)(2,1)S(1)}, bf16[272,256]{1,0:T(8,128)(2,1)S(1)}, u32[]{:S(2)}, u32[]{:S(2)}) collective-permute-start(bf16[272,256]{1,0:T(8,128)(2,1)S(1)} %get-tuple-element.46), channel_id=1, source_target_pairs={{0,2},{1,3},{2,0},{3,1},{4,6},{5,7},{6,4},{7,5},{8,10},{9,11},{10,... | collective-permute-start | bytes 417800 | tf_op jit(solution)/shard_map/ppermute | solution.py:31
  14.2 1.5 %collective-permute-start.4 = (bf16[640,128]{1,0:T(8,128)(2,1)S(1)}, bf16[640,128]{1,0:T(8,128)(2,1)S(1)}, u32[]{:S(2)}, u32[]{:S(2)}) collective-permute-start(bf16[640,128]{1,0:T(8,128)(2,1)S(1)} %get-tuple-element.57), channel_id=1, source_target_pairs={{0,1},{1,0},{2,3},{3,2},{4,5},{5,4},{6,7},{7,6},{8,9},{9,8},{10,11... | collective-permute-start | bytes 491528 | tf_op jit(solution)/shard_map/ppermute | solution.py:48
  15.7 4.8 %collective-permute-start.5 = (bf16[320,128]{1,0:T(8,128)(2,1)S(1)}, bf16[320,128]{1,0:T(8,128)(2,1)S(1)}, u32[]{:S(2)}, u32[]{:S(2)}) collective-permute-start(bf16[320,128]{1,0:T(8,128)(2,1)S(1)} %get-tuple-element.59), channel_id=1, source_target_pairs={{0,3},{1,4},{2,7},{3,0},{4,1},{5,6},{6,5},{7,2},{8,13},{9,10},{10,... | collective-permute-start | bytes 245768 | tf_op jit(solution)/shard_map/ppermute | solution.py:48
  17.9 4.2 %collective-permute-start.10 = (bf16[1,16,512]{2,1,0:T(8,128)(2,1)S(1)}, bf16[1,16,512]{2,1,0:T(8,128)(2,1)S(1)}, u32[]{:S(2)}, u32[]{:S(2)}) collective-permute-start(bf16[1,16,512]{2,1,0:T(8,128)(2,1)S(1)} %get-tuple-element.63), channel_id=1, source_target_pairs={{0,17},{1,16},{2,19},{3,18},{4,21},{5,20},{6,23},{7,22},{8,25},{9,... | collective-permute-start | bytes 49160 | tf_op jit(solution)/shard_map/ppermute | solution.py:48
  20.5 3.5 %collective-permute-start.6 = (bf16[160,128]{1,0:T(8,128)(2,1)S(1)}, bf16[160,128]{1,0:T(8,128)(2,1)S(1)}, u32[]{:S(2)}, u32[]{:S(2)}) collective-permute-start(bf16[160,128]{1,0:T(8,128)(2,1)S(1)} %get-tuple-element.61), channel_id=1, source_target_pairs={{0,5},{1,2},{2,1},{3,6},{4,7},{5,0},{6,3},{7,4},{8,11},{9,12},{10,... | collective-permute-start | bytes 122888 | tf_op jit(solution)/shard_map/ppermute | solution.py:48
  22.1 3.4 %collective-permute-start.11 = (bf16[2,16,512]{2,1,0:T(8,128)(2,1)S(1)}, bf16[2,16,512]{2,1,0:T(8,128)(2,1)S(1)}, u32[]{:S(2)}, u32[]{:S(2)}) collective-permute-start(bf16[2,16,512]{2,1,0:T(8,128)(2,1)S(1)} %bitcast.41), channel_id=1, source_target_pairs={{0,9},{1,8},{2,11},{3,10},{4,13},{5,12},{6,15},{7,14},{8,1},{9,0},... | collective-permute-start | bytes 98312 | tf_op jit(solution)/shard_map/ppermute | solution.py:48
  24.0 3.6 %collective-permute-start.7 = (bf16[160,128]{1,0:T(8,128)(2,1)S(1)}, bf16[160,128]{1,0:T(8,128)(2,1)S(1)}, u32[]{:S(2)}, u32[]{:S(2)}) collective-permute-start(bf16[160,128]{1,0:T(8,128)(2,1)S(1)} %add.3.keep_ref), channel_id=1, source_target_pairs={{0,9},{1,8},{2,11},{3,10},{4,13},{5,12},{6,15},{7,14},{8,1},{9,0},... | collective-permute-start | bytes 122888 | tf_op jit(solution)/shard_map/ppermute | solution.py:48
  25.5 4.5 %collective-permute-start.12 = (bf16[4,16,512]{2,1,0:T(8,128)(2,1)S(1)}, bf16[4,16,512]{2,1,0:T(8,128)(2,1)S(1)}, u32[]{:S(2)}, u32[]{:S(2)}) collective-permute-start(bf16[4,16,512]{2,1,0:T(8,128)(2,1)S(1)} %bitcast.36), channel_id=1, source_target_pairs={{0,3},{1,4},{2,7},{3,0},{4,1},{5,6},{6,5},{7,2},{8,13},{9,10},{10,... | collective-permute-start | bytes 196616 | tf_op jit(solution)/shard_map/ppermute | solution.py:48
  27.6 4.5 %collective-permute-start.8 = (bf16[160,128]{1,0:T(8,128)(2,1)S(1)}, bf16[160,128]{1,0:T(8,128)(2,1)S(1)}, u32[]{:S(2)}, u32[]{:S(2)}) collective-permute-start(bf16[160,128]{1,0:T(8,128)(2,1)S(1)} %add.4.keep_ref), channel_id=1, source_target_pairs={{0,17},{1,16},{2,19},{3,18},{4,21},{5,20},{6,23},{7,22},{8,25},{9,... | collective-permute-start | bytes 122888 | tf_op jit(solution)/shard_map/ppermute | solution.py:48
  30.0 4.5 %collective-permute-start.13 = (bf16[8,16,512]{2,1,0:T(8,128)(2,1)S(1)}, bf16[8,16,512]{2,1,0:T(8,128)(2,1)S(1)}, u32[]{:S(2)}, u32[]{:S(2)}) collective-permute-start(bf16[8,16,512]{2,1,0:T(8,128)(2,1)S(1)} %bitcast.30), channel_id=1, source_target_pairs={{0,5},{1,2},{2,1},{3,6},{4,7},{5,0},{6,3},{7,4},{8,11},{9,12},{10,... | collective-permute-start | bytes 393224 | tf_op jit(solution)/shard_map/ppermute | solution.py:48
  32.2 3.5 %collective-permute-start.9 = (bf16[160,128]{1,0:T(8,128)(2,1)S(1)}, bf16[160,128]{1,0:T(8,128)(2,1)S(1)}, u32[]{:S(2)}, u32[]{:S(2)}) collective-permute-start(bf16[160,128]{1,0:T(8,128)(2,1)S(1)} %add.5), channel_id=1, source_target_pairs={{0,5},{1,2},{2,1},{3,6},{4,7},{5,0},{6,3},{7,4},{8,11},{9,12},{10,... | collective-permute-start | bytes 122888 | tf_op jit(solution)/shard_map/ppermute | solution.py:48
  35.7 3.9 %collective-permute-start.14 = (bf16[320,128]{1,0:T(8,128)(2,1)S(1)}, bf16[320,128]{1,0:T(8,128)(2,1)S(1)}, u32[]{:S(2)}, u32[]{:S(2)}) collective-permute-start(bf16[320,128]{1,0:T(8,128)(2,1)S(1)} %bitcast.33), channel_id=1, source_target_pairs={{0,3},{1,4},{2,7},{3,0},{4,1},{5,6},{6,5},{7,2},{8,13},{9,10},{10,... | collective-permute-start | bytes 245768 | tf_op jit(solution)/shard_map/ppermute | solution.py:48
  37.0 1.5 %collective-permute-start.15 = (bf16[16,16,512]{2,1,0:T(8,128)(2,1)S(1)}, bf16[16,16,512]{2,1,0:T(8,128)(2,1)S(1)}, u32[]{:S(2)}, u32[]{:S(2)}) collective-permute-start(bf16[16,16,512]{2,1,0:T(8,128)(2,1)S(1)} %bitcast.28), channel_id=1, source_target_pairs={{0,1},{1,0},{2,3},{3,2},{4,5},{5,4},{6,7},{7,6},{8,9},{9,8},{10,11... | collective-permute-start | bytes 786440 | tf_op jit(solution)/shard_map/ppermute | solution.py:48
  39.7 2.1 %collective-permute-start.16 = (bf16[640,128]{1,0:T(8,128)(2,1)S(1)}, bf16[640,128]{1,0:T(8,128)(2,1)S(1)}, u32[]{:S(2)}, u32[]{:S(2)}) collective-permute-start(bf16[640,128]{1,0:T(8,128)(2,1)S(1)} %bitcast.26), channel_id=1, source_target_pairs={{0,1},{1,0},{2,3},{3,2},{4,5},{5,4},{6,7},{7,6},{8,9},{9,8},{10,11... | collective-permute-start | bytes 491528 | tf_op jit(solution)/shard_map/ppermute | solution.py:48

commit v13 on v11

--- a/solution.py
+++ b/solution.py
@@ -226,31 +226,35 @@
 
 
 def payload_kernel(target_ref, rows_ref, *refs):
-    even_ref, payload_ref, left_ref, right_ref, half_ref = refs[-5:]
+    payload_ref, left_ref, right_ref, half_ref = refs[-4:]
     main = rows_ref.shape[0]
     payload_ref[0:main, :] = rows_ref[...]
     odd_ref = payload_ref.at[main:]
     half_ref[0] = target_ref[...].astype(bf16)
-    if len(refs) == 6:
+    if len(refs) == 5:
         here = lax.axis_index("cols")
         other = refs[0][...].astype(f32)
         left_ref[...] = jnp.where(here == 0, 0.0, other).astype(bf16)
         right_ref[...] = jnp.where(here == 0, other, 0.0).astype(bf16)
     else:
         left_ref[...], right_ref[...] = refs[0][...], refs[1][...]
+    odd_ref[...] = row_rim(left_ref, right_ref, 1)
+
+
+def row_rim(left_ref, right_ref, last):
     beyond = [ref[c].astype(f32) for ref in (left_ref, right_ref) for c in range(2)]
     rows, width = beyond[0].shape
 
     def rim(r):
         parts = [part[r + k : r + k + 1] for k in range(2) for part in beyond]
-        return jnp.concatenate([*parts, jnp.zeros((8, width), f32)], axis=0).astype(bf16)
-
-    odd = lax.rem(lax.axis_index("rows"), 2)
-    for case, low_ref, high_ref in ((0, odd_ref, even_ref), (1, even_ref, odd_ref)):
-
-        @pl.when(odd == case)
-        def _():
-            low_ref[...], high_ref[...] = rim(0), rim(rows - 2)
+        return jnp.concatenate([*parts, jnp.zeros((8, width), f32)], axis=0)
+
+    parity = lax.rem(lax.axis_index("rows"), 2)
+    return jnp.where(parity == last, rim(rows - 2), rim(0)).astype(bf16)
+
+
+def even_rim_kernel(left_ref, right_ref, _, even_ref):
+    even_ref[...] = row_rim(left_ref, right_ref, 0)
 
 
 def moved_rows(row, before, after):
@@ -586,15 +590,25 @@
     payload_shape = jax.ShapeDtypeStruct((2 * tile_cols + edge, in_width), bf16)
     end_shape = jax.ShapeDtypeStruct((edge, in_width), bf16)
     half_shape = jax.ShapeDtypeStruct((1, *target_gram.shape), bf16)
-    even_rim, odd, left, right, rows = local(
+    odd, left, right, rows = local(
         payload_kernel,
-        (end_shape, payload_shape, rim_shape, rim_shape, half_shape),
+        (payload_shape, rim_shape, rim_shape, half_shape),
         "row_rims",
         target_gram,
         odd,
         *beyond,
     )
-    halo = [even, swap_rows(odds, odd), swap_rows(evens, even_rim)]
+    odd = swap_rows(odds, odd)
+    weights, _ = lax.optimization_barrier((kernel, left))
+    turned = local(
+        turn_kernel,
+        jax.ShapeDtypeStruct((9 * out_width, in_width), bf16),
+        "turn",
+        weights,
+        cost_estimate=chained,
+    )
+    even_rim = local(even_rim_kernel, end_shape, "even_rim", left, right, turned)
+    halo = [even, odd, swap_rows(evens, even_rim)]
     bits = (lax.axis_size("rows") * lax.axis_size("cols")).bit_length() - 1
     gather = Gather(rows)
     far = list(reversed(range(3, bits)))
@@ -619,15 +633,6 @@
         ),
     )(canvas, left, right, kernel, conv_bias)
 
-    weights, in_gram = lax.optimization_barrier((kernel, in_gram))
-    turned = local(
-        turn_kernel,
-        jax.ShapeDtypeStruct((9 * out_width, in_width), bf16),
-        "turn",
-        weights,
-        cost_estimate=waiting,
-    )
-    in_gram, turned = lax.optimization_barrier((in_gram, turned))
     half_gram = (packed_shape.shape[0] // 2, tile)
     halo_scratch = [pltpu.VMEM(payload_shape.shape, bf16), pltpu.VMEM(payload_shape.shape, bf16)]
     out_feat, out_slope, send, keep = pl.pallas_call(

time: 44.8 us -> 45.5 us (1.016)
  waiting for transfers between devices: 9.15 us -> 10.1 us
  starting transfers between devices: 22.6 us -> 22.1 us
    ppermute x13, starting transfers between devices: 18.3 us -> 15.9 us  [swap(): lax.ppermute(value, ('rows', 'cols'), [(i, i ^ flip(i)) for i in range(to...]
    ppermute x3, starting transfers between devices: 3.73 us -> 5.68 us  [swap_rows(): return lax.ppermute(value, ('rows', 'cols'), perm)]
    ppermute x13, waiting for transfers between devices: 9.14 us -> 10.1 us  [swap(): lax.ppermute(value, ('rows', 'cols'), [(i, i ^ flip(i)) for i in range(to...]
    pallas_call x16 -> x17, Pallas kernels: 1.34 us -> 1.35 us  [local(): pl.pallas_call(body, out_shape=out_shape, in_specs=[pl.BlockSpec(memory_s...]
  transfers between devices with their start and end apart: 17 -> 17, of which waited for: 10 -> 10; matrix products, arithmetic and copies ran while one was open for 0% -> 0% of each run, Pallas kernels for 13% -> 12%
where the time goes in v13:
time: 45.5 us; the launch traced here: 45.4 us
  starting transfers between devices  22.1 us (49%)
  Pallas kernels  11.1 us (24%)
  waiting for transfers between devices  10.1 us (22%)
  local copies, waits for them, and re-layouts  1.21 us (3%)
  between operations  0.81 us (2%)
    ppermute x13, starting transfers between devices, swap(): lax.ppermute(value, ('rows', 'cols'), [(i, i ^ flip(i)) for i in range(to...  15.9 us
    ppermute x13, waiting for transfers between devices, swap(): lax.ppermute(value, ('rows', 'cols'), [(i, i ^ flip(i)) for i in range(to...  10.1 us
    ppermute x3, starting transfers between devices, swap_rows(): return lax.ppermute(value, ('rows', 'cols'), perm)  5.68 us
    pallas_call x1, Pallas kernels, on_device(): pl.pallas_call(functools.partial(backward_kernel, shape, pixel_total), ou...  4.44 us
    pallas_call x1, Pallas kernels, on_device(): pl.pallas_call(functools.partial(inner_kernel, shape), out_shape=(jax.Sha...  3.36 us
    pallas_call x17, Pallas kernels, local(): pl.pallas_call(body, out_shape=out_shape, in_specs=[pl.BlockSpec(memory_s...  1.35 us
    unnamed x10, local copies, waits for them, and re-layouts  1.21 us
    pallas_call x1, Pallas kernels, beside(): pl.pallas_call(functools.partial(beyond_kernel, shape), out_shape=(jax.Sh...  1.04 us
  transfers between devices with their start and end apart: 17, of which 10 were waited for; matrix products, arithmetic and copies ran while one was open for 0% of the time, Pallas kernels for 12%

profile of v13, /device:TPU:0, one launch (start us, length us, event | category | flops | bytes accessed | tf_op | source)
XLA Modules:
  0.0 45.4 jit_solution(6298475866631574046)
XLA Ops:
  0.7 1.2 %copy-done.2 = bf16[8,128,256]{2,1,0:T(8,128)(2,1)S(1)} copy-done((bf16[8,128,256]{2,1,0:T(8,128)(2,1)S(1)}, bf16[8,128,256]{2,1,0:T(8,128)(2,1)}, u32[]{:S(2)}) %copy-start.2) | copy-done | bytes 524312
  1.9 0.5 %collective-permute-start.1 = (bf16[2,8,256]{2,1,0:T(8,128)(2,1)S(1)}, bf16[2,8,256]{2,1,0:T(8,128)(2,1)S(1)}, u32[]{:S(2)}, u32[]{:S(2)}) collective-permute-start(bf16[2,8,256]{2,1,0:T(8,128)(2,1)S(1)} %get-tuple-element.42), channel_id=1, source_target_pairs={{0,1},{1,0},{2,3},{3,2},{4,5},{5,4},{6,7},{7,6},{8,9},{9,8},{10,11... | collective-permute-start | bytes 24584 | tf_op jit(solution)/shard_map/ppermute | solution.py:585
  2.4 2.6 %collective-permute-start = (bf16[256,256]{1,0:T(8,128)(2,1)S(1)}, bf16[256,256]{1,0:T(8,128)(2,1)S(1)}, u32[]{:S(2)}, u32[]{:S(2)}) collective-permute-start(bf16[256,256]{1,0:T(8,128)(2,1)S(1)} %get-tuple-element.40), channel_id=1, source_target_pairs={{0,2},{1,3},{2,0},{3,1},{4,6},{5,7},{6,4},{7,5},{8,10},{9,11},{10,... | collective-permute-start | bytes 393224 | tf_op jit(solution)/shard_map/ppermute | solution.py:31
  5.0 0.2 collective-permute-start.2
  5.2 0.7 %turn.1._.turned_ref = bf16[4608,256]{1,0:T(8,128)(2,1)S(1)} custom-call(bf16[2304,512]{1,0:T(8,128)(2,1)S(1)} %bitcast.22), custom_call_target="tpu_custom_call" | custom-call | flops 8000000000 | bytes 100000 | tf_op jit(solution)/shard_map/turn/pallas_call | solution.py:52
  6.0 2.9 %collective-permute-start.3 = (bf16[16,256]{1,0:T(8,128)(2,1)S(1)}, bf16[16,256]{1,0:T(8,128)(2,1)S(1)}, u32[]{:S(2)}, u32[]{:S(2)}) collective-permute-start(bf16[16,256]{1,0:T(8,128)(2,1)S(1)} %even_rim.1), channel_id=1, source_target_pairs={{0,2},{1,3},{2,0},{3,1},{4,6},{5,7},{6,4},{7,5},{8,10},{9,11},{10,... | collective-permute-start | bytes 24584 | tf_op jit(solution)/shard_map/ppermute | solution.py:31
  8.8 3.4 %inner_rows.1 = (bf16[768,512]{1,0:T(8,128)(2,1)S(1)}, bf16[768,512]{1,0:T(8,128)(2,1)S(1)}, f32[1280,128]{1,0:T(8,128)S(1)}, f32[1,512]{1,0:T(1,128)S(1)}, f32[512,512]{1,0:T(8,128)S(1)}) custom-call(bf16[8,128,256]{2,1,0:T(8,128)(2,1)S(1)} %copy-done.3, bf16[2,8,256]{2,1,0:T(8,128)(2,1)S(1)} %get-tuple-element.44.left_ref, ...), custom_call_target="tpu_custom_call" | custom-call | flops 2214592512 | bytes 6000000 | tf_op jit(solution)/shard_map/inner_rows/pallas_call | solution.py:616
  12.2 0.9 %outer_rows.1 = (bf16[256,512]{1,0:T(8,128)(2,1)S(1)}, bf16[256,512]{1,0:T(8,128)(2,1)S(1)}, bf16[640,128]{1,0:T(8,128)(2,1)S(1)}, f32[640,128]{1,0:T(8,128)S(1)}) custom-call(bf16[256,256]{1,0:T(8,128)(2,1)S(1)} %collective-permute-done.even_ref, bf16[272,256]{1,0:T(8,128)(2,1)S(1)} %collective-permute-done.2.odd_ref, ...), custom_call_target="tpu_custom_call" | custom-call | tf_op jit(solution)/shard_map/outer_rows/pallas_call | solution.py:638
  13.2 1.4 %collective-permute-done.4.got_ref = bf16[640,128]{1,0:T(8,128)(2,1)S(1)} collective-permute-done((bf16[640,128]{1,0:T(8,128)(2,1)S(1)}, bf16[640,128]{1,0:T(8,128)(2,1)S(1)}, u32[]{:S(2)}, u32[]{:S(2)}) %collective-permute-start.4) | collective-permute-done | bytes 163872 | tf_op jit(solution)/shard_map/ppermute | solution.py:48
  14.6 2.4 %collective-permute-start.5 = (bf16[320,128]{1,0:T(8,128)(2,1)S(1)}, bf16[320,128]{1,0:T(8,128)(2,1)S(1)}, u32[]{:S(2)}, u32[]{:S(2)}) collective-permute-start(bf16[320,128]{1,0:T(8,128)(2,1)S(1)} %get-tuple-element.52), channel_id=1, source_target_pairs={{0,3},{1,4},{2,7},{3,0},{4,1},{5,6},{6,5},{7,2},{8,13},{9,10},{10,... | collective-permute-start | bytes 245768 | tf_op jit(solution)/shard_map/ppermute | solution.py:48
  17.0 2.6 %collective-permute-start.10 = (bf16[1,16,512]{2,1,0:T(8,128)(2,1)S(1)}, bf16[1,16,512]{2,1,0:T(8,128)(2,1)S(1)}, u32[]{:S(2)}, u32[]{:S(2)}) collective-permute-start(bf16[1,16,512]{2,1,0:T(8,128)(2,1)S(1)} %get-tuple-element.56), channel_id=1, source_target_pairs={{0,17},{1,16},{2,19},{3,18},{4,21},{5,20},{6,23},{7,22},{8,25},{9,... | collective-permute-start | bytes 49160 | tf_op jit(solution)/shard_map/ppermute | solution.py:48
  19.6 0.5 %collective-permute-start.6 = (bf16[160,128]{1,0:T(8,128)(2,1)S(1)}, bf16[160,128]{1,0:T(8,128)(2,1)S(1)}, u32[]{:S(2)}, u32[]{:S(2)}) collective-permute-start(bf16[160,128]{1,0:T(8,128)(2,1)S(1)} %get-tuple-element.54), channel_id=1, source_target_pairs={{0,5},{1,2},{2,1},{3,6},{4,7},{5,0},{6,3},{7,4},{8,11},{9,12},{10,... | collective-permute-start | bytes 122888 | tf_op jit(solution)/shard_map/ppermute | solution.py:48
  20.1 1.0 %collective-permute-done.10 = bf16[1,16,512]{2,1,0:T(8,128)(2,1)S(1)} collective-permute-done((bf16[1,16,512]{2,1,0:T(8,128)(2,1)S(1)}, bf16[1,16,512]{2,1,0:T(8,128)(2,1)S(1)}, u32[]{:S(2)}, u32[]{:S(2)}) %collective-permute-start.10) | collective-permute-done | bytes 16416 | tf_op jit(solution)/shard_map/ppermute | solution.py:48
  21.1 1.6 %collective-permute-start.11 = (bf16[2,16,512]{2,1,0:T(8,128)(2,1)S(1)}, bf16[2,16,512]{2,1,0:T(8,128)(2,1)S(1)}, u32[]{:S(2)}, u32[]{:S(2)}) collective-permute-start(bf16[2,16,512]{2,1,0:T(8,128)(2,1)S(1)} %bitcast.41), channel_id=1, source_target_pairs={{0,9},{1,8},{2,11},{3,10},{4,13},{5,12},{6,15},{7,14},{8,1},{9,0},... | collective-permute-start | bytes 98312 | tf_op jit(solution)/shard_map/ppermute | solution.py:48
  22.7 0.5 %collective-permute-done.6.got_ref = bf16[160,128]{1,0:T(8,128)(2,1)S(1)} collective-permute-done((bf16[160,128]{1,0:T(8,128)(2,1)S(1)}, bf16[160,128]{1,0:T(8,128)(2,1)S(1)}, u32[]{:S(2)}, u32[]{:S(2)}) %collective-permute-start.6) | collective-permute-done | bytes 40992 | tf_op jit(solution)/shard_map/ppermute | solution.py:48
  23.1 1.4 %collective-permute-start.7 = (bf16[160,128]{1,0:T(8,128)(2,1)S(1)}, bf16[160,128]{1,0:T(8,128)(2,1)S(1)}, u32[]{:S(2)}, u32[]{:S(2)}) collective-permute-start(bf16[160,128]{1,0:T(8,128)(2,1)S(1)} %add.3.keep_ref), channel_id=1, source_target_pairs={{0,9},{1,8},{2,11},{3,10},{4,13},{5,12},{6,15},{7,14},{8,1},{9,0},... | collective-permute-start | bytes 122888 | tf_op jit(solution)/shard_map/ppermute | solution.py:48
  24.5 1.6 %collective-permute-start.12 = (bf16[4,16,512]{2,1,0:T(8,128)(2,1)S(1)}, bf16[4,16,512]{2,1,0:T(8,128)(2,1)S(1)}, u32[]{:S(2)}, u32[]{:S(2)}) collective-permute-start(bf16[4,16,512]{2,1,0:T(8,128)(2,1)S(1)} %bitcast.36), channel_id=1, source_target_pairs={{0,3},{1,4},{2,7},{3,0},{4,1},{5,6},{6,5},{7,2},{8,13},{9,10},{10,... | collective-permute-start | bytes 196616 | tf_op jit(solution)/shard_map/ppermute | solution.py:48
  26.1 0.6 %collective-permute-done.7.got_ref = bf16[160,128]{1,0:T(8,128)(2,1)S(1)} collective-permute-done((bf16[160,128]{1,0:T(8,128)(2,1)S(1)}, bf16[160,128]{1,0:T(8,128)(2,1)S(1)}, u32[]{:S(2)}, u32[]{:S(2)}) %collective-permute-start.7) | collective-permute-done | bytes 40992 | tf_op jit(solution)/shard_map/ppermute | solution.py:48
  26.8 2.2 %collective-permute-start.8 = (bf16[160,128]{1,0:T(8,128)(2,1)S(1)}, bf16[160,128]{1,0:T(8,128)(2,1)S(1)}, u32[]{:S(2)}, u32[]{:S(2)}) collective-permute-start(bf16[160,128]{1,0:T(8,128)(2,1)S(1)} %add.4.keep_ref), channel_id=1, source_target_pairs={{0,17},{1,16},{2,19},{3,18},{4,21},{5,20},{6,23},{7,22},{8,25},{9,... | collective-permute-start | bytes 122888 | tf_op jit(solution)/shard_map/ppermute | solution.py:48
  29.0 0.9 %collective-permute-start.13 = (bf16[8,16,512]{2,1,0:T(8,128)(2,1)S(1)}, bf16[8,16,512]{2,1,0:T(8,128)(2,1)S(1)}, u32[]{:S(2)}, u32[]{:S(2)}) collective-permute-start(bf16[8,16,512]{2,1,0:T(8,128)(2,1)S(1)} %bitcast.30), channel_id=1, source_target_pairs={{0,5},{1,2},{2,1},{3,6},{4,7},{5,0},{6,3},{7,4},{8,11},{9,12},{10,... | collective-permute-start | bytes 393224 | tf_op jit(solution)/shard_map/ppermute | solution.py:48
  30.0 1.3 %collective-permute-done.8.got_ref = bf16[160,128]{1,0:T(8,128)(2,1)S(1)} collective-permute-done((bf16[160,128]{1,0:T(8,128)(2,1)S(1)}, bf16[160,128]{1,0:T(8,128)(2,1)S(1)}, u32[]{:S(2)}, u32[]{:S(2)}) %collective-permute-start.8) | collective-permute-done | bytes 40992 | tf_op jit(solution)/shard_map/ppermute | solution.py:48
  31.3 0.3 collective-permute-start.9
  31.6 1.9 %collective-permute-done.13 = bf16[8,16,512]{2,1,0:T(8,128)(2,1)S(1)} collective-permute-done((bf16[8,16,512]{2,1,0:T(8,128)(2,1)S(1)}, bf16[8,16,512]{2,1,0:T(8,128)(2,1)S(1)}, u32[]{:S(2)}, u32[]{:S(2)}) %collective-permute-start.13) | collective-permute-done | bytes 131104 | tf_op jit(solution)/shard_map/ppermute | solution.py:48
  33.5 1.3 %collective-permute-done.9 = bf16[160,128]{1,0:T(8,128)(2,1)S(1)} collective-permute-done((bf16[160,128]{1,0:T(8,128)(2,1)S(1)}, bf16[160,128]{1,0:T(8,128)(2,1)S(1)}, u32[]{:S(2)}, u32[]{:S(2)}) %collective-permute-start.9) | collective-permute-done | bytes 40992 | tf_op jit(solution)/shard_map/ppermute | solution.py:48
  34.8 1.4 %collective-permute-start.14 = (bf16[320,128]{1,0:T(8,128)(2,1)S(1)}, bf16[320,128]{1,0:T(8,128)(2,1)S(1)}, u32[]{:S(2)}, u32[]{:S(2)}) collective-permute-start(bf16[320,128]{1,0:T(8,128)(2,1)S(1)} %bitcast.33), channel_id=1, source_target_pairs={{0,3},{1,4},{2,7},{3,0},{4,1},{5,6},{6,5},{7,2},{8,13},{9,10},{10,... | collective-permute-start | bytes 245768 | tf_op jit(solution)/shard_map/ppermute | solution.py:48
  36.2 1.0 %beyond.1 = (bf16[288,512]{1,0:T(8,128)(2,1)S(1)}, bf16[288,512]{1,0:T(8,128)(2,1)S(1)}) custom-call(bf16[8,128,256]{2,1,0:T(8,128)(2,1)S(1)} %copy-done.3, bf16[256,256]{1,0:T(8,128)(2,1)S(1)} %collective-permute-done.even_ref, bf16[272,256]{1,0:T(8,128)(2,1)S(1)} %collective-permute-done.2.odd_ref, ...), custom_call_target="tpu_custom_call" | custom-call | flops 8000000000 | bytes 100000 | tf_op jit(solution)/shard_map/beyond/pallas_call | solution.py:670
  37.3 0.5 %collective-permute-done.15.other_ref = bf16[16,16,512]{2,1,0:T(8,128)(2,1)S(1)} collective-permute-done((bf16[16,16,512]{2,1,0:T(8,128)(2,1)S(1)}, bf16[16,16,512]{2,1,0:T(8,128)(2,1)S(1)}, u32[]{:S(2)}, u32[]{:S(2)}) %collective-permute-start.15) | collective-permute-done | bytes 262176 | tf_op jit(solution)/shard_map/ppermute | solution.py:48
  37.8 0.9 %collective-permute-done.14 = bf16[320,128]{1,0:T(8,128)(2,1)S(1)} collective-permute-done((bf16[320,128]{1,0:T(8,128)(2,1)S(1)}, bf16[320,128]{1,0:T(8,128)(2,1)S(1)}, u32[]{:S(2)}, u32[]{:S(2)}) %collective-permute-start.14) | collective-permute-done | bytes 81952 | tf_op jit(solution)/shard_map/ppermute | solution.py:48
  38.8 1.1 %collective-permute-start.16 = (bf16[640,128]{1,0:T(8,128)(2,1)S(1)}, bf16[640,128]{1,0:T(8,128)(2,1)S(1)}, u32[]{:S(2)}, u32[]{:S(2)}) collective-permute-start(bf16[640,128]{1,0:T(8,128)(2,1)S(1)} %bitcast.26), channel_id=1, source_target_pairs={{0,1},{1,0},{2,3},{3,2},{4,5},{5,4},{6,7},{7,6},{8,9},{9,8},{10,11... | collective-permute-start | bytes 491528 | tf_op jit(solution)/shard_map/ppermute | solution.py:48
  39.9 0.3 prepare.1.both_ref
  40.2 0.7 %collective-permute-done.16.other_ref = bf16[640,128]{1,0:T(8,128)(2,1)S(1)} collective-permute-done((bf16[640,128]{1,0:T(8,128)(2,1)S(1)}, bf16[640,128]{1,0:T(8,128)(2,1)S(1)}, u32[]{:S(2)}, u32[]{:S(2)}) %collective-permute-start.16) | collective-permute-done | bytes 163872 | tf_op jit(solution)/shard_map/ppermute | solution.py:48
  40.9 4.4 %grad_conv.1 = (f32[16,512]{1,0:T(8,128)}, bf16[1024,256]{1,0:T(8,128)(2,1)}) custom-call(bf16[640,128]{1,0:T(8,128)(2,1)S(1)} %bitcast.27, bf16[640,128]{1,0:T(8,128)(2,1)S(1)} %collective-permute-done.16.other_ref, f32[512,512]{1,0:T(8,128)S(1)} %prepare.1.both_ref, bf16[768,512]{1,0:T(8,128)(2,1)S(1)} %get-tuple-element.72.in_feat_ref, ...), custom_call_target="tpu_custom_call" | custom-call | tf_op jit(solution)/shard_map/grad_conv/pallas_call | solution.py:708
  (33 shorter events, 0.5 us)
Async XLA Ops:
  0.6 4.4 %copy-start.1 = (f32[16,512]{1,0:T(8,128)S(1)}, f32[16,512]{1,0:T(8,128)}, u32[]{:S(2)}) copy-start(f32[16,512]{1,0:T(8,128)} %target_ref.1) | copy-start | bytes 98308
  0.6 4.6 %copy-start = (bf16[3,3,256,512]{3,2,1,0:T(8,128)(2,1)S(1)}, bf16[3,3,256,512]{3,2,1,0:T(8,128)(2,1)}, u32[]{:S(2)}) copy-start(bf16[3,3,256,512]{3,2,1,0:T(8,128)(2,1)} %param.5) | copy-start | bytes 7077892
  0.6 1.2 %copy-start.2 = (bf16[8,128,256]{2,1,0:T(8,128)(2,1)S(1)}, bf16[8,128,256]{2,1,0:T(8,128)(2,1)}, u32[]{:S(2)}) copy-start(bf16[8,128,256]{2,1,0:T(8,128)(2,1)} %own_ref.3) | copy-start | bytes 1572868
  1.9 3.1 %collective-permute-start.1 = (bf16[2,8,256]{2,1,0:T(8,128)(2,1)S(1)}, bf16[2,8,256]{2,1,0:T(8,128)(2,1)S(1)}, u32[]{:S(2)}, u32[]{:S(2)}) collective-permute-start(bf16[2,8,256]{2,1,0:T(8,128)(2,1)S(1)} %get-tuple-element.42), channel_id=1, source_target_pairs={{0,1},{1,0},{2,3},{3,2},{4,5},{5,4},{6,7},{7,6},{8,9},{9,8},{10,11... | collective-permute-start | bytes 24584 | tf_op jit(solution)/shard_map/ppermute | solution.py:585
  2.4 9.8 %collective-permute-start = (bf16[256,256]{1,0:T(8,128)(2,1)S(1)}, bf16[256,256]{1,0:T(8,128)(2,1)S(1)}, u32[]{:S(2)}, u32[]{:S(2)}) collective-permute-start(bf16[256,256]{1,0:T(8,128)(2,1)S(1)} %get-tuple-element.40), channel_id=1, source_target_pairs={{0,2},{1,3},{2,0},{3,1},{4,6},{5,7},{6,4},{7,5},{8,10},{9,11},{10,... | collective-permute-start | bytes 393224 | tf_op jit(solution)/shard_map/ppermute | solution.py:31
  5.0 7.2 %collective-permute-start.2 = (bf16[272,256]{1,0:T(8,128)(2,1)S(1)}, bf16[272,256]{1,0:T(8,128)(2,1)S(1)}, u32[]{:S(2)}, u32[]{:S(2)}) collective-permute-start(bf16[272,256]{1,0:T(8,128)(2,1)S(1)} %get-tuple-element.43), channel_id=1, source_target_pairs={{0,1},{1,0},{2,4},{3,5},{4,2},{5,3},{6,8},{7,9},{8,6},{9,7},{10,12... | collective-permute-start | bytes 417800 | tf_op jit(solution)/shard_map/ppermute | solution.py:31
  5.9 2.9 %copy-start.3 = (bf16[8,128,256]{2,1,0:T(8,128)(2,1)S(1)}, bf16[8,128,256]{2,1,0:T(8,128)(2,1)}, u32[]{:S(2)}) copy-start(bf16[8,128,256]{2,1,0:T(8,128)(2,1)} %own_ref.3) | copy-start | bytes 1572868
  5.9 2.9 %copy-start.4 = (bf16[512]{0:T(512)(128)(2,1)S(1)}, bf16[512]{0:T(512)(128)(2,1)}, u32[]{:S(2)}) copy-start(bf16[512]{0:T(512)(128)(2,1)} %bias_ref.1) | copy-start | bytes 3076
  6.0 6.3 %collective-permute-start.3 = (bf16[16,256]{1,0:T(8,128)(2,1)S(1)}, bf16[16,256]{1,0:T(8,128)(2,1)S(1)}, u32[]{:S(2)}, u32[]{:S(2)}) collective-permute-start(bf16[16,256]{1,0:T(8,128)(2,1)S(1)} %even_rim.1), channel_id=1, source_target_pairs={{0,2},{1,3},{2,0},{3,1},{4,6},{5,7},{6,4},{7,5},{8,10},{9,11},{10,... | collective-permute-start | bytes 24584 | tf_op jit(solution)/shard_map/ppermute | solution.py:31
  13.1 1.5 %collective-permute-start.4 = (bf16[640,128]{1,0:T(8,128)(2,1)S(1)}, bf16[640,128]{1,0:T(8,128)(2,1)S(1)}, u32[]{:S(2)}, u32[]{:S(2)}) collective-permute-start(bf16[640,128]{1,0:T(8,128)(2,1)S(1)} %get-tuple-element.50), channel_id=1, source_target_pairs={{0,1},{1,0},{2,3},{3,2},{4,5},{5,4},{6,7},{7,6},{8,9},{9,8},{10,11... | collective-permute-start | bytes 491528 | tf_op jit(solution)/shard_map/ppermute | solution.py:48
  14.6 5.0 %collective-permute-start.5 = (bf16[320,128]{1,0:T(8,128)(2,1)S(1)}, bf16[320,128]{1,0:T(8,128)(2,1)S(1)}, u32[]{:S(2)}, u32[]{:S(2)}) collective-permute-start(bf16[320,128]{1,0:T(8,128)(2,1)S(1)} %get-tuple-element.52), channel_id=1, source_target_pairs={{0,3},{1,4},{2,7},{3,0},{4,1},{5,6},{6,5},{7,2},{8,13},{9,10},{10,... | collective-permute-start | bytes 245768 | tf_op jit(solution)/shard_map/ppermute | solution.py:48
  17.0 4.1 %collective-permute-start.10 = (bf16[1,16,512]{2,1,0:T(8,128)(2,1)S(1)}, bf16[1,16,512]{2,1,0:T(8,128)(2,1)S(1)}, u32[]{:S(2)}, u32[]{:S(2)}) collective-permute-start(bf16[1,16,512]{2,1,0:T(8,128)(2,1)S(1)} %get-tuple-element.56), channel_id=1, source_target_pairs={{0,17},{1,16},{2,19},{3,18},{4,21},{5,20},{6,23},{7,22},{8,25},{9,... | collective-permute-start | bytes 49160 | tf_op jit(solution)/shard_map/ppermute | solution.py:48
  19.6 3.5 %collective-permute-start.6 = (bf16[160,128]{1,0:T(8,128)(2,1)S(1)}, bf16[160,128]{1,0:T(8,128)(2,1)S(1)}, u32[]{:S(2)}, u32[]{:S(2)}) collective-permute-start(bf16[160,128]{1,0:T(8,128)(2,1)S(1)} %get-tuple-element.54), channel_id=1, source_target_pairs={{0,5},{1,2},{2,1},{3,6},{4,7},{5,0},{6,3},{7,4},{8,11},{9,12},{10,... | collective-permute-start | bytes 122888 | tf_op jit(solution)/shard_map/ppermute | solution.py:48
  21.1 3.4 %collective-permute-start.11 = (bf16[2,16,512]{2,1,0:T(8,128)(2,1)S(1)}, bf16[2,16,512]{2,1,0:T(8,128)(2,1)S(1)}, u32[]{:S(2)}, u32[]{:S(2)}) collective-permute-start(bf16[2,16,512]{2,1,0:T(8,128)(2,1)S(1)} %bitcast.41), channel_id=1, source_target_pairs={{0,9},{1,8},{2,11},{3,10},{4,13},{5,12},{6,15},{7,14},{8,1},{9,0},... | collective-permute-start | bytes 98312 | tf_op jit(solution)/shard_map/ppermute | solution.py:48
  23.1 3.6 %collective-permute-start.7 = (bf16[160,128]{1,0:T(8,128)(2,1)S(1)}, bf16[160,128]{1,0:T(8,128)(2,1)S(1)}, u32[]{:S(2)}, u32[]{:S(2)}) collective-permute-start(bf16[160,128]{1,0:T(8,128)(2,1)S(1)} %add.3.keep_ref), channel_id=1, source_target_pairs={{0,9},{1,8},{2,11},{3,10},{4,13},{5,12},{6,15},{7,14},{8,1},{9,0},... | collective-permute-start | bytes 122888 | tf_op jit(solution)/shard_map/ppermute | solution.py:48
  24.5 4.4 %collective-permute-start.12 = (bf16[4,16,512]{2,1,0:T(8,128)(2,1)S(1)}, bf16[4,16,512]{2,1,0:T(8,128)(2,1)S(1)}, u32[]{:S(2)}, u32[]{:S(2)}) collective-permute-start(bf16[4,16,512]{2,1,0:T(8,128)(2,1)S(1)} %bitcast.36), channel_id=1, source_target_pairs={{0,3},{1,4},{2,7},{3,0},{4,1},{5,6},{6,5},{7,2},{8,13},{9,10},{10,... | collective-permute-start | bytes 196616 | tf_op jit(solution)/shard_map/ppermute | solution.py:48
  26.8 4.5 %collective-permute-start.8 = (bf16[160,128]{1,0:T(8,128)(2,1)S(1)}, bf16[160,128]{1,0:T(8,128)(2,1)S(1)}, u32[]{:S(2)}, u32[]{:S(2)}) collective-permute-start(bf16[160,128]{1,0:T(8,128)(2,1)S(1)} %add.4.keep_ref), channel_id=1, source_target_pairs={{0,17},{1,16},{2,19},{3,18},{4,21},{5,20},{6,23},{7,22},{8,25},{9,... | collective-permute-start | bytes 122888 | tf_op jit(solution)/shard_map/ppermute | solution.py:48
  29.0 4.5 %collective-permute-start.13 = (bf16[8,16,512]{2,1,0:T(8,128)(2,1)S(1)}, bf16[8,16,512]{2,1,0:T(8,128)(2,1)S(1)}, u32[]{:S(2)}, u32[]{:S(2)}) collective-permute-start(bf16[8,16,512]{2,1,0:T(8,128)(2,1)S(1)} %bitcast.30), channel_id=1, source_target_pairs={{0,5},{1,2},{2,1},{3,6},{4,7},{5,0},{6,3},{7,4},{8,11},{9,12},{10,... | collective-permute-start | bytes 393224 | tf_op jit(solution)/shard_map/ppermute | solution.py:48
  31.3 3.5 %collective-permute-start.9 = (bf16[160,128]{1,0:T(8,128)(2,1)S(1)}, bf16[160,128]{1,0:T(8,128)(2,1)S(1)}, u32[]{:S(2)}, u32[]{:S(2)}) collective-permute-start(bf16[160,128]{1,0:T(8,128)(2,1)S(1)} %add.5), channel_id=1, source_target_pairs={{0,5},{1,2},{2,1},{3,6},{4,7},{5,0},{6,3},{7,4},{8,11},{9,12},{10,... | collective-permute-start | bytes 122888 | tf_op jit(solution)/shard_map/ppermute | solution.py:48
  34.8 3.9 %collective-permute-start.14 = (bf16[320,128]{1,0:T(8,128)(2,1)S(1)}, bf16[320,128]{1,0:T(8,128)(2,1)S(1)}, u32[]{:S(2)}, u32[]{:S(2)}) collective-permute-start(bf16[320,128]{1,0:T(8,128)(2,1)S(1)} %bitcast.33), channel_id=1, source_target_pairs={{0,3},{1,4},{2,7},{3,0},{4,1},{5,6},{6,5},{7,2},{8,13},{9,10},{10,... | collective-permute-start | bytes 245768 | tf_op jit(solution)/shard_map/ppermute | solution.py:48
  36.2 1.5 %collective-permute-start.15 = (bf16[16,16,512]{2,1,0:T(8,128)(2,1)S(1)}, bf16[16,16,512]{2,1,0:T(8,128)(2,1)S(1)}, u32[]{:S(2)}, u32[]{:S(2)}) collective-permute-start(bf16[16,16,512]{2,1,0:T(8,128)(2,1)S(1)} %bitcast.28), channel_id=1, source_target_pairs={{0,1},{1,0},{2,3},{3,2},{4,5},{5,4},{6,7},{7,6},{8,9},{9,8},{10,11... | collective-permute-start | bytes 786440 | tf_op jit(solution)/shard_map/ppermute | solution.py:48
  38.8 2.1 %collective-permute-start.16 = (bf16[640,128]{1,0:T(8,128)(2,1)S(1)}, bf16[640,128]{1,0:T(8,128)(2,1)S(1)}, u32[]{:S(2)}, u32[]{:S(2)}) collective-permute-start(bf16[640,128]{1,0:T(8,128)(2,1)S(1)} %bitcast.26), channel_id=1, source_target_pairs={{0,1},{1,0},{2,3},{3,2},{4,5},{5,4},{6,7},{7,6},{8,9},{9,8},{10,11... | collective-permute-start | bytes 491528 | tf_op jit(solution)/shard_map/ppermute | solution.py:48

commit v14 on v11

--- a/solution.py
+++ b/solution.py
@@ -174,7 +174,7 @@
 def sum_all(send, keep, beside):
     bits = (lax.axis_size("rows") * lax.axis_size("cols")).bit_length() - 1
     halving = [(1, 2), (2, 1)]
-    adding = [(bit,) for bit in range(3, bits)]
+    adding = [(bit,) for bit in reversed(range(3, bits))]
 
     got = beside("cores", send, swap(send, 0))
     for n, pair in enumerate(halving):

time: 44.8 us -> 45.4 us (1.013)
  starting transfers between devices: 22.6 us -> 23.1 us
    ppermute x13, starting transfers between devices: 18.3 us -> 18.8 us  [swap(): lax.ppermute(value, ('rows', 'cols'), [(i, i ^ flip(i)) for i in range(to...]
  transfers between devices with their start and end apart: 17 -> 17, of which waited for: 10 -> 11; matrix products, arithmetic and copies ran while one was open for 0% -> 0% of each run, Pallas kernels for 13% -> 12%
where the time goes in v14:
time: 45.4 us; the launch traced here: 45.2 us
  starting transfers between devices  23.1 us (51%)
  Pallas kernels  11.1 us (24%)
  waiting for transfers between devices  9.24 us (20%)
  local copies, waits for them, and re-layouts  1.06 us (2%)
  between operations  0.79 us (2%)
    ppermute x13, starting transfers between devices, swap(): lax.ppermute(value, ('rows', 'cols'), [(i, i ^ flip(i)) for i in range(to...  18.8 us
    ppermute x13, waiting for transfers between devices, swap(): lax.ppermute(value, ('rows', 'cols'), [(i, i ^ flip(i)) for i in range(to...  9.23 us
    pallas_call x1, Pallas kernels, on_device(): pl.pallas_call(functools.partial(backward_kernel, shape, pixel_total), ou...  4.43 us
    ppermute x3, starting transfers between devices, swap_rows(): return lax.ppermute(value, ('rows', 'cols'), perm)  3.73 us
    pallas_call x1, Pallas kernels, on_device(): pl.pallas_call(functools.partial(inner_kernel, shape), out_shape=(jax.Sha...  3.36 us
    pallas_call x16, Pallas kernels, local(): pl.pallas_call(body, out_shape=out_shape, in_specs=[pl.BlockSpec(memory_s...  1.31 us
    unnamed x10, local copies, waits for them, and re-layouts  1.06 us
    pallas_call x1, Pallas kernels, beside(): pl.pallas_call(functools.partial(beyond_kernel, shape), out_shape=(jax.Sh...  1.04 us
  transfers between devices with their start and end apart: 17, of which 11 were waited for; matrix products, arithmetic and copies ran while one was open for 0% of the time, Pallas kernels for 12%

profile of v14, /device:TPU:0, one launch (start us, length us, event | category | flops | bytes accessed | tf_op | source)
XLA Modules:
  0.0 45.2 jit_solution(11732039997785935585)
XLA Ops:
  0.7 1.0 %copy-done.2 = bf16[8,128,256]{2,1,0:T(8,128)(2,1)S(1)} copy-done((bf16[8,128,256]{2,1,0:T(8,128)(2,1)S(1)}, bf16[8,128,256]{2,1,0:T(8,128)(2,1)}, u32[]{:S(2)}) %copy-start.2) | copy-done | bytes 524312
  1.7 0.5 %collective-permute-start.1 = (bf16[2,8,256]{2,1,0:T(8,128)(2,1)S(1)}, bf16[2,8,256]{2,1,0:T(8,128)(2,1)S(1)}, u32[]{:S(2)}, u32[]{:S(2)}) collective-permute-start(bf16[2,8,256]{2,1,0:T(8,128)(2,1)S(1)} %get-tuple-element.46), channel_id=1, source_target_pairs={{0,1},{1,0},{2,3},{3,2},{4,5},{5,4},{6,7},{7,6},{8,9},{9,8},{10,11... | collective-permute-start | bytes 24584 | tf_op jit(solution)/shard_map/ppermute | solution.py:581
  2.3 2.6 %collective-permute-start = (bf16[256,256]{1,0:T(8,128)(2,1)S(1)}, bf16[256,256]{1,0:T(8,128)(2,1)S(1)}, u32[]{:S(2)}, u32[]{:S(2)}) collective-permute-start(bf16[256,256]{1,0:T(8,128)(2,1)S(1)} %get-tuple-element.44), channel_id=1, source_target_pairs={{0,2},{1,3},{2,0},{3,1},{4,6},{5,7},{6,4},{7,5},{8,10},{9,11},{10,... | collective-permute-start | bytes 393224 | tf_op jit(solution)/shard_map/ppermute | solution.py:31
  4.9 1.2 %collective-permute-start.3 = (bf16[16,256]{1,0:T(8,128)(2,1)S(1)}, bf16[16,256]{1,0:T(8,128)(2,1)S(1)}, u32[]{:S(2)}, u32[]{:S(2)}) collective-permute-start(bf16[16,256]{1,0:T(8,128)(2,1)S(1)} %get-tuple-element.48), channel_id=1, source_target_pairs={{0,2},{1,3},{2,0},{3,1},{4,6},{5,7},{6,4},{7,5},{8,10},{9,11},{10,... | collective-permute-start | bytes 24584 | tf_op jit(solution)/shard_map/ppermute | solution.py:31
  6.0 3.4 %inner_rows.1 = (bf16[768,512]{1,0:T(8,128)(2,1)S(1)}, bf16[768,512]{1,0:T(8,128)(2,1)S(1)}, f32[1280,128]{1,0:T(8,128)S(1)}, f32[1,512]{1,0:T(1,128)S(1)}, f32[512,512]{1,0:T(8,128)S(1)}) custom-call(bf16[8,128,256]{2,1,0:T(8,128)(2,1)S(1)} %copy-done.3, bf16[2,8,256]{2,1,0:T(8,128)(2,1)S(1)} %get-tuple-element.49.left_ref, ...), custom_call_target="tpu_custom_call" | custom-call | flops 2214592512 | bytes 6000000 | tf_op jit(solution)/shard_map/inner_rows/pallas_call | solution.py:602
  9.4 0.7 %turn.1.turned_ref = bf16[4608,256]{1,0:T(8,128)(2,1)S(1)} custom-call(bf16[2304,512]{1,0:T(8,128)(2,1)S(1)} %bitcast.23), custom_call_target="tpu_custom_call" | custom-call | flops 1500000000 | bytes 100000 | tf_op jit(solution)/shard_map/turn/pallas_call | solution.py:52
  10.1 0.9 %outer_rows.1 = (bf16[256,512]{1,0:T(8,128)(2,1)S(1)}, bf16[256,512]{1,0:T(8,128)(2,1)S(1)}, bf16[640,128]{1,0:T(8,128)(2,1)S(1)}, f32[640,128]{1,0:T(8,128)S(1)}) custom-call(bf16[256,256]{1,0:T(8,128)(2,1)S(1)} %collective-permute-done.even_ref, bf16[272,256]{1,0:T(8,128)(2,1)S(1)} %collective-permute-done.2.odd_ref, ...), custom_call_target="tpu_custom_call" | custom-call | tf_op jit(solution)/shard_map/outer_rows/pallas_call | solution.py:633
  11.0 0.6 %collective-permute-start.4 = (bf16[640,128]{1,0:T(8,128)(2,1)S(1)}, bf16[640,128]{1,0:T(8,128)(2,1)S(1)}, u32[]{:S(2)}, u32[]{:S(2)}) collective-permute-start(bf16[640,128]{1,0:T(8,128)(2,1)S(1)} %get-tuple-element.57), channel_id=1, source_target_pairs={{0,1},{1,0},{2,3},{3,2},{4,5},{5,4},{6,7},{7,6},{8,9},{9,8},{10,11... | collective-permute-start | bytes 491528 | tf_op jit(solution)/shard_map/ppermute | solution.py:48
  11.6 1.0 %collective-permute-done.4.got_ref = bf16[640,128]{1,0:T(8,128)(2,1)S(1)} collective-permute-done((bf16[640,128]{1,0:T(8,128)(2,1)S(1)}, bf16[640,128]{1,0:T(8,128)(2,1)S(1)}, u32[]{:S(2)}, u32[]{:S(2)}) %collective-permute-start.4) | collective-permute-done | bytes 163872 | tf_op jit(solution)/shard_map/ppermute | solution.py:48
  12.6 4.3 %collective-permute-start.5 = (bf16[320,128]{1,0:T(8,128)(2,1)S(1)}, bf16[320,128]{1,0:T(8,128)(2,1)S(1)}, u32[]{:S(2)}, u32[]{:S(2)}) collective-permute-start(bf16[320,128]{1,0:T(8,128)(2,1)S(1)} %get-tuple-element.59), channel_id=1, source_target_pairs={{0,3},{1,4},{2,7},{3,0},{4,1},{5,6},{6,5},{7,2},{8,13},{9,10},{10,... | collective-permute-start | bytes 245768 | tf_op jit(solution)/shard_map/ppermute | solution.py:48
  17.0 2.6 %collective-permute-start.10 = (bf16[1,16,512]{2,1,0:T(8,128)(2,1)S(1)}, bf16[1,16,512]{2,1,0:T(8,128)(2,1)S(1)}, u32[]{:S(2)}, u32[]{:S(2)}) collective-permute-start(bf16[1,16,512]{2,1,0:T(8,128)(2,1)S(1)} %get-tuple-element.63), channel_id=1, source_target_pairs={{0,17},{1,16},{2,19},{3,18},{4,21},{5,20},{6,23},{7,22},{8,25},{9,... | collective-permute-start | bytes 49160 | tf_op jit(solution)/shard_map/ppermute | solution.py:48
  19.6 0.8 %collective-permute-start.6 = (bf16[160,128]{1,0:T(8,128)(2,1)S(1)}, bf16[160,128]{1,0:T(8,128)(2,1)S(1)}, u32[]{:S(2)}, u32[]{:S(2)}) collective-permute-start(bf16[160,128]{1,0:T(8,128)(2,1)S(1)} %get-tuple-element.61), channel_id=1, source_target_pairs={{0,5},{1,2},{2,1},{3,6},{4,7},{5,0},{6,3},{7,4},{8,11},{9,12},{10,... | collective-permute-start | bytes 122888 | tf_op jit(solution)/shard_map/ppermute | solution.py:48
  20.3 0.7 %collective-permute-done.10 = bf16[1,16,512]{2,1,0:T(8,128)(2,1)S(1)} collective-permute-done((bf16[1,16,512]{2,1,0:T(8,128)(2,1)S(1)}, bf16[1,16,512]{2,1,0:T(8,128)(2,1)S(1)}, u32[]{:S(2)}, u32[]{:S(2)}) %collective-permute-start.10) | collective-permute-done | bytes 16416 | tf_op jit(solution)/shard_map/ppermute | solution.py:48
  21.1 1.5 %collective-permute-start.11 = (bf16[2,16,512]{2,1,0:T(8,128)(2,1)S(1)}, bf16[2,16,512]{2,1,0:T(8,128)(2,1)S(1)}, u32[]{:S(2)}, u32[]{:S(2)}) collective-permute-start(bf16[2,16,512]{2,1,0:T(8,128)(2,1)S(1)} %bitcast.41), channel_id=1, source_target_pairs={{0,9},{1,8},{2,11},{3,10},{4,13},{5,12},{6,15},{7,14},{8,1},{9,0},... | collective-permute-start | bytes 98312 | tf_op jit(solution)/shard_map/ppermute | solution.py:48
  22.6 0.5 %collective-permute-done.6.got_ref = bf16[160,128]{1,0:T(8,128)(2,1)S(1)} collective-permute-done((bf16[160,128]{1,0:T(8,128)(2,1)S(1)}, bf16[160,128]{1,0:T(8,128)(2,1)S(1)}, u32[]{:S(2)}, u32[]{:S(2)}) %collective-permute-start.6) | collective-permute-done | bytes 40992 | tf_op jit(solution)/shard_map/ppermute | solution.py:48
  23.1 2.8 %collective-permute-start.7 = (bf16[160,128]{1,0:T(8,128)(2,1)S(1)}, bf16[160,128]{1,0:T(8,128)(2,1)S(1)}, u32[]{:S(2)}, u32[]{:S(2)}) collective-permute-start(bf16[160,128]{1,0:T(8,128)(2,1)S(1)} %add.3.keep_ref), channel_id=1, source_target_pairs={{0,17},{1,16},{2,19},{3,18},{4,21},{5,20},{6,23},{7,22},{8,25},{9,... | collective-permute-start | bytes 122888 | tf_op jit(solution)/shard_map/ppermute | solution.py:48
  25.8 1.2 %collective-permute-start.12 = (bf16[4,16,512]{2,1,0:T(8,128)(2,1)S(1)}, bf16[4,16,512]{2,1,0:T(8,128)(2,1)S(1)}, u32[]{:S(2)}, u32[]{:S(2)}) collective-permute-start(bf16[4,16,512]{2,1,0:T(8,128)(2,1)S(1)} %bitcast.36), channel_id=1, source_target_pairs={{0,3},{1,4},{2,7},{3,0},{4,1},{5,6},{6,5},{7,2},{8,13},{9,10},{10,... | collective-permute-start | bytes 196616 | tf_op jit(solution)/shard_map/ppermute | solution.py:48
  27.1 0.6 %collective-permute-done.7.got_ref = bf16[160,128]{1,0:T(8,128)(2,1)S(1)} collective-permute-done((bf16[160,128]{1,0:T(8,128)(2,1)S(1)}, bf16[160,128]{1,0:T(8,128)(2,1)S(1)}, u32[]{:S(2)}, u32[]{:S(2)}) %collective-permute-start.7) | collective-permute-done | bytes 40992 | tf_op jit(solution)/shard_map/ppermute | solution.py:48
  27.7 1.5 %collective-permute-start.8 = (bf16[160,128]{1,0:T(8,128)(2,1)S(1)}, bf16[160,128]{1,0:T(8,128)(2,1)S(1)}, u32[]{:S(2)}, u32[]{:S(2)}) collective-permute-start(bf16[160,128]{1,0:T(8,128)(2,1)S(1)} %add.4.keep_ref), channel_id=1, source_target_pairs={{0,9},{1,8},{2,11},{3,10},{4,13},{5,12},{6,15},{7,14},{8,1},{9,0},... | collective-permute-start | bytes 122888 | tf_op jit(solution)/shard_map/ppermute | solution.py:48
  29.2 0.4 collective-permute-done.12
  29.6 0.5 collective-permute-start.13
  30.1 1.3 %collective-permute-done.8.got_ref = bf16[160,128]{1,0:T(8,128)(2,1)S(1)} collective-permute-done((bf16[160,128]{1,0:T(8,128)(2,1)S(1)}, bf16[160,128]{1,0:T(8,128)(2,1)S(1)}, u32[]{:S(2)}, u32[]{:S(2)}) %collective-permute-start.8) | collective-permute-done | bytes 40992 | tf_op jit(solution)/shard_map/ppermute | solution.py:48
  31.4 0.4 collective-permute-start.9
  31.8 2.3 %collective-permute-done.13 = bf16[8,16,512]{2,1,0:T(8,128)(2,1)S(1)} collective-permute-done((bf16[8,16,512]{2,1,0:T(8,128)(2,1)S(1)}, bf16[8,16,512]{2,1,0:T(8,128)(2,1)S(1)}, u32[]{:S(2)}, u32[]{:S(2)}) %collective-permute-start.13) | collective-permute-done | bytes 131104 | tf_op jit(solution)/shard_map/ppermute | solution.py:48
  34.1 0.8 %collective-permute-done.9 = bf16[160,128]{1,0:T(8,128)(2,1)S(1)} collective-permute-done((bf16[160,128]{1,0:T(8,128)(2,1)S(1)}, bf16[160,128]{1,0:T(8,128)(2,1)S(1)}, u32[]{:S(2)}, u32[]{:S(2)}) %collective-permute-start.9) | collective-permute-done | bytes 40992 | tf_op jit(solution)/shard_map/ppermute | solution.py:48
  34.9 2.2 %collective-permute-start.14 = (bf16[320,128]{1,0:T(8,128)(2,1)S(1)}, bf16[320,128]{1,0:T(8,128)(2,1)S(1)}, u32[]{:S(2)}, u32[]{:S(2)}) collective-permute-start(bf16[320,128]{1,0:T(8,128)(2,1)S(1)} %bitcast.33), channel_id=1, source_target_pairs={{0,3},{1,4},{2,7},{3,0},{4,1},{5,6},{6,5},{7,2},{8,13},{9,10},{10,... | collective-permute-start | bytes 245768 | tf_op jit(solution)/shard_map/ppermute | solution.py:48
  37.1 1.0 %beyond.1 = (bf16[288,512]{1,0:T(8,128)(2,1)S(1)}, bf16[288,512]{1,0:T(8,128)(2,1)S(1)}) custom-call(bf16[8,128,256]{2,1,0:T(8,128)(2,1)S(1)} %copy-done.3, bf16[256,256]{1,0:T(8,128)(2,1)S(1)} %collective-permute-done.even_ref, bf16[272,256]{1,0:T(8,128)(2,1)S(1)} %collective-permute-done.2.odd_ref, ...), custom_call_target="tpu_custom_call" | custom-call | flops 8000000000 | bytes 100000 | tf_op jit(solution)/shard_map/beyond/pallas_call | solution.py:665
  38.2 0.5 %collective-permute-done.15.other_ref = bf16[16,16,512]{2,1,0:T(8,128)(2,1)S(1)} collective-permute-done((bf16[16,16,512]{2,1,0:T(8,128)(2,1)S(1)}, bf16[16,16,512]{2,1,0:T(8,128)(2,1)S(1)}, u32[]{:S(2)}, u32[]{:S(2)}) %collective-permute-start.15) | collective-permute-done | bytes 262176 | tf_op jit(solution)/shard_map/ppermute | solution.py:48
  38.7 0.5 %collective-permute-done.14 = bf16[320,128]{1,0:T(8,128)(2,1)S(1)} collective-permute-done((bf16[320,128]{1,0:T(8,128)(2,1)S(1)}, bf16[320,128]{1,0:T(8,128)(2,1)S(1)}, u32[]{:S(2)}, u32[]{:S(2)}) %collective-permute-start.14) | collective-permute-done | bytes 81952 | tf_op jit(solution)/shard_map/ppermute | solution.py:48
  39.3 0.5 %collective-permute-start.16 = (bf16[640,128]{1,0:T(8,128)(2,1)S(1)}, bf16[640,128]{1,0:T(8,128)(2,1)S(1)}, u32[]{:S(2)}, u32[]{:S(2)}) collective-permute-start(bf16[640,128]{1,0:T(8,128)(2,1)S(1)} %bitcast.26), channel_id=1, source_target_pairs={{0,1},{1,0},{2,3},{3,2},{4,5},{5,4},{6,7},{7,6},{8,9},{9,8},{10,11... | collective-permute-start | bytes 491528 | tf_op jit(solution)/shard_map/ppermute | solution.py:48
  40.1 0.7 %collective-permute-done.16.other_ref = bf16[640,128]{1,0:T(8,128)(2,1)S(1)} collective-permute-done((bf16[640,128]{1,0:T(8,128)(2,1)S(1)}, bf16[640,128]{1,0:T(8,128)(2,1)S(1)}, u32[]{:S(2)}, u32[]{:S(2)}) %collective-permute-start.16) | collective-permute-done | bytes 163872 | tf_op jit(solution)/shard_map/ppermute | solution.py:48
  40.8 4.4 %grad_conv.1 = (f32[16,512]{1,0:T(8,128)}, bf16[1024,256]{1,0:T(8,128)(2,1)}) custom-call(bf16[640,128]{1,0:T(8,128)(2,1)S(1)} %bitcast.27, bf16[640,128]{1,0:T(8,128)(2,1)S(1)} %collective-permute-done.16.other_ref, f32[512,512]{1,0:T(8,128)S(1)} %prepare.1.both_ref, bf16[768,512]{1,0:T(8,128)(2,1)S(1)} %get-tuple-element.79.in_feat_ref, ...), custom_call_target="tpu_custom_call" | custom-call | tf_op jit(solution)/shard_map/grad_conv/pallas_call | solution.py:703
  (32 shorter events, 0.7 us)
Async XLA Ops:
  0.6 4.2 %copy-start.1 = (f32[16,512]{1,0:T(8,128)S(1)}, f32[16,512]{1,0:T(8,128)}, u32[]{:S(2)}) copy-start(f32[16,512]{1,0:T(8,128)} %target_ref.1) | copy-start | bytes 98308
  0.6 1.0 %copy-start.2 = (bf16[8,128,256]{2,1,0:T(8,128)(2,1)S(1)}, bf16[8,128,256]{2,1,0:T(8,128)(2,1)}, u32[]{:S(2)}) copy-start(bf16[8,128,256]{2,1,0:T(8,128)(2,1)} %own_ref.3) | copy-start | bytes 1572868
  1.7 4.3 %copy-start = (bf16[3,3,256,512]{3,2,1,0:T(8,128)(2,1)S(1)}, bf16[3,3,256,512]{3,2,1,0:T(8,128)(2,1)}, u32[]{:S(2)}) copy-start(bf16[3,3,256,512]{3,2,1,0:T(8,128)(2,1)} %param.5) | copy-start | bytes 7077892
  1.7 4.3 %copy-start.3 = (bf16[8,128,256]{2,1,0:T(8,128)(2,1)S(1)}, bf16[8,128,256]{2,1,0:T(8,128)(2,1)}, u32[]{:S(2)}) copy-start(bf16[8,128,256]{2,1,0:T(8,128)(2,1)} %own_ref.3) | copy-start | bytes 1572868
  1.7 4.3 %copy-start.4 = (bf16[512]{0:T(512)(128)(2,1)S(1)}, bf16[512]{0:T(512)(128)(2,1)}, u32[]{:S(2)}) copy-start(bf16[512]{0:T(512)(128)(2,1)} %bias_ref.1) | copy-start | bytes 3076
  1.7 3.1 %collective-permute-start.1 = (bf16[2,8,256]{2,1,0:T(8,128)(2,1)S(1)}, bf16[2,8,256]{2,1,0:T(8,128)(2,1)S(1)}, u32[]{:S(2)}, u32[]{:S(2)}) collective-permute-start(bf16[2,8,256]{2,1,0:T(8,128)(2,1)S(1)} %get-tuple-element.46), channel_id=1, source_target_pairs={{0,1},{1,0},{2,3},{3,2},{4,5},{5,4},{6,7},{7,6},{8,9},{9,8},{10,11... | collective-permute-start | bytes 24584 | tf_op jit(solution)/shard_map/ppermute | solution.py:581
  2.3 7.8 %collective-permute-start = (bf16[256,256]{1,0:T(8,128)(2,1)S(1)}, bf16[256,256]{1,0:T(8,128)(2,1)S(1)}, u32[]{:S(2)}, u32[]{:S(2)}) collective-permute-start(bf16[256,256]{1,0:T(8,128)(2,1)S(1)} %get-tuple-element.44), channel_id=1, source_target_pairs={{0,2},{1,3},{2,0},{3,1},{4,6},{5,7},{6,4},{7,5},{8,10},{9,11},{10,... | collective-permute-start | bytes 393224 | tf_op jit(solution)/shard_map/ppermute | solution.py:31
  4.9 5.2 %collective-permute-start.3 = (bf16[16,256]{1,0:T(8,128)(2,1)S(1)}, bf16[16,256]{1,0:T(8,128)(2,1)S(1)}, u32[]{:S(2)}, u32[]{:S(2)}) collective-permute-start(bf16[16,256]{1,0:T(8,128)(2,1)S(1)} %get-tuple-element.48), channel_id=1, source_target_pairs={{0,2},{1,3},{2,0},{3,1},{4,6},{5,7},{6,4},{7,5},{8,10},{9,11},{10,... | collective-permute-start | bytes 24584 | tf_op jit(solution)/shard_map/ppermute | solution.py:31
  6.0 4.1 %collective-permute-start.2 = (bf16[272,256]{1,0:T(8,128)(2,1)S(1)}, bf16[272,256]{1,0:T(8,128)(2,1)S(1)}, u32[]{:S(2)}, u32[]{:S(2)}) collective-permute-start(bf16[272,256]{1,0:T(8,128)(2,1)S(1)} %get-tuple-element.47), channel_id=1, source_target_pairs={{0,1},{1,0},{2,4},{3,5},{4,2},{5,3},{6,8},{7,9},{8,6},{9,7},{10,12... | collective-permute-start | bytes 417800 | tf_op jit(solution)/shard_map/ppermute | solution.py:31
  11.0 1.6 %collective-permute-start.4 = (bf16[640,128]{1,0:T(8,128)(2,1)S(1)}, bf16[640,128]{1,0:T(8,128)(2,1)S(1)}, u32[]{:S(2)}, u32[]{:S(2)}) collective-permute-start(bf16[640,128]{1,0:T(8,128)(2,1)S(1)} %get-tuple-element.57), channel_id=1, source_target_pairs={{0,1},{1,0},{2,3},{3,2},{4,5},{5,4},{6,7},{7,6},{8,9},{9,8},{10,11... | collective-permute-start | bytes 491528 | tf_op jit(solution)/shard_map/ppermute | solution.py:48
  12.6 6.9 %collective-permute-start.5 = (bf16[320,128]{1,0:T(8,128)(2,1)S(1)}, bf16[320,128]{1,0:T(8,128)(2,1)S(1)}, u32[]{:S(2)}, u32[]{:S(2)}) collective-permute-start(bf16[320,128]{1,0:T(8,128)(2,1)S(1)} %get-tuple-element.59), channel_id=1, source_target_pairs={{0,3},{1,4},{2,7},{3,0},{4,1},{5,6},{6,5},{7,2},{8,13},{9,10},{10,... | collective-permute-start | bytes 245768 | tf_op jit(solution)/shard_map/ppermute | solution.py:48
  17.0 4.1 %collective-permute-start.10 = (bf16[1,16,512]{2,1,0:T(8,128)(2,1)S(1)}, bf16[1,16,512]{2,1,0:T(8,128)(2,1)S(1)}, u32[]{:S(2)}, u32[]{:S(2)}) collective-permute-start(bf16[1,16,512]{2,1,0:T(8,128)(2,1)S(1)} %get-tuple-element.63), channel_id=1, source_target_pairs={{0,17},{1,16},{2,19},{3,18},{4,21},{5,20},{6,23},{7,22},{8,25},{9,... | collective-permute-start | bytes 49160 | tf_op jit(solution)/shard_map/ppermute | solution.py:48
  19.6 3.5 %collective-permute-start.6 = (bf16[160,128]{1,0:T(8,128)(2,1)S(1)}, bf16[160,128]{1,0:T(8,128)(2,1)S(1)}, u32[]{:S(2)}, u32[]{:S(2)}) collective-permute-start(bf16[160,128]{1,0:T(8,128)(2,1)S(1)} %get-tuple-element.61), channel_id=1, source_target_pairs={{0,5},{1,2},{2,1},{3,6},{4,7},{5,0},{6,3},{7,4},{8,11},{9,12},{10,... | collective-permute-start | bytes 122888 | tf_op jit(solution)/shard_map/ppermute | solution.py:48
  21.1 4.8 %collective-permute-start.11 = (bf16[2,16,512]{2,1,0:T(8,128)(2,1)S(1)}, bf16[2,16,512]{2,1,0:T(8,128)(2,1)S(1)}, u32[]{:S(2)}, u32[]{:S(2)}) collective-permute-start(bf16[2,16,512]{2,1,0:T(8,128)(2,1)S(1)} %bitcast.41), channel_id=1, source_target_pairs={{0,9},{1,8},{2,11},{3,10},{4,13},{5,12},{6,15},{7,14},{8,1},{9,0},... | collective-permute-start | bytes 98312 | tf_op jit(solution)/shard_map/ppermute | solution.py:48
  23.1 4.6 %collective-permute-start.7 = (bf16[160,128]{1,0:T(8,128)(2,1)S(1)}, bf16[160,128]{1,0:T(8,128)(2,1)S(1)}, u32[]{:S(2)}, u32[]{:S(2)}) collective-permute-start(bf16[160,128]{1,0:T(8,128)(2,1)S(1)} %add.3.keep_ref), channel_id=1, source_target_pairs={{0,17},{1,16},{2,19},{3,18},{4,21},{5,20},{6,23},{7,22},{8,25},{9,... | collective-permute-start | bytes 122888 | tf_op jit(solution)/shard_map/ppermute | solution.py:48
  25.8 3.8 %collective-permute-start.12 = (bf16[4,16,512]{2,1,0:T(8,128)(2,1)S(1)}, bf16[4,16,512]{2,1,0:T(8,128)(2,1)S(1)}, u32[]{:S(2)}, u32[]{:S(2)}) collective-permute-start(bf16[4,16,512]{2,1,0:T(8,128)(2,1)S(1)} %bitcast.36), channel_id=1, source_target_pairs={{0,3},{1,4},{2,7},{3,0},{4,1},{5,6},{6,5},{7,2},{8,13},{9,10},{10,... | collective-permute-start | bytes 196616 | tf_op jit(solution)/shard_map/ppermute | solution.py:48
  27.7 3.6 %collective-permute-start.8 = (bf16[160,128]{1,0:T(8,128)(2,1)S(1)}, bf16[160,128]{1,0:T(8,128)(2,1)S(1)}, u32[]{:S(2)}, u32[]{:S(2)}) collective-permute-start(bf16[160,128]{1,0:T(8,128)(2,1)S(1)} %add.4.keep_ref), channel_id=1, source_target_pairs={{0,9},{1,8},{2,11},{3,10},{4,13},{5,12},{6,15},{7,14},{8,1},{9,0},... | collective-permute-start | bytes 122888 | tf_op jit(solution)/shard_map/ppermute | solution.py:48
  29.6 4.5 %collective-permute-start.13 = (bf16[8,16,512]{2,1,0:T(8,128)(2,1)S(1)}, bf16[8,16,512]{2,1,0:T(8,128)(2,1)S(1)}, u32[]{:S(2)}, u32[]{:S(2)}) collective-permute-start(bf16[8,16,512]{2,1,0:T(8,128)(2,1)S(1)} %bitcast.30), channel_id=1, source_target_pairs={{0,5},{1,2},{2,1},{3,6},{4,7},{5,0},{6,3},{7,4},{8,11},{9,12},{10,... | collective-permute-start | bytes 393224 | tf_op jit(solution)/shard_map/ppermute | solution.py:48
  31.4 3.5 %collective-permute-start.9 = (bf16[160,128]{1,0:T(8,128)(2,1)S(1)}, bf16[160,128]{1,0:T(8,128)(2,1)S(1)}, u32[]{:S(2)}, u32[]{:S(2)}) collective-permute-start(bf16[160,128]{1,0:T(8,128)(2,1)S(1)} %add.5), channel_id=1, source_target_pairs={{0,5},{1,2},{2,1},{3,6},{4,7},{5,0},{6,3},{7,4},{8,11},{9,12},{10,... | collective-permute-start | bytes 122888 | tf_op jit(solution)/shard_map/ppermute | solution.py:48
  34.9 4.4 %collective-permute-start.14 = (bf16[320,128]{1,0:T(8,128)(2,1)S(1)}, bf16[320,128]{1,0:T(8,128)(2,1)S(1)}, u32[]{:S(2)}, u32[]{:S(2)}) collective-permute-start(bf16[320,128]{1,0:T(8,128)(2,1)S(1)} %bitcast.33), channel_id=1, source_target_pairs={{0,3},{1,4},{2,7},{3,0},{4,1},{5,6},{6,5},{7,2},{8,13},{9,10},{10,... | collective-permute-start | bytes 245768 | tf_op jit(solution)/shard_map/ppermute | solution.py:48
  37.1 1.5 %collective-permute-start.15 = (bf16[16,16,512]{2,1,0:T(8,128)(2,1)S(1)}, bf16[16,16,512]{2,1,0:T(8,128)(2,1)S(1)}, u32[]{:S(2)}, u32[]{:S(2)}) collective-permute-start(bf16[16,16,512]{2,1,0:T(8,128)(2,1)S(1)} %bitcast.28), channel_id=1, source_target_pairs={{0,1},{1,0},{2,3},{3,2},{4,5},{5,4},{6,7},{7,6},{8,9},{9,8},{10,11... | collective-permute-start | bytes 786440 | tf_op jit(solution)/shard_map/ppermute | solution.py:48
  39.3 1.5 %collective-permute-start.16 = (bf16[640,128]{1,0:T(8,128)(2,1)S(1)}, bf16[640,128]{1,0:T(8,128)(2,1)S(1)}, u32[]{:S(2)}, u32[]{:S(2)}) collective-permute-start(bf16[640,128]{1,0:T(8,128)(2,1)S(1)} %bitcast.26), channel_id=1, source_target_pairs={{0,1},{1,0},{2,3},{3,2},{4,5},{5,4},{6,7},{7,6},{8,9},{9,8},{10,11... | collective-permute-start | bytes 491528 | tf_op jit(solution)/shard_map/ppermute | solution.py:48
